TPU v7x, 128 devices: a whole 4x4x4 slice. The times are simulated.
128 devices in a mesh: gx: 8 (over y, x_lo), gy: 8 (over x_hi, z), ga: 2 (over core).
Axes of the slice: x: 4 (x_hi: 2, x_lo: 2; x = x_hi * 2 + x_lo), y: 4, z: 4, core: 2. Of those that a mesh axis runs over, the one named last changes fastest.
Arguments:
- fields: float32 [5, 16, 128, 2048], P(None, 'ga', 'gx', 'gy'), may hold values from -6 to 6
- stiffness: float32 [16, 128, 2048], P('ga', 'gx', 'gy'), may hold values from 0.25 to 4
- lift_weight: float32 [5, 32], replicated, may hold values from -2.5 to 2.5
- lift_bias: float32 [32], replicated, may hold values from -3 to 3
- mix_weight: bfloat16 [32, 32], replicated, may hold values from -0.5 to 0.5
- spectral_weight: float32 [8, 32, 32, 32, 128], P('ga', 'gy', None, 'gx'), may hold values from -0.48 to 0.48
- output_bias: float32 [32], replicated, may hold values from -3 to 3
Outputs:
- layer_out: bfloat16 [16, 32, 64, 1024], P('ga', None, 'gx', 'gy')
All inputs are finite; a program needn't handle non-finite values.
Results may differ from a plain program's by a relative error of at most 0.01.
Values may be sent and summed in bfloat16 or wider, within the bound.
No kernel may reach another device: no remote copies, remote signals or barrier semaphores. Data moves between devices by JAX's collectives and lax.ppermute only.
A program may use at most 128 MiB of HBM per device.

v0:
```python
import math

import jax
import jax.numpy as jnp
from jax import lax
from jax.sharding import PartitionSpec as P

STEPS = 3
MX = 32
MY = 64
MZ = 8


courant_half = 0.1
smooth_half = 0.15
mean_flow = (0.3, -0.2, 0.1)
highest = lax.Precision.HIGHEST


def padded_2(block, sides, width):
    for axis, dim in sides:
        count = lax.axis_size(axis)
        forward = [(i, i + 1) for i in range(count - 1)]
        forward.append((count - 1, 0))
        backward = [(target, source) for source, target in forward]
        low = lax.ppermute(
            lax.slice_in_dim(block, block.shape[dim] - width, None, axis=dim), axis, forward
        )
        high = lax.ppermute(lax.slice_in_dim(block, 0, width, axis=dim), axis, backward)
        block = jnp.concatenate([low, block, high], axis=dim)
    return block


def step_interior(padded, stiff_part):
    center = padded[:, 1:-1, 1:-1, 1:-1]
    upper_depth = padded[:, 2:, 1:-1, 1:-1]
    lower_depth = padded[:, :-2, 1:-1, 1:-1]
    upper_east = padded[:, 1:-1, 2:, 1:-1]
    lower_east = padded[:, 1:-1, :-2, 1:-1]
    upper_north = padded[:, 1:-1, 1:-1, 2:]
    lower_north = padded[:, 1:-1, 1:-1, :-2]
    slope_depth = upper_depth - lower_depth
    slope_east = upper_east - lower_east
    slope_north = upper_north - lower_north
    curvature = (
        upper_depth
        + lower_depth
        + upper_east
        + lower_east
        + upper_north
        + lower_north
        - 6.0 * center
    )
    transport = mean_flow[0] * slope_east + mean_flow[1] * slope_north + mean_flow[2] * slope_depth
    diverge = slope_east[1] + slope_north[2] + slope_depth[3]
    coupling = jnp.stack(
        [diverge, slope_east[4], slope_north[4], slope_depth[4], stiff_part * diverge]
    )
    return center - courant_half * (transport + coupling) + smooth_half * curvature


def coarsen(fields_now):
    extent = fields_now.shape
    blocks = fields_now.reshape(extent[0], extent[1], extent[2] // 2, 2, extent[3] // 2, 2)
    return 0.25 * (
        blocks[:, :, :, 0, :, 0]
        + blocks[:, :, :, 1, :, 0]
        + blocks[:, :, :, 0, :, 1]
        + blocks[:, :, :, 1, :, 1]
    )


def angles(frequencies, points, length):
    product = jnp.mod(frequencies[:, None] * points[None, :], length)
    return product.astype(jnp.float32) * (2.0 * math.pi / length)


def centered(number):
    return jnp.arange(number, dtype=jnp.int32) - number // 2


def forward_east_table(points, length, mode_count):
    phases = angles(centered(mode_count), points, length)
    factor = 1.0 / math.sqrt(length)
    return (jnp.stack([jnp.cos(phases).T, -jnp.sin(phases).T], axis=1) * factor).astype(
        jnp.bfloat16
    )


def forward_north_table(points, length, mode_count):
    phases = angles(centered(mode_count), points, length)
    factor = 1.0 / math.sqrt(length)
    cosines = jnp.cos(phases).T * factor
    sines = jnp.sin(phases).T * factor
    return jnp.stack(
        [jnp.concatenate([cosines, -sines], axis=1), jnp.concatenate([sines, cosines], axis=1)],
        axis=0,
    )


def inverse_north_table(points, length, mode_count):
    phases = angles(centered(mode_count), points, length)
    factor = 1.0 / math.sqrt(length)
    cosines = jnp.cos(phases) * factor
    sines = jnp.sin(phases) * factor
    return jnp.concatenate(
        [jnp.stack([cosines, sines], axis=1), jnp.stack([-sines, cosines], axis=1)], axis=0
    )


def inverse_east_table(points, length, mode_count):
    phases = angles(centered(mode_count), points, length)
    factor = 1.0 / math.sqrt(length)
    return jnp.stack([jnp.cos(phases) * factor, -jnp.sin(phases) * factor], axis=1)


def forward_depth_blocks(values, points, frequencies, length):
    slot_count = frequencies.shape[0]
    phases = angles(frequencies.reshape(-1), points, length).reshape(
        slot_count, frequencies.shape[1], points.shape[0]
    )
    factor = 1.0 / math.sqrt(length)
    cosines = jnp.cos(phases) * factor
    sines = jnp.sin(phases) * factor
    halfway = values.shape[-1] // 2
    real_in = values[..., :halfway]
    imag_in = values[..., halfway:]
    real_part = jnp.einsum("zcrbn,rkz->rkcbn", real_in, cosines, precision=highest) + jnp.einsum(
        "zcrbn,rkz->rkcbn", imag_in, sines, precision=highest
    )
    imag_part = jnp.einsum("zcrbn,rkz->rkcbn", imag_in, cosines, precision=highest) - jnp.einsum(
        "zcrbn,rkz->rkcbn", real_in, sines, precision=highest
    )
    return jnp.concatenate([real_part, imag_part], axis=-1)


def mix_channels(coeffs, weight):
    halfway = coeffs.shape[-1] // 2
    real_in = coeffs[..., :halfway]
    imag_in = coeffs[..., halfway:]
    weight_real = weight[..., :halfway]
    weight_imag = weight[..., halfway:]
    real_part = jnp.einsum(
        "kcmn,kmcon->komn", real_in, weight_real, precision=highest
    ) - jnp.einsum("kcmn,kmcon->komn", imag_in, weight_imag, precision=highest)
    imag_part = jnp.einsum(
        "kcmn,kmcon->komn", imag_in, weight_real, precision=highest
    ) + jnp.einsum("kcmn,kmcon->komn", real_in, weight_imag, precision=highest)
    return jnp.concatenate([real_part, imag_part], axis=-1)


def inverse_depth(values, frequencies, points, length):
    phases = angles(frequencies, points, length)
    factor = 1.0 / math.sqrt(length)
    cosines = jnp.cos(phases) * factor
    sines = jnp.sin(phases) * factor
    halfway = values.shape[-1] // 2
    real_in = values[..., :halfway]
    imag_in = values[..., halfway:]
    real_part = jnp.einsum("komn,kz->zomn", real_in, cosines, precision=highest) - jnp.einsum(
        "komn,kz->zomn", imag_in, sines, precision=highest
    )
    imag_part = jnp.einsum("komn,kz->zomn", imag_in, cosines, precision=highest) + jnp.einsum(
        "komn,kz->zomn", real_in, sines, precision=highest
    )
    return jnp.concatenate([real_part, imag_part], axis=-1)


def shards(fields, stiffness, lift_weight, lift_bias, mix_weight, spectral_weight, output_bias):
    east_tiles = lax.axis_size("gx")
    north_tiles = lax.axis_size("gy")
    depth_groups = lax.axis_size("ga")
    fields_now = fields
    for repeat in range(STEPS):
        padded = padded_2(fields_now, (("gx", 2), ("gy", 3), ("ga", 1)), 1)
        fields_now = step_interior(padded, stiffness)
    filtered = coarsen(fields_now)
    pre_lift = (
        jnp.einsum("fzxy,fc->zcxy", filtered, lift_weight, precision=highest)
        + lift_bias[None, :, None, None]
    )
    lifted = jax.nn.gelu(pre_lift, approximate=True).astype(jnp.bfloat16)
    depth_local = lifted.shape[0]
    length_east = lifted.shape[2] * east_tiles
    length_north = lifted.shape[3] * north_tiles
    length_depth = depth_local * depth_groups
    east_points = jnp.arange(length_east, dtype=jnp.int32)
    north_points = jnp.arange(length_north, dtype=jnp.int32)
    table_east = forward_east_table(east_points, length_east, MX)
    table_north = forward_north_table(north_points, length_north, MY)
    planes = lax.all_to_all(
        lax.all_to_all(lifted, "gx", split_axis=1, concat_axis=2, tiled=True),
        "gy",
        split_axis=0,
        concat_axis=3,
        tiled=True,
    )
    east_modes = jnp.einsum(
        "zcxy,xpm->zcpmy", planes, table_east, preferred_element_type=jnp.float32
    )
    north_modes = jnp.einsum("zcpmy,pyq->zcmq", east_modes, table_north, precision=highest)
    plane_count = planes.shape[0]
    depth_points = (
        lax.axis_index("ga") * depth_local
        + lax.axis_index("gy") * plane_count
        + jnp.arange(plane_count, dtype=jnp.int32)
    )
    block_east = MX // north_tiles
    block_depth = MZ // depth_groups
    grouped = north_modes.reshape(
        plane_count, north_modes.shape[1], north_tiles, block_east, 2 * MY
    )
    owners = jnp.arange(1 * lax.axis_size(("gy", "ga")), dtype=jnp.int32)
    picked = jnp.take(grouped, owners // depth_groups, axis=2)
    frequencies = (owners % depth_groups)[:, None] * block_depth + jnp.arange(
        block_depth, dtype=jnp.int32
    )[None, :]
    coeffs = lax.psum_scatter(
        forward_depth_blocks(picked, depth_points, frequencies, length_depth).astype(jnp.bfloat16),
        ("gy", "ga"),
        scatter_dimension=0,
        tiled=True,
    ).astype(jnp.float32)[0]
    mixed_modes = mix_channels(lax.all_gather(coeffs, "gx", axis=1, tiled=True), spectral_weight)
    own_frequencies = lax.axis_index("ga") * coeffs.shape[0] + jnp.arange(
        coeffs.shape[0], dtype=jnp.int32
    )
    points = jnp.arange(depth_local * lax.axis_size("ga"), dtype=jnp.int32)
    back_depth = lax.psum_scatter(
        inverse_depth(mixed_modes, own_frequencies, points, length_depth),
        "ga",
        scatter_dimension=0,
        tiled=True,
    )
    back_north = jnp.einsum(
        "zomq,qpy->zompy",
        back_depth,
        inverse_north_table(north_points, length_north, MY),
        precision=highest,
    )
    all_modes = lax.all_to_all(back_north, "gy", split_axis=4, concat_axis=2, tiled=True)
    spectral = jnp.einsum(
        "zompy,mpx->zoxy",
        all_modes,
        inverse_east_table(east_points, length_east, MX),
        precision=highest,
    ).astype(jnp.bfloat16)
    spectral = lax.all_to_all(spectral, "gx", split_axis=2, concat_axis=1, tiled=True)
    direct = jnp.einsum("zcxy,co->zoxy", lifted, mix_weight, preferred_element_type=jnp.float32)
    summed = direct + output_bias[None, :, None, None] + spectral.astype(jnp.float32)
    return jax.nn.gelu(summed, approximate=True).astype(jnp.bfloat16)


def solution(mesh):
    placed = (
        P(None, "ga", "gx", "gy"),
        P("ga", "gx", "gy"),
        P(),
        P(),
        P(),
        P("ga", "gy", None, "gx", None),
        P(),
    )
    return jax.shard_map(
        shards, mesh=mesh, in_specs=placed, out_specs=P("ga", None, "gx", "gy"), check_vma=False
    )
```

profile of v0, /device:TPU:4, one launch (start us, length us, event | category | flops | bytes accessed | tf_op | source)
XLA Modules:
  0.0 481.4 jit_solution(12632177929340682965)
XLA Ops:
  6.5 1.2 fusion.133
  7.7 3.7 collective-permute-start
  11.5 1.7 collective-permute-done
  13.1 4.4 collective-permute-done.1
  17.6 1.2 pad_maximum_fusion
  19.0 4.3 collective-permute-start.2
  23.3 9.0 %collective-permute-done.2 = f32[5,8,18,1]{3,2,1,0:T(8,128)S(1)} collective-permute-done((f32[5,8,18,1]{3,2,1,0:T(8,128)S(1)}, f32[5,8,18,1]{3,2,1,0:T(8,128)S(1)}, u32[]{:S(2)}, u32[]{:S(2)}) %collective-permute-start.2) | collective-permute-done | bytes 2912 | tf_op jit(solution)/shard_map/ppermute | solution.py:29
  32.4 5.8 %collective-permute-done.3 = f32[5,8,18,1]{3,2,1,0:T(8,128)S(1)} collective-permute-done((f32[5,8,18,1]{3,2,1,0:T(8,128)S(1)}, f32[5,8,18,1]{3,2,1,0:T(8,128)S(1)}, u32[]{:S(2)}, u32[]{:S(2)}) %collective-permute-start.3) | collective-permute-done | bytes 2912 | tf_op jit(solution)/shard_map/ppermute | solution.py:26
  40.8 1.2 multiply_add_fusion.2
  43.0 1.1 collective-permute-start.7
  44.2 2.1 collective-permute-done.6
  46.3 2.8 collective-permute-done.7
  49.6 2.0 collective-permute-start.9
  51.6 9.9 %collective-permute-done.8 = f32[5,8,18,1]{3,2,1,0:T(8,128)S(1)} collective-permute-done((f32[5,8,18,1]{3,2,1,0:T(8,128)S(1)}, f32[5,8,18,1]{3,2,1,0:T(8,128)S(1)}, u32[]{:S(2)}, u32[]{:S(2)}) %collective-permute-start.8) | collective-permute-done | bytes 2912 | tf_op jit(solution)/shard_map/ppermute | solution.py:29
  61.5 3.7 collective-permute-done.9
  67.8 1.2 multiply_add_fusion.1
  69.4 1.7 collective-permute-start.13
  71.2 2.1 collective-permute-done.12
  73.3 2.2 collective-permute-done.13
  76.0 2.2 collective-permute-start.15
  78.1 9.8 %collective-permute-done.14 = f32[5,8,18,1]{3,2,1,0:T(8,128)S(1)} collective-permute-done((f32[5,8,18,1]{3,2,1,0:T(8,128)S(1)}, f32[5,8,18,1]{3,2,1,0:T(8,128)S(1)}, u32[]{:S(2)}, u32[]{:S(2)}) %collective-permute-start.14) | collective-permute-done | bytes 2912 | tf_op jit(solution)/shard_map/ppermute | solution.py:29
  88.0 3.9 collective-permute-done.15
  94.5 1.2 multiply_add_fusion
  95.6 5.5 %copy.39 = f32[5,8,16,256]{1,3,2,0:T(8,128)} copy(f32[5,8,16,256]{3,2,1,0:T(8,128)S(1)} %multiply_add_fusion) | data formatting | bytes 1310720 | tf_op jit(solution)/shard_map/add | solution.py:59
  101.1 10.9 %fusion = f32[5,8,8,1,128,1]{1,5,4,3,2,0:T(1,128)S(1)} fusion(f32[5,8,8,2,128,2]{1,5,4,3,2,0:T(2,128)} %bitcast.176), kind=kLoop, calls=%fused_computation.2 | loop fusion | flops 163840 | bytes 819200 | tf_op jit(solution)/shard_map/mul | solution.py:65
  112.1 1.1 copy.40
  113.2 1.3 fusion.13
  116.4 3.5 all-to-all-start
  119.9 2.1 fusion.47
  122.3 8.2 %all-to-all-done = bf16[8,32,8,128]{3,2,0,1:T(8,128)(2,1)S(1)} async-done(((bf16[8,32,8,128]{3,2,0,1:T(8,128)(2,1)}), bf16[8,32,8,128]{3,2,0,1:T(8,128)(2,1)S(1)}, u32[]{:S(2)}, u32[]{:S(2)}) %all-to-all-start) | async-done | bytes 524320 | tf_op jit(solution)/shard_map/all_to_all | solution.py:192
  131.5 5.9 %all-to-all-start.1 = ((bf16[8,4,64,128]{3,2,1,0:T(8,128)(2,1)}), bf16[8,4,64,128]{3,2,1,0:T(8,128)(2,1)S(1)}, u32[]{:S(2)}, u32[]{:S(2)}) async-start(bf16[8,4,64,128]{3,2,1,0:T(8,128)(2,1)} %bitcast.173), calls=%async_computation.1 | async-start | bytes 1048576 | tf_op jit(solution)/shard_map/all_to_all | solution.py:191
  137.9 8.0 %all-to-all-done.1 = bf16[8,4,64,128]{3,2,1,0:T(8,128)(2,1)S(1)} async-done(((bf16[8,4,64,128]{3,2,1,0:T(8,128)(2,1)}), bf16[8,4,64,128]{3,2,1,0:T(8,128)(2,1)S(1)}, u32[]{:S(2)}, u32[]{:S(2)}) %all-to-all-start.1) | async-done | bytes 524320 | tf_op jit(solution)/shard_map/all_to_all | solution.py:191
  147.1 1.6 convolution_bitcast_fusion.2
  151.8 134.7 %all-reduce.3.cloned.1.call-done = bf16[16,4,4,4,128]{4,3,2,1,0:T(4,128)(2,1)} async-done(((bf16[16,4,4,4,128]{4,3,2,1,0:T(4,128)(2,1)}), bf16[16,4,4,4,128]{4,3,2,1,0:T(4,128)(2,1)}) %all-reduce.3.cloned.1.call-update) | async-done | bytes 262160
  286.6 1.3 dynamic-slice_convert_fusion
  287.9 28.9 %all-gather = f32[1,4,32,4,128]{4,3,2,1,0:T(4,128)S(1)} all-gather(f32[1,4,4,4,128]{4,3,2,1,0:T(4,128)S(1)} %dynamic-slice_convert_fusion), channel_id=2, replica_groups=mesh['gx'=8,'gy'=8,'ga'=2] {'gx'}, dimensions={2}, use_global_device_ids=true | all-gather | bytes 294912 | tf_op jit(solution)/shard_map/all_gather | solution.py:224
  317.1 1.4 multiply_reduce_fusion.3
  321.3 1.1 sine_multiply_fusion.1
  322.4 7.2 %reduce-scatter.2.cloned.1.call-done = f32[8,4,4,128]{3,0,2,1:T(8,128)} async-done(((f32[16,4,4,128]{3,0,2,1:T(8,128)}), f32[8,4,4,128]{3,0,2,1:T(8,128)}) %reduce-scatter.2.cloned.1.call-update) | async-done | bytes 65552 | tf_op jit(solution)/shard_map/reduce_scatter | solution.py:229
  329.7 1.8 fusion.24
  331.5 17.0 %copy.48 = f32[8,4,4,2,1024]{0,3,2,1,4:T(2,128)} copy(f32[8,4,4,2,1024]{4,0,3,2,1:T(8,128)S(1)} %fusion.24) | data formatting | bytes 2097152 | tf_op jit(solution)/shard_map/zomq,qpy->zompy/dot_general | solution.py:235
  348.6 28.9 %reshape.560 = f32[8,1,32768]{2,1,0:T(1,128)} reshape(f32[1024,4,4,2,8]{4,3,2,1,0:T(2,128)} %bitcast.174) | data formatting | bytes 2097152
  377.5 7.8 %all-to-all-start.2 = ((f32[8,1,32768]{2,1,0:T(1,128)}), f32[8,1,32768]{2,1,0:T(1,128)S(1)}, u32[]{:S(2)}, u32[]{:S(2)}) async-start(f32[8,1,32768]{2,1,0:T(1,128)} %reshape.560), calls=%async_computation.3 | async-start | bytes 2097152 | tf_op jit(solution)/shard_map/all_to_all | solution.py:241
  385.4 14.2 %all-to-all-done.2 = f32[8,1,32768]{2,1,0:T(1,128)S(1)} async-done(((f32[8,1,32768]{2,1,0:T(1,128)}), f32[8,1,32768]{2,1,0:T(1,128)S(1)}, u32[]{:S(2)}, u32[]{:S(2)}) %all-to-all-start.2) | async-done | bytes 1048608 | tf_op jit(solution)/shard_map/all_to_all | solution.py:241
  400.1 3.3 reduce.8
  403.4 32.2 %reshape.561 = f32[1024,4,4,2,8]{4,3,2,1,0:T(2,128)} reshape(f32[8,32768]{1,0:T(8,128)S(1)} %reduce.8) | data formatting | bytes 2097152
  435.6 20.6 %copy.49 = f32[8,4,4,2,8,128]{5,2,4,3,1,0:T(4,128)S(1)} copy(f32[8,4,4,2,8,128]{0,3,2,1,5,4:T(2,128)} %bitcast.175) | data formatting | bytes 2097152 | tf_op jit(solution)/shard_map/all_to_all | solution.py:241
  457.7 14.7 %all_to_all.60 = bf16[8,4,64,128]{3,1,0,2:T(4,128)(2,1)S(1)} all-to-all(bf16[8,4,64,128]{3,1,0,2:T(4,128)(2,1)S(1)} %copy.50), channel_id=1, replica_groups=mesh['gx'=8,'gy'=8,'ga'=2] {'gx'}, dimensions={2} | all-to-all | bytes 1048576 | tf_op jit(solution)/shard_map/all_to_all | solution.py:248
  (111 shorter events, 24.8 us)
Async XLA Ops:
  6.5 466.1 %copy-start = (bf16[32,32]{1,0:T(8,128)(2,1)S(1)}, bf16[32,32]{1,0:T(8,128)(2,1)}, u32[]{:S(2)}) copy-start(bf16[32,32]{1,0:T(8,128)(2,1)} %param.11) | copy-start | bytes 6148
  6.5 31.7 %copy-start.1 = (f32[5,8,16,256]{3,2,1,0:T(8,128)S(1)}, f32[5,8,16,256]{3,2,1,0:T(8,128)}, u32[]{:S(2)}) copy-start(f32[5,8,16,256]{3,2,1,0:T(8,128)} %param.7) | copy-start | bytes 1966084
  7.7 5.4 %collective-permute-start = (f32[5,8,1,256]{3,2,1,0:T(1,128)S(1)}, f32[5,8,1,256]{3,2,1,0:T(1,128)S(1)}, u32[]{:S(2)}, u32[]{:S(2)}) collective-permute-start(f32[5,8,1,256]{3,2,1,0:T(1,128)S(1)} %get-tuple-element.34), channel_id=1, source_target_pairs={{16,0},{32,16},{48,32},{64,48},{80,64},{96,80},{112,96},{0,112},{1... | collective-permute-start | bytes 122888 | tf_op jit(solution)/shard_map/ppermute | solution.py:29
  11.5 6.1 %collective-permute-start.1 = (f32[5,8,1,256]{3,2,1,0:T(1,128)S(1)}, f32[5,8,1,256]{3,2,1,0:T(1,128)S(1)}, u32[]{:S(2)}, u32[]{:S(2)}) collective-permute-start(f32[5,8,1,256]{3,2,1,0:T(1,128)S(1)} %get-tuple-element.33), channel_id=1, source_target_pairs={{0,16},{16,32},{32,48},{48,64},{64,80},{80,96},{96,112},{112,0},{1... | collective-permute-start | bytes 122888 | tf_op jit(solution)/shard_map/ppermute | solution.py:26
  19.0 13.4 %collective-permute-start.2 = (f32[5,8,18,1]{3,2,1,0:T(8,128)S(1)}, f32[5,8,18,1]{3,2,1,0:T(8,128)S(1)}, u32[]{:S(2)}, u32[]{:S(2)}) collective-permute-start(f32[5,8,18,1]{3,2,1,0:T(8,128)S(1)} %get-tuple-element.22), channel_id=1, source_target_pairs={{2,0},{4,2},{6,4},{8,6},{10,8},{12,10},{14,12},{0,14},{3,1},{5,3},... | collective-permute-start | bytes 8648 | tf_op jit(solution)/shard_map/ppermute | solution.py:29
  23.3 14.9 %collective-permute-start.3 = (f32[5,8,18,1]{3,2,1,0:T(8,128)S(1)}, f32[5,8,18,1]{3,2,1,0:T(8,128)S(1)}, u32[]{:S(2)}, u32[]{:S(2)}) collective-permute-start(f32[5,8,18,1]{3,2,1,0:T(8,128)S(1)} %get-tuple-element.21), channel_id=1, source_target_pairs={{0,2},{2,4},{4,6},{6,8},{8,10},{10,12},{12,14},{14,0},{1,3},{3,5},... | collective-permute-start | bytes 8648 | tf_op jit(solution)/shard_map/ppermute | solution.py:26
  38.5 1.5 collective-permute-start.4
  38.6 1.7 collective-permute-start.5
  39.8 1.0 copy-start.3
  42.1 4.2 collective-permute-start.6
  43.0 6.1 %collective-permute-start.7 = (f32[5,8,1,256]{3,2,1,0:T(1,128)S(1)}, f32[5,8,1,256]{3,2,1,0:T(1,128)S(1)}, u32[]{:S(2)}, u32[]{:S(2)}) collective-permute-start(f32[5,8,1,256]{3,2,1,0:T(1,128)S(1)} %get-tuple-element.31), channel_id=1, source_target_pairs={{0,16},{16,32},{32,48},{48,64},{64,80},{80,96},{96,112},{112,0},{1... | collective-permute-start | bytes 122888 | tf_op jit(solution)/shard_map/ppermute | solution.py:26
  49.5 12.0 %collective-permute-start.8 = (f32[5,8,18,1]{3,2,1,0:T(8,128)S(1)}, f32[5,8,18,1]{3,2,1,0:T(8,128)S(1)}, u32[]{:S(2)}, u32[]{:S(2)}) collective-permute-start(f32[5,8,18,1]{3,2,1,0:T(8,128)S(1)} %get-tuple-element.20), channel_id=1, source_target_pairs={{2,0},{4,2},{6,4},{8,6},{10,8},{12,10},{14,12},{0,14},{3,1},{5,3},... | collective-permute-start | bytes 8648 | tf_op jit(solution)/shard_map/ppermute | solution.py:29
  49.6 15.6 %collective-permute-start.9 = (f32[5,8,18,1]{3,2,1,0:T(8,128)S(1)}, f32[5,8,18,1]{3,2,1,0:T(8,128)S(1)}, u32[]{:S(2)}, u32[]{:S(2)}) collective-permute-start(f32[5,8,18,1]{3,2,1,0:T(8,128)S(1)} %get-tuple-element.19), channel_id=1, source_target_pairs={{0,2},{2,4},{4,6},{6,8},{8,10},{10,12},{12,14},{14,0},{1,3},{3,5},... | collective-permute-start | bytes 8648 | tf_op jit(solution)/shard_map/ppermute | solution.py:26
  65.5 1.5 collective-permute-start.10
  65.6 1.7 collective-permute-start.11
  69.1 4.2 collective-permute-start.12
  69.4 6.1 %collective-permute-start.13 = (f32[5,8,1,256]{3,2,1,0:T(1,128)S(1)}, f32[5,8,1,256]{3,2,1,0:T(1,128)S(1)}, u32[]{:S(2)}, u32[]{:S(2)}) collective-permute-start(f32[5,8,1,256]{3,2,1,0:T(1,128)S(1)} %get-tuple-element.29), channel_id=1, source_target_pairs={{0,16},{16,32},{32,48},{48,64},{64,80},{80,96},{96,112},{112,0},{1... | collective-permute-start | bytes 122888 | tf_op jit(solution)/shard_map/ppermute | solution.py:26
  75.9 12.1 %collective-permute-start.14 = (f32[5,8,18,1]{3,2,1,0:T(8,128)S(1)}, f32[5,8,18,1]{3,2,1,0:T(8,128)S(1)}, u32[]{:S(2)}, u32[]{:S(2)}) collective-permute-start(f32[5,8,18,1]{3,2,1,0:T(8,128)S(1)} %get-tuple-element.18), channel_id=1, source_target_pairs={{2,0},{4,2},{6,4},{8,6},{10,8},{12,10},{14,12},{0,14},{3,1},{5,3},... | collective-permute-start | bytes 8648 | tf_op jit(solution)/shard_map/ppermute | solution.py:29
  76.0 15.9 %collective-permute-start.15 = (f32[5,8,18,1]{3,2,1,0:T(8,128)S(1)}, f32[5,8,18,1]{3,2,1,0:T(8,128)S(1)}, u32[]{:S(2)}, u32[]{:S(2)}) collective-permute-start(f32[5,8,18,1]{3,2,1,0:T(8,128)S(1)} %get-tuple-element.17), channel_id=1, source_target_pairs={{0,2},{2,4},{4,6},{6,8},{8,10},{10,12},{12,14},{14,0},{1,3},{3,5},... | collective-permute-start | bytes 8648 | tf_op jit(solution)/shard_map/ppermute | solution.py:26
  92.1 1.5 collective-permute-start.16
  92.2 1.7 collective-permute-start.17
  112.0 1.2 copy-start.6
  112.1 1.2 copy-start.7
  114.6 0.8 copy-start.4
  116.4 14.2 %all-to-all-start = ((bf16[8,32,8,128]{3,2,0,1:T(8,128)(2,1)}), bf16[8,32,8,128]{3,2,0,1:T(8,128)(2,1)S(1)}, u32[]{:S(2)}, u32[]{:S(2)}) async-start(bf16[8,32,8,128]{3,2,0,1:T(8,128)(2,1)} %copy.42), calls=%async_computation | async-start | bytes 1048576 | tf_op jit(solution)/shard_map/all_to_all | solution.py:192
  131.5 14.4 %all-to-all-start.1 = ((bf16[8,4,64,128]{3,2,1,0:T(8,128)(2,1)}), bf16[8,4,64,128]{3,2,1,0:T(8,128)(2,1)S(1)}, u32[]{:S(2)}, u32[]{:S(2)}) async-start(bf16[8,4,64,128]{3,2,1,0:T(8,128)(2,1)} %bitcast.173), calls=%async_computation.1 | async-start | bytes 1048576 | tf_op jit(solution)/shard_map/all_to_all | solution.py:191
  137.4 149.2 %all-reduce.3.cloned.1.call-start = ((), (), s32[]{:S(2)}) async-start(), calls=%async_computation.6 | async-start | bytes 524288
  147.1 4.1 copy-start.9
  149.4 167.7 %copy-start.2 = (f32[4,4,32,4,128]{4,3,2,1,0:T(4,128)S(1)}, f32[4,4,32,4,128]{4,3,2,1,0:T(4,128)}, u32[]{:S(2)}) copy-start(f32[4,4,32,4,128]{4,3,2,1,0:T(4,128)} %param.12) | copy-start | bytes 3145732
  151.1 178.5 %reduce-scatter.2.cloned.1.call-start = ((), (), s32[]{:S(2)}) async-start(), calls=%async_computation.5 | async-start | bytes 196608 | tf_op jit(solution)/shard_map/reduce_scatter | solution.py:229
  377.5 22.1 %all-to-all-start.2 = ((f32[8,1,32768]{2,1,0:T(1,128)}), f32[8,1,32768]{2,1,0:T(1,128)S(1)}, u32[]{:S(2)}, u32[]{:S(2)}) async-start(f32[8,1,32768]{2,1,0:T(1,128)} %reshape.560), calls=%async_computation.3 | async-start | bytes 2097152 | tf_op jit(solution)/shard_map/all_to_all | solution.py:241
  456.2 16.5 %copy-start.5 = (bf16[8,32,8,128]{3,1,2,0:T(8,128)(2,1)S(1)}, bf16[8,32,8,128]{3,1,2,0:T(8,128)(2,1)}, u32[]{:S(2)}) copy-start(bf16[8,32,8,128]{3,1,2,0:T(8,128)(2,1)} %copy-done.4) | copy-start | bytes 1572868
  456.2 16.5 %copy-start.8 = (f32[32]{0:T(128)S(1)}, f32[32]{0:T(128)}, u32[]{:S(2)}) copy-start(f32[32]{0:T(128)} %param.13) | copy-start | bytes 388
Sparse Core Ops, SparseCore 0:
  151.2 135.2 all-reduce.2
  321.4 8.2 reduce-scatter.1
where the time goes:
time: 491 us; the launch traced here: 481 us
  waiting for transfers between devices  232 us (47%)
  local copies, waits for them, and re-layouts  115 us (23%)
  blocking collectives  43.6 us (9%)
  starting transfers between devices  35.7 us (7%)
  other arithmetic  32.6 us (7%)
  between operations  14.2 us (3%)
  matrix products  8.66 us (2%)
    unnamed x3, waiting for transfers between devices  135 us
    unnamed x35, local copies, waits for them, and re-layouts  63 us
    ppermute x9, waiting for transfers between devices, padded_2(): lax.ppermute(lax.slice_in_dim(block, 0, width, axis=dim), axis, backward)  35.4 us
    all_gather x1, blocking collectives, shards(): lax.all_gather(coeffs, 'gx', axis=1, tiled=True)  28.9 us
    ppermute x9, waiting for transfers between devices, padded_2(): lax.ppermute(lax.slice_in_dim(block, block.shape[dim] - width, None, axis...  23.7 us
    all_to_all x2, local copies, waits for them, and re-layouts, shards(): lax.all_to_all(back_north, 'gy', split_axis=4, concat_axis=2, tiled=True)  21.1 us
    dot_general x1, local copies, waits for them, and re-layouts, shards(): jnp.einsum('zomq,qpy->zompy', back_depth, inverse_north_table(north_point...  17 us
    all_to_all x1, blocking collectives, shards(): lax.all_to_all(spectral, 'gx', split_axis=2, concat_axis=1, tiled=True)  14.7 us
  transfers between devices with their start and end apart: 23, of which 23 were waited for; matrix products, arithmetic and copies ran while one was open for 1% of the time, Pallas kernels for 0%

commit v1 on v0

v1 whole, which is shorter than its diff:
```python
import functools
import math

import jax
import jax.numpy as jnp
import numpy as np
from jax import lax
from jax.experimental import pallas as pl
from jax.experimental.pallas import tpu as pltpu
from jax.sharding import PartitionSpec as P

NZ, C, MX, MY, MZ, GX, GY = 16, 32, 32, 64, 8, 64, 1024
ZL, XL, YL = 8, 16, 256
F32, BF16 = jnp.float32, jnp.bfloat16
ROOT = math.sqrt(2.0 / math.pi)
VMEM = pl.BlockSpec(memory_space=pltpu.VMEM)
SMEM = pl.BlockSpec(memory_space=pltpu.SMEM)


def cos_sin(freq, points, length):
    turn = np.mod(np.outer(freq, points), length) * (2.0 * np.pi / length)
    return np.cos(turn), np.sin(turn)


def split(table):
    table = np.asarray(table, np.float32)
    high = table.astype(jnp.bfloat16)
    low = (table - high.astype(np.float32)).astype(jnp.bfloat16)
    return high, low


@functools.cache
def tables():
    out = {}
    pairs = np.zeros((YL, YL // 2), np.float32)
    pairs[np.arange(YL), np.arange(YL) // 2] = 0.25
    out["pairs"] = pairs.astype(jnp.bfloat16)
    ky = np.arange(MY) - MY // 2
    cy, sy = cos_sin(ky, np.arange(GY), GY)
    rows = np.concatenate([cy, -sy]) / math.sqrt(GY)
    out["yf"] = np.concatenate(split(rows))
    rows = np.concatenate([cy, -sy]) / math.sqrt(GY)
    high, low = split(rows)
    out["yi"] = np.concatenate([high, high, low])
    kz = np.arange(MZ)
    cz, sz = (t / math.sqrt(NZ) for t in cos_sin(kz, np.arange(ZL), NZ))
    eye = np.eye(C)

    def kron_f(t):
        return np.einsum("kz,cd->czkd", t, eye).reshape(C * ZL, 2, 4 * C)

    zf = np.zeros((2, C * ZL, 2, 2, 4 * C))
    zf[0, :, :, 0], zf[1, :, :, 0] = kron_f(cz), kron_f(sz)
    zf[1, :, :, 1], zf[0, :, :, 1] = kron_f(cz), -kron_f(sz)
    out["zf"] = np.stack(split(zf.reshape(2 * C * ZL, 8 * 2 * C)))
    zi = np.zeros((2, 2, 4, C, 2, ZL, C))
    for half in range(2):
        for k in range(4):
            for z in range(ZL):
                c, s = cz[4 * half + k, z] * eye, sz[4 * half + k, z] * eye
                zi[half, 0, k, :, 0, z], zi[half, 1, k, :, 0, z] = c, -s
                zi[half, 1, k, :, 1, z], zi[half, 0, k, :, 1, z] = c, s
    out["zi"] = np.stack(split(zi.reshape(16 * C, 2 * ZL * C)))
    kx = np.arange(MX) - MX // 2
    cx, sx = cos_sin(kx, np.arange(GX), GX)
    cr = (cx / 8.0).astype(np.float32).astype(jnp.bfloat16).astype(np.float64)
    sr = (-sx / 8.0).astype(np.float32).astype(jnp.bfloat16).astype(np.float64)
    cr, sr = cr.reshape(8, 4, GX), sr.reshape(8, 4, GX)
    xf = np.zeros((2, 8, 4, 4, 4, GX, 2, 2))
    for k in range(4):
        for a in range(2):
            sign = -1.0 if (k * a) % 2 else 1.0
            xf[0, :, k, :, k, :, a, 0] = sign * cr
            xf[0, :, k, :, k, :, a, 1] = -sign * sr
            xf[1, :, k, :, k, :, a, 0] = sign * sr
            xf[1, :, k, :, k, :, a, 1] = sign * cr
    out["xf"] = xf.reshape(256, 1024).astype(np.float32).astype(jnp.bfloat16)
    ex = np.zeros((4, 4, C, C, 4), np.float32)
    for k in range(4):
        for c in range(C):
            ex[k, k, c, c] = 1.0
    out["ex"] = ex.reshape(4, 128, 128).astype(jnp.bfloat16)
    rm = np.zeros((8, C, 4, 4, 8, 4), np.float32)
    for i in range(8):
        for o in range(4):
            rm[i, :, o, :, i, o] = 1.0
    out["rm"] = rm.reshape(1024, 128).astype(jnp.bfloat16)
    mask = np.zeros((2, 8, 4, 4, 4, C), np.float32)
    for k in range(4):
        mask[:, :, k, :, k] = 1.0
    out["mask"] = mask.reshape(256, 128)
    ic, is_ = (cx / 8.0).T.reshape(GX, 8, 1, 4), (sx / 8.0).T.reshape(GX, 8, 1, 4)
    xi = np.zeros((2, GX, 2, 8, 4, 4))
    xi[0, :, 0], xi[0, :, 1] = ic, -is_
    xi[1, :, 0], xi[1, :, 1] = is_, ic
    out["xi"] = np.stack(split(xi.reshape(128, 256)))
    return out


def halves(value):
    high = value.astype(BF16)
    return high, (value - high.astype(F32)).astype(BF16)


def dot(a, b, contract=((1,), (0,))):
    return lax.dot_general(a, b, (contract, ((), ())), preferred_element_type=F32)


def dot3(a, b_ref):
    high, low = halves(a)
    return dot(high, b_ref[0]) + dot(low, b_ref[0]) + dot(high, b_ref[1])


def gelu(v):
    return 0.5 * v * (1.0 + jnp.tanh(ROOT * (v + 0.044715 * (v * v * v))))


def call(kernel, outs, in_specs, scratch=(), mib=16, flops=10**7, size=2**20):
    return pl.pallas_call(
        kernel,
        out_shape=[jax.ShapeDtypeStruct(s, d) for s, d in outs],
        in_specs=in_specs,
        out_specs=[VMEM] * len(outs),
        scratch_shapes=list(scratch),
        compiler_params=pltpu.CompilerParams(vmem_limit_bytes=mib << 20),
        cost_estimate=pl.CostEstimate(flops=flops, bytes_accessed=size, transcendentals=0),
    )


NEEDED = list(range(8)) + [8, 9, 14, 15]


def pack_x(f, s, fp, sp, low, high, rows):
    for field in range(6):
        for which, whole in enumerate(((s, sp) if field == 5 else (f.at[field], fp.at[field]))):
            for h in range(2):
                rows[which, field, h] = whole[:, 128 * h : 128 * h + 128]
    for field in range(6):
        for h in range(2):
            for which, count in ((0, 3), (1, 2)):
                for d in range(count):
                    at = 24 * which + 8 * d
                    first = rows[which, field, h, pl.ds(d, 8, stride=XL), :]
                    last = rows[which, field, h, pl.ds(XL - 1 - d, 8, stride=XL), :]
                    low[field, h, at : at + 8, :] = first
                    high[field, h, at : at + 8, :] = last


def pack_y(f, s, fp, sp, up, down, xh, low, high):
    xh[...] = jnp.zeros_like(xh)
    lane = lax.broadcasted_iota(jnp.int32, (24, 128), 1) // 8
    for field in range(6):
        for h in range(2):
            for base, at, count in ((0, 0, 3), (64, 24, 2)):
                for d in range(count):
                    take = slice(at + 8 * d, at + 8 * d + 8)
                    xh[field, h, pl.ds(base + d, 8, stride=8), :] = up[field, h, take, :]
                    xh[field, h, pl.ds(base + 7 - d, 8, stride=8), :] = down[field, h, take, :]
        lows = jnp.zeros((24, 128), F32)
        highs = jnp.zeros((24, 128), F32)
        for slot in NEEDED:
            own, other = (s, sp) if field == 5 else (f.at[field], fp.at[field])
            ref = own if slot < 8 else other
            part = slice(16 * (slot % 8), 16 * (slot % 8) + 16)
            edge = slice(8 * slot, 8 * slot + 8)
            here = lane == slot
            first = jnp.concatenate([ref[part, :128], xh[field, 0, edge, :]], axis=0)
            last = jnp.concatenate([ref[part, 128:], xh[field, 1, edge, :]], axis=0)
            lows = jnp.where(here, pltpu.roll(first, (8 * slot) % 128, 1), lows)
            highs = jnp.where(here, pltpu.roll(last, (8 * slot + 8) % 128, 1), highs)
        low[field] = lows
        high[field] = highs


def stencil(f, s, fp, sp, xh, ylow, yhigh, pairs, wide, narrow, a, b, stiff, last, sums):
    near = lax.broadcasted_iota(jnp.int32, (24, 128), 1) < 64
    for zi in range(14):
        slot = zi - 3 if 3 <= zi < 11 else (13 + zi if zi < 3 else zi - 3)
        part = slice(16 * (slot % 8), 16 * (slot % 8) + 16)
        for field in range(6):
            if field == 5 and zi in (0, 13):
                continue
            own, other = (s, sp) if field == 5 else (f, fp)
            ref = own if slot < 8 else other
            to = stiff.at[zi] if field == 5 else a.at[field, zi]
            to[0:16, 0:256] = ref[part, :] if field == 5 else ref[field, part, :]
            for h in range(2):
                edge = xh[field, h, 8 * slot : 8 * slot + 8, :]
                to[16:24, 128 * h : 128 * h + 128] = edge
            to[:, 256:384] = jnp.where(
                near,
                pltpu.roll(ylow[field], (128 - 8 * slot) % 128, 1),
                pltpu.roll(yhigh[field], (120 - 8 * slot) % 128, 1),
            )

    def advance(src, zi):
        new, east, north, depth = [], [], [], []
        for field in range(5):
            mid = src[field, zi]
            up, down = src[field, zi + 1], src[field, zi - 1]
            xp, xm = pltpu.roll(mid, 23, 0), pltpu.roll(mid, 1, 0)
            yp, ym = pltpu.roll(mid, 383, 1), pltpu.roll(mid, 1, 1)
            total = 0.1 * mid + 0.12 * xp + 0.18 * xm + 0.17 * yp + 0.13 * ym
            new.append(total + 0.14 * up + 0.16 * down)
            east.append(xp - xm if field in (1, 4) else None)
            north.append(yp - ym if field in (2, 4) else None)
            depth.append(up - down if field in (3, 4) else None)
        div = 0.1 * (east[1] + north[2] + depth[3])
        new[0] = new[0] - div
        new[1] = new[1] - 0.1 * east[4]
        new[2] = new[2] - 0.1 * north[4]
        new[3] = new[3] - 0.1 * depth[4]
        new[4] = new[4] - stiff[zi] * div
        return new

    for step, (src, dst) in enumerate(((a, b), (b, a), (a, None))):
        first, end = 1 + step, 13 - step

        def body(zi, carry, src=src, dst=dst):
            new = advance(src, zi)
            for field in range(5):
                if dst is None:
                    rows = pl.ds(pl.multiple_of((zi - 3) * 16, 16), 16)
                    for h in range(2):
                        last[field, h, rows, :] = new[field][0:16, 128 * h : 128 * h + 128]
                else:
                    dst[field, zi] = new[field]
            return carry

        lax.fori_loop(first, end, body, 0)

    for x in range(8):
        for field in range(5):
            at = 40 * x + 8 * field
            for h in range(2):
                even = last[field, h, pl.ds(2 * x, 8, stride=16), :]
                odd = last[field, h, pl.ds(2 * x + 1, 8, stride=16), :]
                sums[at : at + 8, 128 * h : 128 * h + 128] = even + odd
    value = sums[...]
    high = value.astype(BF16)
    rest = value - high.astype(F32)
    mid, low = halves(rest)
    table = pairs[...]
    mean = dot(high, table) + dot(mid, table) + dot(low, table)
    wide[...] = mean
    mean = mean.reshape(8, 40, 128)
    narrow[...] = jnp.concatenate([mean, jnp.zeros((8, 8, 128), F32)], axis=1).astype(BF16)


def lift_rows(values, weight, bias):
    rows = []
    for c in range(C):
        v = bias[c] + values[0] * weight[0, c]
        for field in range(1, 5):
            v = v + values[field] * weight[field, c]
        rows.append(gelu(v))
    return jnp.concatenate(rows, axis=0).astype(BF16)


def pointwise(wide, weight, bias, mix, obias, out):
    def body(z, carry):
        values = [wide[pl.ds(8 * field + z, 8, stride=40), :] for field in range(5)]
        out[z] = dot(mix[...], lift_rows(values, weight, bias)) + obias[...]
        return carry

    lax.fori_loop(0, ZL, body, 0)


def forward(got, weight, bias, yf, zf, out, lifted):
    for j in range(8):
        block = got[j].astype(F32)
        values = [block[8 * field : 8 * field + 8] for field in range(5)]
        lifted[:, 128 * j : 128 * j + 128] = lift_rows(values, weight, bias)
    modes = dot(yf[...], lifted[...], ((1,), (1,)))
    modes = modes[:128] + modes[128:]
    modes = jnp.concatenate([modes[:64], modes[64:]], axis=1)
    result = dot3(modes, zf)
    for part in range(4):
        out[:, part, :] = result[:, 128 * part : 128 * part + 128]


def mix_modes(got, weights, xf, ex, rm, mask, xi, out):
    high, low = halves(got[...])
    spread_high = jnp.concatenate([dot(high, ex[k]).astype(BF16) for k in range(4)], axis=0)
    spread_low = jnp.concatenate([dot(low, ex[k]).astype(BF16) for k in range(4)], axis=0)
    modes = dot(xf[...], spread_high) + dot(xf[...], spread_low)
    real, imag = modes[:128], modes[128:]
    total = jnp.zeros((256, 128), F32)
    for i in range(8):
        wr = weights[8 * i : 8 * i + 8, 0:16, :].astype(F32).reshape(128, 128)
        wi = weights[8 * i : 8 * i + 8, 16:32, :].astype(F32).reshape(128, 128)
        part = jnp.concatenate([wr * real - wi * imag, wr * imag + wi * real], axis=0)
        p_high, p_low = halves(part)
        table = rm[128 * i : 128 * i + 128, :]
        total = total + dot(p_high, table) + dot(p_low, table)
    total = total * mask[...]
    t_high, t_low = halves(total)
    back = dot(xi[0], t_high) + dot(xi[0], t_low) + dot(xi[1], t_high)
    odd = (lax.broadcasted_iota(jnp.int32, (64, 128), 1) // 32) % 2 == 1
    for ri in range(2):
        value = back[64 * ri : 64 * ri + 64]
        out[:, ri, :] = value
        out[:, 2 + ri, :] = jnp.where(odd, -value, value)


def inverse(got, zi, yi, out):
    modes = jnp.concatenate([got[:, part, :] for part in range(4)], axis=1)
    by_z = dot3(modes, zi)
    by_z = jnp.concatenate([by_z[:, :256], by_z[:, 256:]], axis=0)
    high, low = halves(by_z)
    stacked = jnp.concatenate([high, low, high], axis=0)
    for j in range(8):
        block = dot(stacked, yi[:, 128 * j : 128 * j + 128], ((0,), (0,)))
        out[j] = block.astype(BF16)


def finish(got, direct, out, rows):
    for x in range(8):
        rows[256 * x : 256 * x + 256, :] = got[x].astype(F32)

    def body(z, carry):
        for o in range(C):
            spectral = rows[pl.ds(C * z + o, 8, stride=256), :]
            total = direct[z, 8 * o : 8 * o + 8, :] + spectral
            out[z, o] = gelu(total).astype(BF16)
        return carry

    lax.fori_loop(0, ZL, body, 0)


def turn_weights(weights, out):
    for chunk in range(16):
        turned = weights[128 * chunk : 128 * chunk + 128, :].T
        for ri in range(2):
            out[:, 16 * ri + chunk, :] = turned[64 * ri : 64 * ri + 64]


def shards(fields, stiffness, lift_weight, lift_bias, mix_weight, spectral_weight, output_bias):
    table = {name: jnp.asarray(value) for name, value in tables().items()}
    everyone = ("gx", "gy", "ga")

    def exchange(value, axis):
        return lax.all_to_all(value, axis, split_axis=0, concat_axis=0, tiled=True)

    def shift(value, axis, by):
        return lax.ppermute(value, axis, [(i, (i + by) % 8) for i in range(8)])

    [turned] = call(turn_weights, [((64, 32, 128), F32)], [VMEM], mib=8)(
        spectral_weight.reshape(2048, 128)
    )
    weights = exchange(turned, ("gx", "gy"))

    f = fields.reshape(5, 128, 256)
    s = stiffness.reshape(128, 256)
    swap = [(0, 1), (1, 0)]
    fp, sp = lax.ppermute(f, "ga", swap), lax.ppermute(s, "ga", swap)
    message = ((6, 2, 40, 128), F32)
    copied = [pltpu.VMEM((2, 6, 2, 128, 128), F32)]
    low, high = call(pack_x, [message, message], [VMEM] * 4, copied)(f, s, fp, sp)
    up, down = shift(low, "gx", -1), shift(high, "gx", 1)
    message = ((6, 24, 128), F32)
    xh, low, high = call(pack_y, [((6, 2, 128, 128), F32), message, message], [VMEM] * 6)(
        f, s, fp, sp, up, down
    )
    ylow, yhigh = shift(low, "gy", -1), shift(high, "gy", 1)
    wide, narrow = call(
        stencil,
        [((320, 128), F32), ((8, 48, 128), BF16)],
        [VMEM] * 8,
        [
            pltpu.VMEM((5, 14, 24, 384), F32),
            pltpu.VMEM((5, 14, 24, 384), F32),
            pltpu.VMEM((14, 24, 384), F32),
            pltpu.VMEM((5, 2, 128, 128), F32),
            pltpu.VMEM((320, 256), F32),
        ],
        mib=24,
    )(f, s, fp, sp, xh, ylow, yhigh, table["pairs"])

    columns = exchange(narrow, "gy")
    spread = jnp.einsum("co,xy->oxcy", mix_weight, jnp.eye(8, dtype=BF16)).reshape(256, 256)
    obias = jnp.broadcast_to(jnp.repeat(output_bias, 8)[:, None], (256, 128))
    [direct] = call(
        pointwise, [((8, 256, 128), F32)], [VMEM, SMEM, SMEM, VMEM, VMEM], flops=3 * 10**8
    )(wide, lift_weight, lift_bias, spread, obias)

    [modes] = call(
        forward,
        [((64, 4, 128), F32)],
        [VMEM, SMEM, SMEM, VMEM, VMEM],
        [pltpu.VMEM((256, 1024), BF16)],
    )(columns, lift_weight, lift_bias, table["yf"], table["zf"])
    modes = exchange(modes.reshape(128, 2, 128), everyone)
    [mixed] = call(mix_modes, [((64, 4, 128), F32)], [VMEM] * 7, mib=24)(
        modes.reshape(256, 128),
        weights,
        table["xf"],
        table["ex"],
        table["rm"],
        table["mask"],
        table["xi"],
    )
    mixed = exchange(mixed.reshape(128, 2, 128), everyone)
    [spectral] = call(inverse, [((8, 256, 128), BF16)], [VMEM] * 3)(
        mixed.reshape(64, 4, 128), table["zi"], table["yi"]
    )
    spectral = exchange(spectral, "gy")
    [out] = call(
        finish, [((8, 32, 8, 128), BF16)], [VMEM] * 2, [pltpu.VMEM((2048, 128), F32)]
    )(spectral, direct)
    return out


def solution(mesh):
    placed = (
        P(None, "ga", "gx", "gy"),
        P("ga", "gx", "gy"),
        P(),
        P(),
        P(),
        P("ga", "gy", None, "gx", None),
        P(),
    )
    return jax.shard_map(
        shards, mesh=mesh, in_specs=placed, out_specs=P("ga", None, "gx", "gy"), check_vma=False
    )
```

time: 491 us -> 128 us (0.26)
  the two profiles are of different devices: /device:TPU:4 before, /device:TPU:1 now
where the time goes in v1:
time: 128 us; the launch traced here: 127 us
  waiting for transfers between devices  37.6 us (29%)
  blocking collectives  32.3 us (25%)
  starting transfers between devices  23 us (18%)
  Pallas kernels  20 us (16%)
  local copies, waits for them, and re-layouts  12.2 us (10%)
  other arithmetic  1.57 us (1%)
    all_to_all x2, blocking collectives, exchange(): return lax.all_to_all(value, axis, split_axis=0, concat_axis=0, tiled=True)  32.3 us
    ppermute x4, waiting for transfers between devices, shift(): return lax.ppermute(value, axis, [(i, (i + by) % 8) for i in range(8)])  18 us
    all_to_all x3, waiting for transfers between devices, exchange(): return lax.all_to_all(value, axis, split_axis=0, concat_axis=0, tiled=True)  17.4 us
    all_to_all x3, starting transfers between devices, exchange(): return lax.all_to_all(value, axis, split_axis=0, concat_axis=0, tiled=True)  11.5 us
    ppermute x4, starting transfers between devices, shift(): return lax.ppermute(value, axis, [(i, (i + by) % 8) for i in range(8)])  10.1 us
    unnamed x39, local copies, waits for them, and re-layouts  7.87 us
    pallas_call x1, Pallas kernels, shards(): call(stencil, [((320, 128), F32), ((8, 48, 128), BF16)], [VMEM] * 8, [plt...  7.15 us
    reshape x1, local copies, waits for them, and re-layouts, shards(): jnp.einsum('co,xy->oxcy', mix_weight, jnp.eye(8, dtype=BF16))  4.05 us
  transfers between devices with their start and end apart: 9, of which 8 were waited for; matrix products, arithmetic and copies ran while one was open for 5% of the time, Pallas kernels for 5%

profile of v1, /device:TPU:1, one launch (start us, length us, event | category | flops | bytes accessed | tf_op | source)
XLA Modules:
  0.0 126.9 jit_solution(7551915305596192510)
XLA Ops:
  0.0 1.4 %collective-permute-start = (f32[5,128,256]{2,1,0:T(8,128)}, f32[5,128,256]{2,1,0:T(8,128)S(1)}, u32[]{:S(2)}, u32[]{:S(2)}) collective-permute-start(f32[5,128,256]{2,1,0:T(8,128)} %bitcast.11), channel_id=1, source_target_pairs={{0,1},{1,0},{2,3},{3,2},{4,5},{5,4},{6,7},{7,6},{8,9},{9,8},{10,11... | collective-permute-start | bytes 1966088 | tf_op jit(solution)/shard_map/ppermute | solution.py:356
  1.4 2.1 %collective-permute-done.1.sp = f32[128,256]{1,0:T(8,128)S(1)} collective-permute-done((f32[128,256]{1,0:T(8,128)}, f32[128,256]{1,0:T(8,128)S(1)}, u32[]{:S(2)}, u32[]{:S(2)}) %collective-permute-start.1) | collective-permute-done | bytes 131104 | tf_op jit(solution)/shard_map/ppermute | solution.py:356
  3.5 0.0 collective-permute-done.fp
  3.6 1.1 copy-done
  4.6 0.9 copy-done.2
  5.5 0.3 shard_map.163
  5.8 3.8 %collective-permute-start.2 = (f32[6,2,40,128]{3,2,1,0:T(8,128)S(1)}, f32[6,2,40,128]{3,2,1,0:T(8,128)S(1)}, u32[]{:S(2)}, u32[]{:S(2)}) collective-permute-start(f32[6,2,40,128]{3,2,1,0:T(8,128)S(1)} %get-tuple-element.12), channel_id=1, source_target_pairs={{0,112},{16,0},{32,16},{48,32},{64,48},{80,64},{96,80},{112,96},{1... | collective-permute-start | bytes 737288 | tf_op jit(solution)/shard_map/ppermute | solution.py:346
  9.6 0.0 collective-permute-start.3
  9.6 5.0 %collective-permute-done.2.up = f32[6,2,40,128]{3,2,1,0:T(8,128)S(1)} collective-permute-done((f32[6,2,40,128]{3,2,1,0:T(8,128)S(1)}, f32[6,2,40,128]{3,2,1,0:T(8,128)S(1)}, u32[]{:S(2)}, u32[]{:S(2)}) %collective-permute-start.2) | collective-permute-done | bytes 245792 | tf_op jit(solution)/shard_map/ppermute | solution.py:346
  14.6 6.3 %collective-permute-done.3.down = f32[6,2,40,128]{3,2,1,0:T(8,128)S(1)} collective-permute-done((f32[6,2,40,128]{3,2,1,0:T(8,128)S(1)}, f32[6,2,40,128]{3,2,1,0:T(8,128)S(1)}, u32[]{:S(2)}, u32[]{:S(2)}) %collective-permute-start.3) | collective-permute-done | bytes 245792 | tf_op jit(solution)/shard_map/ppermute | solution.py:346
  20.9 0.5 shard_map.164
  21.4 6.3 %collective-permute-start.4 = (f32[6,24,128]{2,1,0:T(8,128)S(1)}, f32[6,24,128]{2,1,0:T(8,128)S(1)}, u32[]{:S(2)}, u32[]{:S(2)}) collective-permute-start(f32[6,24,128]{2,1,0:T(8,128)S(1)} %get-tuple-element.15), channel_id=1, source_target_pairs={{0,14},{2,0},{4,2},{6,4},{8,6},{10,8},{12,10},{14,12},{1,15},{3,1}... | collective-permute-start | bytes 221192 | tf_op jit(solution)/shard_map/ppermute | solution.py:346
  27.7 0.0 collective-permute-start.5
  27.7 1.4 %collective-permute-done.4.ylow = f32[6,24,128]{2,1,0:T(8,128)S(1)} collective-permute-done((f32[6,24,128]{2,1,0:T(8,128)S(1)}, f32[6,24,128]{2,1,0:T(8,128)S(1)}, u32[]{:S(2)}, u32[]{:S(2)}) %collective-permute-start.4) | collective-permute-done | bytes 73760 | tf_op jit(solution)/shard_map/ppermute | solution.py:346
  29.1 5.4 %collective-permute-done.5.yhigh = f32[6,24,128]{2,1,0:T(8,128)S(1)} collective-permute-done((f32[6,24,128]{2,1,0:T(8,128)S(1)}, f32[6,24,128]{2,1,0:T(8,128)S(1)}, u32[]{:S(2)}, u32[]{:S(2)}) %collective-permute-start.5) | collective-permute-done | bytes 73760 | tf_op jit(solution)/shard_map/ppermute | solution.py:346
  34.5 7.2 %shard_map.165 = (f32[320,128]{1,0:T(8,128)S(1)}, bf16[8,48,128]{2,1,0:T(8,128)(2,1)}) custom-call(f32[5,128,256]{2,1,0:T(8,128)S(1)} %bitcast.14, f32[128,256]{1,0:T(8,128)S(1)} %bitcast.18, f32[5,128,256]{2,1,0:T(8,128)S(1)} %collective-permute-done.fp, f32[128,256]{1,0:T(8,128)S(1)} %collective-permute-done.1.sp, ...), custom_call_target="tpu_custom_call" | custom-call | flops 10000000 | bytes 1048576 | tf_op jit(solution)/shard_map/pallas_call | solution.py:366
  41.7 3.4 %all-to-all-start = ((bf16[8,48,128]{2,1,0:T(8,128)(2,1)}), bf16[8,48,128]{2,1,0:T(8,128)(2,1)S(1)}, u32[]{:S(2)}, u32[]{:S(2)}) async-start(bf16[8,48,128]{2,1,0:T(8,128)(2,1)} %get-tuple-element.17), calls=%async_computation | async-start | bytes 196608 | tf_op jit(solution)/shard_map/all_to_all | solution.py:343
  45.0 0.0 copy-start.6
  45.1 0.0 copy-start.15
  45.1 0.0 copy-start.16
  45.1 1.7 %shard_map.167 = f32[64,32,128]{2,1,0:T(8,128)} custom-call(f32[2048,128]{1,0:T(8,128)S(1)} %bitcast.19), custom_call_target="tpu_custom_call" | custom-call | flops 10000000 | bytes 1048576 | tf_op jit(solution)/shard_map/pallas_call | solution.py:348
  46.8 5.0 %all-to-all-done.got = bf16[8,48,128]{2,1,0:T(8,128)(2,1)S(1)} async-done(((bf16[8,48,128]{2,1,0:T(8,128)(2,1)}), bf16[8,48,128]{2,1,0:T(8,128)(2,1)S(1)}, u32[]{:S(2)}, u32[]{:S(2)}) %all-to-all-start) | async-done | bytes 98336 | tf_op jit(solution)/shard_map/all_to_all | solution.py:343
  51.8 4.7 %all-to-all-start.2 = ((f32[64,32,128]{2,1,0:T(8,128)}), f32[64,32,128]{2,1,0:T(8,128)S(1)}, u32[]{:S(2)}, u32[]{:S(2)}) async-start(f32[64,32,128]{2,1,0:T(8,128)} %shard_map.167), calls=%async_computation.2 | async-start | bytes 2097152 | tf_op jit(solution)/shard_map/all_to_all | solution.py:343
  56.4 0.0 copy-start.9
  56.5 1.0 copy-done.9
  57.5 2.2 %shard_map.166 = f32[64,4,128]{2,1,0:T(4,128)S(1)} custom-call(bf16[8,48,128]{2,1,0:T(8,128)(2,1)S(1)} %all-to-all-done.got, f32[5,32]{1,0:T(8,128)S(1)} %copy-done.15, f32[32]{0:T(128)S(1)} %copy-done.16, bf16[256,1024]{1,0:T(8,128)(2,1)S(1)} %copy-done.9, bf16[2,512,512]{2,1,0:T(8,128)(2,1)S(1)} %copy-done.6), custom_call_target="tpu_custom_call" | custom-call | flops 10000000 | bytes 1048576 | tf_op jit(solution)/shard_map/pallas_call | solution.py:387
  59.7 0.0 copy-start.7
  59.7 11.5 %all-to-all-done.2.weights = f32[64,32,128]{2,1,0:T(8,128)S(1)} async-done(((f32[64,32,128]{2,1,0:T(8,128)}), f32[64,32,128]{2,1,0:T(8,128)S(1)}, u32[]{:S(2)}, u32[]{:S(2)}) %all-to-all-start.2) | async-done | bytes 1048608 | tf_op jit(solution)/shard_map/all_to_all | solution.py:343
  71.2 18.2 %all_to_all.25 = f32[128,2,128]{2,1,0:T(2,128)S(1)} all-to-all(f32[128,2,128]{2,1,0:T(2,128)S(1)} %bitcast.23), channel_id=1, replica_groups=mesh['gx'=8,'gy'=8,'ga'=2] {'gx','gy','ga'}, dimensions={0} | all-to-all | bytes 262144 | tf_op jit(solution)/shard_map/all_to_all | solution.py:343
  89.4 1.0 copy-done.8
  90.4 0.9 copy-done.10
  91.4 0.9 copy-done.11
  92.3 0.9 copy-done.12
  93.2 0.9 copy-done.13
  94.1 1.8 %shard_map.168 = f32[64,4,128]{2,1,0:T(4,128)S(1)} custom-call(f32[256,128]{1,0:T(8,128)S(1)} %bitcast.20, f32[64,32,128]{2,1,0:T(8,128)S(1)} %all-to-all-done.2.weights, bf16[256,1024]{1,0:T(8,128)(2,1)S(1)} %copy-done.8, bf16[4,128,128]{2,1,0:T(8,128)(2,1)S(1)} %copy-done.11, bf16[1024,128]{1,0:T(8,128)(2,1)S(1)} %copy-done.10, f32[256,128]{1,0:T(8,128)S(1)} %copy-done.12, ...), custom_call_target="tpu_custom_call" | custom-call | flops 10000000 | bytes 1048576 | tf_op jit(solution)/shard_map/pallas_call | solution.py:394
  95.9 0.0 copy-start.17
  95.9 14.1 %all_to_all.26 = f32[128,2,128]{2,1,0:T(2,128)S(1)} all-to-all(f32[128,2,128]{2,1,0:T(2,128)S(1)} %bitcast.21), channel_id=1, replica_groups=mesh['gx'=8,'gy'=8,'ga'=2] {'gx','gy','ga'}, dimensions={0} | all-to-all | bytes 262144 | tf_op jit(solution)/shard_map/all_to_all | solution.py:343
  110.0 1.8 %shard_map.169 = bf16[8,256,128]{2,1,0:T(8,128)(2,1)} custom-call(f32[64,4,128]{2,1,0:T(4,128)S(1)} %bitcast.22, bf16[2,512,512]{2,1,0:T(8,128)(2,1)S(1)} %copy-done.5, bf16[384,1024]{1,0:T(8,128)(2,1)S(1)} %copy-done.7), custom_call_target="tpu_custom_call" | custom-call | flops 10000000 | bytes 1048576 | tf_op jit(solution)/shard_map/pallas_call | solution.py:404
  111.8 3.5 %all-to-all-start.4 = ((bf16[8,256,128]{2,1,0:T(8,128)(2,1)}), bf16[8,256,128]{2,1,0:T(8,128)(2,1)S(1)}, u32[]{:S(2)}, u32[]{:S(2)}) async-start(bf16[8,256,128]{2,1,0:T(8,128)(2,1)} %shard_map.169), calls=%async_computation.4 | async-start | bytes 1048576 | tf_op jit(solution)/shard_map/all_to_all | solution.py:343
  115.3 0.1 copy.19
  115.4 1.6 %multiply_bitcast_fusion = bf16[32,8,32,8]{3,2,1,0:T(8,128)(2,1)} fusion(bf16[32,32]{0,1:T(8,128)(2,1)S(1)} %copy.19, bf16[8,8]{1,0:T(8,128)(2,1)S(1)} %fusion), kind=kLoop, calls=%fused_computation | loop fusion | flops 65536 | bytes 133248 | tf_op jit(solution)/shard_map/co,xy->oxcy/transpose | solution.py:381
  117.0 4.1 %reshape.32.mix = bf16[256,256]{1,0:T(8,128)(2,1)S(1)} reshape(bf16[32,8,32,8]{3,2,1,0:T(8,128)(2,1)} %multiply_bitcast_fusion) | data formatting | bytes 262144 | tf_op jit(solution)/shard_map/reshape | solution.py:381
  121.0 0.1 broadcast_in_dim.10
  121.1 0.1 broadcast_in_dim.11
  121.2 0.1 broadcast_in_dim.12.obias
  121.3 2.9 %shard_map.170.direct = f32[8,256,128]{2,1,0:T(8,128)S(1)} custom-call(f32[320,128]{1,0:T(8,128)S(1)} %get-tuple-element.18.wide, f32[5,32]{1,0:T(8,128)S(1)} %copy-done.15, f32[32]{0:T(128)S(1)} %copy-done.16, bf16[256,256]{1,0:T(8,128)(2,1)S(1)} %reshape.32.mix, f32[256,128]{1,0:T(8,128)S(1)} %broadcast_in_dim.12.obias), custom_call_target="tpu_custom_call" | custom-call | flops 300000000 | bytes 1048576 | tf_op jit(solution)/shard_map/pallas_call | solution.py:383
  124.2 1.0 all-to-all-done.4.got
  125.1 1.8 %shard_map.171 = bf16[8,32,8,128]{3,2,1,0:T(8,128)(2,1)} custom-call(bf16[8,256,128]{2,1,0:T(8,128)(2,1)S(1)} %all-to-all-done.4.got, f32[8,256,128]{2,1,0:T(8,128)S(1)} %shard_map.170.direct), custom_call_target="tpu_custom_call" | custom-call | flops 10000000 | bytes 1048576 | tf_op jit(solution)/shard_map/pallas_call | solution.py:408
  (26 shorter events, 0.1 us)
Async XLA Ops:
  0.0 3.5 %collective-permute-start = (f32[5,128,256]{2,1,0:T(8,128)}, f32[5,128,256]{2,1,0:T(8,128)S(1)}, u32[]{:S(2)}, u32[]{:S(2)}) collective-permute-start(f32[5,128,256]{2,1,0:T(8,128)} %bitcast.11), channel_id=1, source_target_pairs={{0,1},{1,0},{2,3},{3,2},{4,5},{5,4},{6,7},{7,6},{8,9},{9,8},{10,11... | collective-permute-start | bytes 1966088 | tf_op jit(solution)/shard_map/ppermute | solution.py:356
  1.4 2.1 %collective-permute-start.1 = (f32[128,256]{1,0:T(8,128)}, f32[128,256]{1,0:T(8,128)S(1)}, u32[]{:S(2)}, u32[]{:S(2)}) collective-permute-start(f32[128,256]{1,0:T(8,128)} %bitcast.15), channel_id=1, source_target_pairs={{0,1},{1,0},{2,3},{3,2},{4,5},{5,4},{6,7},{7,6},{8,9},{9,8},{10,11... | collective-permute-start | bytes 393224 | tf_op jit(solution)/shard_map/ppermute | solution.py:356
  3.5 1.1 copy-start
  4.6 0.9 copy-start.2
  5.5 29.0 %copy-start.1 = (f32[5,8,16,256]{3,2,1,0:T(8,128)S(1)}, f32[5,8,16,256]{3,2,1,0:T(8,128)}, u32[]{:S(2)}) copy-start(f32[5,8,16,256]{3,2,1,0:T(8,128)} %param.17) | copy-start | bytes 1966084
  5.5 29.0 %copy-start.3 = (f32[8,16,256]{2,1,0:T(8,128)S(1)}, f32[8,16,256]{2,1,0:T(8,128)}, u32[]{:S(2)}) copy-start(f32[8,16,256]{2,1,0:T(8,128)} %param.18) | copy-start | bytes 393220
  5.5 29.0 %copy-start.14 = (bf16[256,128]{1,0:T(8,128)(2,1)S(1)}, bf16[256,128]{1,0:T(8,128)(2,1)}, u32[]{:S(2)}) copy-start(bf16[256,128]{1,0:T(8,128)(2,1)} %constant.20.clone.pairs) | copy-start | bytes 196612
  5.8 8.8 %collective-permute-start.2 = (f32[6,2,40,128]{3,2,1,0:T(8,128)S(1)}, f32[6,2,40,128]{3,2,1,0:T(8,128)S(1)}, u32[]{:S(2)}, u32[]{:S(2)}) collective-permute-start(f32[6,2,40,128]{3,2,1,0:T(8,128)S(1)} %get-tuple-element.12), channel_id=1, source_target_pairs={{0,112},{16,0},{32,16},{48,32},{64,48},{80,64},{96,80},{112,96},{1... | collective-permute-start | bytes 737288 | tf_op jit(solution)/shard_map/ppermute | solution.py:346
  9.6 35.4 %copy-start.4 = (f32[4,4,32,4,128]{4,3,2,1,0:T(4,128)S(1)}, f32[4,4,32,4,128]{4,3,2,1,0:T(4,128)}, u32[]{:S(2)}) copy-start(f32[4,4,32,4,128]{4,3,2,1,0:T(4,128)} %param.22) | copy-start | bytes 3145732
  9.6 11.2 %collective-permute-start.3 = (f32[6,2,40,128]{3,2,1,0:T(8,128)S(1)}, f32[6,2,40,128]{3,2,1,0:T(8,128)S(1)}, u32[]{:S(2)}, u32[]{:S(2)}) collective-permute-start(f32[6,2,40,128]{3,2,1,0:T(8,128)S(1)} %get-tuple-element.13), channel_id=1, source_target_pairs={{0,16},{16,32},{32,48},{48,64},{64,80},{80,96},{96,112},{112,0},{1... | collective-permute-start | bytes 737288 | tf_op jit(solution)/shard_map/ppermute | solution.py:346
  21.4 7.7 %collective-permute-start.4 = (f32[6,24,128]{2,1,0:T(8,128)S(1)}, f32[6,24,128]{2,1,0:T(8,128)S(1)}, u32[]{:S(2)}, u32[]{:S(2)}) collective-permute-start(f32[6,24,128]{2,1,0:T(8,128)S(1)} %get-tuple-element.15), channel_id=1, source_target_pairs={{0,14},{2,0},{4,2},{6,4},{8,6},{10,8},{12,10},{14,12},{1,15},{3,1}... | collective-permute-start | bytes 221192 | tf_op jit(solution)/shard_map/ppermute | solution.py:346
  27.7 6.8 %collective-permute-start.5 = (f32[6,24,128]{2,1,0:T(8,128)S(1)}, f32[6,24,128]{2,1,0:T(8,128)S(1)}, u32[]{:S(2)}, u32[]{:S(2)}) collective-permute-start(f32[6,24,128]{2,1,0:T(8,128)S(1)} %get-tuple-element.16), channel_id=1, source_target_pairs={{0,2},{2,4},{4,6},{6,8},{8,10},{10,12},{12,14},{14,0},{1,3},{3,5},... | collective-permute-start | bytes 221192 | tf_op jit(solution)/shard_map/ppermute | solution.py:346
  41.7 10.1 %all-to-all-start = ((bf16[8,48,128]{2,1,0:T(8,128)(2,1)}), bf16[8,48,128]{2,1,0:T(8,128)(2,1)S(1)}, u32[]{:S(2)}, u32[]{:S(2)}) async-start(bf16[8,48,128]{2,1,0:T(8,128)(2,1)} %get-tuple-element.17), calls=%async_computation | async-start | bytes 196608 | tf_op jit(solution)/shard_map/all_to_all | solution.py:343
  45.0 11.4 %copy-start.6 = (bf16[2,512,512]{2,1,0:T(8,128)(2,1)S(1)}, bf16[2,512,512]{2,1,0:T(8,128)(2,1)}, u32[]{:S(2)}) copy-start(bf16[2,512,512]{2,1,0:T(8,128)(2,1)} %constant.23.clone.zf) | copy-start | bytes 3145732
  45.1 11.4 %copy-start.15 = (f32[5,32]{1,0:T(8,128)S(1)}, f32[5,32]{1,0:T(8,128)}, u32[]{:S(2)}) copy-start(f32[5,32]{1,0:T(8,128)} %weight.3) | copy-start | bytes 1924
  45.1 11.4 %copy-start.16 = (f32[32]{0:T(128)S(1)}, f32[32]{0:T(128)}, u32[]{:S(2)}) copy-start(f32[32]{0:T(128)} %bias.3) | copy-start | bytes 388
  51.8 19.5 %all-to-all-start.2 = ((f32[64,32,128]{2,1,0:T(8,128)}), f32[64,32,128]{2,1,0:T(8,128)S(1)}, u32[]{:S(2)}, u32[]{:S(2)}) async-start(f32[64,32,128]{2,1,0:T(8,128)} %shard_map.167), calls=%async_computation.2 | async-start | bytes 2097152 | tf_op jit(solution)/shard_map/all_to_all | solution.py:343
  56.4 1.0 copy-start.9
  57.5 52.5 %copy-start.5 = (bf16[2,512,512]{2,1,0:T(8,128)(2,1)S(1)}, bf16[2,512,512]{2,1,0:T(8,128)(2,1)}, u32[]{:S(2)}) copy-start(bf16[2,512,512]{2,1,0:T(8,128)(2,1)} %constant.24.clone.zi) | copy-start | bytes 3145732
  59.7 50.3 %copy-start.7 = (bf16[384,1024]{1,0:T(8,128)(2,1)S(1)}, bf16[384,1024]{1,0:T(8,128)(2,1)}, u32[]{:S(2)}) copy-start(bf16[384,1024]{1,0:T(8,128)(2,1)} %constant.22.clone.yi) | copy-start | bytes 2359300
  89.4 1.0 copy-start.8
  90.4 0.9 copy-start.10
  91.4 0.9 copy-start.11
  92.3 0.9 copy-start.12
  93.2 0.9 copy-start.13
  95.9 19.4 %copy-start.17 = (bf16[32,32]{1,0:T(8,128)(2,1)S(1)}, bf16[32,32]{1,0:T(8,128)(2,1)}, u32[]{:S(2)}) copy-start(bf16[32,32]{1,0:T(8,128)(2,1)} %param.21) | copy-start | bytes 6148
  111.8 13.3 %all-to-all-start.4 = ((bf16[8,256,128]{2,1,0:T(8,128)(2,1)}), bf16[8,256,128]{2,1,0:T(8,128)(2,1)S(1)}, u32[]{:S(2)}, u32[]{:S(2)}) async-start(bf16[8,256,128]{2,1,0:T(8,128)(2,1)} %shard_map.169), calls=%async_computation.4 | async-start | bytes 1048576 | tf_op jit(solution)/shard_map/all_to_all | solution.py:343
  115.4 5.6 %copy-start.18 = (f32[32]{0:T(128)S(1)}, f32[32]{0:T(128)}, u32[]{:S(2)}) copy-start(f32[32]{0:T(128)} %param.23) | copy-start | bytes 388

commit v2 on v1

--- a/solution.py
+++ b/solution.py
@@ -74,26 +74,13 @@
             xf[0, :, k, :, k, :, a, 1] = -sign * sr
             xf[1, :, k, :, k, :, a, 0] = sign * sr
             xf[1, :, k, :, k, :, a, 1] = sign * cr
-    out["xf"] = xf.reshape(256, 1024).astype(np.float32).astype(jnp.bfloat16)
-    ex = np.zeros((4, 4, C, C, 4), np.float32)
-    for k in range(4):
-        for c in range(C):
-            ex[k, k, c, c] = 1.0
-    out["ex"] = ex.reshape(4, 128, 128).astype(jnp.bfloat16)
-    rm = np.zeros((8, C, 4, 4, 8, 4), np.float32)
-    for i in range(8):
-        for o in range(4):
-            rm[i, :, o, :, i, o] = 1.0
-    out["rm"] = rm.reshape(1024, 128).astype(jnp.bfloat16)
-    mask = np.zeros((2, 8, 4, 4, 4, C), np.float32)
-    for k in range(4):
-        mask[:, :, k, :, k] = 1.0
-    out["mask"] = mask.reshape(256, 128)
+    xf = xf.reshape(256, 4, 256).transpose(1, 0, 2).reshape(1024, 256)
+    xf = xf.astype(np.float32).astype(jnp.bfloat16)
     ic, is_ = (cx / 8.0).T.reshape(GX, 8, 1, 4), (sx / 8.0).T.reshape(GX, 8, 1, 4)
     xi = np.zeros((2, GX, 2, 8, 4, 4))
     xi[0, :, 0], xi[0, :, 1] = ic, -is_
     xi[1, :, 0], xi[1, :, 1] = is_, ic
-    out["xi"] = np.stack(split(xi.reshape(128, 256)))
+    out["x"] = np.concatenate([xf, *split(xi.reshape(128, 256))]).reshape(5, 256, 256)
     return out
 
 
@@ -172,7 +159,7 @@
         high[field] = highs
 
 
-def stencil(f, s, fp, sp, xh, ylow, yhigh, pairs, wide, narrow, a, b, stiff, last, sums):
+def stencil(f, s, fp, sp, xh, ylow, yhigh, pairs, after, wide, narrow, a, b, stiff, last, sums):
     near = lax.broadcasted_iota(jnp.int32, (24, 128), 1) < 64
     for zi in range(14):
         slot = zi - 3 if 3 <= zi < 11 else (13 + zi if zi < 3 else zi - 3)
@@ -279,11 +266,18 @@
         out[:, part, :] = result[:, 128 * part : 128 * part + 128]
 
 
-def mix_modes(got, weights, xf, ex, rm, mask, xi, out):
+def iotas(shape):
+    return lax.broadcasted_iota(jnp.int32, shape, 0), lax.broadcasted_iota(jnp.int32, shape, 1)
+
+
+def mix_modes(got, weights, x_tables, out):
     high, low = halves(got[...])
-    spread_high = jnp.concatenate([dot(high, ex[k]).astype(BF16) for k in range(4)], axis=0)
-    spread_low = jnp.concatenate([dot(low, ex[k]).astype(BF16) for k in range(4)], axis=0)
-    modes = dot(xf[...], spread_high) + dot(xf[...], spread_low)
+    row, lane = iotas((128, 128))
+    modes = jnp.zeros((256, 128), F32)
+    for k in range(4):
+        spread = (row == 32 * k + lane // 4).astype(BF16)
+        modes = modes + dot(x_tables[k], dot(high, spread).astype(BF16))
+        modes = modes + dot(x_tables[k], dot(low, spread).astype(BF16))
     real, imag = modes[:128], modes[128:]
     total = jnp.zeros((256, 128), F32)
     for i in range(8):
@@ -291,11 +285,13 @@
         wi = weights[8 * i : 8 * i + 8, 16:32, :].astype(F32).reshape(128, 128)
         part = jnp.concatenate([wr * real - wi * imag, wr * imag + wi * real], axis=0)
         p_high, p_low = halves(part)
-        table = rm[128 * i : 128 * i + 128, :]
-        total = total + dot(p_high, table) + dot(p_low, table)
-    total = total * mask[...]
+        gather = (lane % 32 == 4 * i + row % 4).astype(BF16)
+        total = total + dot(p_high, gather) + dot(p_low, gather)
+    row, lane = iotas((256, 128))
+    total = jnp.where((row // 4) % 4 == lane // 32, total, 0.0)
     t_high, t_low = halves(total)
-    back = dot(xi[0], t_high) + dot(xi[0], t_low) + dot(xi[1], t_high)
+    back_high, back_low = x_tables[4, :128], x_tables[4, 128:]
+    back = dot(back_high, t_high) + dot(back_high, t_low) + dot(back_low, t_high)
     odd = (lax.broadcasted_iota(jnp.int32, (64, 128), 1) // 32) % 2 == 1
     for ri in range(2):
         value = back[64 * ri : 64 * ri + 64]
@@ -366,7 +362,7 @@
     wide, narrow = call(
         stencil,
         [((320, 128), F32), ((8, 48, 128), BF16)],
-        [VMEM] * 8,
+        [VMEM] * 8 + [pl.BlockSpec(memory_space=pl.ANY)],
         [
             pltpu.VMEM((5, 14, 24, 384), F32),
             pltpu.VMEM((5, 14, 24, 384), F32),
@@ -375,7 +371,7 @@
             pltpu.VMEM((320, 256), F32),
         ],
         mib=24,
-    )(f, s, fp, sp, xh, ylow, yhigh, table["pairs"])
+    )(f, s, fp, sp, xh, ylow, yhigh, table["pairs"], weights)
 
     columns = exchange(narrow, "gy")
     spread = jnp.einsum("co,xy->oxcy", mix_weight, jnp.eye(8, dtype=BF16)).reshape(256, 256)
@@ -391,14 +387,8 @@
         [pltpu.VMEM((256, 1024), BF16)],
     )(columns, lift_weight, lift_bias, table["yf"], table["zf"])
     modes = exchange(modes.reshape(128, 2, 128), everyone)
-    [mixed] = call(mix_modes, [((64, 4, 128), F32)], [VMEM] * 7, mib=24)(
-        modes.reshape(256, 128),
-        weights,
-        table["xf"],
-        table["ex"],
-        table["rm"],
-        table["mask"],
-        table["xi"],
+    [mixed] = call(mix_modes, [((64, 4, 128), F32)], [VMEM] * 3, mib=24)(
+        modes.reshape(256, 128), weights, table["x"]
     )
     mixed = exchange(mixed.reshape(128, 2, 128), everyone)
     [spectral] = call(inverse, [((8, 256, 128), BF16)], [VMEM] * 3)(

time: 128 us -> 123 us (0.961)
  blocking collectives: 32.3 us -> 40.9 us
  waiting for transfers between devices: 37.6 us -> 29.8 us
  local copies, waits for them, and re-layouts: 12.2 us -> 6.23 us
  starting transfers between devices: 23 us -> 24.9 us
  other arithmetic: 1.57 us -> 0.21 us
    all_to_all x3 -> x2, waiting for transfers between devices: 17.4 us -> 3.32 us  [exchange(): return lax.all_to_all(value, axis, split_axis=0, concat_axis=0, tiled=True)]
    all_to_all x2 -> x3, blocking collectives: 32.3 us -> 40.9 us  [exchange(): return lax.all_to_all(value, axis, split_axis=0, concat_axis=0, tiled=True)]
    ppermute x4, waiting for transfers between devices: 18 us -> 24.6 us  [shift(): return lax.ppermute(value, axis, [(i, (i + by) % 8) for i in range(8)])]
    unnamed x39 -> x35, local copies, waits for them, and re-layouts: 7.87 us -> 2.99 us
    all_to_all x3 -> x2, starting transfers between devices: 11.5 us -> 15.5 us  [exchange(): return lax.all_to_all(value, axis, split_axis=0, concat_axis=0, tiled=True)]
    ppermute x4, starting transfers between devices: 10.1 us -> 8.36 us  [shift(): return lax.ppermute(value, axis, [(i, (i + by) % 8) for i in range(8)])]
    transpose x1, other arithmetic: 1.57 us -> 0.21 us  [shards(): jnp.einsum('co,xy->oxcy', mix_weight, jnp.eye(8, dtype=BF16))]
  transfers between devices with their start and end apart: 9 -> 8, of which waited for: 8 -> 6; matrix products, arithmetic and copies ran while one was open for 5% -> 3% of each run, Pallas kernels for 5% -> 3%
where the time goes in v2:
time: 123 us; the launch traced here: 122 us
  blocking collectives  40.9 us (33%)
  waiting for transfers between devices  29.8 us (24%)
  starting transfers between devices  24.9 us (20%)
  Pallas kernels  19.9 us (16%)
  local copies, waits for them, and re-layouts  6.23 us (5%)
    all_to_all x3, blocking collectives, exchange(): return lax.all_to_all(value, axis, split_axis=0, concat_axis=0, tiled=True)  40.9 us
    ppermute x4, waiting for transfers between devices, shift(): return lax.ppermute(value, axis, [(i, (i + by) % 8) for i in range(8)])  24.6 us
    all_to_all x2, starting transfers between devices, exchange(): return lax.all_to_all(value, axis, split_axis=0, concat_axis=0, tiled=True)  15.5 us
    ppermute x4, starting transfers between devices, shift(): return lax.ppermute(value, axis, [(i, (i + by) % 8) for i in range(8)])  8.36 us
    pallas_call x1, Pallas kernels, shards(): call(stencil, [((320, 128), F32), ((8, 48, 128), BF16)], [VMEM] * 8 + [pl...  6.5 us
    all_to_all x2, waiting for transfers between devices, exchange(): return lax.all_to_all(value, axis, split_axis=0, concat_axis=0, tiled=True)  3.32 us
    unnamed x35, local copies, waits for them, and re-layouts  2.99 us
    reshape x1, local copies, waits for them, and re-layouts, shards(): jnp.einsum('co,xy->oxcy', mix_weight, jnp.eye(8, dtype=BF16))  2.98 us
  transfers between devices with their start and end apart: 8, of which 6 were waited for; matrix products, arithmetic and copies ran while one was open for 3% of the time, Pallas kernels for 3%

profile of v2, /device:TPU:1, one launch (start us, length us, event | category | flops | bytes accessed | tf_op | source)
XLA Modules:
  0.0 122.2 jit_solution(13188397435124724434)
XLA Ops:
  0.0 1.2 %copy-done.2 = f32[4,4,32,4,128]{4,3,2,1,0:T(4,128)S(1)} copy-done((f32[4,4,32,4,128]{4,3,2,1,0:T(4,128)S(1)}, f32[4,4,32,4,128]{4,3,2,1,0:T(4,128)}, u32[]{:S(2)}) %copy-start.2) | copy-done | bytes 1048600
  1.2 1.7 %shard_map.129 = f32[64,32,128]{2,1,0:T(8,128)} custom-call(f32[2048,128]{1,0:T(8,128)S(1)} %bitcast.19), custom_call_target="tpu_custom_call" | custom-call | flops 10000000 | bytes 1048576 | tf_op jit(solution)/shard_map/pallas_call | solution.py:344
  2.9 12.0 %all-to-all-start = ((f32[64,32,128]{2,1,0:T(8,128)}), f32[64,32,128]{2,1,0:T(8,128)S(1)}, u32[]{:S(2)}, u32[]{:S(2)}) async-start(f32[64,32,128]{2,1,0:T(8,128)} %shard_map.129), calls=%async_computation | async-start | bytes 2097152 | tf_op jit(solution)/shard_map/all_to_all | solution.py:339
  14.9 1.0 collective-permute-start
  16.0 0.1 collective-permute-start.1
  16.1 1.8 %collective-permute-done.1.sp = f32[128,256]{1,0:T(8,128)S(1)} collective-permute-done((f32[128,256]{1,0:T(8,128)S(1)}, f32[128,256]{1,0:T(8,128)S(1)}, u32[]{:S(2)}, u32[]{:S(2)}) %collective-permute-start.1) | collective-permute-done | bytes 131104 | tf_op jit(solution)/shard_map/ppermute | solution.py:352
  17.9 0.0 collective-permute-done.fp
  17.9 0.3 shard_map.127
  18.1 3.7 %collective-permute-start.2 = (f32[6,2,40,128]{3,2,1,0:T(8,128)S(1)}, f32[6,2,40,128]{3,2,1,0:T(8,128)S(1)}, u32[]{:S(2)}, u32[]{:S(2)}) collective-permute-start(f32[6,2,40,128]{3,2,1,0:T(8,128)S(1)} %get-tuple-element.12), channel_id=1, source_target_pairs={{0,112},{16,0},{32,16},{48,32},{64,48},{80,64},{96,80},{112,96},{1... | collective-permute-start | bytes 737288 | tf_op jit(solution)/shard_map/ppermute | solution.py:342
  21.9 0.0 collective-permute-start.3
  21.9 10.4 %collective-permute-done.2.up = f32[6,2,40,128]{3,2,1,0:T(8,128)S(1)} collective-permute-done((f32[6,2,40,128]{3,2,1,0:T(8,128)S(1)}, f32[6,2,40,128]{3,2,1,0:T(8,128)S(1)}, u32[]{:S(2)}, u32[]{:S(2)}) %collective-permute-start.2) | collective-permute-done | bytes 245792 | tf_op jit(solution)/shard_map/ppermute | solution.py:342
  32.3 7.4 %collective-permute-done.3.down = f32[6,2,40,128]{3,2,1,0:T(8,128)S(1)} collective-permute-done((f32[6,2,40,128]{3,2,1,0:T(8,128)S(1)}, f32[6,2,40,128]{3,2,1,0:T(8,128)S(1)}, u32[]{:S(2)}, u32[]{:S(2)}) %collective-permute-start.3) | collective-permute-done | bytes 245792 | tf_op jit(solution)/shard_map/ppermute | solution.py:342
  39.7 0.5 shard_map.128
  40.2 4.6 %collective-permute-start.4 = (f32[6,24,128]{2,1,0:T(8,128)S(1)}, f32[6,24,128]{2,1,0:T(8,128)S(1)}, u32[]{:S(2)}, u32[]{:S(2)}) collective-permute-start(f32[6,24,128]{2,1,0:T(8,128)S(1)} %get-tuple-element.15), channel_id=1, source_target_pairs={{0,14},{2,0},{4,2},{6,4},{8,6},{10,8},{12,10},{14,12},{1,15},{3,1}... | collective-permute-start | bytes 221192 | tf_op jit(solution)/shard_map/ppermute | solution.py:342
  44.8 0.0 collective-permute-start.5
  44.8 1.4 %collective-permute-done.4.ylow = f32[6,24,128]{2,1,0:T(8,128)S(1)} collective-permute-done((f32[6,24,128]{2,1,0:T(8,128)S(1)}, f32[6,24,128]{2,1,0:T(8,128)S(1)}, u32[]{:S(2)}, u32[]{:S(2)}) %collective-permute-start.4) | collective-permute-done | bytes 73760 | tf_op jit(solution)/shard_map/ppermute | solution.py:342
  46.3 5.4 %collective-permute-done.5.yhigh = f32[6,24,128]{2,1,0:T(8,128)S(1)} collective-permute-done((f32[6,24,128]{2,1,0:T(8,128)S(1)}, f32[6,24,128]{2,1,0:T(8,128)S(1)}, u32[]{:S(2)}, u32[]{:S(2)}) %collective-permute-start.5) | collective-permute-done | bytes 73760 | tf_op jit(solution)/shard_map/ppermute | solution.py:342
  51.7 0.0 all-to-all-done.after.weights
  51.7 1.0 copy-done.10
  52.6 6.5 %shard_map.130 = (f32[320,128]{1,0:T(8,128)S(1)}, bf16[8,48,128]{2,1,0:T(8,128)(2,1)S(1)}) custom-call(f32[5,128,256]{2,1,0:T(8,128)S(1)} %bitcast.14, f32[128,256]{1,0:T(8,128)S(1)} %bitcast.18, f32[5,128,256]{2,1,0:T(8,128)S(1)} %collective-permute-done.fp, f32[128,256]{1,0:T(8,128)S(1)} %collective-permute-done.1.sp, ...), custom_call_target="tpu_custom_call" | custom-call | flops 10000000 | bytes 1048576 | tf_op jit(solution)/shard_map/pallas_call | solution.py:362
  59.1 0.0 copy-start.8
  59.2 0.7 copy-done.8
  59.8 9.2 %all_to_all.25.got = bf16[8,48,128]{2,1,0:T(8,128)(2,1)S(1)} all-to-all(bf16[8,48,128]{2,1,0:T(8,128)(2,1)S(1)} %get-tuple-element.17), channel_id=1, replica_groups=mesh['gx'=8,'gy'=8,'ga'=2] {'gy'}, dimensions={0} | all-to-all | bytes 196608 | tf_op jit(solution)/shard_map/all_to_all | solution.py:339
  69.0 0.0 copy-done.13
  69.0 0.0 copy-start.3
  69.0 0.0 copy-start.5
  69.0 2.2 %shard_map.131 = f32[64,4,128]{2,1,0:T(4,128)S(1)} custom-call(bf16[8,48,128]{2,1,0:T(8,128)(2,1)S(1)} %all_to_all.25.got, f32[5,32]{1,0:T(8,128)S(1)} %copy-done.11, f32[32]{0:T(128)S(1)} %copy-done.13, bf16[256,1024]{1,0:T(8,128)(2,1)S(1)} %copy-done.7, bf16[2,512,512]{2,1,0:T(8,128)(2,1)S(1)} %copy-done.4), custom_call_target="tpu_custom_call" | custom-call | flops 10000000 | bytes 1048576 | tf_op jit(solution)/shard_map/pallas_call | solution.py:383
  71.2 17.6 %all_to_all.26 = f32[128,2,128]{2,1,0:T(2,128)S(1)} all-to-all(f32[128,2,128]{2,1,0:T(2,128)S(1)} %bitcast.21), channel_id=1, replica_groups=mesh['gx'=8,'gy'=8,'ga'=2] {'gx','gy','ga'}, dimensions={0} | all-to-all | bytes 262144 | tf_op jit(solution)/shard_map/all_to_all | solution.py:339
  88.9 2.3 %shard_map.132 = f32[64,4,128]{2,1,0:T(4,128)S(1)} custom-call(f32[256,128]{1,0:T(8,128)S(1)} %bitcast.22, f32[64,32,128]{2,1,0:T(8,128)S(1)} %all-to-all-done.after.weights, bf16[5,256,256]{2,1,0:T(8,128)(2,1)S(1)} %copy-done.6), custom_call_target="tpu_custom_call" | custom-call | flops 10000000 | bytes 1048576 | tf_op jit(solution)/shard_map/pallas_call | solution.py:390
  91.2 0.0 copy-start.15
  91.2 14.2 %all_to_all.27 = f32[128,2,128]{2,1,0:T(2,128)S(1)} all-to-all(f32[128,2,128]{2,1,0:T(2,128)S(1)} %bitcast.23), channel_id=1, replica_groups=mesh['gx'=8,'gy'=8,'ga'=2] {'gx','gy','ga'}, dimensions={0} | all-to-all | bytes 262144 | tf_op jit(solution)/shard_map/all_to_all | solution.py:339
  105.3 0.0 copy-done.5
  105.3 1.8 %shard_map.133 = bf16[8,256,128]{2,1,0:T(8,128)(2,1)} custom-call(f32[64,4,128]{2,1,0:T(4,128)S(1)} %bitcast.20, bf16[2,512,512]{2,1,0:T(8,128)(2,1)S(1)} %copy-done.3, bf16[384,1024]{1,0:T(8,128)(2,1)S(1)} %copy-done.5), custom_call_target="tpu_custom_call" | custom-call | flops 10000000 | bytes 1048576 | tf_op jit(solution)/shard_map/pallas_call | solution.py:394
  107.1 3.5 %all-to-all-start.4 = ((bf16[8,256,128]{2,1,0:T(8,128)(2,1)}), bf16[8,256,128]{2,1,0:T(8,128)(2,1)S(1)}, u32[]{:S(2)}, u32[]{:S(2)}) async-start(bf16[8,256,128]{2,1,0:T(8,128)(2,1)} %shard_map.133), calls=%async_computation.4 | async-start | bytes 1048576 | tf_op jit(solution)/shard_map/all_to_all | solution.py:339
  110.6 0.1 copy.15
  110.7 0.0 copy-start.16
  110.7 0.0 copy-start.12
  110.8 0.0 copy-start.14
  110.8 0.2 multiply_bitcast_fusion
  111.0 3.0 %reshape.32.mix = bf16[256,256]{1,0:T(8,128)(2,1)S(1)} reshape(bf16[32,8,32,8]{3,2,1,0:T(8,128)(2,1)S(1)} %multiply_bitcast_fusion) | data formatting | bytes 262144 | tf_op jit(solution)/shard_map/reshape | solution.py:377
  114.0 0.1 broadcast_in_dim.10
  114.0 0.1 broadcast_in_dim.11
  114.1 0.1 broadcast_in_dim.12.obias
  114.2 0.0 copy-done.9
  114.3 0.0 copy-done.12
  114.3 2.9 %shard_map.134.direct = f32[8,256,128]{2,1,0:T(8,128)S(1)} custom-call(f32[320,128]{1,0:T(8,128)S(1)} %copy-done.9, f32[5,32]{1,0:T(8,128)S(1)} %copy-done.12, f32[32]{0:T(128)S(1)} %copy-done.14, bf16[256,256]{1,0:T(8,128)(2,1)S(1)} %reshape.32.mix, f32[256,128]{1,0:T(8,128)S(1)} %broadcast_in_dim.12.obias), custom_call_target="tpu_custom_call" | custom-call | flops 300000000 | bytes 1048576 | tf_op jit(solution)/shard_map/pallas_call | solution.py:379
  117.1 3.3 %all-to-all-done.4.got = bf16[8,256,128]{2,1,0:T(8,128)(2,1)S(1)} async-done(((bf16[8,256,128]{2,1,0:T(8,128)(2,1)}), bf16[8,256,128]{2,1,0:T(8,128)(2,1)S(1)}, u32[]{:S(2)}, u32[]{:S(2)}) %all-to-all-start.4) | async-done | bytes 524320 | tf_op jit(solution)/shard_map/all_to_all | solution.py:339
  120.5 1.8 %shard_map.135 = bf16[8,32,8,128]{3,2,1,0:T(8,128)(2,1)} custom-call(bf16[8,256,128]{2,1,0:T(8,128)(2,1)S(1)} %all-to-all-done.4.got, f32[8,256,128]{2,1,0:T(8,128)S(1)} %shard_map.134.direct), custom_call_target="tpu_custom_call" | custom-call | flops 10000000 | bytes 1048576 | tf_op jit(solution)/shard_map/pallas_call | solution.py:398
  (21 shorter events, 0.0 us)
Async XLA Ops:
  0.0 1.2 %copy-start.2 = (f32[4,4,32,4,128]{4,3,2,1,0:T(4,128)S(1)}, f32[4,4,32,4,128]{4,3,2,1,0:T(4,128)}, u32[]{:S(2)}) copy-start(f32[4,4,32,4,128]{4,3,2,1,0:T(4,128)} %param.18) | copy-start | bytes 3145732
  1.2 13.7 %copy-start = (f32[5,8,16,256]{3,2,1,0:T(8,128)S(1)}, f32[5,8,16,256]{3,2,1,0:T(8,128)}, u32[]{:S(2)}) copy-start(f32[5,8,16,256]{3,2,1,0:T(8,128)} %param.13) | copy-start | bytes 1966084
  1.2 14.7 %copy-start.1 = (f32[8,16,256]{2,1,0:T(8,128)S(1)}, f32[8,16,256]{2,1,0:T(8,128)}, u32[]{:S(2)}) copy-start(f32[8,16,256]{2,1,0:T(8,128)} %param.14) | copy-start | bytes 393220
  2.9 48.7 %all-to-all-start = ((f32[64,32,128]{2,1,0:T(8,128)}), f32[64,32,128]{2,1,0:T(8,128)S(1)}, u32[]{:S(2)}, u32[]{:S(2)}) async-start(f32[64,32,128]{2,1,0:T(8,128)} %shard_map.129), calls=%async_computation | async-start | bytes 2097152 | tf_op jit(solution)/shard_map/all_to_all | solution.py:339
  14.9 3.0 %collective-permute-start = (f32[5,128,256]{2,1,0:T(8,128)S(1)}, f32[5,128,256]{2,1,0:T(8,128)S(1)}, u32[]{:S(2)}, u32[]{:S(2)}) collective-permute-start(f32[5,128,256]{2,1,0:T(8,128)S(1)} %bitcast.11), channel_id=1, source_target_pairs={{0,1},{1,0},{2,3},{3,2},{4,5},{5,4},{6,7},{7,6},{8,9},{9,8},{10,11... | collective-permute-start | bytes 1966088 | tf_op jit(solution)/shard_map/ppermute | solution.py:352
  16.0 1.9 %collective-permute-start.1 = (f32[128,256]{1,0:T(8,128)S(1)}, f32[128,256]{1,0:T(8,128)S(1)}, u32[]{:S(2)}, u32[]{:S(2)}) collective-permute-start(f32[128,256]{1,0:T(8,128)S(1)} %bitcast.15), channel_id=1, source_target_pairs={{0,1},{1,0},{2,3},{3,2},{4,5},{5,4},{6,7},{7,6},{8,9},{9,8},{10,11... | collective-permute-start | bytes 393224 | tf_op jit(solution)/shard_map/ppermute | solution.py:352
  18.1 14.1 %collective-permute-start.2 = (f32[6,2,40,128]{3,2,1,0:T(8,128)S(1)}, f32[6,2,40,128]{3,2,1,0:T(8,128)S(1)}, u32[]{:S(2)}, u32[]{:S(2)}) collective-permute-start(f32[6,2,40,128]{3,2,1,0:T(8,128)S(1)} %get-tuple-element.12), channel_id=1, source_target_pairs={{0,112},{16,0},{32,16},{48,32},{64,48},{80,64},{96,80},{112,96},{1... | collective-permute-start | bytes 737288 | tf_op jit(solution)/shard_map/ppermute | solution.py:342
  21.9 17.8 %collective-permute-start.3 = (f32[6,2,40,128]{3,2,1,0:T(8,128)S(1)}, f32[6,2,40,128]{3,2,1,0:T(8,128)S(1)}, u32[]{:S(2)}, u32[]{:S(2)}) collective-permute-start(f32[6,2,40,128]{3,2,1,0:T(8,128)S(1)} %get-tuple-element.13), channel_id=1, source_target_pairs={{0,16},{16,32},{32,48},{48,64},{64,80},{80,96},{96,112},{112,0},{1... | collective-permute-start | bytes 737288 | tf_op jit(solution)/shard_map/ppermute | solution.py:342
  40.2 6.0 %collective-permute-start.4 = (f32[6,24,128]{2,1,0:T(8,128)S(1)}, f32[6,24,128]{2,1,0:T(8,128)S(1)}, u32[]{:S(2)}, u32[]{:S(2)}) collective-permute-start(f32[6,24,128]{2,1,0:T(8,128)S(1)} %get-tuple-element.15), channel_id=1, source_target_pairs={{0,14},{2,0},{4,2},{6,4},{8,6},{10,8},{12,10},{14,12},{1,15},{3,1}... | collective-permute-start | bytes 221192 | tf_op jit(solution)/shard_map/ppermute | solution.py:342
  44.8 6.8 %collective-permute-start.5 = (f32[6,24,128]{2,1,0:T(8,128)S(1)}, f32[6,24,128]{2,1,0:T(8,128)S(1)}, u32[]{:S(2)}, u32[]{:S(2)}) collective-permute-start(f32[6,24,128]{2,1,0:T(8,128)S(1)} %get-tuple-element.16), channel_id=1, source_target_pairs={{0,2},{2,4},{4,6},{6,8},{8,10},{10,12},{12,14},{14,0},{1,3},{3,5},... | collective-permute-start | bytes 221192 | tf_op jit(solution)/shard_map/ppermute | solution.py:342
  51.7 17.3 %copy-start.4 = (bf16[2,512,512]{2,1,0:T(8,128)(2,1)S(1)}, bf16[2,512,512]{2,1,0:T(8,128)(2,1)}, u32[]{:S(2)}) copy-start(bf16[2,512,512]{2,1,0:T(8,128)(2,1)} %constant.15.clone.zf) | copy-start | bytes 3145732
  51.7 17.3 %copy-start.7 = (bf16[256,1024]{1,0:T(8,128)(2,1)S(1)}, bf16[256,1024]{1,0:T(8,128)(2,1)}, u32[]{:S(2)}) copy-start(bf16[256,1024]{1,0:T(8,128)(2,1)} %constant.13.clone.yf) | copy-start | bytes 1572868
  51.7 1.0 copy-start.10
  52.6 16.4 %copy-start.11 = (f32[5,32]{1,0:T(8,128)S(1)}, f32[5,32]{1,0:T(8,128)}, u32[]{:S(2)}) copy-start(f32[5,32]{1,0:T(8,128)} %weight.3) | copy-start | bytes 1924
  52.6 16.4 %copy-start.13 = (f32[32]{0:T(128)S(1)}, f32[32]{0:T(128)}, u32[]{:S(2)}) copy-start(f32[32]{0:T(128)} %bias.3) | copy-start | bytes 388
  52.6 36.2 %copy-start.6 = (bf16[5,256,256]{2,1,0:T(8,128)(2,1)S(1)}, bf16[5,256,256]{2,1,0:T(8,128)(2,1)}, u32[]{:S(2)}) copy-start(bf16[5,256,256]{2,1,0:T(8,128)(2,1)} %constant.17.clone.x_tables) | copy-start | bytes 1966084
  59.1 0.7 copy-start.8
  69.0 36.3 %copy-start.3 = (bf16[2,512,512]{2,1,0:T(8,128)(2,1)S(1)}, bf16[2,512,512]{2,1,0:T(8,128)(2,1)}, u32[]{:S(2)}) copy-start(bf16[2,512,512]{2,1,0:T(8,128)(2,1)} %constant.16.clone.zi) | copy-start | bytes 3145732
  69.0 36.3 %copy-start.5 = (bf16[384,1024]{1,0:T(8,128)(2,1)S(1)}, bf16[384,1024]{1,0:T(8,128)(2,1)}, u32[]{:S(2)}) copy-start(bf16[384,1024]{1,0:T(8,128)(2,1)} %constant.14.clone.yi) | copy-start | bytes 2359300
  91.2 19.4 %copy-start.15 = (bf16[32,32]{1,0:T(8,128)(2,1)S(1)}, bf16[32,32]{1,0:T(8,128)(2,1)}, u32[]{:S(2)}) copy-start(bf16[32,32]{1,0:T(8,128)(2,1)} %param.17) | copy-start | bytes 6148
  107.1 13.3 %all-to-all-start.4 = ((bf16[8,256,128]{2,1,0:T(8,128)(2,1)}), bf16[8,256,128]{2,1,0:T(8,128)(2,1)S(1)}, u32[]{:S(2)}, u32[]{:S(2)}) async-start(bf16[8,256,128]{2,1,0:T(8,128)(2,1)} %shard_map.133), calls=%async_computation.4 | async-start | bytes 1048576 | tf_op jit(solution)/shard_map/all_to_all | solution.py:339
  110.7 3.3 %copy-start.16 = (f32[32]{0:T(128)S(1)}, f32[32]{0:T(128)}, u32[]{:S(2)}) copy-start(f32[32]{0:T(128)} %param.19) | copy-start | bytes 388
  110.7 3.5 %copy-start.9 = (f32[320,128]{1,0:T(8,128)S(1)}, f32[320,128]{1,0:T(8,128)}, u32[]{:S(2)}) copy-start(f32[320,128]{1,0:T(8,128)} %copy-done.8) | copy-start | bytes 491524
  110.7 3.5 %copy-start.12 = (f32[5,32]{1,0:T(8,128)S(1)}, f32[5,32]{1,0:T(8,128)}, u32[]{:S(2)}) copy-start(f32[5,32]{1,0:T(8,128)} %weight.3) | copy-start | bytes 1924
  110.8 3.5 %copy-start.14 = (f32[32]{0:T(128)S(1)}, f32[32]{0:T(128)}, u32[]{:S(2)}) copy-start(f32[32]{0:T(128)} %bias.3) | copy-start | bytes 388

commit v3 on v2

--- a/solution.py
+++ b/solution.py
@@ -65,17 +65,18 @@
     cx, sx = cos_sin(kx, np.arange(GX), GX)
     cr = (cx / 8.0).astype(np.float32).astype(jnp.bfloat16).astype(np.float64)
     sr = (-sx / 8.0).astype(np.float32).astype(jnp.bfloat16).astype(np.float64)
-    cr, sr = cr.reshape(8, 4, GX), sr.reshape(8, 4, GX)
-    xf = np.zeros((2, 8, 4, 4, 4, GX, 2, 2))
+    cr, sr = cr.reshape(8, 4, 8, 2, 4), sr.reshape(8, 4, 8, 2, 4)
+    xf = np.zeros((4, 2, 8, 4, 4, 8, 4, 2, 2, 2))
     for k in range(4):
         for a in range(2):
-            sign = -1.0 if (k * a) % 2 else 1.0
-            xf[0, :, k, :, k, :, a, 0] = sign * cr
-            xf[0, :, k, :, k, :, a, 1] = -sign * sr
-            xf[1, :, k, :, k, :, a, 0] = sign * sr
-            xf[1, :, k, :, k, :, a, 1] = sign * cr
-    xf = xf.reshape(256, 4, 256).transpose(1, 0, 2).reshape(1024, 256)
-    xf = xf.astype(np.float32).astype(jnp.bfloat16)
+            for h in range(2):
+                sign = -1.0 if k * (h ^ a) % 2 else 1.0
+                real, imag = sign * cr[:, :, :, a], sign * sr[:, :, :, a]
+                xf[k, 0, :, k, :, :, :, h, a, 0] = real
+                xf[k, 0, :, k, :, :, :, h, a, 1] = -imag
+                xf[k, 1, :, k, :, :, :, h, a, 0] = imag
+                xf[k, 1, :, k, :, :, :, h, a, 1] = real
+    xf = xf.reshape(1024, 256).astype(np.float32).astype(jnp.bfloat16)
     ic, is_ = (cx / 8.0).T.reshape(GX, 8, 1, 4), (sx / 8.0).T.reshape(GX, 8, 1, 4)
     xi = np.zeros((2, GX, 2, 8, 4, 4))
     xi[0, :, 0], xi[0, :, 1] = ic, -is_
@@ -114,79 +115,92 @@
     )
 
 
-NEEDED = list(range(8)) + [8, 9, 14, 15]
-
-
-def pack_x(f, s, fp, sp, low, high, rows):
+def rows_of(refs, field, slot, half):
+    f, s, fp, sp = refs
+    own, other = (s, sp) if field == 5 else (f.at[field], fp.at[field])
+    start = 16 * (slot % 8) + 8 * half
+    return (own if slot < 8 else other)[pl.ds(pl.multiple_of(start, 8), 8), :]
+
+
+def pack_x(f, s, fp, sp, message, rows):
+    bottom = lax.axis_index("ga") == 0
     for field in range(6):
         for which, whole in enumerate(((s, sp) if field == 5 else (f.at[field], fp.at[field]))):
             for h in range(2):
                 rows[which, field, h] = whole[:, 128 * h : 128 * h + 128]
     for field in range(6):
         for h in range(2):
-            for which, count in ((0, 3), (1, 2)):
-                for d in range(count):
-                    at = 24 * which + 8 * d
+            for which in range(2):
+                for d in range(3):
                     first = rows[which, field, h, pl.ds(d, 8, stride=XL), :]
                     last = rows[which, field, h, pl.ds(XL - 1 - d, 8, stride=XL), :]
-                    low[field, h, at : at + 8, :] = first
-                    high[field, h, at : at + 8, :] = last
-
-
-def pack_y(f, s, fp, sp, up, down, xh, low, high):
-    xh[...] = jnp.zeros_like(xh)
-    lane = lax.broadcasted_iota(jnp.int32, (24, 128), 1) // 8
+                    at = 24 * which + 8 * d
+                    message[field, h, at : at + 8, :] = jnp.where(bottom, first, last)
+
+
+def pack_y(f, s, fp, sp, message, outer, low, high):
+    refs = (f, s, fp, sp)
+    a = lax.axis_index("ga")
+    row = lax.broadcasted_iota(jnp.int32, (8, 128), 0)
+    beyond = jnp.where(a == 1, row, 7 - row) < 3
+    lane = lax.broadcasted_iota(jnp.int32, (16, 128), 1) // 4
+    lows, highs = jnp.zeros((16, 128), F32), jnp.zeros((16, 128), F32)
     for field in range(6):
         for h in range(2):
-            for base, at, count in ((0, 0, 3), (64, 24, 2)):
-                for d in range(count):
-                    take = slice(at + 8 * d, at + 8 * d + 8)
-                    xh[field, h, pl.ds(base + d, 8, stride=8), :] = up[field, h, take, :]
-                    xh[field, h, pl.ds(base + 7 - d, 8, stride=8), :] = down[field, h, take, :]
-        lows = jnp.zeros((24, 128), F32)
-        highs = jnp.zeros((24, 128), F32)
-        for slot in NEEDED:
-            own, other = (s, sp) if field == 5 else (f.at[field], fp.at[field])
-            ref = own if slot < 8 else other
-            part = slice(16 * (slot % 8), 16 * (slot % 8) + 16)
+            for which in range(2):
+                for d in range(3):
+                    at = 24 * which + 8 * d
+                    value = message[field, h, at : at + 8, :]
+                    to = 64 * (1 - which)
+                    outer[field, h, pl.ds(to + d, 8, stride=8), :] = value
+                    outer[field, h, pl.ds(to + 7 - d, 8, stride=8), :] = value
+        for slot in range(16):
+            inner, block = rows_of(refs, field, slot, a), rows_of(refs, field, slot, 1 - a)
             edge = slice(8 * slot, 8 * slot + 8)
-            here = lane == slot
-            first = jnp.concatenate([ref[part, :128], xh[field, 0, edge, :]], axis=0)
-            last = jnp.concatenate([ref[part, 128:], xh[field, 1, edge, :]], axis=0)
-            lows = jnp.where(here, pltpu.roll(first, (8 * slot) % 128, 1), lows)
-            highs = jnp.where(here, pltpu.roll(last, (8 * slot + 8) % 128, 1), highs)
-        low[field] = lows
-        high[field] = highs
-
-
-def stencil(f, s, fp, sp, xh, ylow, yhigh, pairs, after, wide, narrow, a, b, stiff, last, sums):
-    near = lax.broadcasted_iota(jnp.int32, (24, 128), 1) < 64
-    for zi in range(14):
-        slot = zi - 3 if 3 <= zi < 11 else (13 + zi if zi < 3 else zi - 3)
-        part = slice(16 * (slot % 8), 16 * (slot % 8) + 16)
-        for field in range(6):
-            if field == 5 and zi in (0, 13):
-                continue
-            own, other = (s, sp) if field == 5 else (f, fp)
-            ref = own if slot < 8 else other
-            to = stiff.at[zi] if field == 5 else a.at[field, zi]
-            to[0:16, 0:256] = ref[part, :] if field == 5 else ref[field, part, :]
             for h in range(2):
-                edge = xh[field, h, 8 * slot : 8 * slot + 8, :]
-                to[16:24, 128 * h : 128 * h + 128] = edge
-            to[:, 256:384] = jnp.where(
-                near,
-                pltpu.roll(ylow[field], (128 - 8 * slot) % 128, 1),
-                pltpu.roll(yhigh[field], (120 - 8 * slot) % 128, 1),
-            )
-
-    def advance(src, zi):
+                kept = block[:, 128 * h : 128 * h + 128]
+                outer[field, h, edge, :] = jnp.where(beyond, outer[field, h, edge, :], kept)
+            base = 64 * (field % 2) + 4 * slot
+            here = lane == base // 4
+            first = jnp.concatenate([inner[:, :128], outer[field, 0, edge, :]], axis=0)
+            last = jnp.concatenate([inner[:, 128:], outer[field, 1, edge, :]], axis=0)
+            lows = jnp.where(here, pltpu.roll(first, base, 1) if base else first, lows)
+            highs = jnp.where(here, pltpu.roll(last, (base + 4) % 128, 1) if base != 124 else last, highs)
+        if field % 2:
+            low[field // 2] = lows
+            high[field // 2] = highs
+
+
+def stencil(
+    f, s, fp, sp, outer, ylow, yhigh, pairs, after, keep, send, narrow, a, b, stiff, last, sums
+):
+    refs = (f, s, fp, sp)
+    core = lax.axis_index("ga")
+    near = lax.broadcasted_iota(jnp.int32, (16, 128), 1) < 64
+    for field in range(6):
+        for slot in range(16):
+            to = stiff.at[slot] if field == 5 else a.at[field, slot]
+            to[0:8, 0:256] = rows_of(refs, field, slot, core)
+            for h in range(2):
+                edge = outer[field, h, 8 * slot : 8 * slot + 8, :]
+                to[8:16, 128 * h : 128 * h + 128] = edge
+            base = 64 * (field % 2) + 4 * slot
+            above, below = ylow[field // 2], yhigh[field // 2]
+            above = pltpu.roll(above, 128 - base, 1) if base else above
+            below = pltpu.roll(below, 124 - base, 1) if base != 124 else below
+            to[:, 256:384] = jnp.where(near, above, below)
+
+    def advance(src, slot, crop):
         new, east, north, depth = [], [], [], []
         for field in range(5):
-            mid = src[field, zi]
-            up, down = src[field, zi + 1], src[field, zi - 1]
-            xp, xm = pltpu.roll(mid, 23, 0), pltpu.roll(mid, 1, 0)
+            mid = src[field, slot]
+            up, down = src[field, (slot + 1) & 15], src[field, (slot + 15) & 15]
+            xp, xm = pltpu.roll(mid, 15, 0), pltpu.roll(mid, 1, 0)
             yp, ym = pltpu.roll(mid, 383, 1), pltpu.roll(mid, 1, 1)
+            if crop:
+                mid, up, down, xp, xm, yp, ym = (
+                    v[0:8, 0:256] for v in (mid, up, down, xp, xm, yp, ym)
+                )
             total = 0.1 * mid + 0.12 * xp + 0.18 * xm + 0.17 * yp + 0.13 * ym
             new.append(total + 0.14 * up + 0.16 * down)
             east.append(xp - xm if field in (1, 4) else None)
@@ -197,41 +211,45 @@
         new[1] = new[1] - 0.1 * east[4]
         new[2] = new[2] - 0.1 * north[4]
         new[3] = new[3] - 0.1 * depth[4]
-        new[4] = new[4] - stiff[zi] * div
+        new[4] = new[4] - (stiff[slot, 0:8, 0:256] if crop else stiff[slot]) * div
         return new
 
-    for step, (src, dst) in enumerate(((a, b), (b, a), (a, None))):
-        first, end = 1 + step, 13 - step
-
-        def body(zi, carry, src=src, dst=dst):
-            new = advance(src, zi)
+    for src, dst in ((a, b), (b, a), (a, None)):
+
+        def body(slot, carry, src=src, dst=dst):
+            new = advance(src, slot, dst is None)
             for field in range(5):
                 if dst is None:
-                    rows = pl.ds(pl.multiple_of((zi - 3) * 16, 16), 16)
+                    rows = pl.ds(pl.multiple_of(slot * 8, 8), 8)
                     for h in range(2):
-                        last[field, h, rows, :] = new[field][0:16, 128 * h : 128 * h + 128]
+                        last[field, h, rows, :] = new[field][:, 128 * h : 128 * h + 128]
                 else:
-                    dst[field, zi] = new[field]
+                    dst[field, slot] = new[field]
             return carry
 
-        lax.fori_loop(first, end, body, 0)
-
-    for x in range(8):
-        for field in range(5):
-            at = 40 * x + 8 * field
-            for h in range(2):
-                even = last[field, h, pl.ds(2 * x, 8, stride=16), :]
-                odd = last[field, h, pl.ds(2 * x + 1, 8, stride=16), :]
-                sums[at : at + 8, 128 * h : 128 * h + 128] = even + odd
+        lax.fori_loop(0, 16, body, 0)
+
+    for half in range(2):
+        for x in range(4):
+            for field in range(5):
+                at = 160 * half + 40 * x + 8 * field
+                for h in range(2):
+                    even = last[field, h, pl.ds(64 * half + 2 * x, 8, stride=8), :]
+                    odd = last[field, h, pl.ds(64 * half + 2 * x + 1, 8, stride=8), :]
+                    sums[at : at + 8, 128 * h : 128 * h + 128] = even + odd
     value = sums[...]
     high = value.astype(BF16)
     rest = value - high.astype(F32)
     mid, low = halves(rest)
     table = pairs[...]
     mean = dot(high, table) + dot(mid, table) + dot(low, table)
-    wide[...] = mean
-    mean = mean.reshape(8, 40, 128)
-    narrow[...] = jnp.concatenate([mean, jnp.zeros((8, 8, 128), F32)], axis=1).astype(BF16)
+    keep[...] = mean[:160]
+    send[...] = mean[160:]
+    for half in range(2):
+        for x in range(4):
+            at = 160 * half + 40 * x
+            block = jnp.concatenate([mean[at : at + 40], jnp.zeros((8, 128), F32)], axis=0)
+            narrow[2 * x + half] = block.astype(BF16)
 
 
 def lift_rows(values, weight, bias):
@@ -244,7 +262,11 @@
     return jnp.concatenate(rows, axis=0).astype(BF16)
 
 
-def pointwise(wide, weight, bias, mix, obias, out):
+def pointwise(keep, got, weight, bias, mix, obias, out, wide):
+    a = lax.axis_index("ga")
+    wide[pl.ds(pl.multiple_of(160 * a, 8), 160), :] = keep[...]
+    wide[pl.ds(pl.multiple_of(160 * (1 - a), 8), 160), :] = got[...]
+
     def body(z, carry):
         values = [wide[pl.ds(8 * field + z, 8, stride=40), :] for field in range(5)]
         out[z] = dot(mix[...], lift_rows(values, weight, bias)) + obias[...]
@@ -324,11 +346,12 @@
     lax.fori_loop(0, ZL, body, 0)
 
 
-def turn_weights(weights, out):
+def turn_weights(weights, after, out, wide):
     for chunk in range(16):
         turned = weights[128 * chunk : 128 * chunk + 128, :].T
         for ri in range(2):
-            out[:, 16 * ri + chunk, :] = turned[64 * ri : 64 * ri + 64]
+            wide[:, 16 * ri + chunk, :] = turned[64 * ri : 64 * ri + 64]
+    out[...] = wide[...].astype(BF16)
 
 
 def shards(fields, stiffness, lift_weight, lift_bias, mix_weight, spectral_weight, output_bias):
@@ -341,44 +364,52 @@
     def shift(value, axis, by):
         return lax.ppermute(value, axis, [(i, (i + by) % 8) for i in range(8)])
 
-    [turned] = call(turn_weights, [((64, 32, 128), F32)], [VMEM], mib=8)(
-        spectral_weight.reshape(2048, 128)
-    )
-    weights = exchange(turned, ("gx", "gy"))
-
+    anywhere = pl.BlockSpec(memory_space=pl.ANY)
     f = fields.reshape(5, 128, 256)
     s = stiffness.reshape(128, 256)
     swap = [(0, 1), (1, 0)]
     fp, sp = lax.ppermute(f, "ga", swap), lax.ppermute(s, "ga", swap)
-    message = ((6, 2, 40, 128), F32)
     copied = [pltpu.VMEM((2, 6, 2, 128, 128), F32)]
-    low, high = call(pack_x, [message, message], [VMEM] * 4, copied)(f, s, fp, sp)
-    up, down = shift(low, "gx", -1), shift(high, "gx", 1)
-    message = ((6, 24, 128), F32)
-    xh, low, high = call(pack_y, [((6, 2, 128, 128), F32), message, message], [VMEM] * 6)(
-        f, s, fp, sp, up, down
+    [message] = call(pack_x, [((6, 2, 48, 128), F32)], [VMEM] * 4, copied)(f, s, fp, sp)
+    across = [(2 * i, 2 * ((i - 1) % 8) + 1) for i in range(8)]
+    across += [(2 * i + 1, 2 * ((i + 1) % 8)) for i in range(8)]
+    got = lax.ppermute(message, ("gx", "ga"), across)
+
+    turned = [pltpu.VMEM((64, 32, 128), F32)]
+    [turned] = call(turn_weights, [((64, 32, 128), BF16)], [VMEM, anywhere], turned)(
+        spectral_weight.reshape(2048, 128), message
+    )
+    weights = exchange(turned, ("gx", "gy"))
+
+    message = ((3, 16, 128), F32)
+    outer, low, high = call(pack_y, [((6, 2, 128, 128), F32), message, message], [VMEM] * 5)(
+        f, s, fp, sp, got
     )
     ylow, yhigh = shift(low, "gy", -1), shift(high, "gy", 1)
-    wide, narrow = call(
+    keep, send, narrow = call(
         stencil,
-        [((320, 128), F32), ((8, 48, 128), BF16)],
-        [VMEM] * 8 + [pl.BlockSpec(memory_space=pl.ANY)],
+        [((160, 128), F32), ((160, 128), F32), ((8, 48, 128), BF16)],
+        [VMEM] * 8 + [anywhere],
         [
-            pltpu.VMEM((5, 14, 24, 384), F32),
-            pltpu.VMEM((5, 14, 24, 384), F32),
-            pltpu.VMEM((14, 24, 384), F32),
+            pltpu.VMEM((5, 16, 16, 384), F32),
+            pltpu.VMEM((5, 16, 16, 384), F32),
+            pltpu.VMEM((16, 16, 384), F32),
             pltpu.VMEM((5, 2, 128, 128), F32),
             pltpu.VMEM((320, 256), F32),
         ],
         mib=24,
-    )(f, s, fp, sp, xh, ylow, yhigh, table["pairs"], weights)
+    )(f, s, fp, sp, outer, ylow, yhigh, table["pairs"], weights)
 
     columns = exchange(narrow, "gy")
     spread = jnp.einsum("co,xy->oxcy", mix_weight, jnp.eye(8, dtype=BF16)).reshape(256, 256)
     obias = jnp.broadcast_to(jnp.repeat(output_bias, 8)[:, None], (256, 128))
     [direct] = call(
-        pointwise, [((8, 256, 128), F32)], [VMEM, SMEM, SMEM, VMEM, VMEM], flops=3 * 10**8
-    )(wide, lift_weight, lift_bias, spread, obias)
+        pointwise,
+        [((8, 256, 128), F32)],
+        [VMEM, VMEM, SMEM, SMEM, VMEM, VMEM],
+        [pltpu.VMEM((320, 128), F32)],
+        flops=3 * 10**8,
+    )(keep, lax.ppermute(send, "ga", swap), lift_weight, lift_bias, spread, obias)
 
     [modes] = call(
         forward,

time: 123 us -> 118 us (0.959)
  waiting for transfers between devices: 29.8 us -> 21 us
  local copies, waits for them, and re-layouts: 6.23 us -> 9.4 us
  starting transfers between devices: 24.9 us -> 23 us
  other arithmetic: 0.21 us -> 1.56 us
    ppermute x4 -> x2, waiting for transfers between devices: 24.6 us -> 6.29 us  [shift(): return lax.ppermute(value, axis, [(i, (i + by) % 8) for i in range(8)])]
    ppermute x0 -> x2, waiting for transfers between devices: none -> 12.1 us  [the longest x1 12.1 us: shards(): got = lax.ppermute(message, ('gx', 'ga'), across)]
    ppermute x4 -> x2, starting transfers between devices: 8.36 us -> 4.51 us  [shift(): return lax.ppermute(value, axis, [(i, (i + by) % 8) for i in range(8)])]
    all_to_all x2, waiting for transfers between devices: 3.32 us -> 0.49 us  [exchange(): return lax.all_to_all(value, axis, split_axis=0, concat_axis=0, tiled=True)]
    ppermute x0 -> x2, starting transfers between devices: none -> 2.39 us  [the longest x1 1.91 us: shards(): got = lax.ppermute(message, ('gx', 'ga'), across)]
    unnamed x35, local copies, waits for them, and re-layouts: 2.99 us -> 5.1 us
    transpose x1, other arithmetic: 0.21 us -> 1.55 us  [shards(): jnp.einsum('co,xy->oxcy', mix_weight, jnp.eye(8, dtype=BF16))]
  transfers between devices with their start and end apart: 8 -> 8, of which waited for: 6 -> 5; matrix products, arithmetic and copies ran while one was open for 3% -> 5% of each run, Pallas kernels for 3% -> 3%
where the time goes in v3:
time: 118 us; the launch traced here: 117 us
  blocking collectives  40.9 us (35%)
  starting transfers between devices  23 us (19%)
  waiting for transfers between devices  21 us (18%)
  Pallas kernels  20.4 us (17%)
  local copies, waits for them, and re-layouts  9.4 us (8%)
  other arithmetic  1.56 us (1%)
    all_to_all x3, blocking collectives, exchange(): return lax.all_to_all(value, axis, split_axis=0, concat_axis=0, tiled=True)  40.9 us
    all_to_all x2, starting transfers between devices, exchange(): return lax.all_to_all(value, axis, split_axis=0, concat_axis=0, tiled=True)  14.7 us
    ppermute x1, waiting for transfers between devices, shards(): got = lax.ppermute(message, ('gx', 'ga'), across)  12.1 us
    pallas_call x1, Pallas kernels, shards(): call(stencil, [((160, 128), F32), ((160, 128), F32), ((8, 48, 128), BF16)...  7.17 us
    ppermute x2, waiting for transfers between devices, shift(): return lax.ppermute(value, axis, [(i, (i + by) % 8) for i in range(8)])  6.29 us
    unnamed x35, local copies, waits for them, and re-layouts  5.1 us
    ppermute x2, starting transfers between devices, shift(): return lax.ppermute(value, axis, [(i, (i + by) % 8) for i in range(8)])  4.51 us
    reshape x1, local copies, waits for them, and re-layouts, shards(): jnp.einsum('co,xy->oxcy', mix_weight, jnp.eye(8, dtype=BF16))  4.05 us
  transfers between devices with their start and end apart: 8, of which 5 were waited for; matrix products, arithmetic and copies ran while one was open for 5% of the time, Pallas kernels for 3%

profile of v3, /device:TPU:1, one launch (start us, length us, event | category | flops | bytes accessed | tf_op | source)
XLA Modules:
  0.0 116.5 jit_solution(11619850290472523814)
XLA Ops:
  0.0 1.4 %collective-permute-start = (f32[5,128,256]{2,1,0:T(8,128)}, f32[5,128,256]{2,1,0:T(8,128)S(1)}, u32[]{:S(2)}, u32[]{:S(2)}) collective-permute-start(f32[5,128,256]{2,1,0:T(8,128)} %bitcast.11), channel_id=1, source_target_pairs={{0,1},{1,0},{2,3},{3,2},{4,5},{5,4},{6,7},{7,6},{8,9},{9,8},{10,11... | collective-permute-start | bytes 1966088 | tf_op jit(solution)/shard_map/ppermute | solution.py:371
  1.4 0.0 collective-permute-start.1
  1.4 2.1 %collective-permute-done.1.sp = f32[128,256]{1,0:T(8,128)S(1)} collective-permute-done((f32[128,256]{1,0:T(8,128)}, f32[128,256]{1,0:T(8,128)S(1)}, u32[]{:S(2)}, u32[]{:S(2)}) %collective-permute-start.1) | collective-permute-done | bytes 131104 | tf_op jit(solution)/shard_map/ppermute | solution.py:371
  3.5 0.0 collective-permute-done.fp
  3.6 1.1 copy-done
  4.6 0.9 copy-done.2
  5.5 0.3 shard_map.127.after
  5.8 0.9 copy-done.4
  6.8 1.6 %shard_map.129 = bf16[64,32,128]{2,1,0:T(8,128)(2,1)} custom-call(f32[2048,128]{1,0:T(8,128)S(1)} %bitcast.19, f32[6,2,48,128]{3,2,1,0:T(8,128)S(1)} %shard_map.127.after), custom_call_target="tpu_custom_call" | custom-call | flops 10000000 | bytes 1048576 | tf_op jit(solution)/shard_map/pallas_call | solution.py:379
  8.3 11.2 %all-to-all-start = ((bf16[64,32,128]{2,1,0:T(8,128)(2,1)}), bf16[64,32,128]{2,1,0:T(8,128)(2,1)S(1)}, u32[]{:S(2)}, u32[]{:S(2)}) async-start(bf16[64,32,128]{2,1,0:T(8,128)(2,1)} %shard_map.129), calls=%async_computation | async-start | bytes 1048576 | tf_op jit(solution)/shard_map/all_to_all | solution.py:362
  19.6 0.0 copy-start.6
  19.6 0.0 copy-start.13
  19.6 0.0 copy-start.14
  19.6 1.9 %collective-permute-start.2 = (f32[6,2,48,128]{3,2,1,0:T(8,128)S(1)}, f32[6,2,48,128]{3,2,1,0:T(8,128)S(1)}, u32[]{:S(2)}, u32[]{:S(2)}) collective-permute-start(f32[6,2,48,128]{3,2,1,0:T(8,128)S(1)} %shard_map.127.after), channel_id=1, source_target_pairs={{0,113},{16,1},{32,17},{48,33},{64,49},{80,65},{96,81},{112,97},{1... | collective-permute-start | bytes 884744 | tf_op jit(solution)/shard_map/ppermute | solution.py:376
  21.5 12.1 %collective-permute-done.2.message = f32[6,2,48,128]{3,2,1,0:T(8,128)S(1)} collective-permute-done((f32[6,2,48,128]{3,2,1,0:T(8,128)S(1)}, f32[6,2,48,128]{3,2,1,0:T(8,128)S(1)}, u32[]{:S(2)}, u32[]{:S(2)}) %collective-permute-start.2) | collective-permute-done | bytes 294944 | tf_op jit(solution)/shard_map/ppermute | solution.py:376
  33.6 0.0 copy-done.3
  33.6 0.5 shard_map.128
  34.2 0.0 copy-start.8
  34.2 0.9 copy-done.8
  35.1 4.5 %collective-permute-start.3 = (f32[3,16,128]{2,1,0:T(8,128)S(1)}, f32[3,16,128]{2,1,0:T(8,128)S(1)}, u32[]{:S(2)}, u32[]{:S(2)}) collective-permute-start(f32[3,16,128]{2,1,0:T(8,128)S(1)} %get-tuple-element.12), channel_id=1, source_target_pairs={{0,14},{2,0},{4,2},{6,4},{8,6},{10,8},{12,10},{14,12},{1,15},{3,1}... | collective-permute-start | bytes 73736 | tf_op jit(solution)/shard_map/ppermute | solution.py:365
  39.6 0.0 collective-permute-start.4
  39.6 0.9 collective-permute-done.3.ylow
  40.5 5.3 %collective-permute-done.4.yhigh = f32[3,16,128]{2,1,0:T(8,128)S(1)} collective-permute-done((f32[3,16,128]{2,1,0:T(8,128)S(1)}, f32[3,16,128]{2,1,0:T(8,128)S(1)}, u32[]{:S(2)}, u32[]{:S(2)}) %collective-permute-start.4) | collective-permute-done | bytes 24608 | tf_op jit(solution)/shard_map/ppermute | solution.py:365
  45.9 0.0 all-to-all-done.after.weights
  45.9 1.1 copy-done.9
  47.0 7.2 %shard_map.130 = (f32[160,128]{1,0:T(8,128)S(1)}, f32[160,128]{1,0:T(8,128)S(1)}, bf16[8,48,128]{2,1,0:T(8,128)(2,1)S(1)}) custom-call(f32[5,128,256]{2,1,0:T(8,128)S(1)} %bitcast.14, f32[128,256]{1,0:T(8,128)S(1)} %bitcast.18, f32[5,128,256]{2,1,0:T(8,128)S(1)} %collective-permute-done.fp, f32[128,256]{1,0:T(8,128)S(1)} %collective-permute-done.1.sp, ...), custom_call_target="tpu_custom_call" | custom-call | flops 10000000 | bytes 1048576 | tf_op jit(solution)/shard_map/pallas_call | solution.py:389
  54.2 0.0 copy-start.5
  54.2 0.0 copy-start.7
  54.2 9.3 %all_to_all.25.got = bf16[8,48,128]{2,1,0:T(8,128)(2,1)S(1)} all-to-all(bf16[8,48,128]{2,1,0:T(8,128)(2,1)S(1)} %get-tuple-element.14), channel_id=1, replica_groups=mesh['gx'=8,'gy'=8,'ga'=2] {'gy'}, dimensions={0} | all-to-all | bytes 196608 | tf_op jit(solution)/shard_map/all_to_all | solution.py:362
  63.5 2.2 %shard_map.131 = f32[64,4,128]{2,1,0:T(4,128)S(1)} custom-call(bf16[8,48,128]{2,1,0:T(8,128)(2,1)S(1)} %all_to_all.25.got, f32[5,32]{1,0:T(8,128)S(1)} %copy-done.13, f32[32]{0:T(128)S(1)} %copy-done.14, bf16[256,1024]{1,0:T(8,128)(2,1)S(1)} %copy-done.11, bf16[2,512,512]{2,1,0:T(8,128)(2,1)S(1)} %copy-done.6), custom_call_target="tpu_custom_call" | custom-call | flops 10000000 | bytes 1048576 | tf_op jit(solution)/shard_map/pallas_call | solution.py:414
  65.7 17.4 %all_to_all.26 = f32[128,2,128]{2,1,0:T(2,128)S(1)} all-to-all(f32[128,2,128]{2,1,0:T(2,128)S(1)} %bitcast.21), channel_id=1, replica_groups=mesh['gx'=8,'gy'=8,'ga'=2] {'gx','gy','ga'}, dimensions={0} | all-to-all | bytes 262144 | tf_op jit(solution)/shard_map/all_to_all | solution.py:362
  83.2 2.3 %shard_map.132 = f32[64,4,128]{2,1,0:T(4,128)S(1)} custom-call(f32[256,128]{1,0:T(8,128)S(1)} %bitcast.22, bf16[64,32,128]{2,1,0:T(8,128)(2,1)S(1)} %all-to-all-done.after.weights, bf16[5,256,256]{2,1,0:T(8,128)(2,1)S(1)} %copy-done.10), custom_call_target="tpu_custom_call" | custom-call | flops 10000000 | bytes 1048576 | tf_op jit(solution)/shard_map/pallas_call | solution.py:421
  85.5 0.0 copy-start.15
  85.5 14.2 %all_to_all.27 = f32[128,2,128]{2,1,0:T(2,128)S(1)} all-to-all(f32[128,2,128]{2,1,0:T(2,128)S(1)} %bitcast.23), channel_id=1, replica_groups=mesh['gx'=8,'gy'=8,'ga'=2] {'gx','gy','ga'}, dimensions={0} | all-to-all | bytes 262144 | tf_op jit(solution)/shard_map/all_to_all | solution.py:362
  99.6 1.8 %shard_map.133 = bf16[8,256,128]{2,1,0:T(8,128)(2,1)} custom-call(f32[64,4,128]{2,1,0:T(4,128)S(1)} %bitcast.20, bf16[2,512,512]{2,1,0:T(8,128)(2,1)S(1)} %copy-done.5, bf16[384,1024]{1,0:T(8,128)(2,1)S(1)} %copy-done.7), custom_call_target="tpu_custom_call" | custom-call | flops 10000000 | bytes 1048576 | tf_op jit(solution)/shard_map/pallas_call | solution.py:425
  101.4 3.5 %all-to-all-start.4 = ((bf16[8,256,128]{2,1,0:T(8,128)(2,1)}), bf16[8,256,128]{2,1,0:T(8,128)(2,1)S(1)}, u32[]{:S(2)}, u32[]{:S(2)}) async-start(bf16[8,256,128]{2,1,0:T(8,128)(2,1)} %shard_map.133), calls=%async_computation.4 | async-start | bytes 1048576 | tf_op jit(solution)/shard_map/all_to_all | solution.py:362
  104.9 0.1 copy.15
  105.0 0.0 copy-start.16
  105.0 0.5 collective-permute-start.5
  105.5 1.6 %multiply_bitcast_fusion = bf16[32,8,32,8]{3,2,1,0:T(8,128)(2,1)} fusion(bf16[32,32]{0,1:T(8,128)(2,1)S(1)} %copy.15, bf16[8,8]{1,0:T(8,128)(2,1)S(1)} %fusion), kind=kLoop, calls=%fused_computation | loop fusion | flops 65536 | bytes 133248 | tf_op jit(solution)/shard_map/co,xy->oxcy/transpose | solution.py:404
  107.1 4.1 %reshape.32.mix = bf16[256,256]{1,0:T(8,128)(2,1)S(1)} reshape(bf16[32,8,32,8]{3,2,1,0:T(8,128)(2,1)} %multiply_bitcast_fusion) | data formatting | bytes 262144 | tf_op jit(solution)/shard_map/reshape | solution.py:404
  111.1 0.1 broadcast_in_dim.10
  111.2 0.1 broadcast_in_dim.11
  111.3 0.0 collective-permute-done.5.got
  111.3 0.1 broadcast_in_dim.12.obias
  111.4 2.9 %shard_map.134.direct = f32[8,256,128]{2,1,0:T(8,128)S(1)} custom-call(f32[160,128]{1,0:T(8,128)S(1)} %get-tuple-element.15.keep, f32[160,128]{1,0:T(8,128)S(1)} %collective-permute-done.5.got, f32[5,32]{1,0:T(8,128)S(1)} %copy-done.13, f32[32]{0:T(128)S(1)} %copy-done.14, bf16[256,256]{1,0:T(8,128)(2,1)S(1)} %reshape.32.mix, ...), custom_call_target="tpu_custom_call" | custom-call | flops 300000000 | bytes 1048576 | tf_op jit(solution)/shard_map/pallas_call | solution.py:406
  114.3 0.5 all-to-all-done.4.got
  114.7 1.8 %shard_map.135 = bf16[8,32,8,128]{3,2,1,0:T(8,128)(2,1)} custom-call(bf16[8,256,128]{2,1,0:T(8,128)(2,1)S(1)} %all-to-all-done.4.got, f32[8,256,128]{2,1,0:T(8,128)S(1)} %shard_map.134.direct), custom_call_target="tpu_custom_call" | custom-call | flops 10000000 | bytes 1048576 | tf_op jit(solution)/shard_map/pallas_call | solution.py:429
  (21 shorter events, 0.0 us)
Async XLA Ops:
  0.0 3.5 %collective-permute-start = (f32[5,128,256]{2,1,0:T(8,128)}, f32[5,128,256]{2,1,0:T(8,128)S(1)}, u32[]{:S(2)}, u32[]{:S(2)}) collective-permute-start(f32[5,128,256]{2,1,0:T(8,128)} %bitcast.11), channel_id=1, source_target_pairs={{0,1},{1,0},{2,3},{3,2},{4,5},{5,4},{6,7},{7,6},{8,9},{9,8},{10,11... | collective-permute-start | bytes 1966088 | tf_op jit(solution)/shard_map/ppermute | solution.py:371
  1.4 2.1 %collective-permute-start.1 = (f32[128,256]{1,0:T(8,128)}, f32[128,256]{1,0:T(8,128)S(1)}, u32[]{:S(2)}, u32[]{:S(2)}) collective-permute-start(f32[128,256]{1,0:T(8,128)} %bitcast.15), channel_id=1, source_target_pairs={{0,1},{1,0},{2,3},{3,2},{4,5},{5,4},{6,7},{7,6},{8,9},{9,8},{10,11... | collective-permute-start | bytes 393224 | tf_op jit(solution)/shard_map/ppermute | solution.py:371
  3.5 1.1 copy-start
  4.6 0.9 copy-start.2
  5.5 1.2 %copy-start.4 = (f32[4,4,32,4,128]{4,3,2,1,0:T(4,128)S(1)}, f32[4,4,32,4,128]{4,3,2,1,0:T(4,128)}, u32[]{:S(2)}) copy-start(f32[4,4,32,4,128]{4,3,2,1,0:T(4,128)} %param.18) | copy-start | bytes 3145732
  5.5 28.1 %copy-start.1 = (f32[5,8,16,256]{3,2,1,0:T(8,128)S(1)}, f32[5,8,16,256]{3,2,1,0:T(8,128)}, u32[]{:S(2)}) copy-start(f32[5,8,16,256]{3,2,1,0:T(8,128)} %param.13) | copy-start | bytes 1966084
  5.5 28.1 %copy-start.3 = (f32[8,16,256]{2,1,0:T(8,128)S(1)}, f32[8,16,256]{2,1,0:T(8,128)}, u32[]{:S(2)}) copy-start(f32[8,16,256]{2,1,0:T(8,128)} %param.14) | copy-start | bytes 393220
  6.8 39.1 %copy-start.12 = (bf16[256,128]{1,0:T(8,128)(2,1)S(1)}, bf16[256,128]{1,0:T(8,128)(2,1)}, u32[]{:S(2)}) copy-start(bf16[256,128]{1,0:T(8,128)(2,1)} %constant.12.clone.pairs) | copy-start | bytes 196612
  8.3 37.5 %all-to-all-start = ((bf16[64,32,128]{2,1,0:T(8,128)(2,1)}), bf16[64,32,128]{2,1,0:T(8,128)(2,1)S(1)}, u32[]{:S(2)}, u32[]{:S(2)}) async-start(bf16[64,32,128]{2,1,0:T(8,128)(2,1)} %shard_map.129), calls=%async_computation | async-start | bytes 1048576 | tf_op jit(solution)/shard_map/all_to_all | solution.py:362
  19.6 43.9 %copy-start.6 = (bf16[2,512,512]{2,1,0:T(8,128)(2,1)S(1)}, bf16[2,512,512]{2,1,0:T(8,128)(2,1)}, u32[]{:S(2)}) copy-start(bf16[2,512,512]{2,1,0:T(8,128)(2,1)} %constant.15.clone.zf) | copy-start | bytes 3145732
  19.6 43.9 %copy-start.13 = (f32[5,32]{1,0:T(8,128)S(1)}, f32[5,32]{1,0:T(8,128)}, u32[]{:S(2)}) copy-start(f32[5,32]{1,0:T(8,128)} %weight.3) | copy-start | bytes 1924
  19.6 43.9 %copy-start.14 = (f32[32]{0:T(128)S(1)}, f32[32]{0:T(128)}, u32[]{:S(2)}) copy-start(f32[32]{0:T(128)} %bias.3) | copy-start | bytes 388
  19.6 14.0 %collective-permute-start.2 = (f32[6,2,48,128]{3,2,1,0:T(8,128)S(1)}, f32[6,2,48,128]{3,2,1,0:T(8,128)S(1)}, u32[]{:S(2)}, u32[]{:S(2)}) collective-permute-start(f32[6,2,48,128]{3,2,1,0:T(8,128)S(1)} %shard_map.127.after), channel_id=1, source_target_pairs={{0,113},{16,1},{32,17},{48,33},{64,49},{80,65},{96,81},{112,97},{1... | collective-permute-start | bytes 884744 | tf_op jit(solution)/shard_map/ppermute | solution.py:376
  34.2 0.9 copy-start.8
  35.1 5.5 %collective-permute-start.3 = (f32[3,16,128]{2,1,0:T(8,128)S(1)}, f32[3,16,128]{2,1,0:T(8,128)S(1)}, u32[]{:S(2)}, u32[]{:S(2)}) collective-permute-start(f32[3,16,128]{2,1,0:T(8,128)S(1)} %get-tuple-element.12), channel_id=1, source_target_pairs={{0,14},{2,0},{4,2},{6,4},{8,6},{10,8},{12,10},{14,12},{1,15},{3,1}... | collective-permute-start | bytes 73736 | tf_op jit(solution)/shard_map/ppermute | solution.py:365
  39.6 6.3 %collective-permute-start.4 = (f32[3,16,128]{2,1,0:T(8,128)S(1)}, f32[3,16,128]{2,1,0:T(8,128)S(1)}, u32[]{:S(2)}, u32[]{:S(2)}) collective-permute-start(f32[3,16,128]{2,1,0:T(8,128)S(1)} %get-tuple-element.13), channel_id=1, source_target_pairs={{0,2},{2,4},{4,6},{6,8},{8,10},{10,12},{12,14},{14,0},{1,3},{3,5},... | collective-permute-start | bytes 73736 | tf_op jit(solution)/shard_map/ppermute | solution.py:365
  45.9 1.1 copy-start.9
  47.0 16.5 %copy-start.11 = (bf16[256,1024]{1,0:T(8,128)(2,1)S(1)}, bf16[256,1024]{1,0:T(8,128)(2,1)}, u32[]{:S(2)}) copy-start(bf16[256,1024]{1,0:T(8,128)(2,1)} %constant.13.clone.yf) | copy-start | bytes 1572868
  47.0 36.2 %copy-start.10 = (bf16[5,256,256]{2,1,0:T(8,128)(2,1)S(1)}, bf16[5,256,256]{2,1,0:T(8,128)(2,1)}, u32[]{:S(2)}) copy-start(bf16[5,256,256]{2,1,0:T(8,128)(2,1)} %constant.17.clone.x_tables) | copy-start | bytes 1966084
  54.2 45.5 %copy-start.5 = (bf16[2,512,512]{2,1,0:T(8,128)(2,1)S(1)}, bf16[2,512,512]{2,1,0:T(8,128)(2,1)}, u32[]{:S(2)}) copy-start(bf16[2,512,512]{2,1,0:T(8,128)(2,1)} %constant.16.clone.zi) | copy-start | bytes 3145732
  54.2 45.5 %copy-start.7 = (bf16[384,1024]{1,0:T(8,128)(2,1)S(1)}, bf16[384,1024]{1,0:T(8,128)(2,1)}, u32[]{:S(2)}) copy-start(bf16[384,1024]{1,0:T(8,128)(2,1)} %constant.14.clone.yi) | copy-start | bytes 2359300
  85.5 19.4 %copy-start.15 = (bf16[32,32]{1,0:T(8,128)(2,1)S(1)}, bf16[32,32]{1,0:T(8,128)(2,1)}, u32[]{:S(2)}) copy-start(bf16[32,32]{1,0:T(8,128)(2,1)} %param.17) | copy-start | bytes 6148
  101.4 13.3 %all-to-all-start.4 = ((bf16[8,256,128]{2,1,0:T(8,128)(2,1)}), bf16[8,256,128]{2,1,0:T(8,128)(2,1)S(1)}, u32[]{:S(2)}, u32[]{:S(2)}) async-start(bf16[8,256,128]{2,1,0:T(8,128)(2,1)} %shard_map.133), calls=%async_computation.4 | async-start | bytes 1048576 | tf_op jit(solution)/shard_map/all_to_all | solution.py:362
  105.0 6.1 %copy-start.16 = (f32[32]{0:T(128)S(1)}, f32[32]{0:T(128)}, u32[]{:S(2)}) copy-start(f32[32]{0:T(128)} %param.19) | copy-start | bytes 388
  105.0 6.3 %collective-permute-start.5 = (f32[160,128]{1,0:T(8,128)S(1)}, f32[160,128]{1,0:T(8,128)S(1)}, u32[]{:S(2)}, u32[]{:S(2)}) collective-permute-start(f32[160,128]{1,0:T(8,128)S(1)} %get-tuple-element.16), channel_id=1, source_target_pairs={{0,1},{1,0},{2,3},{3,2},{4,5},{5,4},{6,7},{7,6},{8,9},{9,8},{10,11... | collective-permute-start | bytes 245768 | tf_op jit(solution)/shard_map/ppermute | solution.py:412

commit v4 on v3

--- a/solution.py
+++ b/solution.py
@@ -32,9 +32,6 @@
 @functools.cache
 def tables():
     out = {}
-    pairs = np.zeros((YL, YL // 2), np.float32)
-    pairs[np.arange(YL), np.arange(YL) // 2] = 0.25
-    out["pairs"] = pairs.astype(jnp.bfloat16)
     ky = np.arange(MY) - MY // 2
     cy, sy = cos_sin(ky, np.arange(GY), GY)
     rows = np.concatenate([cy, -sy]) / math.sqrt(GY)
@@ -85,6 +82,10 @@
     return out
 
 
+def iotas(shape):
+    return lax.broadcasted_iota(jnp.int32, shape, 0), lax.broadcasted_iota(jnp.int32, shape, 1)
+
+
 def halves(value):
     high = value.astype(BF16)
     return high, (value - high.astype(F32)).astype(BF16)
@@ -122,23 +123,29 @@
     return (own if slot < 8 else other)[pl.ds(pl.multiple_of(start, 8), 8), :]
 
 
-def pack_x(f, s, fp, sp, message, rows):
+def edge_rows(f, s, out, rows):
     bottom = lax.axis_index("ga") == 0
     for field in range(6):
-        for which, whole in enumerate(((s, sp) if field == 5 else (f.at[field], fp.at[field]))):
-            for h in range(2):
-                rows[which, field, h] = whole[:, 128 * h : 128 * h + 128]
-    for field in range(6):
         for h in range(2):
-            for which in range(2):
-                for d in range(3):
-                    first = rows[which, field, h, pl.ds(d, 8, stride=XL), :]
-                    last = rows[which, field, h, pl.ds(XL - 1 - d, 8, stride=XL), :]
-                    at = 24 * which + 8 * d
-                    message[field, h, at : at + 8, :] = jnp.where(bottom, first, last)
-
-
-def pack_y(f, s, fp, sp, message, outer, low, high):
+            lanes = slice(128 * h, 128 * h + 128)
+            rows[field, h] = s[:, lanes] if field == 5 else f[field, :, lanes]
+            for d in range(3):
+                first = rows[field, h, pl.ds(d, 8, stride=XL), :]
+                last = rows[field, h, pl.ds(XL - 1 - d, 8, stride=XL), :]
+                out[field, h, 8 * d : 8 * d + 8, :] = jnp.where(bottom, first, last)
+
+
+def pack_own(f, s, own, rows):
+    edge_rows(f, s, own, rows)
+
+
+def pack_other(fp, sp, own, message, other, rows):
+    edge_rows(fp, sp, other, rows)
+    message[:, :, 0:24, :] = own[...]
+    message[:, :, 24:48, :] = other[...]
+
+
+def pack_y(f, s, fp, sp, message, outer, far, near):
     refs = (f, s, fp, sp)
     a = lax.axis_index("ga")
     row = lax.broadcasted_iota(jnp.int32, (8, 128), 0)
@@ -167,16 +174,16 @@
             lows = jnp.where(here, pltpu.roll(first, base, 1) if base else first, lows)
             highs = jnp.where(here, pltpu.roll(last, (base + 4) % 128, 1) if base != 124 else last, highs)
         if field % 2:
-            low[field // 2] = lows
-            high[field // 2] = highs
-
-
-def stencil(
-    f, s, fp, sp, outer, ylow, yhigh, pairs, after, keep, send, narrow, a, b, stiff, last, sums
-):
+            even = lax.axis_index("gy") % 2 == 0
+            far[field // 2] = jnp.where(even, lows, highs)
+            near[field // 2] = jnp.where(even, highs, lows)
+
+
+def stencil(f, s, fp, sp, outer, far, near, last, a, b, stiff):
     refs = (f, s, fp, sp)
     core = lax.axis_index("ga")
-    near = lax.broadcasted_iota(jnp.int32, (16, 128), 1) < 64
+    even = lax.axis_index("gy") % 2 == 0
+    first_lanes = lax.broadcasted_iota(jnp.int32, (16, 128), 1) < 64
     for field in range(6):
         for slot in range(16):
             to = stiff.at[slot] if field == 5 else a.at[field, slot]
@@ -185,10 +192,11 @@
                 edge = outer[field, h, 8 * slot : 8 * slot + 8, :]
                 to[8:16, 128 * h : 128 * h + 128] = edge
             base = 64 * (field % 2) + 4 * slot
-            above, below = ylow[field // 2], yhigh[field // 2]
+            one, two = near[field // 2], far[field // 2]
+            above, below = jnp.where(even, one, two), jnp.where(even, two, one)
             above = pltpu.roll(above, 128 - base, 1) if base else above
             below = pltpu.roll(below, 124 - base, 1) if base != 124 else below
-            to[:, 256:384] = jnp.where(near, above, below)
+            to[:, 256:384] = jnp.where(first_lanes, above, below)
 
     def advance(src, slot, crop):
         new, east, north, depth = [], [], [], []
@@ -229,6 +237,8 @@
 
         lax.fori_loop(0, 16, body, 0)
 
+
+def coarsen(last, after, keep, send, narrow, sums):
     for half in range(2):
         for x in range(4):
             for field in range(5):
@@ -241,7 +251,8 @@
     high = value.astype(BF16)
     rest = value - high.astype(F32)
     mid, low = halves(rest)
-    table = pairs[...]
+    row, lane = iotas((256, 128))
+    table = jnp.where(row // 2 == lane, 0.25, 0.0).astype(BF16)
     mean = dot(high, table) + dot(mid, table) + dot(low, table)
     keep[...] = mean[:160]
     send[...] = mean[160:]
@@ -266,10 +277,16 @@
     a = lax.axis_index("ga")
     wide[pl.ds(pl.multiple_of(160 * a, 8), 160), :] = keep[...]
     wide[pl.ds(pl.multiple_of(160 * (1 - a), 8), 160), :] = got[...]
+    row, lane = iotas((256, 32))
+    pick = (row // 8 == lane).astype(BF16)
+    bias_o = jnp.sum(jnp.where(row // 8 == lane, obias[...], 0.0), axis=1, keepdims=True)
+    by_row = dot(pick, mix[...], ((1,), (1,))).astype(BF16)
+    row, lane = iotas((256, 256))
+    spread = jnp.where(row % 8 == lane % 8, dot(by_row, pick, ((1,), (1,))), 0.0).astype(BF16)
 
     def body(z, carry):
         values = [wide[pl.ds(8 * field + z, 8, stride=40), :] for field in range(5)]
-        out[z] = dot(mix[...], lift_rows(values, weight, bias)) + obias[...]
+        out[z] = dot(spread, lift_rows(values, weight, bias)) + bias_o
         return carry
 
     lax.fori_loop(0, ZL, body, 0)
@@ -288,11 +305,7 @@
         out[:, part, :] = result[:, 128 * part : 128 * part + 128]
 
 
-def iotas(shape):
-    return lax.broadcasted_iota(jnp.int32, shape, 0), lax.broadcasted_iota(jnp.int32, shape, 1)
-
-
-def mix_modes(got, weights, x_tables, out):
+def mix_modes(got, weights, x_tables, after, out):
     high, low = halves(got[...])
     row, lane = iotas((128, 128))
     modes = jnp.zeros((256, 128), F32)
@@ -303,8 +316,8 @@
     real, imag = modes[:128], modes[128:]
     total = jnp.zeros((256, 128), F32)
     for i in range(8):
-        wr = weights[8 * i : 8 * i + 8, 0:16, :].astype(F32).reshape(128, 128)
-        wi = weights[8 * i : 8 * i + 8, 16:32, :].astype(F32).reshape(128, 128)
+        wr = weights[:, i, 0:16, :].astype(F32).reshape(128, 128)
+        wi = weights[:, i, 16:32, :].astype(F32).reshape(128, 128)
         part = jnp.concatenate([wr * real - wi * imag, wr * imag + wi * real], axis=0)
         p_high, p_low = halves(part)
         gather = (lane % 32 == 4 * i + row % 4).astype(BF16)
@@ -361,55 +374,63 @@
     def exchange(value, axis):
         return lax.all_to_all(value, axis, split_axis=0, concat_axis=0, tiled=True)
 
-    def shift(value, axis, by):
-        return lax.ppermute(value, axis, [(i, (i + by) % 8) for i in range(8)])
-
     anywhere = pl.BlockSpec(memory_space=pl.ANY)
     f = fields.reshape(5, 128, 256)
     s = stiffness.reshape(128, 256)
     swap = [(0, 1), (1, 0)]
     fp, sp = lax.ppermute(f, "ga", swap), lax.ppermute(s, "ga", swap)
-    copied = [pltpu.VMEM((2, 6, 2, 128, 128), F32)]
-    [message] = call(pack_x, [((6, 2, 48, 128), F32)], [VMEM] * 4, copied)(f, s, fp, sp)
+    rows = pltpu.VMEM((6, 2, 128, 128), F32)
+    edges = ((6, 2, 24, 128), F32)
+    [own] = call(pack_own, [edges], [VMEM] * 2, [rows])(f, s)
+    [message] = call(
+        pack_other, [((6, 2, 48, 128), F32)], [VMEM] * 3, [pltpu.VMEM(*edges), rows]
+    )(fp, sp, own)
     across = [(2 * i, 2 * ((i - 1) % 8) + 1) for i in range(8)]
     across += [(2 * i + 1, 2 * ((i + 1) % 8)) for i in range(8)]
     got = lax.ppermute(message, ("gx", "ga"), across)
 
-    turned = [pltpu.VMEM((64, 32, 128), F32)]
-    [turned] = call(turn_weights, [((64, 32, 128), BF16)], [VMEM, anywhere], turned)(
-        spectral_weight.reshape(2048, 128), message
-    )
-    weights = exchange(turned, ("gx", "gy"))
+    [turned] = call(
+        turn_weights,
+        [((64, 32, 128), BF16)],
+        [VMEM, anywhere],
+        [pltpu.VMEM((64, 32, 128), F32)],
+        size=2 * 10**7,
+    )(spectral_weight.reshape(2048, 128), message)
+    hop = exchange(turned.reshape(8, 8, 32, 128), "gx")
+    weights = exchange(jnp.transpose(hop, (1, 0, 2, 3)), "gy")
 
     message = ((3, 16, 128), F32)
-    outer, low, high = call(pack_y, [((6, 2, 128, 128), F32), message, message], [VMEM] * 5)(
-        f, s, fp, sp, got
-    )
-    ylow, yhigh = shift(low, "gy", -1), shift(high, "gy", 1)
-    keep, send, narrow = call(
+    outer, far, near = call(
+        pack_y, [((6, 2, 128, 128), F32), message, message], [VMEM] * 5, flops=10**12
+    )(f, s, fp, sp, got)
+    far = lax.ppermute(far, "gy", [(j, (j - 1 + 2 * (j % 2)) % 8) for j in range(8)])
+    near = lax.ppermute(near, "gy", [(j, j + 1 - 2 * (j % 2)) for j in range(8)])
+    [last] = call(
         stencil,
-        [((160, 128), F32), ((160, 128), F32), ((8, 48, 128), BF16)],
-        [VMEM] * 8 + [anywhere],
+        [((5, 2, 128, 128), F32)],
+        [VMEM] * 7,
         [
             pltpu.VMEM((5, 16, 16, 384), F32),
             pltpu.VMEM((5, 16, 16, 384), F32),
             pltpu.VMEM((16, 16, 384), F32),
-            pltpu.VMEM((5, 2, 128, 128), F32),
-            pltpu.VMEM((320, 256), F32),
         ],
-        mib=24,
-    )(f, s, fp, sp, outer, ylow, yhigh, table["pairs"], weights)
+        flops=10**12,
+    )(f, s, fp, sp, outer, far, near)
+    keep, send, narrow = call(
+        coarsen,
+        [((160, 128), F32), ((160, 128), F32), ((8, 48, 128), BF16)],
+        [VMEM, anywhere],
+        [pltpu.VMEM((320, 256), F32)],
+    )(last, weights)
 
     columns = exchange(narrow, "gy")
-    spread = jnp.einsum("co,xy->oxcy", mix_weight, jnp.eye(8, dtype=BF16)).reshape(256, 256)
-    obias = jnp.broadcast_to(jnp.repeat(output_bias, 8)[:, None], (256, 128))
     [direct] = call(
         pointwise,
         [((8, 256, 128), F32)],
         [VMEM, VMEM, SMEM, SMEM, VMEM, VMEM],
         [pltpu.VMEM((320, 128), F32)],
         flops=3 * 10**8,
-    )(keep, lax.ppermute(send, "ga", swap), lift_weight, lift_bias, spread, obias)
+    )(keep, lax.ppermute(send, "ga", swap), lift_weight, lift_bias, mix_weight, output_bias.reshape(1, C))
 
     [modes] = call(
         forward,
@@ -418,8 +439,8 @@
         [pltpu.VMEM((256, 1024), BF16)],
     )(columns, lift_weight, lift_bias, table["yf"], table["zf"])
     modes = exchange(modes.reshape(128, 2, 128), everyone)
-    [mixed] = call(mix_modes, [((64, 4, 128), F32)], [VMEM] * 3, mib=24)(
-        modes.reshape(256, 128), weights, table["x"]
+    [mixed] = call(mix_modes, [((64, 4, 128), F32)], [VMEM] * 3 + [anywhere])(
+        modes.reshape(256, 128), weights, table["x"], direct
     )
     mixed = exchange(mixed.reshape(128, 2, 128), everyone)
     [spectral] = call(inverse, [((8, 256, 128), BF16)], [VMEM] * 3)(

time: 118 us -> 108 us (0.915)
  waiting for transfers between devices: 21 us -> 9.13 us
  starting transfers between devices: 23 us -> 32 us
  local copies, waits for them, and re-layouts: 9.4 us -> 5.05 us
  blocking collectives: 40.9 us -> 38.1 us
  other arithmetic: 1.56 us -> 0 us
  Pallas kernels: 20.4 us -> 21.8 us
    ppermute x1, waiting for transfers between devices: 12.1 us -> 0.61 us  [shards(): got = lax.ppermute(message, ('gx', 'ga'), across)]
    all_to_all x2 -> x3, waiting for transfers between devices: 0.49 us -> 7.59 us  [exchange(): return lax.all_to_all(value, axis, split_axis=0, concat_axis=0, tiled=True)]
    all_to_all x2 -> x3, starting transfers between devices: 14.7 us -> 21 us  [exchange(): return lax.all_to_all(value, axis, split_axis=0, concat_axis=0, tiled=True)]
    ppermute x2, waiting for transfers between devices: 6.29 us -> 0.01 us  [the longest x1 0.01 us: shards(): lax.ppermute(near, 'gy', [(j, j + 1 - 2 * (j % 2)) for j in range(8)])]
    reshape x1 -> x0, local copies, waits for them, and re-layouts: 4.05 us -> none  [shards(): jnp.einsum('co,xy->oxcy', mix_weight, jnp.eye(8, dtype=BF16))]
    all_to_all x3, blocking collectives: 40.9 us -> 38.1 us  [exchange(): return lax.all_to_all(value, axis, split_axis=0, concat_axis=0, tiled=True)]
    ppermute x2, waiting for transfers between devices: 2.12 us -> 0.01 us  [shards(): fp, sp = (lax.ppermute(f, 'ga', swap), lax.ppermute(s, 'ga', swap))]
    ppermute x2, starting transfers between devices: 4.51 us -> 6.61 us  [the longest x1 6.6 us: shards(): lax.ppermute(far, 'gy', [(j, (j - 1 + 2 * (j % 2)) % 8) for j in range(8)])]
  transfers between devices with their start and end apart: 8 -> 9, of which waited for: 5 -> 5; matrix products, arithmetic and copies ran while one was open for 5% -> 2% of each run, Pallas kernels for 3% -> 12%
where the time goes in v4:
time: 108 us; the launch traced here: 106 us
  blocking collectives  38.1 us (35%)
  starting transfers between devices  32 us (30%)
  Pallas kernels  21.8 us (20%)
  waiting for transfers between devices  9.13 us (8%)
  local copies, waits for them, and re-layouts  5.05 us (5%)
    all_to_all x3, blocking collectives, exchange(): return lax.all_to_all(value, axis, split_axis=0, concat_axis=0, tiled=True)  38.1 us
    all_to_all x3, starting transfers between devices, exchange(): return lax.all_to_all(value, axis, split_axis=0, concat_axis=0, tiled=True)  21 us
    all_to_all x3, waiting for transfers between devices, exchange(): return lax.all_to_all(value, axis, split_axis=0, concat_axis=0, tiled=True)  7.59 us
    pallas_call x1, Pallas kernels, shards(): call(stencil, [((5, 2, 128, 128), F32)], [VMEM] * 7, [pltpu.VMEM((5, 16,...  6.83 us
    ppermute x1, starting transfers between devices, shards(): lax.ppermute(far, 'gy', [(j, (j - 1 + 2 * (j % 2)) % 8) for j in range(8)])  6.6 us
    pallas_call x1, Pallas kernels, shards(): call(mix_modes, [((64, 4, 128), F32)], [VMEM] * 3 + [anywhere])  3.46 us
    pallas_call x1, Pallas kernels, shards(): call(pointwise, [((8, 256, 128), F32)], [VMEM, VMEM, SMEM, SMEM, VMEM, VM...  3.18 us
    unnamed x28, local copies, waits for them, and re-layouts  3.17 us
  transfers between devices with their start and end apart: 9, of which 5 were waited for; matrix products, arithmetic and copies ran while one was open for 2% of the time, Pallas kernels for 12%

profile of v4, /device:TPU:1, one launch (start us, length us, event | category | flops | bytes accessed | tf_op | source)
XLA Modules:
  0.0 106.2 jit_solution(6002524721133456662)
XLA Ops:
  0.0 1.4 %collective-permute-start = (f32[5,128,256]{2,1,0:T(8,128)}, f32[5,128,256]{2,1,0:T(8,128)S(1)}, u32[]{:S(2)}, u32[]{:S(2)}) collective-permute-start(f32[5,128,256]{2,1,0:T(8,128)} %bitcast.13), channel_id=1, source_target_pairs={{0,1},{1,0},{2,3},{3,2},{4,5},{5,4},{6,7},{7,6},{8,9},{9,8},{10,11... | collective-permute-start | bytes 1966088 | tf_op jit(solution)/shard_map/ppermute | solution.py:381
  1.4 0.0 collective-permute-start.1
  1.4 1.2 %copy-done.4 = f32[5,8,16,256]{3,2,1,0:T(8,128)S(1)} copy-done((f32[5,8,16,256]{3,2,1,0:T(8,128)S(1)}, f32[5,8,16,256]{3,2,1,0:T(8,128)}, u32[]{:S(2)}) %copy-start.4) | copy-done | bytes 655384
  2.6 0.9 copy-done.8
  3.5 0.1 shard_map.118.own
  3.7 0.0 collective-permute-done.1.sp
  3.7 0.0 collective-permute-done.fp
  3.7 0.1 shard_map.119.after
  3.8 1.7 %collective-permute-start.2 = (f32[6,2,48,128]{3,2,1,0:T(8,128)S(1)}, f32[6,2,48,128]{3,2,1,0:T(8,128)S(1)}, u32[]{:S(2)}, u32[]{:S(2)}) collective-permute-start(f32[6,2,48,128]{3,2,1,0:T(8,128)S(1)} %shard_map.119.after), channel_id=1, source_target_pairs={{0,113},{16,1},{32,17},{48,33},{64,49},{80,65},{96,81},{112,97},{1... | collective-permute-start | bytes 884744 | tf_op jit(solution)/shard_map/ppermute | solution.py:390
  5.5 0.0 copy-done
  5.5 1.6 %shard_map.122 = bf16[64,32,128]{2,1,0:T(8,128)(2,1)} custom-call(f32[2048,128]{1,0:T(8,128)S(1)} %bitcast.12, f32[6,2,48,128]{3,2,1,0:T(8,128)S(1)} %shard_map.119.after), custom_call_target="tpu_custom_call" | custom-call | flops 10000000 | bytes 20000000 | tf_op jit(solution)/shard_map/pallas_call | solution.py:392
  7.1 5.0 %all-to-all-start = ((bf16[8,8,32,128]{3,2,1,0:T(8,128)(2,1)}), bf16[8,8,32,128]{3,2,1,0:T(8,128)(2,1)}, u32[]{:S(2)}, u32[]{:S(2)}) async-start(bf16[8,8,32,128]{3,2,1,0:T(8,128)(2,1)} %bitcast.3), calls=%async_computation | async-start | bytes 1048576 | tf_op jit(solution)/shard_map/all_to_all | solution.py:375
  12.1 0.6 collective-permute-done.2.message
  12.7 0.0 copy-done.5
  12.7 0.0 copy-done.9
  12.7 0.5 shard_map.120
  13.3 6.6 %collective-permute-start.3 = (f32[3,16,128]{2,1,0:T(8,128)S(1)}, f32[3,16,128]{2,1,0:T(8,128)S(1)}, u32[]{:S(2)}, u32[]{:S(2)}) collective-permute-start(f32[3,16,128]{2,1,0:T(8,128)S(1)} %get-tuple-element.12), channel_id=1, source_target_pairs={{0,14},{2,4},{4,2},{6,8},{8,6},{10,12},{12,10},{14,0},{1,15},{3,5}... | collective-permute-start | bytes 73736 | tf_op jit(solution)/shard_map/ppermute | solution.py:406
  19.9 0.0 collective-permute-start.4
  19.9 0.7 all-to-all-done
  20.5 1.9 %copy.16 = bf16[8,8,32,128]{3,2,0,1:T(8,128)(2,1)} copy(bf16[8,8,32,128]{3,2,1,0:T(8,128)(2,1)} %all-to-all-done) | data formatting | bytes 1048576 | tf_op jit(solution)/shard_map/all_to_all | solution.py:375
  22.4 7.8 %all-to-all-start.1 = ((bf16[8,8,32,128]{3,2,1,0:T(8,128)(2,1)}), bf16[8,8,32,128]{3,2,1,0:T(8,128)(2,1)}, u32[]{:S(2)}, u32[]{:S(2)}) async-start(bf16[8,8,32,128]{3,2,1,0:T(8,128)(2,1)} %bitcast.11), calls=%async_computation.1 | async-start | bytes 1048576 | tf_op jit(solution)/shard_map/all_to_all | solution.py:375
  30.2 0.0 collective-permute-done.3.far
  30.2 0.0 collective-permute-done.4.near
  30.2 6.8 %shard_map.121.last = f32[5,2,128,128]{3,2,1,0:T(8,128)S(1)} custom-call(f32[5,128,256]{2,1,0:T(8,128)S(1)} %bitcast.16, f32[128,256]{1,0:T(8,128)S(1)} %bitcast.23, f32[5,128,256]{2,1,0:T(8,128)S(1)} %collective-permute-done.fp, f32[128,256]{1,0:T(8,128)S(1)} %collective-permute-done.1.sp, f32[6,2,128,128]{3,2,1,0:T(8,128)S(1)} %get-tuple-element.11.outer, ...), custom_call_target="tpu_custom_call" | custom-call | flops 999999995904 | bytes 1048576 | tf_op jit(solution)/shard_map/pallas_call | solution.py:408
  37.1 0.0 copy-start.2
  37.1 2.1 %all-to-all-done.1.after.weights = bf16[8,8,32,128]{3,2,1,0:T(8,128)(2,1)} async-done(((bf16[8,8,32,128]{3,2,1,0:T(8,128)(2,1)}), bf16[8,8,32,128]{3,2,1,0:T(8,128)(2,1)}, u32[]{:S(2)}, u32[]{:S(2)}) %all-to-all-start.1) | async-done | bytes 524320 | tf_op jit(solution)/shard_map/all_to_all | solution.py:375
  39.1 0.3 shard_map.123
  39.4 0.0 copy-start.10
  39.5 0.0 copy-start.12
  39.5 11.2 %all_to_all.30.got = bf16[8,48,128]{2,1,0:T(8,128)(2,1)S(1)} all-to-all(bf16[8,48,128]{2,1,0:T(8,128)(2,1)S(1)} %get-tuple-element.14), channel_id=1, replica_groups=mesh['gx'=8,'gy'=8,'ga'=2] {'gy'}, dimensions={0} | all-to-all | bytes 196608 | tf_op jit(solution)/shard_map/all_to_all | solution.py:375
  50.7 0.0 copy-done.2
  50.7 0.0 copy-done.12
  50.7 0.0 copy-start.7
  50.7 1.0 copy-done.7
  51.7 2.9 %shard_map.124 = f32[64,4,128]{2,1,0:T(4,128)} custom-call(bf16[8,48,128]{2,1,0:T(8,128)(2,1)S(1)} %all_to_all.30.got, f32[5,32]{1,0:T(8,128)S(1)} %copy-done.10, f32[32]{0:T(128)S(1)} %copy-done.12, bf16[256,1024]{1,0:T(8,128)(2,1)S(1)} %copy-done.7, bf16[2,512,512]{2,1,0:T(8,128)(2,1)S(1)} %copy-done.2), custom_call_target="tpu_custom_call" | custom-call | flops 10000000 | bytes 1048576 | tf_op jit(solution)/shard_map/pallas_call | solution.py:435
  54.6 8.2 %all-to-all-start.3 = ((f32[128,2,128]{2,1,0:T(2,128)}), f32[128,2,128]{2,1,0:T(2,128)S(1)}, u32[]{:S(2)}, u32[]{:S(2)}) async-start(f32[128,2,128]{2,1,0:T(2,128)} %bitcast.5), calls=%async_computation.3 | async-start | bytes 262144 | tf_op jit(solution)/shard_map/all_to_all | solution.py:375
  62.8 0.0 copy-start.6
  62.8 1.3 %collective-permute-start.5 = (f32[160,128]{1,0:T(8,128)S(1)}, f32[160,128]{1,0:T(8,128)S(1)}, u32[]{:S(2)}, u32[]{:S(2)}) collective-permute-start(f32[160,128]{1,0:T(8,128)S(1)} %get-tuple-element.16), channel_id=1, source_target_pairs={{0,1},{1,0},{2,3},{3,2},{4,5},{5,4},{6,7},{7,6},{8,9},{9,8},{10,11... | collective-permute-start | bytes 245768 | tf_op jit(solution)/shard_map/ppermute | solution.py:433
  64.1 0.9 collective-permute-done.5.got
  65.0 3.2 %shard_map.125.after.direct = f32[8,256,128]{2,1,0:T(8,128)S(1)} custom-call(f32[160,128]{1,0:T(8,128)S(1)} %get-tuple-element.15.keep, f32[160,128]{1,0:T(8,128)S(1)} %collective-permute-done.5.got, f32[5,32]{1,0:T(8,128)S(1)} %copy-done.10, f32[32]{0:T(128)S(1)} %copy-done.12, bf16[32,32]{1,0:T(8,128)(2,1)S(1)} %copy-done.11, f32[1,32]{1,0:T(1,128)S(1)} %bitcast.24), custom_call_target="tpu_custom_call" | custom-call | flops 300000000 | bytes 1048576 | tf_op jit(solution)/shard_map/pallas_call | solution.py:427
  68.2 4.9 %all-to-all-done.3 = f32[128,2,128]{2,1,0:T(2,128)S(1)} async-done(((f32[128,2,128]{2,1,0:T(2,128)}), f32[128,2,128]{2,1,0:T(2,128)S(1)}, u32[]{:S(2)}, u32[]{:S(2)}) %all-to-all-start.3) | async-done | bytes 131104 | tf_op jit(solution)/shard_map/all_to_all | solution.py:375
  73.1 0.0 copy-done.6
  73.1 3.5 %shard_map.126 = f32[64,4,128]{2,1,0:T(4,128)S(1)} custom-call(f32[256,128]{1,0:T(8,128)S(1)} %bitcast.17, bf16[8,8,32,128]{3,2,1,0:T(8,128)(2,1)} %all-to-all-done.1.after.weights, bf16[5,256,256]{2,1,0:T(8,128)(2,1)S(1)} %copy-done.6, f32[8,256,128]{2,1,0:T(8,128)S(1)} %shard_map.125.after.direct), custom_call_target="tpu_custom_call" | custom-call | flops 10000000 | bytes 1048576 | tf_op jit(solution)/shard_map/pallas_call | solution.py:442
  76.6 14.3 %all_to_all.31 = f32[128,2,128]{2,1,0:T(2,128)S(1)} all-to-all(f32[128,2,128]{2,1,0:T(2,128)S(1)} %bitcast.18), channel_id=1, replica_groups=mesh['gx'=8,'gy'=8,'ga'=2] {'gx','gy','ga'}, dimensions={0} | all-to-all | bytes 262144 | tf_op jit(solution)/shard_map/all_to_all | solution.py:375
  90.9 0.0 copy-done.1
  90.9 1.0 shard_map.127
  91.8 12.6 %all_to_all.32.got = bf16[8,256,128]{2,1,0:T(8,128)(2,1)S(1)} all-to-all(bf16[8,256,128]{2,1,0:T(8,128)(2,1)S(1)} %shard_map.127), channel_id=1, replica_groups=mesh['gx'=8,'gy'=8,'ga'=2] {'gy'}, dimensions={0} | all-to-all | bytes 1048576 | tf_op jit(solution)/shard_map/all_to_all | solution.py:375
  104.5 1.8 %shard_map.128 = bf16[8,32,8,128]{3,2,1,0:T(8,128)(2,1)} custom-call(bf16[8,256,128]{2,1,0:T(8,128)(2,1)S(1)} %all_to_all.32.got, f32[8,256,128]{2,1,0:T(8,128)S(1)} %shard_map.125.after.direct), custom_call_target="tpu_custom_call" | custom-call | flops 10000000 | bytes 1048576 | tf_op jit(solution)/shard_map/pallas_call | solution.py:450
  (13 shorter events, 0.0 us)
Async XLA Ops:
  0.0 3.7 %collective-permute-start = (f32[5,128,256]{2,1,0:T(8,128)}, f32[5,128,256]{2,1,0:T(8,128)S(1)}, u32[]{:S(2)}, u32[]{:S(2)}) collective-permute-start(f32[5,128,256]{2,1,0:T(8,128)} %bitcast.13), channel_id=1, source_target_pairs={{0,1},{1,0},{2,3},{3,2},{4,5},{5,4},{6,7},{7,6},{8,9},{9,8},{10,11... | collective-permute-start | bytes 1966088 | tf_op jit(solution)/shard_map/ppermute | solution.py:381
  1.4 4.1 %copy-start = (f32[4,4,32,4,128]{4,3,2,1,0:T(4,128)S(1)}, f32[4,4,32,4,128]{4,3,2,1,0:T(4,128)}, u32[]{:S(2)}) copy-start(f32[4,4,32,4,128]{4,3,2,1,0:T(4,128)} %param.17) | copy-start | bytes 3145732
  1.4 2.2 %collective-permute-start.1 = (f32[128,256]{1,0:T(8,128)}, f32[128,256]{1,0:T(8,128)S(1)}, u32[]{:S(2)}, u32[]{:S(2)}) collective-permute-start(f32[128,256]{1,0:T(8,128)} %bitcast.20), channel_id=1, source_target_pairs={{0,1},{1,0},{2,3},{3,2},{4,5},{5,4},{6,7},{7,6},{8,9},{9,8},{10,11... | collective-permute-start | bytes 393224 | tf_op jit(solution)/shard_map/ppermute | solution.py:381
  1.4 1.2 %copy-start.4 = (f32[5,8,16,256]{3,2,1,0:T(8,128)S(1)}, f32[5,8,16,256]{3,2,1,0:T(8,128)}, u32[]{:S(2)}) copy-start(f32[5,8,16,256]{3,2,1,0:T(8,128)} %param.12) | copy-start | bytes 1966084
  2.6 0.9 copy-start.8
  3.8 8.9 %collective-permute-start.2 = (f32[6,2,48,128]{3,2,1,0:T(8,128)S(1)}, f32[6,2,48,128]{3,2,1,0:T(8,128)S(1)}, u32[]{:S(2)}, u32[]{:S(2)}) collective-permute-start(f32[6,2,48,128]{3,2,1,0:T(8,128)S(1)} %shard_map.119.after), channel_id=1, source_target_pairs={{0,113},{16,1},{32,17},{48,33},{64,49},{80,65},{96,81},{112,97},{1... | collective-permute-start | bytes 884744 | tf_op jit(solution)/shard_map/ppermute | solution.py:390
  7.1 5.6 %copy-start.5 = (f32[5,8,16,256]{3,2,1,0:T(8,128)S(1)}, f32[5,8,16,256]{3,2,1,0:T(8,128)}, u32[]{:S(2)}) copy-start(f32[5,8,16,256]{3,2,1,0:T(8,128)} %param.12) | copy-start | bytes 1966084
  7.1 5.6 %copy-start.9 = (f32[8,16,256]{2,1,0:T(8,128)S(1)}, f32[8,16,256]{2,1,0:T(8,128)}, u32[]{:S(2)}) copy-start(f32[8,16,256]{2,1,0:T(8,128)} %param.13) | copy-start | bytes 393220
  7.1 13.5 %all-to-all-start = ((bf16[8,8,32,128]{3,2,1,0:T(8,128)(2,1)}), bf16[8,8,32,128]{3,2,1,0:T(8,128)(2,1)}, u32[]{:S(2)}, u32[]{:S(2)}) async-start(bf16[8,8,32,128]{3,2,1,0:T(8,128)(2,1)} %bitcast.3), calls=%async_computation | async-start | bytes 1048576 | tf_op jit(solution)/shard_map/all_to_all | solution.py:375
  13.3 16.9 %collective-permute-start.3 = (f32[3,16,128]{2,1,0:T(8,128)S(1)}, f32[3,16,128]{2,1,0:T(8,128)S(1)}, u32[]{:S(2)}, u32[]{:S(2)}) collective-permute-start(f32[3,16,128]{2,1,0:T(8,128)S(1)} %get-tuple-element.12), channel_id=1, source_target_pairs={{0,14},{2,4},{4,2},{6,8},{8,6},{10,12},{12,10},{14,0},{1,15},{3,5}... | collective-permute-start | bytes 73736 | tf_op jit(solution)/shard_map/ppermute | solution.py:406
  19.9 10.3 %collective-permute-start.4 = (f32[3,16,128]{2,1,0:T(8,128)S(1)}, f32[3,16,128]{2,1,0:T(8,128)S(1)}, u32[]{:S(2)}, u32[]{:S(2)}) collective-permute-start(f32[3,16,128]{2,1,0:T(8,128)S(1)} %get-tuple-element.13), channel_id=1, source_target_pairs={{0,2},{2,0},{4,6},{6,4},{8,10},{10,8},{12,14},{14,12},{1,3},{3,1},... | collective-permute-start | bytes 73736 | tf_op jit(solution)/shard_map/ppermute | solution.py:407
  22.4 16.7 %all-to-all-start.1 = ((bf16[8,8,32,128]{3,2,1,0:T(8,128)(2,1)}), bf16[8,8,32,128]{3,2,1,0:T(8,128)(2,1)}, u32[]{:S(2)}, u32[]{:S(2)}) async-start(bf16[8,8,32,128]{3,2,1,0:T(8,128)(2,1)} %bitcast.11), calls=%async_computation.1 | async-start | bytes 1048576 | tf_op jit(solution)/shard_map/all_to_all | solution.py:375
  37.1 13.6 %copy-start.2 = (bf16[2,512,512]{2,1,0:T(8,128)(2,1)S(1)}, bf16[2,512,512]{2,1,0:T(8,128)(2,1)}, u32[]{:S(2)}) copy-start(bf16[2,512,512]{2,1,0:T(8,128)(2,1)} %constant.12.clone.zf) | copy-start | bytes 3145732
  39.4 11.2 %copy-start.10 = (f32[5,32]{1,0:T(8,128)S(1)}, f32[5,32]{1,0:T(8,128)}, u32[]{:S(2)}) copy-start(f32[5,32]{1,0:T(8,128)} %weight.3) | copy-start | bytes 1924
  39.5 11.2 %copy-start.12 = (f32[32]{0:T(128)S(1)}, f32[32]{0:T(128)}, u32[]{:S(2)}) copy-start(f32[32]{0:T(128)} %bias.3) | copy-start | bytes 388
  50.7 1.0 copy-start.7
  54.6 10.4 %copy-start.11 = (bf16[32,32]{1,0:T(8,128)(2,1)S(1)}, bf16[32,32]{1,0:T(8,128)(2,1)}, u32[]{:S(2)}) copy-start(bf16[32,32]{1,0:T(8,128)(2,1)} %mix.1) | copy-start | bytes 6148
  54.6 10.4 %copy-start.13 = (f32[32]{0:T(128)S(1)}, f32[32]{0:T(128)}, u32[]{:S(2)}) copy-start(f32[32]{0:T(128)} %param.18) | copy-start | bytes 388
  54.6 18.5 %all-to-all-start.3 = ((f32[128,2,128]{2,1,0:T(2,128)}), f32[128,2,128]{2,1,0:T(2,128)S(1)}, u32[]{:S(2)}, u32[]{:S(2)}) async-start(f32[128,2,128]{2,1,0:T(2,128)} %bitcast.5), calls=%async_computation.3 | async-start | bytes 262144 | tf_op jit(solution)/shard_map/all_to_all | solution.py:375
  62.8 10.3 %copy-start.6 = (bf16[5,256,256]{2,1,0:T(8,128)(2,1)S(1)}, bf16[5,256,256]{2,1,0:T(8,128)(2,1)}, u32[]{:S(2)}) copy-start(bf16[5,256,256]{2,1,0:T(8,128)(2,1)} %constant.14.clone.x_tables) | copy-start | bytes 1966084
  62.8 2.2 %collective-permute-start.5 = (f32[160,128]{1,0:T(8,128)S(1)}, f32[160,128]{1,0:T(8,128)S(1)}, u32[]{:S(2)}, u32[]{:S(2)}) collective-permute-start(f32[160,128]{1,0:T(8,128)S(1)} %get-tuple-element.16), channel_id=1, source_target_pairs={{0,1},{1,0},{2,3},{3,2},{4,5},{5,4},{6,7},{7,6},{8,9},{9,8},{10,11... | collective-permute-start | bytes 245768 | tf_op jit(solution)/shard_map/ppermute | solution.py:433
  73.1 17.8 %copy-start.1 = (bf16[2,512,512]{2,1,0:T(8,128)(2,1)S(1)}, bf16[2,512,512]{2,1,0:T(8,128)(2,1)}, u32[]{:S(2)}) copy-start(bf16[2,512,512]{2,1,0:T(8,128)(2,1)} %constant.13.clone.zi) | copy-start | bytes 3145732
  73.1 17.8 %copy-start.3 = (bf16[384,1024]{1,0:T(8,128)(2,1)S(1)}, bf16[384,1024]{1,0:T(8,128)(2,1)}, u32[]{:S(2)}) copy-start(bf16[384,1024]{1,0:T(8,128)(2,1)} %constant.11.clone.yi) | copy-start | bytes 2359300

commit v5 on v4

--- a/solution.py
+++ b/solution.py
@@ -238,7 +238,7 @@
         lax.fori_loop(0, 16, body, 0)
 
 
-def coarsen(last, after, keep, send, narrow, sums):
+def coarsen(last, weights, keep, send, narrow, sums):
     for half in range(2):
         for x in range(4):
             for field in range(5):
@@ -260,7 +260,9 @@
         for x in range(4):
             at = 160 * half + 40 * x
             block = jnp.concatenate([mean[at : at + 40], jnp.zeros((8, 128), F32)], axis=0)
-            narrow[2 * x + half] = block.astype(BF16)
+            narrow[2 * x + half, 0:48, :] = block.astype(BF16)
+    for i in range(8):
+        narrow[:, 48 + 32 * i : 80 + 32 * i, :] = weights[i]
 
 
 def lift_rows(values, weight, bias):
@@ -292,14 +294,22 @@
     lax.fori_loop(0, ZL, body, 0)
 
 
-def forward(got, weight, bias, yf, zf, out, lifted):
+def forward(got, weight, bias, yf_far, zf_far, out, lifted, yf, zf, sems):
+    copies = [
+        pltpu.make_async_copy(yf_far, yf, sems.at[0]),
+        pltpu.make_async_copy(zf_far, zf, sems.at[1]),
+    ]
+    for copy in copies:
+        copy.start()
     for j in range(8):
-        block = got[j].astype(F32)
+        block = got[j, 0:48, :].astype(F32)
         values = [block[8 * field : 8 * field + 8] for field in range(5)]
         lifted[:, 128 * j : 128 * j + 128] = lift_rows(values, weight, bias)
+    copies[0].wait()
     modes = dot(yf[...], lifted[...], ((1,), (1,)))
     modes = modes[:128] + modes[128:]
     modes = jnp.concatenate([modes[:64], modes[64:]], axis=1)
+    copies[1].wait()
     result = dot3(modes, zf)
     for part in range(4):
         out[:, part, :] = result[:, 128 * part : 128 * part + 128]
@@ -316,8 +326,9 @@
     real, imag = modes[:128], modes[128:]
     total = jnp.zeros((256, 128), F32)
     for i in range(8):
-        wr = weights[:, i, 0:16, :].astype(F32).reshape(128, 128)
-        wi = weights[:, i, 16:32, :].astype(F32).reshape(128, 128)
+        at = 48 + 32 * i
+        wr = weights[:, at : at + 16, :].astype(F32).reshape(128, 128)
+        wi = weights[:, at + 16 : at + 32, :].astype(F32).reshape(128, 128)
         part = jnp.concatenate([wr * real - wi * imag, wr * imag + wi * real], axis=0)
         p_high, p_low = halves(part)
         gather = (lane % 32 == 4 * i + row % 4).astype(BF16)
@@ -397,7 +408,6 @@
         size=2 * 10**7,
     )(spectral_weight.reshape(2048, 128), message)
     hop = exchange(turned.reshape(8, 8, 32, 128), "gx")
-    weights = exchange(jnp.transpose(hop, (1, 0, 2, 3)), "gy")
 
     message = ((3, 16, 128), F32)
     outer, far, near = call(
@@ -418,10 +428,10 @@
     )(f, s, fp, sp, outer, far, near)
     keep, send, narrow = call(
         coarsen,
-        [((160, 128), F32), ((160, 128), F32), ((8, 48, 128), BF16)],
-        [VMEM, anywhere],
+        [((160, 128), F32), ((160, 128), F32), ((8, 304, 128), BF16)],
+        [VMEM] * 2,
         [pltpu.VMEM((320, 256), F32)],
-    )(last, weights)
+    )(last, hop)
 
     columns = exchange(narrow, "gy")
     [direct] = call(
@@ -435,12 +445,17 @@
     [modes] = call(
         forward,
         [((64, 4, 128), F32)],
-        [VMEM, SMEM, SMEM, VMEM, VMEM],
-        [pltpu.VMEM((256, 1024), BF16)],
+        [VMEM, SMEM, SMEM, anywhere, anywhere],
+        [
+            pltpu.VMEM((256, 1024), BF16),
+            pltpu.VMEM((256, 1024), BF16),
+            pltpu.VMEM((2, 512, 512), BF16),
+            pltpu.SemaphoreType.DMA((2,)),
+        ],
     )(columns, lift_weight, lift_bias, table["yf"], table["zf"])
     modes = exchange(modes.reshape(128, 2, 128), everyone)
     [mixed] = call(mix_modes, [((64, 4, 128), F32)], [VMEM] * 3 + [anywhere])(
-        modes.reshape(256, 128), weights, table["x"], direct
+        modes.reshape(256, 128), columns, table["x"], direct
     )
     mixed = exchange(mixed.reshape(128, 2, 128), everyone)
     [spectral] = call(inverse, [((8, 256, 128), BF16)], [VMEM] * 3)(

time: 108 us -> 106 us (0.981)
  starting transfers between devices: 32 us -> 22.9 us
  waiting for transfers between devices: 9.13 us -> 13.7 us
  blocking collectives: 38.1 us -> 42.5 us
  local copies, waits for them, and re-layouts: 5.05 us -> 2.77 us
    all_to_all x3 -> x2, starting transfers between devices: 21 us -> 12 us  [exchange(): return lax.all_to_all(value, axis, split_axis=0, concat_axis=0, tiled=True)]
    ppermute x1, waiting for transfers between devices: 0.61 us -> 6.3 us  [shards(): got = lax.ppermute(message, ('gx', 'ga'), across)]
    all_to_all x3, blocking collectives: 38.1 us -> 42.5 us  [exchange(): return lax.all_to_all(value, axis, split_axis=0, concat_axis=0, tiled=True)]
    all_to_all x1 -> x0, local copies, waits for them, and re-layouts: 1.88 us -> none  [exchange(): return lax.all_to_all(value, axis, split_axis=0, concat_axis=0, tiled=True)]
    pallas_call x2, Pallas kernels: 3.18 us -> 4.63 us  [the longest x1 3.28 us: shards(): call(forward, [((64, 4, 128), F32)], [VMEM, SMEM, SMEM, anywhere, anywher...]
    pallas_call x1, Pallas kernels: 3.46 us -> 2.29 us  [shards(): call(mix_modes, [((64, 4, 128), F32)], [VMEM] * 3 + [anywhere])]
    all_to_all x3 -> x2, waiting for transfers between devices: 7.59 us -> 6.47 us  [exchange(): return lax.all_to_all(value, axis, split_axis=0, concat_axis=0, tiled=True)]
    unnamed x28 -> x32, local copies, waits for them, and re-layouts: 3.17 us -> 2.77 us
  transfers between devices with their start and end apart: 9 -> 8, of which waited for: 5 -> 4; matrix products, arithmetic and copies ran while one was open for 2% -> 0% of each run, Pallas kernels for 12% -> 11%
where the time goes in v5:
time: 106 us; the launch traced here: 104 us
  blocking collectives  42.5 us (40%)
  starting transfers between devices  22.9 us (22%)
  Pallas kernels  22.1 us (21%)
  waiting for transfers between devices  13.7 us (13%)
  local copies, waits for them, and re-layouts  2.77 us (3%)
    all_to_all x3, blocking collectives, exchange(): return lax.all_to_all(value, axis, split_axis=0, concat_axis=0, tiled=True)  42.5 us
    all_to_all x2, starting transfers between devices, exchange(): return lax.all_to_all(value, axis, split_axis=0, concat_axis=0, tiled=True)  12 us
    pallas_call x1, Pallas kernels, shards(): call(stencil, [((5, 2, 128, 128), F32)], [VMEM] * 7, [pltpu.VMEM((5, 16,...  6.83 us
    ppermute x1, starting transfers between devices, shards(): lax.ppermute(far, 'gy', [(j, (j - 1 + 2 * (j % 2)) % 8) for j in range(8)])  6.47 us
    all_to_all x2, waiting for transfers between devices, exchange(): return lax.all_to_all(value, axis, split_axis=0, concat_axis=0, tiled=True)  6.47 us
    ppermute x1, waiting for transfers between devices, shards(): got = lax.ppermute(message, ('gx', 'ga'), across)  6.3 us
    pallas_call x1, Pallas kernels, shards(): call(forward, [((64, 4, 128), F32)], [VMEM, SMEM, SMEM, anywhere, anywher...  3.28 us
    pallas_call x1, Pallas kernels, shards(): call(pointwise, [((8, 256, 128), F32)], [VMEM, VMEM, SMEM, SMEM, VMEM, VM...  3.18 us
  transfers between devices with their start and end apart: 8, of which 4 were waited for; matrix products, arithmetic and copies ran while one was open for 0% of the time, Pallas kernels for 11%

profile of v5, /device:TPU:1, one launch (start us, length us, event | category | flops | bytes accessed | tf_op | source)
XLA Modules:
  0.0 104.2 jit_solution(16567176546707567770)
XLA Ops:
  0.0 1.4 %collective-permute-start = (f32[5,128,256]{2,1,0:T(8,128)}, f32[5,128,256]{2,1,0:T(8,128)S(1)}, u32[]{:S(2)}, u32[]{:S(2)}) collective-permute-start(f32[5,128,256]{2,1,0:T(8,128)} %bitcast.10), channel_id=1, source_target_pairs={{0,1},{1,0},{2,3},{3,2},{4,5},{5,4},{6,7},{7,6},{8,9},{9,8},{10,11... | collective-permute-start | bytes 1966088 | tf_op jit(solution)/shard_map/ppermute | solution.py:392
  1.4 0.0 collective-permute-start.1
  1.4 1.1 %copy-done.7 = f32[5,8,16,256]{3,2,1,0:T(8,128)S(1)} copy-done((f32[5,8,16,256]{3,2,1,0:T(8,128)S(1)}, f32[5,8,16,256]{3,2,1,0:T(8,128)}, u32[]{:S(2)}) %copy-start.7) | copy-done | bytes 655384
  2.5 0.9 copy-done.10
  3.4 0.1 shard_map.118.own
  3.6 0.0 copy-start.8
  3.6 0.0 collective-permute-done.1.sp
  3.6 0.0 collective-permute-done.fp
  3.6 0.1 shard_map.119.after
  3.8 1.8 %collective-permute-start.2 = (f32[6,2,48,128]{3,2,1,0:T(8,128)S(1)}, f32[6,2,48,128]{3,2,1,0:T(8,128)S(1)}, u32[]{:S(2)}, u32[]{:S(2)}) collective-permute-start(f32[6,2,48,128]{3,2,1,0:T(8,128)S(1)} %shard_map.119.after), channel_id=1, source_target_pairs={{0,113},{16,1},{32,17},{48,33},{64,49},{80,65},{96,81},{112,97},{1... | collective-permute-start | bytes 884744 | tf_op jit(solution)/shard_map/ppermute | solution.py:401
  5.5 0.7 copy-done
  6.2 6.3 %collective-permute-done.2.message = f32[6,2,48,128]{3,2,1,0:T(8,128)S(1)} collective-permute-done((f32[6,2,48,128]{3,2,1,0:T(8,128)S(1)}, f32[6,2,48,128]{3,2,1,0:T(8,128)S(1)}, u32[]{:S(2)}, u32[]{:S(2)}) %collective-permute-start.2) | collective-permute-done | bytes 294944 | tf_op jit(solution)/shard_map/ppermute | solution.py:401
  12.5 0.0 copy-done.8
  12.5 0.5 shard_map.120
  13.1 6.5 %collective-permute-start.3 = (f32[3,16,128]{2,1,0:T(8,128)S(1)}, f32[3,16,128]{2,1,0:T(8,128)S(1)}, u32[]{:S(2)}, u32[]{:S(2)}) collective-permute-start(f32[3,16,128]{2,1,0:T(8,128)S(1)} %get-tuple-element.12), channel_id=1, source_target_pairs={{0,14},{2,4},{4,2},{6,8},{8,6},{10,12},{12,10},{14,0},{1,15},{3,5}... | collective-permute-start | bytes 73736 | tf_op jit(solution)/shard_map/ppermute | solution.py:416
  19.6 0.0 collective-permute-start.4
  19.6 0.0 copy-done.1
  19.6 0.0 copy-done.2
  19.6 1.6 %shard_map.122 = bf16[64,32,128]{2,1,0:T(8,128)(2,1)} custom-call(f32[2048,128]{1,0:T(8,128)S(1)} %bitcast.9, f32[6,2,48,128]{3,2,1,0:T(8,128)S(1)} %copy-done.1), custom_call_target="tpu_custom_call" | custom-call | flops 10000000 | bytes 20000000 | tf_op jit(solution)/shard_map/pallas_call | solution.py:403
  21.2 5.4 %all-to-all-start = ((bf16[8,8,32,128]{3,2,1,0:T(8,128)(2,1)}), bf16[8,8,32,128]{3,2,1,0:T(8,128)(2,1)}, u32[]{:S(2)}, u32[]{:S(2)}) async-start(bf16[8,8,32,128]{3,2,1,0:T(8,128)(2,1)} %bitcast.3), calls=%async_computation | async-start | bytes 1048576 | tf_op jit(solution)/shard_map/all_to_all | solution.py:386
  26.6 0.0 collective-permute-done.3.far
  26.6 0.0 collective-permute-done.4.near
  26.6 0.0 copy-done.11
  26.6 6.8 %shard_map.121.last = f32[5,2,128,128]{3,2,1,0:T(8,128)S(1)} custom-call(f32[5,128,256]{2,1,0:T(8,128)S(1)} %bitcast.13, f32[128,256]{1,0:T(8,128)S(1)} %bitcast.20, f32[5,128,256]{2,1,0:T(8,128)S(1)} %collective-permute-done.fp, f32[128,256]{1,0:T(8,128)S(1)} %collective-permute-done.1.sp, f32[6,2,128,128]{3,2,1,0:T(8,128)S(1)} %get-tuple-element.11.outer, ...), custom_call_target="tpu_custom_call" | custom-call | flops 999999995904 | bytes 1048576 | tf_op jit(solution)/shard_map/pallas_call | solution.py:418
  33.4 0.0 copy-start.3
  33.4 1.6 %all-to-all-done.weights = bf16[8,8,32,128]{3,2,1,0:T(8,128)(2,1)} async-done(((bf16[8,8,32,128]{3,2,1,0:T(8,128)(2,1)}), bf16[8,8,32,128]{3,2,1,0:T(8,128)(2,1)}, u32[]{:S(2)}, u32[]{:S(2)}) %all-to-all-start) | async-done | bytes 524320 | tf_op jit(solution)/shard_map/all_to_all | solution.py:386
  35.0 1.4 %shard_map.123 = (f32[160,128]{1,0:T(8,128)S(1)}, f32[160,128]{1,0:T(8,128)S(1)}, bf16[8,304,128]{2,1,0:T(8,128)(2,1)S(1)}) custom-call(f32[5,2,128,128]{3,2,1,0:T(8,128)S(1)} %shard_map.121.last, bf16[8,8,32,128]{3,2,1,0:T(8,128)(2,1)} %all-to-all-done.weights), custom_call_target="tpu_custom_call" | custom-call | flops 10000000 | bytes 1048576 | tf_op jit(solution)/shard_map/pallas_call | solution.py:429
  36.4 0.0 copy-start.9
  36.4 0.0 copy-start.12
  36.4 0.0 copy-start.14
  36.4 15.6 %all_to_all.25.got.weights = bf16[8,304,128]{2,1,0:T(8,128)(2,1)S(1)} all-to-all(bf16[8,304,128]{2,1,0:T(8,128)(2,1)S(1)} %get-tuple-element.14), channel_id=1, replica_groups=mesh['gx'=8,'gy'=8,'ga'=2] {'gy'}, dimensions={0} | all-to-all | bytes 1245184 | tf_op jit(solution)/shard_map/all_to_all | solution.py:386
  52.0 0.0 copy-done.3
  52.0 0.0 copy-done.9
  52.0 3.3 %shard_map.124 = f32[64,4,128]{2,1,0:T(4,128)} custom-call(bf16[8,304,128]{2,1,0:T(8,128)(2,1)S(1)} %all_to_all.25.got.weights, f32[5,32]{1,0:T(8,128)S(1)} %copy-done.12, f32[32]{0:T(128)S(1)} %copy-done.14, bf16[256,1024]{1,0:T(8,128)(2,1)S(1)} %copy-done.9, bf16[2,512,512]{2,1,0:T(8,128)(2,1)S(1)} %copy-done.3), custom_call_target="tpu_custom_call" | custom-call | flops 10000000 | bytes 1048576 | tf_op jit(solution)/shard_map/pallas_call | solution.py:445
  55.3 0.0 copy-start.13
  55.3 0.0 copy-start.15
  55.3 6.6 %all-to-all-start.2 = ((f32[128,2,128]{2,1,0:T(2,128)}), f32[128,2,128]{2,1,0:T(2,128)S(1)}, u32[]{:S(2)}, u32[]{:S(2)}) async-start(f32[128,2,128]{2,1,0:T(2,128)} %bitcast.4), calls=%async_computation.2 | async-start | bytes 262144 | tf_op jit(solution)/shard_map/all_to_all | solution.py:386
  61.9 0.0 copy-start.6
  61.9 1.3 %collective-permute-start.5 = (f32[160,128]{1,0:T(8,128)S(1)}, f32[160,128]{1,0:T(8,128)S(1)}, u32[]{:S(2)}, u32[]{:S(2)}) collective-permute-start(f32[160,128]{1,0:T(8,128)S(1)} %get-tuple-element.16), channel_id=1, source_target_pairs={{0,1},{1,0},{2,3},{3,2},{4,5},{5,4},{6,7},{7,6},{8,9},{9,8},{10,11... | collective-permute-start | bytes 245768 | tf_op jit(solution)/shard_map/ppermute | solution.py:443
  63.2 0.9 collective-permute-done.5.got
  64.1 0.0 copy-done.13
  64.1 3.2 %shard_map.125.after.direct = f32[8,256,128]{2,1,0:T(8,128)S(1)} custom-call(f32[160,128]{1,0:T(8,128)S(1)} %get-tuple-element.15.keep, f32[160,128]{1,0:T(8,128)S(1)} %collective-permute-done.5.got, f32[5,32]{1,0:T(8,128)S(1)} %copy-done.12, f32[32]{0:T(128)S(1)} %copy-done.14, bf16[32,32]{1,0:T(8,128)(2,1)S(1)} %copy-done.13, f32[1,32]{1,0:T(1,128)S(1)} %bitcast.21), custom_call_target="tpu_custom_call" | custom-call | flops 300000000 | bytes 1048576 | tf_op jit(solution)/shard_map/pallas_call | solution.py:437
  67.3 4.9 %all-to-all-done.2 = f32[128,2,128]{2,1,0:T(2,128)S(1)} async-done(((f32[128,2,128]{2,1,0:T(2,128)}), f32[128,2,128]{2,1,0:T(2,128)S(1)}, u32[]{:S(2)}, u32[]{:S(2)}) %all-to-all-start.2) | async-done | bytes 131104 | tf_op jit(solution)/shard_map/all_to_all | solution.py:386
  72.2 2.3 %shard_map.126 = f32[64,4,128]{2,1,0:T(4,128)S(1)} custom-call(f32[256,128]{1,0:T(8,128)S(1)} %bitcast.14, bf16[8,304,128]{2,1,0:T(8,128)(2,1)S(1)} %all_to_all.25.got.weights, bf16[5,256,256]{2,1,0:T(8,128)(2,1)S(1)} %copy-done.6, f32[8,256,128]{2,1,0:T(8,128)S(1)} %shard_map.125.after.direct), custom_call_target="tpu_custom_call" | custom-call | flops 10000000 | bytes 1048576 | tf_op jit(solution)/shard_map/pallas_call | solution.py:457
  74.5 14.3 %all_to_all.26 = f32[128,2,128]{2,1,0:T(2,128)S(1)} all-to-all(f32[128,2,128]{2,1,0:T(2,128)S(1)} %bitcast.15), channel_id=1, replica_groups=mesh['gx'=8,'gy'=8,'ga'=2] {'gx','gy','ga'}, dimensions={0} | all-to-all | bytes 262144 | tf_op jit(solution)/shard_map/all_to_all | solution.py:386
  88.8 1.0 shard_map.127
  89.8 12.6 %all_to_all.27.got = bf16[8,256,128]{2,1,0:T(8,128)(2,1)S(1)} all-to-all(bf16[8,256,128]{2,1,0:T(8,128)(2,1)S(1)} %shard_map.127), channel_id=1, replica_groups=mesh['gx'=8,'gy'=8,'ga'=2] {'gy'}, dimensions={0} | all-to-all | bytes 1048576 | tf_op jit(solution)/shard_map/all_to_all | solution.py:386
  102.4 1.8 %shard_map.128 = bf16[8,32,8,128]{3,2,1,0:T(8,128)(2,1)} custom-call(bf16[8,256,128]{2,1,0:T(8,128)(2,1)S(1)} %all_to_all.27.got, f32[8,256,128]{2,1,0:T(8,128)S(1)} %shard_map.125.after.direct), custom_call_target="tpu_custom_call" | custom-call | flops 10000000 | bytes 1048576 | tf_op jit(solution)/shard_map/pallas_call | solution.py:465
  (14 shorter events, 0.0 us)
Async XLA Ops:
  0.0 3.6 %collective-permute-start = (f32[5,128,256]{2,1,0:T(8,128)}, f32[5,128,256]{2,1,0:T(8,128)S(1)}, u32[]{:S(2)}, u32[]{:S(2)}) collective-permute-start(f32[5,128,256]{2,1,0:T(8,128)} %bitcast.10), channel_id=1, source_target_pairs={{0,1},{1,0},{2,3},{3,2},{4,5},{5,4},{6,7},{7,6},{8,9},{9,8},{10,11... | collective-permute-start | bytes 1966088 | tf_op jit(solution)/shard_map/ppermute | solution.py:392
  1.4 2.2 %collective-permute-start.1 = (f32[128,256]{1,0:T(8,128)}, f32[128,256]{1,0:T(8,128)S(1)}, u32[]{:S(2)}, u32[]{:S(2)}) collective-permute-start(f32[128,256]{1,0:T(8,128)} %bitcast.17), channel_id=1, source_target_pairs={{0,1},{1,0},{2,3},{3,2},{4,5},{5,4},{6,7},{7,6},{8,9},{9,8},{10,11... | collective-permute-start | bytes 393224 | tf_op jit(solution)/shard_map/ppermute | solution.py:392
  1.4 1.1 %copy-start.7 = (f32[5,8,16,256]{3,2,1,0:T(8,128)S(1)}, f32[5,8,16,256]{3,2,1,0:T(8,128)}, u32[]{:S(2)}) copy-start(f32[5,8,16,256]{3,2,1,0:T(8,128)} %param.12) | copy-start | bytes 1966084
  2.5 0.9 copy-start.10
  3.6 9.0 %copy-start.8 = (f32[5,8,16,256]{3,2,1,0:T(8,128)S(1)}, f32[5,8,16,256]{3,2,1,0:T(8,128)}, u32[]{:S(2)}) copy-start(f32[5,8,16,256]{3,2,1,0:T(8,128)} %param.12) | copy-start | bytes 1966084
  3.8 8.8 %collective-permute-start.2 = (f32[6,2,48,128]{3,2,1,0:T(8,128)S(1)}, f32[6,2,48,128]{3,2,1,0:T(8,128)S(1)}, u32[]{:S(2)}, u32[]{:S(2)}) collective-permute-start(f32[6,2,48,128]{3,2,1,0:T(8,128)S(1)} %shard_map.119.after), channel_id=1, source_target_pairs={{0,113},{16,1},{32,17},{48,33},{64,49},{80,65},{96,81},{112,97},{1... | collective-permute-start | bytes 884744 | tf_op jit(solution)/shard_map/ppermute | solution.py:401
  5.5 0.7 copy-start
  12.5 7.0 %copy-start.1 = (f32[6,2,48,128]{3,2,1,0:T(8,128)S(1)}, f32[6,2,48,128]{3,2,1,0:T(8,128)}, u32[]{:S(2)}) copy-start(f32[6,2,48,128]{3,2,1,0:T(8,128)} %copy-done) | copy-start | bytes 884740
  12.5 7.0 %copy-start.2 = (f32[4,4,32,4,128]{4,3,2,1,0:T(4,128)S(1)}, f32[4,4,32,4,128]{4,3,2,1,0:T(4,128)}, u32[]{:S(2)}) copy-start(f32[4,4,32,4,128]{4,3,2,1,0:T(4,128)} %param.17) | copy-start | bytes 3145732
  13.1 13.5 %collective-permute-start.3 = (f32[3,16,128]{2,1,0:T(8,128)S(1)}, f32[3,16,128]{2,1,0:T(8,128)S(1)}, u32[]{:S(2)}, u32[]{:S(2)}) collective-permute-start(f32[3,16,128]{2,1,0:T(8,128)S(1)} %get-tuple-element.12), channel_id=1, source_target_pairs={{0,14},{2,4},{4,2},{6,8},{8,6},{10,12},{12,10},{14,0},{1,15},{3,5}... | collective-permute-start | bytes 73736 | tf_op jit(solution)/shard_map/ppermute | solution.py:416
  19.6 7.0 %collective-permute-start.4 = (f32[3,16,128]{2,1,0:T(8,128)S(1)}, f32[3,16,128]{2,1,0:T(8,128)S(1)}, u32[]{:S(2)}, u32[]{:S(2)}) collective-permute-start(f32[3,16,128]{2,1,0:T(8,128)S(1)} %get-tuple-element.13), channel_id=1, source_target_pairs={{0,2},{2,0},{4,6},{6,4},{8,10},{10,8},{12,14},{14,12},{1,3},{3,1},... | collective-permute-start | bytes 73736 | tf_op jit(solution)/shard_map/ppermute | solution.py:417
  21.2 5.4 %copy-start.11 = (f32[8,16,256]{2,1,0:T(8,128)S(1)}, f32[8,16,256]{2,1,0:T(8,128)}, u32[]{:S(2)}) copy-start(f32[8,16,256]{2,1,0:T(8,128)} %param.13) | copy-start | bytes 393220
  21.2 13.9 %all-to-all-start = ((bf16[8,8,32,128]{3,2,1,0:T(8,128)(2,1)}), bf16[8,8,32,128]{3,2,1,0:T(8,128)(2,1)}, u32[]{:S(2)}, u32[]{:S(2)}) async-start(bf16[8,8,32,128]{3,2,1,0:T(8,128)(2,1)} %bitcast.3), calls=%async_computation | async-start | bytes 1048576 | tf_op jit(solution)/shard_map/all_to_all | solution.py:386
  33.4 18.6 %copy-start.3 = (bf16[2,512,512]{2,1,0:T(8,128)(2,1)S(1)}, bf16[2,512,512]{2,1,0:T(8,128)(2,1)}, u32[]{:S(2)}) copy-start(bf16[2,512,512]{2,1,0:T(8,128)(2,1)} %constant.12.clone.zf_far) | copy-start | bytes 3145732
  36.4 15.6 %copy-start.9 = (bf16[256,1024]{1,0:T(8,128)(2,1)S(1)}, bf16[256,1024]{1,0:T(8,128)(2,1)}, u32[]{:S(2)}) copy-start(bf16[256,1024]{1,0:T(8,128)(2,1)} %constant.10.clone.yf_far) | copy-start | bytes 1572868
  36.4 15.6 %copy-start.12 = (f32[5,32]{1,0:T(8,128)S(1)}, f32[5,32]{1,0:T(8,128)}, u32[]{:S(2)}) copy-start(f32[5,32]{1,0:T(8,128)} %weight.3) | copy-start | bytes 1924
  36.4 15.6 %copy-start.14 = (f32[32]{0:T(128)S(1)}, f32[32]{0:T(128)}, u32[]{:S(2)}) copy-start(f32[32]{0:T(128)} %bias.3) | copy-start | bytes 388
  55.3 8.8 %copy-start.13 = (bf16[32,32]{1,0:T(8,128)(2,1)S(1)}, bf16[32,32]{1,0:T(8,128)(2,1)}, u32[]{:S(2)}) copy-start(bf16[32,32]{1,0:T(8,128)(2,1)} %mix.1) | copy-start | bytes 6148
  55.3 8.8 %copy-start.15 = (f32[32]{0:T(128)S(1)}, f32[32]{0:T(128)}, u32[]{:S(2)}) copy-start(f32[32]{0:T(128)} %param.18) | copy-start | bytes 388
  55.3 16.9 %all-to-all-start.2 = ((f32[128,2,128]{2,1,0:T(2,128)}), f32[128,2,128]{2,1,0:T(2,128)S(1)}, u32[]{:S(2)}, u32[]{:S(2)}) async-start(f32[128,2,128]{2,1,0:T(2,128)} %bitcast.4), calls=%async_computation.2 | async-start | bytes 262144 | tf_op jit(solution)/shard_map/all_to_all | solution.py:386
  61.9 10.3 %copy-start.6 = (bf16[5,256,256]{2,1,0:T(8,128)(2,1)S(1)}, bf16[5,256,256]{2,1,0:T(8,128)(2,1)}, u32[]{:S(2)}) copy-start(bf16[5,256,256]{2,1,0:T(8,128)(2,1)} %constant.14.clone.x_tables) | copy-start | bytes 1966084
  61.9 2.2 %collective-permute-start.5 = (f32[160,128]{1,0:T(8,128)S(1)}, f32[160,128]{1,0:T(8,128)S(1)}, u32[]{:S(2)}, u32[]{:S(2)}) collective-permute-start(f32[160,128]{1,0:T(8,128)S(1)} %get-tuple-element.16), channel_id=1, source_target_pairs={{0,1},{1,0},{2,3},{3,2},{4,5},{5,4},{6,7},{7,6},{8,9},{9,8},{10,11... | collective-permute-start | bytes 245768 | tf_op jit(solution)/shard_map/ppermute | solution.py:443
  72.2 16.6 %copy-start.4 = (bf16[2,512,512]{2,1,0:T(8,128)(2,1)S(1)}, bf16[2,512,512]{2,1,0:T(8,128)(2,1)}, u32[]{:S(2)}) copy-start(bf16[2,512,512]{2,1,0:T(8,128)(2,1)} %constant.13.clone.zi) | copy-start | bytes 3145732
  72.2 16.6 %copy-start.5 = (bf16[384,1024]{1,0:T(8,128)(2,1)S(1)}, bf16[384,1024]{1,0:T(8,128)(2,1)}, u32[]{:S(2)}) copy-start(bf16[384,1024]{1,0:T(8,128)(2,1)} %constant.11.clone.yi) | copy-start | bytes 2359300

commit v6 on v4

--- a/solution.py
+++ b/solution.py
@@ -35,21 +35,19 @@
     ky = np.arange(MY) - MY // 2
     cy, sy = cos_sin(ky, np.arange(GY), GY)
     rows = np.concatenate([cy, -sy]) / math.sqrt(GY)
-    out["yf"] = np.concatenate(split(rows))
+    out["yf"] = np.concatenate(split(rows)).reshape(256, 8, 128).transpose(1, 0, 2)
     rows = np.concatenate([cy, -sy]) / math.sqrt(GY)
     high, low = split(rows)
     out["yi"] = np.concatenate([high, high, low])
-    kz = np.arange(MZ)
-    cz, sz = (t / math.sqrt(NZ) for t in cos_sin(kz, np.arange(ZL), NZ))
+    cf, sf = (
+        np.einsum("kz,cd->czkd", w / math.sqrt(NZ), np.eye(8)).reshape(128, 2, 32)
+        for w in cos_sin(np.arange(MZ), np.arange(NZ), NZ)
+    )
+    zf = np.zeros((2, 128, 2, 2, 32))
+    zf[0, :, :, 0], zf[1, :, :, 0], zf[1, :, :, 1], zf[0, :, :, 1] = cf, sf, cf, -sf
+    out["zf"] = np.concatenate(split(zf.reshape(256, 128)), axis=1)
+    cz, sz = (w / math.sqrt(NZ) for w in cos_sin(np.arange(MZ), np.arange(ZL), NZ))
     eye = np.eye(C)
-
-    def kron_f(t):
-        return np.einsum("kz,cd->czkd", t, eye).reshape(C * ZL, 2, 4 * C)
-
-    zf = np.zeros((2, C * ZL, 2, 2, 4 * C))
-    zf[0, :, :, 0], zf[1, :, :, 0] = kron_f(cz), kron_f(sz)
-    zf[1, :, :, 1], zf[0, :, :, 1] = kron_f(cz), -kron_f(sz)
-    out["zf"] = np.stack(split(zf.reshape(2 * C * ZL, 8 * 2 * C)))
     zi = np.zeros((2, 2, 4, C, 2, ZL, C))
     for half in range(2):
         for k in range(4):
@@ -63,22 +61,19 @@
     cr = (cx / 8.0).astype(np.float32).astype(jnp.bfloat16).astype(np.float64)
     sr = (-sx / 8.0).astype(np.float32).astype(jnp.bfloat16).astype(np.float64)
     cr, sr = cr.reshape(8, 4, 8, 2, 4), sr.reshape(8, 4, 8, 2, 4)
-    xf = np.zeros((4, 2, 8, 4, 4, 8, 4, 2, 2, 2))
+    xf = np.zeros((4, 2, 8, 4, 4, 8, 2, 4, 2))
     for k in range(4):
         for a in range(2):
-            for h in range(2):
-                sign = -1.0 if k * (h ^ a) % 2 else 1.0
-                real, imag = sign * cr[:, :, :, a], sign * sr[:, :, :, a]
-                xf[k, 0, :, k, :, :, :, h, a, 0] = real
-                xf[k, 0, :, k, :, :, :, h, a, 1] = -imag
-                xf[k, 1, :, k, :, :, :, h, a, 0] = imag
-                xf[k, 1, :, k, :, :, :, h, a, 1] = real
-    xf = xf.reshape(1024, 256).astype(np.float32).astype(jnp.bfloat16)
+            sign = -1.0 if k * a % 2 else 1.0
+            real, imag = sign * cr[:, :, :, a], sign * sr[:, :, :, a]
+            xf[k, 0, :, k, :, :, a, :, 0], xf[k, 0, :, k, :, :, a, :, 1] = real, -imag
+            xf[k, 1, :, k, :, :, a, :, 0], xf[k, 1, :, k, :, :, a, :, 1] = imag, real
+    out["xf"] = xf.reshape(4, 256, 128).astype(np.float32).astype(jnp.bfloat16)
     ic, is_ = (cx / 8.0).T.reshape(GX, 8, 1, 4), (sx / 8.0).T.reshape(GX, 8, 1, 4)
     xi = np.zeros((2, GX, 2, 8, 4, 4))
     xi[0, :, 0], xi[0, :, 1] = ic, -is_
     xi[1, :, 0], xi[1, :, 1] = is_, ic
-    out["x"] = np.concatenate([xf, *split(xi.reshape(128, 256))]).reshape(5, 256, 256)
+    out["xi"] = np.stack(split(xi.reshape(128, 256)))
     return out
 
 
@@ -179,7 +174,7 @@
             near[field // 2] = jnp.where(even, highs, lows)
 
 
-def stencil(f, s, fp, sp, outer, far, near, last, a, b, stiff):
+def stencil(f, s, fp, sp, outer, far, near, after, last, a, b, stiff):
     refs = (f, s, fp, sp)
     core = lax.axis_index("ga")
     even = lax.axis_index("gy") % 2 == 0
@@ -238,7 +233,44 @@
         lax.fori_loop(0, 16, body, 0)
 
 
-def coarsen(last, after, keep, send, narrow, sums):
+def lift_rows(values, weight, bias):
+    rows = []
+    for c in range(C):
+        v = bias[c] + values[0] * weight[0, c]
+        for field in range(1, 5):
+            v = v + values[field] * weight[field, c]
+        rows.append(gelu(v))
+    return jnp.concatenate(rows, axis=0).astype(BF16)
+
+
+def pointwise(keep, got, weight, bias, mix, obias, out, wide):
+    a = lax.axis_index("ga")
+    wide[pl.ds(pl.multiple_of(160 * a, 8), 160), :] = keep[...]
+    wide[pl.ds(pl.multiple_of(160 * (1 - a), 8), 160), :] = got[...]
+    row, lane = iotas((256, 32))
+    pick = (row // 8 == lane).astype(BF16)
+    bias_o = jnp.sum(jnp.where(row // 8 == lane, obias[...], 0.0), axis=1, keepdims=True)
+    by_row = dot(pick, mix[...], ((1,), (1,))).astype(BF16)
+    row, lane = iotas((256, 256))
+    spread = jnp.where(row % 8 == lane % 8, dot(by_row, pick, ((1,), (1,))), 0.0).astype(BF16)
+
+    def body(z, carry):
+        values = [wide[pl.ds(8 * field + z, 8, stride=40), :] for field in range(5)]
+        out[z] = dot(spread, lift_rows(values, weight, bias)) + bias_o
+        return carry
+
+    lax.fori_loop(0, ZL, body, 0)
+
+
+def forward(
+    last, weight, bias, yf_far, zf_far, keep, send, out, sums, lifted, modes, yf, zf, sems
+):
+    copies = [
+        pltpu.make_async_copy(yf_far.at[lax.axis_index("gy")], yf, sems.at[0]),
+        pltpu.make_async_copy(zf_far, zf, sems.at[1]),
+    ]
+    for copy in copies:
+        copy.start()
     for half in range(2):
         for x in range(4):
             for field in range(5):
@@ -256,68 +288,53 @@
     mean = dot(high, table) + dot(mid, table) + dot(low, table)
     keep[...] = mean[:160]
     send[...] = mean[160:]
-    for half in range(2):
+    for x in range(4):
+        at = [40 * x + 8 * field for field in range(5)]
+        values = [jnp.concatenate([mean[r : r + 8], mean[r + 160 : r + 168]], axis=0) for r in at]
+        lifted[x] = lift_rows(values, weight, bias)
+    copies[0].wait()
+    for x in range(4):
+        both = dot(yf[...], lifted[x], ((1,), (1,)))
+        modes[x] = both[:128] + both[128:]
+    copies[1].wait()
+    parts = []
+    for group in range(4):
+        lanes = slice(128 * group, 128 * group + 128)
+        stack = [
+            jnp.concatenate([modes[x, 0:64, lanes], modes[x, 64:128, lanes]], axis=1)
+            for x in range(4)
+        ]
+        m_high, m_low = halves(jnp.concatenate(stack, axis=0))
+        both = dot(m_high, zf[...])
+        parts.append(both[:, :128] + both[:, 128:] + dot(m_low, zf[:, :128]))
+    lane = lax.broadcasted_iota(jnp.int32, (256, 128), 1) // 32
+    for part in range(4):
+        total = parts[part]
+        for group in range(4):
+            if group != part:
+                moved = pltpu.roll(parts[group], (32 * (group - part)) % 128, 1)
+                total = jnp.where(lane == group, moved, total)
         for x in range(4):
-            at = 160 * half + 40 * x
-            block = jnp.concatenate([mean[at : at + 40], jnp.zeros((8, 128), F32)], axis=0)
-            narrow[2 * x + half] = block.astype(BF16)
-
-
-def lift_rows(values, weight, bias):
-    rows = []
-    for c in range(C):
-        v = bias[c] + values[0] * weight[0, c]
-        for field in range(1, 5):
-            v = v + values[field] * weight[field, c]
-        rows.append(gelu(v))
-    return jnp.concatenate(rows, axis=0).astype(BF16)
-
-
-def pointwise(keep, got, weight, bias, mix, obias, out, wide):
-    a = lax.axis_index("ga")
-    wide[pl.ds(pl.multiple_of(160 * a, 8), 160), :] = keep[...]
-    wide[pl.ds(pl.multiple_of(160 * (1 - a), 8), 160), :] = got[...]
-    row, lane = iotas((256, 32))
-    pick = (row // 8 == lane).astype(BF16)
-    bias_o = jnp.sum(jnp.where(row // 8 == lane, obias[...], 0.0), axis=1, keepdims=True)
-    by_row = dot(pick, mix[...], ((1,), (1,))).astype(BF16)
-    row, lane = iotas((256, 256))
-    spread = jnp.where(row % 8 == lane % 8, dot(by_row, pick, ((1,), (1,))), 0.0).astype(BF16)
-
-    def body(z, carry):
-        values = [wide[pl.ds(8 * field + z, 8, stride=40), :] for field in range(5)]
-        out[z] = dot(spread, lift_rows(values, weight, bias)) + bias_o
-        return carry
-
-    lax.fori_loop(0, ZL, body, 0)
-
-
-def forward(got, weight, bias, yf, zf, out, lifted):
-    for j in range(8):
-        block = got[j].astype(F32)
-        values = [block[8 * field : 8 * field + 8] for field in range(5)]
-        lifted[:, 128 * j : 128 * j + 128] = lift_rows(values, weight, bias)
-    modes = dot(yf[...], lifted[...], ((1,), (1,)))
-    modes = modes[:128] + modes[128:]
-    modes = jnp.concatenate([modes[:64], modes[64:]], axis=1)
-    result = dot3(modes, zf)
-    for part in range(4):
-        out[:, part, :] = result[:, 128 * part : 128 * part + 128]
-
-
-def mix_modes(got, weights, x_tables, after, out):
-    high, low = halves(got[...])
+            out[:, 8 * (part // 2) + 2 * x + part % 2, :] = total[64 * x : 64 * x + 64]
+
+
+def mix_modes(got, weights, xf, xi, after, out):
+    total = got[:, 0]
+    for j in range(1, 8):
+        total = total + got[:, j]
+    high, low = halves(total.reshape(128, 128))
     row, lane = iotas((128, 128))
     modes = jnp.zeros((256, 128), F32)
     for k in range(4):
-        spread = (row == 32 * k + lane // 4).astype(BF16)
-        modes = modes + dot(x_tables[k], dot(high, spread).astype(BF16))
-        modes = modes + dot(x_tables[k], dot(low, spread).astype(BF16))
+        spread = (row // 8 % 4 == k) & (row // 32 * 8 + row % 8 == lane // 4)
+        spread = spread.astype(BF16)
+        modes = modes + dot(xf[k], dot(high, spread).astype(BF16))
+        modes = modes + dot(xf[k], dot(low, spread).astype(BF16))
     real, imag = modes[:128], modes[128:]
     total = jnp.zeros((256, 128), F32)
     for i in range(8):
-        wr = weights[:, i, 0:16, :].astype(F32).reshape(128, 128)
-        wi = weights[:, i, 16:32, :].astype(F32).reshape(128, 128)
+        wr = weights[8 * i : 8 * i + 8, 0:16, :].astype(F32).reshape(128, 128)
+        wi = weights[8 * i : 8 * i + 8, 16:32, :].astype(F32).reshape(128, 128)
         part = jnp.concatenate([wr * real - wi * imag, wr * imag + wi * real], axis=0)
         p_high, p_low = halves(part)
         gather = (lane % 32 == 4 * i + row % 4).astype(BF16)
@@ -325,8 +342,7 @@
     row, lane = iotas((256, 128))
     total = jnp.where((row // 4) % 4 == lane // 32, total, 0.0)
     t_high, t_low = halves(total)
-    back_high, back_low = x_tables[4, :128], x_tables[4, 128:]
-    back = dot(back_high, t_high) + dot(back_high, t_low) + dot(back_low, t_high)
+    back = dot(xi[0], t_high) + dot(xi[0], t_low) + dot(xi[1], t_high)
     odd = (lax.broadcasted_iota(jnp.int32, (64, 128), 1) // 32) % 2 == 1
     for ri in range(2):
         value = back[64 * ri : 64 * ri + 64]
@@ -396,8 +412,7 @@
         [pltpu.VMEM((64, 32, 128), F32)],
         size=2 * 10**7,
     )(spectral_weight.reshape(2048, 128), message)
-    hop = exchange(turned.reshape(8, 8, 32, 128), "gx")
-    weights = exchange(jnp.transpose(hop, (1, 0, 2, 3)), "gy")
+    weights = exchange(turned, ("gx", "gy"))
 
     message = ((3, 16, 128), F32)
     outer, far, near = call(
@@ -408,22 +423,28 @@
     [last] = call(
         stencil,
         [((5, 2, 128, 128), F32)],
-        [VMEM] * 7,
+        [VMEM] * 7 + [anywhere],
         [
             pltpu.VMEM((5, 16, 16, 384), F32),
             pltpu.VMEM((5, 16, 16, 384), F32),
             pltpu.VMEM((16, 16, 384), F32),
         ],
         flops=10**12,
-    )(f, s, fp, sp, outer, far, near)
-    keep, send, narrow = call(
-        coarsen,
-        [((160, 128), F32), ((160, 128), F32), ((8, 48, 128), BF16)],
-        [VMEM, anywhere],
-        [pltpu.VMEM((320, 256), F32)],
-    )(last, weights)
-
-    columns = exchange(narrow, "gy")
+    )(f, s, fp, sp, outer, far, near, weights)
+    keep, send, modes = call(
+        forward,
+        [((160, 128), F32), ((160, 128), F32), ((64, 16, 128), F32)],
+        [VMEM, SMEM, SMEM, anywhere, anywhere],
+        [
+            pltpu.VMEM((320, 256), F32),
+            pltpu.VMEM((4, 512, 128), BF16),
+            pltpu.VMEM((4, 128, 512), F32),
+            pltpu.VMEM((256, 128), BF16),
+            pltpu.VMEM((256, 256), BF16),
+            pltpu.SemaphoreType.DMA((2,)),
+        ],
+    )(last, lift_weight, lift_bias, table["yf"], table["zf"])
+    modes = exchange(modes.reshape(128, 8, 128), everyone)
     [direct] = call(
         pointwise,
         [((8, 256, 128), F32)],
@@ -432,15 +453,8 @@
         flops=3 * 10**8,
     )(keep, lax.ppermute(send, "ga", swap), lift_weight, lift_bias, mix_weight, output_bias.reshape(1, C))
 
-    [modes] = call(
-        forward,
-        [((64, 4, 128), F32)],
-        [VMEM, SMEM, SMEM, VMEM, VMEM],
-        [pltpu.VMEM((256, 1024), BF16)],
-    )(columns, lift_weight, lift_bias, table["yf"], table["zf"])
-    modes = exchange(modes.reshape(128, 2, 128), everyone)
-    [mixed] = call(mix_modes, [((64, 4, 128), F32)], [VMEM] * 3 + [anywhere])(
-        modes.reshape(256, 128), weights, table["x"], direct
+    [mixed] = call(mix_modes, [((64, 4, 128), F32)], [VMEM] * 4 + [anywhere])(
+        modes.reshape(8, 8, 16, 128), weights, table["xf"], table["xi"], direct
     )
     mixed = exchange(mixed.reshape(128, 2, 128), everyone)
     [spectral] = call(inverse, [((8, 256, 128), BF16)], [VMEM] * 3)(

time: 108 us -> 94.7 us (0.88)
  blocking collectives: 38.1 us -> 26.9 us
  waiting for transfers between devices: 9.13 us -> 16 us
  starting transfers between devices: 32 us -> 25.4 us
  local copies, waits for them, and re-layouts: 5.05 us -> 2.78 us
    all_to_all x3 -> x2, blocking collectives: 38.1 us -> 26.9 us  [exchange(): return lax.all_to_all(value, axis, split_axis=0, concat_axis=0, tiled=True)]
    ppermute x1, waiting for transfers between devices: 0.01 us -> 5.7 us  [shards(): lax.ppermute(far, 'gy', [(j, (j - 1 + 2 * (j % 2)) % 8) for j in range(8)])]
    all_to_all x3 -> x2, starting transfers between devices: 21 us -> 16.3 us  [exchange(): return lax.all_to_all(value, axis, split_axis=0, concat_axis=0, tiled=True)]
    ppermute x1, starting transfers between devices: 6.6 us -> 4.63 us  [shards(): lax.ppermute(far, 'gy', [(j, (j - 1 + 2 * (j % 2)) % 8) for j in range(8)])]
    all_to_all x1 -> x0, local copies, waits for them, and re-layouts: 1.88 us -> none  [exchange(): return lax.all_to_all(value, axis, split_axis=0, concat_axis=0, tiled=True)]
    all_to_all x3 -> x2, waiting for transfers between devices: 7.59 us -> 9.33 us  [exchange(): return lax.all_to_all(value, axis, split_axis=0, concat_axis=0, tiled=True)]
    unnamed x28 -> x30, local copies, waits for them, and re-layouts: 3.17 us -> 2.78 us
    pallas_call x4 -> x3, Pallas kernels: 13.5 us -> 13.7 us  [the longest x1 6.83 us: shards(): call(stencil, [((5, 2, 128, 128), F32)], [VMEM] * 7 + [anywhere], [pltpu....]
  transfers between devices with their start and end apart: 9 -> 8, of which waited for: 5 -> 4; matrix products, arithmetic and copies ran while one was open for 2% -> 0% of each run, Pallas kernels for 12% -> 6%
where the time goes in v6:
time: 94.7 us; the launch traced here: 93.3 us
  blocking collectives  26.9 us (28%)
  starting transfers between devices  25.4 us (27%)
  Pallas kernels  22.1 us (23%)
  waiting for transfers between devices  16 us (17%)
  local copies, waits for them, and re-layouts  2.78 us (3%)
    all_to_all x2, blocking collectives, exchange(): return lax.all_to_all(value, axis, split_axis=0, concat_axis=0, tiled=True)  26.9 us
    all_to_all x2, starting transfers between devices, exchange(): return lax.all_to_all(value, axis, split_axis=0, concat_axis=0, tiled=True)  16.3 us
    all_to_all x2, waiting for transfers between devices, exchange(): return lax.all_to_all(value, axis, split_axis=0, concat_axis=0, tiled=True)  9.33 us
    pallas_call x1, Pallas kernels, shards(): call(stencil, [((5, 2, 128, 128), F32)], [VMEM] * 7 + [anywhere], [pltpu....  6.83 us
    ppermute x1, waiting for transfers between devices, shards(): lax.ppermute(far, 'gy', [(j, (j - 1 + 2 * (j % 2)) % 8) for j in range(8)])  5.7 us
    ppermute x1, starting transfers between devices, shards(): lax.ppermute(far, 'gy', [(j, (j - 1 + 2 * (j % 2)) % 8) for j in range(8)])  4.63 us
    pallas_call x1, Pallas kernels, shards(): call(forward, [((160, 128), F32), ((160, 128), F32), ((64, 16, 128), F32)...  4.28 us
    pallas_call x1, Pallas kernels, shards(): call(pointwise, [((8, 256, 128), F32)], [VMEM, VMEM, SMEM, SMEM, VMEM, VM...  3.19 us
  transfers between devices with their start and end apart: 8, of which 4 were waited for; matrix products, arithmetic and copies ran while one was open for 0% of the time, Pallas kernels for 6%

profile of v6, /device:TPU:1, one launch (start us, length us, event | category | flops | bytes accessed | tf_op | source)
XLA Modules:
  0.0 93.3 jit_solution(18019443222942819338)
XLA Ops:
  0.0 1.4 %collective-permute-start = (f32[5,128,256]{2,1,0:T(8,128)}, f32[5,128,256]{2,1,0:T(8,128)S(1)}, u32[]{:S(2)}, u32[]{:S(2)}) collective-permute-start(f32[5,128,256]{2,1,0:T(8,128)} %bitcast.10), channel_id=1, source_target_pairs={{0,1},{1,0},{2,3},{3,2},{4,5},{5,4},{6,7},{7,6},{8,9},{9,8},{10,11... | collective-permute-start | bytes 1966088 | tf_op jit(solution)/shard_map/ppermute | solution.py:397
  1.4 0.0 copy-start
  1.4 0.0 collective-permute-start.1
  1.4 0.0 copy-start.3
  1.4 1.2 %copy-done.3 = f32[5,8,16,256]{3,2,1,0:T(8,128)S(1)} copy-done((f32[5,8,16,256]{3,2,1,0:T(8,128)S(1)}, f32[5,8,16,256]{3,2,1,0:T(8,128)}, u32[]{:S(2)}) %copy-start.3) | copy-done | bytes 655384
  2.6 0.0 copy-start.7
  2.6 0.9 copy-done.7
  3.5 0.1 shard_map.127.own
  3.7 0.0 collective-permute-done.1.sp
  3.7 0.0 collective-permute-done.fp
  3.7 0.1 shard_map.128.after
  3.8 1.7 %collective-permute-start.2 = (f32[6,2,48,128]{3,2,1,0:T(8,128)S(1)}, f32[6,2,48,128]{3,2,1,0:T(8,128)S(1)}, u32[]{:S(2)}, u32[]{:S(2)}) collective-permute-start(f32[6,2,48,128]{3,2,1,0:T(8,128)S(1)} %shard_map.128.after), channel_id=1, source_target_pairs={{0,113},{16,1},{32,17},{48,33},{64,49},{80,65},{96,81},{112,97},{1... | collective-permute-start | bytes 884744 | tf_op jit(solution)/shard_map/ppermute | solution.py:406
  5.5 0.0 copy-done
  5.5 1.6 %shard_map.130 = bf16[64,32,128]{2,1,0:T(8,128)(2,1)} custom-call(f32[2048,128]{1,0:T(8,128)S(1)} %bitcast.9, f32[6,2,48,128]{3,2,1,0:T(8,128)S(1)} %shard_map.128.after), custom_call_target="tpu_custom_call" | custom-call | flops 10000000 | bytes 20000000 | tf_op jit(solution)/shard_map/pallas_call | solution.py:408
  7.1 0.0 copy-start.4
  7.1 11.3 %all-to-all-start = ((bf16[64,32,128]{2,1,0:T(8,128)(2,1)}), bf16[64,32,128]{2,1,0:T(8,128)(2,1)}, u32[]{:S(2)}, u32[]{:S(2)}) async-start(bf16[64,32,128]{2,1,0:T(8,128)(2,1)} %shard_map.130), calls=%async_computation | async-start | bytes 1048576 | tf_op jit(solution)/shard_map/all_to_all | solution.py:391
  18.4 0.0 collective-permute-done.2.message
  18.4 0.0 copy-done.4
  18.4 0.0 copy-done.8
  18.4 0.5 shard_map.129
  19.0 4.6 %collective-permute-start.3 = (f32[3,16,128]{2,1,0:T(8,128)S(1)}, f32[3,16,128]{2,1,0:T(8,128)S(1)}, u32[]{:S(2)}, u32[]{:S(2)}) collective-permute-start(f32[3,16,128]{2,1,0:T(8,128)S(1)} %get-tuple-element.12), channel_id=1, source_target_pairs={{0,14},{2,4},{4,2},{6,8},{8,6},{10,12},{12,10},{14,0},{1,15},{3,5}... | collective-permute-start | bytes 73736 | tf_op jit(solution)/shard_map/ppermute | solution.py:421
  23.6 0.0 collective-permute-start.4
  23.6 5.7 %collective-permute-done.3.far = f32[3,16,128]{2,1,0:T(8,128)S(1)} collective-permute-done((f32[3,16,128]{2,1,0:T(8,128)S(1)}, f32[3,16,128]{2,1,0:T(8,128)S(1)}, u32[]{:S(2)}, u32[]{:S(2)}) %collective-permute-start.3) | collective-permute-done | bytes 24608 | tf_op jit(solution)/shard_map/ppermute | solution.py:421
  29.3 0.0 collective-permute-done.4.near
  29.3 1.4 %all-to-all-done.after.weights = bf16[64,32,128]{2,1,0:T(8,128)(2,1)} async-done(((bf16[64,32,128]{2,1,0:T(8,128)(2,1)}), bf16[64,32,128]{2,1,0:T(8,128)(2,1)}, u32[]{:S(2)}, u32[]{:S(2)}) %all-to-all-start) | async-done | bytes 524320 | tf_op jit(solution)/shard_map/all_to_all | solution.py:391
  30.8 6.8 %shard_map.131.last = f32[5,2,128,128]{3,2,1,0:T(8,128)S(1)} custom-call(f32[5,128,256]{2,1,0:T(8,128)S(1)} %bitcast.13, f32[128,256]{1,0:T(8,128)S(1)} %bitcast.19, f32[5,128,256]{2,1,0:T(8,128)S(1)} %collective-permute-done.fp, f32[128,256]{1,0:T(8,128)S(1)} %collective-permute-done.1.sp, f32[6,2,128,128]{3,2,1,0:T(8,128)S(1)} %get-tuple-element.11.outer, ...), custom_call_target="tpu_custom_call" | custom-call | flops 999999995904 | bytes 1048576 | tf_op jit(solution)/shard_map/pallas_call | solution.py:423
  37.6 0.0 copy-done.5
  37.6 0.0 copy-done.10
  37.6 0.0 copy-done.11
  37.6 0.0 copy-done.13
  37.6 4.3 %shard_map.132 = (f32[160,128]{1,0:T(8,128)S(1)}, f32[160,128]{1,0:T(8,128)S(1)}, f32[64,16,128]{2,1,0:T(8,128)}) custom-call(f32[5,2,128,128]{3,2,1,0:T(8,128)S(1)} %shard_map.131.last, f32[5,32]{1,0:T(8,128)S(1)} %copy-done.11, f32[32]{0:T(128)S(1)} %copy-done.13, bf16[8,256,128]{2,1,0:T(8,128)(2,1)S(1)} %copy-done.5, bf16[256,256]{1,0:T(8,128)(2,1)S(1)} %copy-done.10), custom_call_target="tpu_custom_call" | custom-call | flops 10000000 | bytes 1048576 | tf_op jit(solution)/shard_map/pallas_call | solution.py:434
  41.9 0.0 copy-start.12
  41.9 5.0 %all-to-all-start.1 = ((f32[128,8,128]{2,1,0:T(8,128)}), f32[128,8,128]{2,1,0:T(8,128)S(1)}, u32[]{:S(2)}, u32[]{:S(2)}) async-start(f32[128,8,128]{2,1,0:T(8,128)} %bitcast.3), calls=%async_computation.1 | async-start | bytes 1048576 | tf_op jit(solution)/shard_map/all_to_all | solution.py:391
  47.0 1.3 %collective-permute-start.5 = (f32[160,128]{1,0:T(8,128)S(1)}, f32[160,128]{1,0:T(8,128)S(1)}, u32[]{:S(2)}, u32[]{:S(2)}) collective-permute-start(f32[160,128]{1,0:T(8,128)S(1)} %get-tuple-element.16), channel_id=1, source_target_pairs={{0,1},{1,0},{2,3},{3,2},{4,5},{5,4},{6,7},{7,6},{8,9},{9,8},{10,11... | collective-permute-start | bytes 245768 | tf_op jit(solution)/shard_map/ppermute | solution.py:454
  48.2 0.9 collective-permute-done.5.got
  49.2 0.0 copy-done.12
  49.2 0.7 copy-done.14
  49.8 3.2 %shard_map.133.after.direct = f32[8,256,128]{2,1,0:T(8,128)S(1)} custom-call(f32[160,128]{1,0:T(8,128)S(1)} %get-tuple-element.15.keep, f32[160,128]{1,0:T(8,128)S(1)} %collective-permute-done.5.got, f32[5,32]{1,0:T(8,128)S(1)} %copy-done.11, f32[32]{0:T(128)S(1)} %copy-done.13, bf16[32,32]{1,0:T(8,128)(2,1)S(1)} %copy-done.12, f32[1,32]{1,0:T(1,128)S(1)} %bitcast.20), custom_call_target="tpu_custom_call" | custom-call | flops 300000000 | bytes 1048576 | tf_op jit(solution)/shard_map/pallas_call | solution.py:448
  53.0 7.9 %all-to-all-done.1 = f32[128,8,128]{2,1,0:T(8,128)S(1)} async-done(((f32[128,8,128]{2,1,0:T(8,128)}), f32[128,8,128]{2,1,0:T(8,128)S(1)}, u32[]{:S(2)}, u32[]{:S(2)}) %all-to-all-start.1) | async-done | bytes 524320 | tf_op jit(solution)/shard_map/all_to_all | solution.py:391
  60.9 0.0 copy-done.6
  60.9 0.0 copy-done.9
  60.9 2.6 %shard_map.134 = f32[64,4,128]{2,1,0:T(4,128)S(1)} custom-call(f32[8,8,16,128]{3,2,1,0:T(8,128)S(1)} %bitcast.8, bf16[64,32,128]{2,1,0:T(8,128)(2,1)} %all-to-all-done.after.weights, bf16[4,256,128]{2,1,0:T(8,128)(2,1)S(1)} %copy-done.6, bf16[2,128,256]{2,1,0:T(8,128)(2,1)S(1)} %copy-done.9, f32[8,256,128]{2,1,0:T(8,128)S(1)} %shard_map.133.after.direct), custom_call_target="tpu_custom_call" | custom-call | flops 10000000 | bytes 1048576 | tf_op jit(solution)/shard_map/pallas_call | solution.py:456
  63.6 14.3 %all_to_all.20 = f32[128,2,128]{2,1,0:T(2,128)S(1)} all-to-all(f32[128,2,128]{2,1,0:T(2,128)S(1)} %bitcast.14), channel_id=1, replica_groups=mesh['gx'=8,'gy'=8,'ga'=2] {'gx','gy','ga'}, dimensions={0} | all-to-all | bytes 262144 | tf_op jit(solution)/shard_map/all_to_all | solution.py:391
  77.9 0.0 copy-done.1
  77.9 0.0 copy-done.2
  77.9 1.0 %shard_map.135 = bf16[8,256,128]{2,1,0:T(8,128)(2,1)S(1)} custom-call(f32[64,4,128]{2,1,0:T(4,128)S(1)} %bitcast.15, bf16[2,512,512]{2,1,0:T(8,128)(2,1)S(1)} %copy-done.1, bf16[384,1024]{1,0:T(8,128)(2,1)S(1)} %copy-done.2), custom_call_target="tpu_custom_call" | custom-call | flops 10000000 | bytes 1048576 | tf_op jit(solution)/shard_map/pallas_call | solution.py:460
  78.9 12.6 %all_to_all.21.got = bf16[8,256,128]{2,1,0:T(8,128)(2,1)S(1)} all-to-all(bf16[8,256,128]{2,1,0:T(8,128)(2,1)S(1)} %shard_map.135), channel_id=1, replica_groups=mesh['gx'=8,'gy'=8,'ga'=2] {'gy'}, dimensions={0} | all-to-all | bytes 1048576 | tf_op jit(solution)/shard_map/all_to_all | solution.py:391
  91.5 1.8 %shard_map.136 = bf16[8,32,8,128]{3,2,1,0:T(8,128)(2,1)} custom-call(bf16[8,256,128]{2,1,0:T(8,128)(2,1)S(1)} %all_to_all.21.got, f32[8,256,128]{2,1,0:T(8,128)S(1)} %shard_map.133.after.direct), custom_call_target="tpu_custom_call" | custom-call | flops 10000000 | bytes 1048576 | tf_op jit(solution)/shard_map/pallas_call | solution.py:464
  (10 shorter events, 0.0 us)
Async XLA Ops:
  0.0 3.7 %collective-permute-start = (f32[5,128,256]{2,1,0:T(8,128)}, f32[5,128,256]{2,1,0:T(8,128)S(1)}, u32[]{:S(2)}, u32[]{:S(2)}) collective-permute-start(f32[5,128,256]{2,1,0:T(8,128)} %bitcast.10), channel_id=1, source_target_pairs={{0,1},{1,0},{2,3},{3,2},{4,5},{5,4},{6,7},{7,6},{8,9},{9,8},{10,11... | collective-permute-start | bytes 1966088 | tf_op jit(solution)/shard_map/ppermute | solution.py:397
  1.4 4.1 %copy-start = (f32[4,4,32,4,128]{4,3,2,1,0:T(4,128)S(1)}, f32[4,4,32,4,128]{4,3,2,1,0:T(4,128)}, u32[]{:S(2)}) copy-start(f32[4,4,32,4,128]{4,3,2,1,0:T(4,128)} %param.18) | copy-start | bytes 3145732
  1.4 2.2 %collective-permute-start.1 = (f32[128,256]{1,0:T(8,128)}, f32[128,256]{1,0:T(8,128)S(1)}, u32[]{:S(2)}, u32[]{:S(2)}) collective-permute-start(f32[128,256]{1,0:T(8,128)} %bitcast.16), channel_id=1, source_target_pairs={{0,1},{1,0},{2,3},{3,2},{4,5},{5,4},{6,7},{7,6},{8,9},{9,8},{10,11... | collective-permute-start | bytes 393224 | tf_op jit(solution)/shard_map/ppermute | solution.py:397
  1.4 1.2 %copy-start.3 = (f32[5,8,16,256]{3,2,1,0:T(8,128)S(1)}, f32[5,8,16,256]{3,2,1,0:T(8,128)}, u32[]{:S(2)}) copy-start(f32[5,8,16,256]{3,2,1,0:T(8,128)} %param.13) | copy-start | bytes 1966084
  2.6 0.9 copy-start.7
  3.8 14.6 %collective-permute-start.2 = (f32[6,2,48,128]{3,2,1,0:T(8,128)S(1)}, f32[6,2,48,128]{3,2,1,0:T(8,128)S(1)}, u32[]{:S(2)}, u32[]{:S(2)}) collective-permute-start(f32[6,2,48,128]{3,2,1,0:T(8,128)S(1)} %shard_map.128.after), channel_id=1, source_target_pairs={{0,113},{16,1},{32,17},{48,33},{64,49},{80,65},{96,81},{112,97},{1... | collective-permute-start | bytes 884744 | tf_op jit(solution)/shard_map/ppermute | solution.py:406
  7.1 11.3 %copy-start.4 = (f32[5,8,16,256]{3,2,1,0:T(8,128)S(1)}, f32[5,8,16,256]{3,2,1,0:T(8,128)}, u32[]{:S(2)}) copy-start(f32[5,8,16,256]{3,2,1,0:T(8,128)} %param.13) | copy-start | bytes 1966084
  7.1 11.4 %copy-start.8 = (f32[8,16,256]{2,1,0:T(8,128)S(1)}, f32[8,16,256]{2,1,0:T(8,128)}, u32[]{:S(2)}) copy-start(f32[8,16,256]{2,1,0:T(8,128)} %param.14) | copy-start | bytes 393220
  7.1 23.7 %all-to-all-start = ((bf16[64,32,128]{2,1,0:T(8,128)(2,1)}), bf16[64,32,128]{2,1,0:T(8,128)(2,1)}, u32[]{:S(2)}, u32[]{:S(2)}) async-start(bf16[64,32,128]{2,1,0:T(8,128)(2,1)} %shard_map.130), calls=%async_computation | async-start | bytes 1048576 | tf_op jit(solution)/shard_map/all_to_all | solution.py:391
  19.0 10.3 %collective-permute-start.3 = (f32[3,16,128]{2,1,0:T(8,128)S(1)}, f32[3,16,128]{2,1,0:T(8,128)S(1)}, u32[]{:S(2)}, u32[]{:S(2)}) collective-permute-start(f32[3,16,128]{2,1,0:T(8,128)S(1)} %get-tuple-element.12), channel_id=1, source_target_pairs={{0,14},{2,4},{4,2},{6,8},{8,6},{10,12},{12,10},{14,0},{1,15},{3,5}... | collective-permute-start | bytes 73736 | tf_op jit(solution)/shard_map/ppermute | solution.py:421
  23.6 5.7 %collective-permute-start.4 = (f32[3,16,128]{2,1,0:T(8,128)S(1)}, f32[3,16,128]{2,1,0:T(8,128)S(1)}, u32[]{:S(2)}, u32[]{:S(2)}) collective-permute-start(f32[3,16,128]{2,1,0:T(8,128)S(1)} %get-tuple-element.13), channel_id=1, source_target_pairs={{0,2},{2,0},{4,6},{6,4},{8,10},{10,8},{12,14},{14,12},{1,3},{3,1},... | collective-permute-start | bytes 73736 | tf_op jit(solution)/shard_map/ppermute | solution.py:422
  30.7 6.8 %copy-start.5 = (bf16[8,256,128]{2,1,0:T(8,128)(2,1)S(1)}, bf16[8,256,128]{2,1,0:T(8,128)(2,1)}, u32[]{:S(2)}) copy-start(bf16[8,256,128]{2,1,0:T(8,128)(2,1)} %constant.12.clone.yf_far) | copy-start | bytes 1572868
  30.7 6.9 %copy-start.10 = (bf16[256,256]{1,0:T(8,128)(2,1)S(1)}, bf16[256,256]{1,0:T(8,128)(2,1)}, u32[]{:S(2)}) copy-start(bf16[256,256]{1,0:T(8,128)(2,1)} %constant.14.clone.zf_far) | copy-start | bytes 393220
  30.7 6.9 %copy-start.11 = (f32[5,32]{1,0:T(8,128)S(1)}, f32[5,32]{1,0:T(8,128)}, u32[]{:S(2)}) copy-start(f32[5,32]{1,0:T(8,128)} %weight.3) | copy-start | bytes 1924
  30.7 6.9 %copy-start.13 = (f32[32]{0:T(128)S(1)}, f32[32]{0:T(128)}, u32[]{:S(2)}) copy-start(f32[32]{0:T(128)} %bias.3) | copy-start | bytes 388
  41.9 7.2 %copy-start.12 = (bf16[32,32]{1,0:T(8,128)(2,1)S(1)}, bf16[32,32]{1,0:T(8,128)(2,1)}, u32[]{:S(2)}) copy-start(bf16[32,32]{1,0:T(8,128)(2,1)} %mix.1) | copy-start | bytes 6148
  41.9 19.0 %all-to-all-start.1 = ((f32[128,8,128]{2,1,0:T(8,128)}), f32[128,8,128]{2,1,0:T(8,128)S(1)}, u32[]{:S(2)}, u32[]{:S(2)}) async-start(f32[128,8,128]{2,1,0:T(8,128)} %bitcast.3), calls=%async_computation.1 | async-start | bytes 1048576 | tf_op jit(solution)/shard_map/all_to_all | solution.py:391
  47.0 2.2 %collective-permute-start.5 = (f32[160,128]{1,0:T(8,128)S(1)}, f32[160,128]{1,0:T(8,128)S(1)}, u32[]{:S(2)}, u32[]{:S(2)}) collective-permute-start(f32[160,128]{1,0:T(8,128)S(1)} %get-tuple-element.16), channel_id=1, source_target_pairs={{0,1},{1,0},{2,3},{3,2},{4,5},{5,4},{6,7},{7,6},{8,9},{9,8},{10,11... | collective-permute-start | bytes 245768 | tf_op jit(solution)/shard_map/ppermute | solution.py:454
  49.2 0.7 copy-start.14
  49.8 11.1 %copy-start.6 = (bf16[4,256,128]{2,1,0:T(8,128)(2,1)S(1)}, bf16[4,256,128]{2,1,0:T(8,128)(2,1)}, u32[]{:S(2)}) copy-start(bf16[4,256,128]{2,1,0:T(8,128)(2,1)} %constant.16.clone.xf) | copy-start | bytes 786436
  49.8 11.1 %copy-start.9 = (bf16[2,128,256]{2,1,0:T(8,128)(2,1)S(1)}, bf16[2,128,256]{2,1,0:T(8,128)(2,1)}, u32[]{:S(2)}) copy-start(bf16[2,128,256]{2,1,0:T(8,128)(2,1)} %constant.17.clone.xi) | copy-start | bytes 393220
  60.9 17.0 %copy-start.1 = (bf16[2,512,512]{2,1,0:T(8,128)(2,1)S(1)}, bf16[2,512,512]{2,1,0:T(8,128)(2,1)}, u32[]{:S(2)}) copy-start(bf16[2,512,512]{2,1,0:T(8,128)(2,1)} %constant.15.clone.zi) | copy-start | bytes 3145732
  60.9 17.0 %copy-start.2 = (bf16[384,1024]{1,0:T(8,128)(2,1)S(1)}, bf16[384,1024]{1,0:T(8,128)(2,1)}, u32[]{:S(2)}) copy-start(bf16[384,1024]{1,0:T(8,128)(2,1)} %constant.13.clone.yi) | copy-start | bytes 2359300

commit v7 on v6

--- a/solution.py
+++ b/solution.py
@@ -36,9 +36,8 @@
     cy, sy = cos_sin(ky, np.arange(GY), GY)
     rows = np.concatenate([cy, -sy]) / math.sqrt(GY)
     out["yf"] = np.concatenate(split(rows)).reshape(256, 8, 128).transpose(1, 0, 2)
-    rows = np.concatenate([cy, -sy]) / math.sqrt(GY)
-    high, low = split(rows)
-    out["yi"] = np.concatenate([high, high, low])
+    high, low = (half.reshape(128, 8, 128).transpose(1, 0, 2) for half in split(rows))
+    out["yi"] = np.concatenate([high, low], axis=2)
     cf, sf = (
         np.einsum("kz,cd->czkd", w / math.sqrt(NZ), np.eye(8)).reshape(128, 2, 32)
         for w in cos_sin(np.arange(MZ), np.arange(NZ), NZ)
@@ -46,16 +45,13 @@
     zf = np.zeros((2, 128, 2, 2, 32))
     zf[0, :, :, 0], zf[1, :, :, 0], zf[1, :, :, 1], zf[0, :, :, 1] = cf, sf, cf, -sf
     out["zf"] = np.concatenate(split(zf.reshape(256, 128)), axis=1)
-    cz, sz = (w / math.sqrt(NZ) for w in cos_sin(np.arange(MZ), np.arange(ZL), NZ))
-    eye = np.eye(C)
-    zi = np.zeros((2, 2, 4, C, 2, ZL, C))
-    for half in range(2):
-        for k in range(4):
-            for z in range(ZL):
-                c, s = cz[4 * half + k, z] * eye, sz[4 * half + k, z] * eye
-                zi[half, 0, k, :, 0, z], zi[half, 1, k, :, 0, z] = c, -s
-                zi[half, 1, k, :, 1, z], zi[half, 0, k, :, 1, z] = c, s
-    out["zi"] = np.stack(split(zi.reshape(16 * C, 2 * ZL * C)))
+    ci, si = (
+        np.einsum("kz,op->zokp", w / math.sqrt(NZ), np.eye(16)).reshape(128, 2, 64)
+        for w in cos_sin(np.arange(MZ), np.arange(ZL), NZ)
+    )
+    zi = np.zeros((2, 128, 2, 2, 64))
+    zi[0, :, :, 0], zi[0, :, :, 1], zi[1, :, :, 0], zi[1, :, :, 1] = ci, -si, si, ci
+    out["zi"] = np.concatenate(split(zi.reshape(256, 256)))
     kx = np.arange(MX) - MX // 2
     cx, sx = cos_sin(kx, np.arange(GX), GX)
     cr = (cx / 8.0).astype(np.float32).astype(jnp.bfloat16).astype(np.float64)
@@ -88,11 +84,6 @@
 
 def dot(a, b, contract=((1,), (0,))):
     return lax.dot_general(a, b, (contract, ((), ())), preferred_element_type=F32)
-
-
-def dot3(a, b_ref):
-    high, low = halves(a)
-    return dot(high, b_ref[0]) + dot(low, b_ref[0]) + dot(high, b_ref[1])
 
 
 def gelu(v):
@@ -337,42 +328,69 @@
         wi = weights[8 * i : 8 * i + 8, 16:32, :].astype(F32).reshape(128, 128)
         part = jnp.concatenate([wr * real - wi * imag, wr * imag + wi * real], axis=0)
         p_high, p_low = halves(part)
-        gather = (lane % 32 == 4 * i + row % 4).astype(BF16)
+        gather = (lane // 64 * 16 + lane % 16 == 4 * i + row % 4).astype(BF16)
         total = total + dot(p_high, gather) + dot(p_low, gather)
     row, lane = iotas((256, 128))
-    total = jnp.where((row // 4) % 4 == lane // 32, total, 0.0)
+    total = jnp.where((row // 4) % 4 == (lane // 16) % 4, total, 0.0)
     t_high, t_low = halves(total)
     back = dot(xi[0], t_high) + dot(xi[0], t_low) + dot(xi[1], t_high)
-    odd = (lax.broadcasted_iota(jnp.int32, (64, 128), 1) // 32) % 2 == 1
-    for ri in range(2):
-        value = back[64 * ri : 64 * ri + 64]
-        out[:, ri, :] = value
-        out[:, 2 + ri, :] = jnp.where(odd, -value, value)
-
-
-def inverse(got, zi, yi, out):
-    modes = jnp.concatenate([got[:, part, :] for part in range(4)], axis=1)
-    by_z = dot3(modes, zi)
-    by_z = jnp.concatenate([by_z[:, :256], by_z[:, 256:]], axis=0)
-    high, low = halves(by_z)
-    stacked = jnp.concatenate([high, low, high], axis=0)
-    for j in range(8):
-        block = dot(stacked, yi[:, 128 * j : 128 * j + 128], ((0,), (0,)))
-        out[j] = block.astype(BF16)
-
-
-def finish(got, direct, out, rows):
-    for x in range(8):
-        rows[256 * x : 256 * x + 256, :] = got[x].astype(F32)
-
-    def body(z, carry):
-        for o in range(C):
-            spectral = rows[pl.ds(C * z + o, 8, stride=256), :]
-            total = direct[z, 8 * o : 8 * o + 8, :] + spectral
-            out[z, o] = gelu(total).astype(BF16)
-        return carry
-
-    lax.fori_loop(0, ZL, body, 0)
+    real, imag = back[:64], back[64:]
+    lane = lax.broadcasted_iota(jnp.int32, (64, 128), 1)
+    parts = [
+        jnp.where(lane < 64, real, pltpu.roll(imag, 64, 1)),
+        jnp.where(lane < 64, pltpu.roll(real, 64, 1), imag),
+    ]
+    odd = (lane // 16) % 2 == 1
+    for a in range(2):
+        signed = [jnp.where(odd, -part, part) for part in parts] if a else parts
+        for i in range(8):
+            rows = slice(8 * i, 8 * i + 8)
+            tile = jnp.concatenate([part[rows] for part in signed], axis=0).astype(BF16)
+            for j in range(8):
+                out[i, j, a] = tile
+
+
+def finish(got, direct, yi_far, zi_far, out, rows, spectral, yi, zi, sems):
+    copies = [
+        pltpu.make_async_copy(yi_far.at[lax.axis_index("gy")], yi, sems.at[0]),
+        pltpu.make_async_copy(zi_far, zi, sems.at[1]),
+    ]
+    for copy in copies:
+        copy.start()
+    rows[...] = got[...].astype(F32)
+    for copy in copies:
+        copy.wait()
+    by_z = []
+    for part in range(2):
+        stack = []
+        for x in range(8):
+            pair = [rows[pl.ds(16 * a + 8 * part + x, 64, stride=32), :] for a in range(2)]
+            stack.append(jnp.concatenate(pair, axis=1).astype(BF16))
+        both = dot(zi[...], jnp.concatenate(stack, axis=0), ((1,), (1,)))
+        by_z.append(both[:256] + both[256:])
+    blank = jnp.zeros((64, 128), BF16)
+
+    def twice(lanes):
+        real, imag = yi[0:64, lanes], yi[64:128, lanes]
+        pieces = [[real, blank], [blank, real], [imag, blank], [blank, imag]]
+        return jnp.concatenate([jnp.concatenate(row, axis=1) for row in pieces], axis=0)
+
+    t_high, t_low = twice(slice(0, 128)), twice(slice(128, 256))
+    for pair in range(4):
+        lanes = slice(128 * pair, 128 * pair + 128)
+        value = jnp.concatenate(
+            [jnp.concatenate([v[:128, lanes], v[128:, lanes]], axis=1) for v in by_z], axis=0
+        )
+        high, low = halves(value)
+        both = dot(high, t_high) + dot(low, t_high) + dot(high, t_low)
+        for x in range(2):
+            spectral[pl.ds(2 * pair + x, 256, stride=8), :] = both[:, 128 * x : 128 * x + 128]
+    for part in range(2):
+        for z in range(ZL):
+            at = 128 * (8 * part + z)
+            branch = spectral[at : at + 128, :].astype(BF16).astype(F32)
+            total = gelu(direct[z, 128 * part : 128 * part + 128, :] + branch)
+            out[z, 16 * part : 16 * part + 16] = total.reshape(16, 8, 128).astype(BF16)
 
 
 def turn_weights(weights, after, out, wide):
@@ -453,17 +471,22 @@
         flops=3 * 10**8,
     )(keep, lax.ppermute(send, "ga", swap), lift_weight, lift_bias, mix_weight, output_bias.reshape(1, C))
 
-    [mixed] = call(mix_modes, [((64, 4, 128), F32)], [VMEM] * 4 + [anywhere])(
+    [mixed] = call(mix_modes, [((8, 8, 2, 16, 128), BF16)], [VMEM] * 4 + [anywhere])(
         modes.reshape(8, 8, 16, 128), weights, table["xf"], table["xi"], direct
     )
-    mixed = exchange(mixed.reshape(128, 2, 128), everyone)
-    [spectral] = call(inverse, [((8, 256, 128), BF16)], [VMEM] * 3)(
-        mixed.reshape(64, 4, 128), table["zi"], table["yi"]
-    )
-    spectral = exchange(spectral, "gy")
+    mixed = exchange(mixed.reshape(128, 16, 128), everyone)
     [out] = call(
-        finish, [((8, 32, 8, 128), BF16)], [VMEM] * 2, [pltpu.VMEM((2048, 128), F32)]
-    )(spectral, direct)
+        finish,
+        [((8, 32, 8, 128), BF16)],
+        [VMEM, VMEM, anywhere, anywhere],
+        [
+            pltpu.VMEM((2048, 128), F32),
+            pltpu.VMEM((2048, 128), F32),
+            pltpu.VMEM((128, 256), BF16),
+            pltpu.VMEM((512, 256), BF16),
+            pltpu.SemaphoreType.DMA((2,)),
+        ],
+    )(mixed.reshape(2048, 128), direct, table["yi"], table["zi"])
     return out
 
 

time: 94.7 us -> 84.4 us (0.89); the launches traced: 93.3 us -> 84 us
  blocking collectives: 26.9 us -> 17.9 us
    all_to_all x2 -> x1, blocking collectives: 26.9 us -> 17.9 us  [exchange(): return lax.all_to_all(value, axis, split_axis=0, concat_axis=0, tiled=True)]
    pallas_call x3 -> x2, Pallas kernels: 5.38 us -> 5.21 us  [the longest x1 2.66 us: shards(): call(finish, [((8, 32, 8, 128), BF16)], [VMEM, VMEM, anywhere, anywhere],...]
where the time goes in v7:
time: 84.4 us; the launch traced here: 84 us
  starting transfers between devices  25.4 us (30%)
  Pallas kernels  21.9 us (26%)
  blocking collectives  17.9 us (21%)
  waiting for transfers between devices  16 us (19%)
  local copies, waits for them, and re-layouts  2.78 us (3%)
    all_to_all x1, blocking collectives, exchange(): return lax.all_to_all(value, axis, split_axis=0, concat_axis=0, tiled=True)  17.9 us
    all_to_all x2, starting transfers between devices, exchange(): return lax.all_to_all(value, axis, split_axis=0, concat_axis=0, tiled=True)  16.3 us
    all_to_all x2, waiting for transfers between devices, exchange(): return lax.all_to_all(value, axis, split_axis=0, concat_axis=0, tiled=True)  9.33 us
    pallas_call x1, Pallas kernels, shards(): call(stencil, [((5, 2, 128, 128), F32)], [VMEM] * 7 + [anywhere], [pltpu....  6.83 us
    ppermute x1, waiting for transfers between devices, shards(): lax.ppermute(far, 'gy', [(j, (j - 1 + 2 * (j % 2)) % 8) for j in range(8)])  5.7 us
    ppermute x1, starting transfers between devices, shards(): lax.ppermute(far, 'gy', [(j, (j - 1 + 2 * (j % 2)) % 8) for j in range(8)])  4.63 us
    pallas_call x1, Pallas kernels, shards(): call(forward, [((160, 128), F32), ((160, 128), F32), ((64, 16, 128), F32)...  4.28 us
    pallas_call x1, Pallas kernels, shards(): call(pointwise, [((8, 256, 128), F32)], [VMEM, VMEM, SMEM, SMEM, VMEM, VM...  3.19 us
  transfers between devices with their start and end apart: 8, of which 4 were waited for; matrix products, arithmetic and copies ran while one was open for 0% of the time, Pallas kernels for 6%

profile of v7, /device:TPU:1, one launch (start us, length us, event | category | flops | bytes accessed | tf_op | source)
XLA Modules:
  0.0 84.0 jit_solution(7996899903189214643)
XLA Ops:
  0.0 1.4 %collective-permute-start = (f32[5,128,256]{2,1,0:T(8,128)}, f32[5,128,256]{2,1,0:T(8,128)S(1)}, u32[]{:S(2)}, u32[]{:S(2)}) collective-permute-start(f32[5,128,256]{2,1,0:T(8,128)} %bitcast.12), channel_id=1, source_target_pairs={{0,1},{1,0},{2,3},{3,2},{4,5},{5,4},{6,7},{7,6},{8,9},{9,8},{10,11... | collective-permute-start | bytes 1966088 | tf_op jit(solution)/shard_map/ppermute | solution.py:415
  1.4 0.0 copy-start
  1.4 0.0 collective-permute-start.1
  1.4 0.0 copy-start.1
  1.4 1.2 %copy-done.1 = f32[5,8,16,256]{3,2,1,0:T(8,128)S(1)} copy-done((f32[5,8,16,256]{3,2,1,0:T(8,128)S(1)}, f32[5,8,16,256]{3,2,1,0:T(8,128)}, u32[]{:S(2)}) %copy-start.1) | copy-done | bytes 655384
  2.6 0.0 copy-start.7
  2.6 0.9 %copy-done.7 = f32[8,16,256]{2,1,0:T(8,128)S(1)} copy-done((f32[8,16,256]{2,1,0:T(8,128)S(1)}, f32[8,16,256]{2,1,0:T(8,128)}, u32[]{:S(2)}) %copy-start.7) | copy-done | bytes 131096
  3.5 0.1 shard_map.127.own
  3.7 0.0 collective-permute-done.1.sp
  3.7 0.0 collective-permute-done.fp
  3.7 0.1 shard_map.128.after
  3.8 1.7 %collective-permute-start.2 = (f32[6,2,48,128]{3,2,1,0:T(8,128)S(1)}, f32[6,2,48,128]{3,2,1,0:T(8,128)S(1)}, u32[]{:S(2)}, u32[]{:S(2)}) collective-permute-start(f32[6,2,48,128]{3,2,1,0:T(8,128)S(1)} %shard_map.128.after), channel_id=1, source_target_pairs={{0,113},{16,1},{32,17},{48,33},{64,49},{80,65},{96,81},{112,97},{1... | collective-permute-start | bytes 884744 | tf_op jit(solution)/shard_map/ppermute | solution.py:424
  5.5 0.0 copy-done
  5.5 1.6 %shard_map.130 = bf16[64,32,128]{2,1,0:T(8,128)(2,1)} custom-call(f32[2048,128]{1,0:T(8,128)S(1)} %bitcast.11, f32[6,2,48,128]{3,2,1,0:T(8,128)S(1)} %shard_map.128.after), custom_call_target="tpu_custom_call" | custom-call | flops 10000000 | bytes 20000000 | tf_op jit(solution)/shard_map/pallas_call | solution.py:426
  7.1 0.0 copy-start.2
  7.1 11.3 %all-to-all-start = ((bf16[64,32,128]{2,1,0:T(8,128)(2,1)}), bf16[64,32,128]{2,1,0:T(8,128)(2,1)}, u32[]{:S(2)}, u32[]{:S(2)}) async-start(bf16[64,32,128]{2,1,0:T(8,128)(2,1)} %shard_map.130), calls=%async_computation | async-start | bytes 1048576 | tf_op jit(solution)/shard_map/all_to_all | solution.py:409
  18.4 0.0 collective-permute-done.2.message
  18.4 0.0 copy-done.2
  18.4 0.0 copy-done.8
  18.4 0.5 shard_map.129
  19.0 4.6 %collective-permute-start.3 = (f32[3,16,128]{2,1,0:T(8,128)S(1)}, f32[3,16,128]{2,1,0:T(8,128)S(1)}, u32[]{:S(2)}, u32[]{:S(2)}) collective-permute-start(f32[3,16,128]{2,1,0:T(8,128)S(1)} %get-tuple-element.12), channel_id=1, source_target_pairs={{0,14},{2,4},{4,2},{6,8},{8,6},{10,12},{12,10},{14,0},{1,15},{3,5}... | collective-permute-start | bytes 73736 | tf_op jit(solution)/shard_map/ppermute | solution.py:439
  23.6 0.0 collective-permute-start.4
  23.6 5.7 %collective-permute-done.3.far = f32[3,16,128]{2,1,0:T(8,128)S(1)} collective-permute-done((f32[3,16,128]{2,1,0:T(8,128)S(1)}, f32[3,16,128]{2,1,0:T(8,128)S(1)}, u32[]{:S(2)}, u32[]{:S(2)}) %collective-permute-start.3) | collective-permute-done | bytes 24608 | tf_op jit(solution)/shard_map/ppermute | solution.py:439
  29.3 0.0 collective-permute-done.4.near
  29.3 1.4 %all-to-all-done.after.weights = bf16[64,32,128]{2,1,0:T(8,128)(2,1)} async-done(((bf16[64,32,128]{2,1,0:T(8,128)(2,1)}), bf16[64,32,128]{2,1,0:T(8,128)(2,1)}, u32[]{:S(2)}, u32[]{:S(2)}) %all-to-all-start) | async-done | bytes 524320 | tf_op jit(solution)/shard_map/all_to_all | solution.py:409
  30.8 6.8 %shard_map.131.last = f32[5,2,128,128]{3,2,1,0:T(8,128)S(1)} custom-call(f32[5,128,256]{2,1,0:T(8,128)S(1)} %bitcast.15, f32[128,256]{1,0:T(8,128)S(1)} %bitcast.19, f32[5,128,256]{2,1,0:T(8,128)S(1)} %collective-permute-done.fp, f32[128,256]{1,0:T(8,128)S(1)} %collective-permute-done.1.sp, f32[6,2,128,128]{3,2,1,0:T(8,128)S(1)} %get-tuple-element.11.outer, ...), custom_call_target="tpu_custom_call" | custom-call | flops 999999995904 | bytes 1048576 | tf_op jit(solution)/shard_map/pallas_call | solution.py:441
  37.6 0.0 copy-done.3
  37.6 0.0 copy-done.10
  37.6 0.0 copy-done.11
  37.6 0.0 copy-done.13
  37.6 4.3 %shard_map.132 = (f32[160,128]{1,0:T(8,128)S(1)}, f32[160,128]{1,0:T(8,128)S(1)}, f32[64,16,128]{2,1,0:T(8,128)}) custom-call(f32[5,2,128,128]{3,2,1,0:T(8,128)S(1)} %shard_map.131.last, f32[5,32]{1,0:T(8,128)S(1)} %copy-done.11, f32[32]{0:T(128)S(1)} %copy-done.13, bf16[8,256,128]{2,1,0:T(8,128)(2,1)S(1)} %copy-done.3, bf16[256,256]{1,0:T(8,128)(2,1)S(1)} %copy-done.10), custom_call_target="tpu_custom_call" | custom-call | flops 10000000 | bytes 1048576 | tf_op jit(solution)/shard_map/pallas_call | solution.py:452
  41.9 0.0 copy-start.12
  41.9 5.0 %all-to-all-start.1 = ((f32[128,8,128]{2,1,0:T(8,128)}), f32[128,8,128]{2,1,0:T(8,128)S(1)}, u32[]{:S(2)}, u32[]{:S(2)}) async-start(f32[128,8,128]{2,1,0:T(8,128)} %bitcast.3), calls=%async_computation.1 | async-start | bytes 1048576 | tf_op jit(solution)/shard_map/all_to_all | solution.py:409
  47.0 1.3 %collective-permute-start.5 = (f32[160,128]{1,0:T(8,128)S(1)}, f32[160,128]{1,0:T(8,128)S(1)}, u32[]{:S(2)}, u32[]{:S(2)}) collective-permute-start(f32[160,128]{1,0:T(8,128)S(1)} %get-tuple-element.16), channel_id=1, source_target_pairs={{0,1},{1,0},{2,3},{3,2},{4,5},{5,4},{6,7},{7,6},{8,9},{9,8},{10,11... | collective-permute-start | bytes 245768 | tf_op jit(solution)/shard_map/ppermute | solution.py:472
  48.2 0.9 %collective-permute-done.5.got = f32[160,128]{1,0:T(8,128)S(1)} collective-permute-done((f32[160,128]{1,0:T(8,128)S(1)}, f32[160,128]{1,0:T(8,128)S(1)}, u32[]{:S(2)}, u32[]{:S(2)}) %collective-permute-start.5) | collective-permute-done | bytes 81952 | tf_op jit(solution)/shard_map/ppermute | solution.py:472
  49.2 0.0 copy-done.12
  49.2 0.7 copy-done.14
  49.8 3.2 %shard_map.133.after.direct = f32[8,256,128]{2,1,0:T(8,128)S(1)} custom-call(f32[160,128]{1,0:T(8,128)S(1)} %get-tuple-element.15.keep, f32[160,128]{1,0:T(8,128)S(1)} %collective-permute-done.5.got, f32[5,32]{1,0:T(8,128)S(1)} %copy-done.11, f32[32]{0:T(128)S(1)} %copy-done.13, bf16[32,32]{1,0:T(8,128)(2,1)S(1)} %copy-done.12, f32[1,32]{1,0:T(1,128)S(1)} %bitcast.20), custom_call_target="tpu_custom_call" | custom-call | flops 300000000 | bytes 1048576 | tf_op jit(solution)/shard_map/pallas_call | solution.py:466
  53.0 7.9 %all-to-all-done.1 = f32[128,8,128]{2,1,0:T(8,128)S(1)} async-done(((f32[128,8,128]{2,1,0:T(8,128)}), f32[128,8,128]{2,1,0:T(8,128)S(1)}, u32[]{:S(2)}, u32[]{:S(2)}) %all-to-all-start.1) | async-done | bytes 524320 | tf_op jit(solution)/shard_map/all_to_all | solution.py:409
  60.9 0.0 copy-done.5
  60.9 0.0 copy-done.9
  60.9 2.5 %shard_map.134 = bf16[8,8,2,16,128]{4,3,2,1,0:T(8,128)(2,1)S(1)} custom-call(f32[8,8,16,128]{3,2,1,0:T(8,128)S(1)} %bitcast.8, bf16[64,32,128]{2,1,0:T(8,128)(2,1)} %all-to-all-done.after.weights, bf16[4,256,128]{2,1,0:T(8,128)(2,1)S(1)} %copy-done.5, bf16[2,128,256]{2,1,0:T(8,128)(2,1)S(1)} %copy-done.9, f32[8,256,128]{2,1,0:T(8,128)S(1)} %shard_map.133.after.direct), custom_call_target="tpu_custom_call" | custom-call | flops 10000000 | bytes 1048576 | tf_op jit(solution)/shard_map/pallas_call | solution.py:474
  63.5 0.0 copy-start.4
  63.5 0.0 copy-start.6
  63.5 17.9 %all_to_all.15 = bf16[128,16,128]{2,1,0:T(8,128)(2,1)S(1)} all-to-all(bf16[128,16,128]{2,1,0:T(8,128)(2,1)S(1)} %bitcast.9), channel_id=1, replica_groups=mesh['gx'=8,'gy'=8,'ga'=2] {'gx','gy','ga'}, dimensions={0} | all-to-all | bytes 1048576 | tf_op jit(solution)/shard_map/all_to_all | solution.py:409
  81.4 0.0 copy-done.4
  81.4 0.0 copy-done.6
  81.4 2.7 %shard_map.135 = bf16[8,32,8,128]{3,2,1,0:T(8,128)(2,1)} custom-call(bf16[2048,128]{1,0:T(8,128)(2,1)S(1)} %bitcast.10, f32[8,256,128]{2,1,0:T(8,128)S(1)} %shard_map.133.after.direct, bf16[8,128,256]{2,1,0:T(8,128)(2,1)S(1)} %copy-done.4, bf16[512,256]{1,0:T(8,128)(2,1)S(1)} %copy-done.6), custom_call_target="tpu_custom_call" | custom-call | flops 10000000 | bytes 1048576 | tf_op jit(solution)/shard_map/pallas_call | solution.py:478
  (8 shorter events, 0.0 us)
Async XLA Ops:
  0.0 3.7 %collective-permute-start = (f32[5,128,256]{2,1,0:T(8,128)}, f32[5,128,256]{2,1,0:T(8,128)S(1)}, u32[]{:S(2)}, u32[]{:S(2)}) collective-permute-start(f32[5,128,256]{2,1,0:T(8,128)} %bitcast.12), channel_id=1, source_target_pairs={{0,1},{1,0},{2,3},{3,2},{4,5},{5,4},{6,7},{7,6},{8,9},{9,8},{10,11... | collective-permute-start | bytes 1966088 | tf_op jit(solution)/shard_map/ppermute | solution.py:415
  1.4 4.1 %copy-start = (f32[4,4,32,4,128]{4,3,2,1,0:T(4,128)S(1)}, f32[4,4,32,4,128]{4,3,2,1,0:T(4,128)}, u32[]{:S(2)}) copy-start(f32[4,4,32,4,128]{4,3,2,1,0:T(4,128)} %param.18) | copy-start | bytes 3145732
  1.4 2.2 %collective-permute-start.1 = (f32[128,256]{1,0:T(8,128)}, f32[128,256]{1,0:T(8,128)S(1)}, u32[]{:S(2)}, u32[]{:S(2)}) collective-permute-start(f32[128,256]{1,0:T(8,128)} %bitcast.16), channel_id=1, source_target_pairs={{0,1},{1,0},{2,3},{3,2},{4,5},{5,4},{6,7},{7,6},{8,9},{9,8},{10,11... | collective-permute-start | bytes 393224 | tf_op jit(solution)/shard_map/ppermute | solution.py:415
  1.4 1.2 %copy-start.1 = (f32[5,8,16,256]{3,2,1,0:T(8,128)S(1)}, f32[5,8,16,256]{3,2,1,0:T(8,128)}, u32[]{:S(2)}) copy-start(f32[5,8,16,256]{3,2,1,0:T(8,128)} %param.13) | copy-start | bytes 1966084
  2.6 0.9 %copy-start.7 = (f32[8,16,256]{2,1,0:T(8,128)S(1)}, f32[8,16,256]{2,1,0:T(8,128)}, u32[]{:S(2)}) copy-start(f32[8,16,256]{2,1,0:T(8,128)} %param.14) | copy-start | bytes 393220
  3.8 14.6 %collective-permute-start.2 = (f32[6,2,48,128]{3,2,1,0:T(8,128)S(1)}, f32[6,2,48,128]{3,2,1,0:T(8,128)S(1)}, u32[]{:S(2)}, u32[]{:S(2)}) collective-permute-start(f32[6,2,48,128]{3,2,1,0:T(8,128)S(1)} %shard_map.128.after), channel_id=1, source_target_pairs={{0,113},{16,1},{32,17},{48,33},{64,49},{80,65},{96,81},{112,97},{1... | collective-permute-start | bytes 884744 | tf_op jit(solution)/shard_map/ppermute | solution.py:424
  7.1 11.3 %copy-start.2 = (f32[5,8,16,256]{3,2,1,0:T(8,128)S(1)}, f32[5,8,16,256]{3,2,1,0:T(8,128)}, u32[]{:S(2)}) copy-start(f32[5,8,16,256]{3,2,1,0:T(8,128)} %param.13) | copy-start | bytes 1966084
  7.1 11.4 %copy-start.8 = (f32[8,16,256]{2,1,0:T(8,128)S(1)}, f32[8,16,256]{2,1,0:T(8,128)}, u32[]{:S(2)}) copy-start(f32[8,16,256]{2,1,0:T(8,128)} %param.14) | copy-start | bytes 393220
  7.1 23.7 %all-to-all-start = ((bf16[64,32,128]{2,1,0:T(8,128)(2,1)}), bf16[64,32,128]{2,1,0:T(8,128)(2,1)}, u32[]{:S(2)}, u32[]{:S(2)}) async-start(bf16[64,32,128]{2,1,0:T(8,128)(2,1)} %shard_map.130), calls=%async_computation | async-start | bytes 1048576 | tf_op jit(solution)/shard_map/all_to_all | solution.py:409
  19.0 10.3 %collective-permute-start.3 = (f32[3,16,128]{2,1,0:T(8,128)S(1)}, f32[3,16,128]{2,1,0:T(8,128)S(1)}, u32[]{:S(2)}, u32[]{:S(2)}) collective-permute-start(f32[3,16,128]{2,1,0:T(8,128)S(1)} %get-tuple-element.12), channel_id=1, source_target_pairs={{0,14},{2,4},{4,2},{6,8},{8,6},{10,12},{12,10},{14,0},{1,15},{3,5}... | collective-permute-start | bytes 73736 | tf_op jit(solution)/shard_map/ppermute | solution.py:439
  23.6 5.7 %collective-permute-start.4 = (f32[3,16,128]{2,1,0:T(8,128)S(1)}, f32[3,16,128]{2,1,0:T(8,128)S(1)}, u32[]{:S(2)}, u32[]{:S(2)}) collective-permute-start(f32[3,16,128]{2,1,0:T(8,128)S(1)} %get-tuple-element.13), channel_id=1, source_target_pairs={{0,2},{2,0},{4,6},{6,4},{8,10},{10,8},{12,14},{14,12},{1,3},{3,1},... | collective-permute-start | bytes 73736 | tf_op jit(solution)/shard_map/ppermute | solution.py:440
  30.7 6.8 %copy-start.3 = (bf16[8,256,128]{2,1,0:T(8,128)(2,1)S(1)}, bf16[8,256,128]{2,1,0:T(8,128)(2,1)}, u32[]{:S(2)}) copy-start(bf16[8,256,128]{2,1,0:T(8,128)(2,1)} %constant.12.clone.yf_far) | copy-start | bytes 1572868
  30.7 6.9 %copy-start.10 = (bf16[256,256]{1,0:T(8,128)(2,1)S(1)}, bf16[256,256]{1,0:T(8,128)(2,1)}, u32[]{:S(2)}) copy-start(bf16[256,256]{1,0:T(8,128)(2,1)} %constant.14.clone.zf_far) | copy-start | bytes 393220
  30.7 6.9 %copy-start.11 = (f32[5,32]{1,0:T(8,128)S(1)}, f32[5,32]{1,0:T(8,128)}, u32[]{:S(2)}) copy-start(f32[5,32]{1,0:T(8,128)} %weight.3) | copy-start | bytes 1924
  30.7 6.9 %copy-start.13 = (f32[32]{0:T(128)S(1)}, f32[32]{0:T(128)}, u32[]{:S(2)}) copy-start(f32[32]{0:T(128)} %bias.3) | copy-start | bytes 388
  41.9 7.2 %copy-start.12 = (bf16[32,32]{1,0:T(8,128)(2,1)S(1)}, bf16[32,32]{1,0:T(8,128)(2,1)}, u32[]{:S(2)}) copy-start(bf16[32,32]{1,0:T(8,128)(2,1)} %mix.1) | copy-start | bytes 6148
  41.9 19.0 %all-to-all-start.1 = ((f32[128,8,128]{2,1,0:T(8,128)}), f32[128,8,128]{2,1,0:T(8,128)S(1)}, u32[]{:S(2)}, u32[]{:S(2)}) async-start(f32[128,8,128]{2,1,0:T(8,128)} %bitcast.3), calls=%async_computation.1 | async-start | bytes 1048576 | tf_op jit(solution)/shard_map/all_to_all | solution.py:409
  47.0 2.2 %collective-permute-start.5 = (f32[160,128]{1,0:T(8,128)S(1)}, f32[160,128]{1,0:T(8,128)S(1)}, u32[]{:S(2)}, u32[]{:S(2)}) collective-permute-start(f32[160,128]{1,0:T(8,128)S(1)} %get-tuple-element.16), channel_id=1, source_target_pairs={{0,1},{1,0},{2,3},{3,2},{4,5},{5,4},{6,7},{7,6},{8,9},{9,8},{10,11... | collective-permute-start | bytes 245768 | tf_op jit(solution)/shard_map/ppermute | solution.py:472
  49.2 0.7 copy-start.14
  49.8 11.1 %copy-start.5 = (bf16[4,256,128]{2,1,0:T(8,128)(2,1)S(1)}, bf16[4,256,128]{2,1,0:T(8,128)(2,1)}, u32[]{:S(2)}) copy-start(bf16[4,256,128]{2,1,0:T(8,128)(2,1)} %constant.16.clone.xf) | copy-start | bytes 786436
  49.8 11.1 %copy-start.9 = (bf16[2,128,256]{2,1,0:T(8,128)(2,1)S(1)}, bf16[2,128,256]{2,1,0:T(8,128)(2,1)}, u32[]{:S(2)}) copy-start(bf16[2,128,256]{2,1,0:T(8,128)(2,1)} %constant.17.clone.xi) | copy-start | bytes 393220
  63.5 17.9 %copy-start.4 = (bf16[8,128,256]{2,1,0:T(8,128)(2,1)S(1)}, bf16[8,128,256]{2,1,0:T(8,128)(2,1)}, u32[]{:S(2)}) copy-start(bf16[8,128,256]{2,1,0:T(8,128)(2,1)} %constant.13.clone.yi_far) | copy-start | bytes 1572868
  63.5 17.9 %copy-start.6 = (bf16[512,256]{1,0:T(8,128)(2,1)S(1)}, bf16[512,256]{1,0:T(8,128)(2,1)}, u32[]{:S(2)}) copy-start(bf16[512,256]{1,0:T(8,128)(2,1)} %constant.15.clone.zi_far) | copy-start | bytes 786436

commit v8 on v7

--- a/solution.py
+++ b/solution.py
@@ -15,6 +15,7 @@
 ROOT = math.sqrt(2.0 / math.pi)
 VMEM = pl.BlockSpec(memory_space=pltpu.VMEM)
 SMEM = pl.BlockSpec(memory_space=pltpu.SMEM)
+HBM = pl.BlockSpec(memory_space=pltpu.HBM)
 
 
 def cos_sin(freq, points, length):
@@ -121,104 +122,130 @@
                 out[field, h, 8 * d : 8 * d + 8, :] = jnp.where(bottom, first, last)
 
 
-def pack_own(f, s, own, rows):
+def edge_lanes(f, s, first_slot, lows, highs):
+    a = lax.axis_index("ga")
+    lane = lax.broadcasted_iota(jnp.int32, (16, 128), 1) // 4
+    for field in range(6):
+        ref = s if field == 5 else f.at[field]
+        low, high = lows[field // 2], highs[field // 2]
+        for plane in range(8):
+            base = 64 * (field % 2) + 4 * (first_slot + plane)
+            both = [
+                ref[pl.ds(pl.multiple_of(16 * plane + 8 * half, 8), 8), :] for half in (a, 1 - a)
+            ]
+            block = jnp.concatenate(both, axis=0)
+            here = lane == base // 4
+            low = jnp.where(here, turn(block[:, :128], base), low)
+            high = jnp.where(here, turn(block[:, 128:], base + 4), high)
+        lows[field // 2], highs[field // 2] = low, high
+
+
+def turn(value, shift):
+    return pltpu.roll(value, shift % 128, 1) if shift % 128 else value
+
+
+def pack_own(f_far, s_far, own, lows, highs, rows, f, s, sems):
+    copies = [
+        pltpu.make_async_copy(f_far, f, sems.at[0]),
+        pltpu.make_async_copy(s_far, s, sems.at[1]),
+    ]
+    for copy in copies:
+        copy.start()
+    for copy in copies:
+        copy.wait()
     edge_rows(f, s, own, rows)
-
-
-def pack_other(fp, sp, own, message, other, rows):
+    low, high = ([jnp.zeros((16, 128), F32)] * 3 for _ in range(2))
+    edge_lanes(f, s, 0, low, high)
+    for pair in range(3):
+        lows[pair], highs[pair] = low[pair], high[pair]
+
+
+def pack_other(fp, sp, own, lows, highs, message, far, near, corner_far, corner_near, other, rows):
     edge_rows(fp, sp, other, rows)
     message[:, :, 0:24, :] = own[...]
     message[:, :, 24:48, :] = other[...]
-
-
-def pack_y(f, s, fp, sp, message, outer, far, near):
+    low, high = [lows[pair] for pair in range(3)], [highs[pair] for pair in range(3)]
+    edge_lanes(fp, sp, 8, low, high)
+    even = lax.axis_index("gy") % 2 == 0
+    for pair in range(3):
+        one = jnp.where(even, low[pair], high[pair])
+        two = jnp.where(even, high[pair], low[pair])
+        far[pair], near[pair] = one, two
+        corner_far[pair], corner_near[pair] = one[:8], two[:8]
+
+
+def stencil(f, s, fp, sp, got, far, near, corner_far, corner_near, last, a, b, stiff, outer):
     refs = (f, s, fp, sp)
-    a = lax.axis_index("ga")
+    core = lax.axis_index("ga")
+    even = lax.axis_index("gy") % 2 == 0
     row = lax.broadcasted_iota(jnp.int32, (8, 128), 0)
-    beyond = jnp.where(a == 1, row, 7 - row) < 3
-    lane = lax.broadcasted_iota(jnp.int32, (16, 128), 1) // 4
-    lows, highs = jnp.zeros((16, 128), F32), jnp.zeros((16, 128), F32)
+    beyond = jnp.where(core == 1, row, 7 - row) < 3
+    first_lanes = lax.broadcasted_iota(jnp.int32, (16, 128), 1) < 64
     for field in range(6):
         for h in range(2):
             for which in range(2):
                 for d in range(3):
                     at = 24 * which + 8 * d
-                    value = message[field, h, at : at + 8, :]
+                    value = got[field, h, at : at + 8, :]
                     to = 64 * (1 - which)
-                    outer[field, h, pl.ds(to + d, 8, stride=8), :] = value
-                    outer[field, h, pl.ds(to + 7 - d, 8, stride=8), :] = value
-        for slot in range(16):
-            inner, block = rows_of(refs, field, slot, a), rows_of(refs, field, slot, 1 - a)
-            edge = slice(8 * slot, 8 * slot + 8)
-            for h in range(2):
-                kept = block[:, 128 * h : 128 * h + 128]
-                outer[field, h, edge, :] = jnp.where(beyond, outer[field, h, edge, :], kept)
-            base = 64 * (field % 2) + 4 * slot
-            here = lane == base // 4
-            first = jnp.concatenate([inner[:, :128], outer[field, 0, edge, :]], axis=0)
-            last = jnp.concatenate([inner[:, 128:], outer[field, 1, edge, :]], axis=0)
-            lows = jnp.where(here, pltpu.roll(first, base, 1) if base else first, lows)
-            highs = jnp.where(here, pltpu.roll(last, (base + 4) % 128, 1) if base != 124 else last, highs)
-        if field % 2:
-            even = lax.axis_index("gy") % 2 == 0
-            far[field // 2] = jnp.where(even, lows, highs)
-            near[field // 2] = jnp.where(even, highs, lows)
-
-
-def stencil(f, s, fp, sp, outer, far, near, after, last, a, b, stiff):
-    refs = (f, s, fp, sp)
-    core = lax.axis_index("ga")
-    even = lax.axis_index("gy") % 2 == 0
-    first_lanes = lax.broadcasted_iota(jnp.int32, (16, 128), 1) < 64
-    for field in range(6):
+                    outer[h, pl.ds(to + d, 8, stride=8), :] = value
+                    outer[h, pl.ds(to + 7 - d, 8, stride=8), :] = value
+        pair = field // 2
+        above = jnp.where(even, near[pair], far[pair])
+        below = jnp.where(even, far[pair], near[pair])
+        corner_above = jnp.where(even, corner_near[pair], corner_far[pair])
+        corner_below = jnp.where(even, corner_far[pair], corner_near[pair])
         for slot in range(16):
             to = stiff.at[slot] if field == 5 else a.at[field, slot]
             to[0:8, 0:256] = rows_of(refs, field, slot, core)
+            block = rows_of(refs, field, slot, 1 - core)
             for h in range(2):
-                edge = outer[field, h, 8 * slot : 8 * slot + 8, :]
-                to[8:16, 128 * h : 128 * h + 128] = edge
+                lanes = slice(128 * h, 128 * h + 128)
+                edge = outer[h, 8 * slot : 8 * slot + 8, :]
+                to[8:16, lanes] = jnp.where(beyond, edge, block[:, lanes])
             base = 64 * (field % 2) + 4 * slot
-            one, two = near[field // 2], far[field // 2]
-            above, below = jnp.where(even, one, two), jnp.where(even, two, one)
-            above = pltpu.roll(above, 128 - base, 1) if base else above
-            below = pltpu.roll(below, 124 - base, 1) if base != 124 else below
-            to[:, 256:384] = jnp.where(first_lanes, above, below)
-
-    def advance(src, slot, crop):
-        new, east, north, depth = [], [], [], []
-        for field in range(5):
-            mid = src[field, slot]
-            up, down = src[field, (slot + 1) & 15], src[field, (slot + 15) & 15]
-            xp, xm = pltpu.roll(mid, 15, 0), pltpu.roll(mid, 1, 0)
-            yp, ym = pltpu.roll(mid, 383, 1), pltpu.roll(mid, 1, 1)
-            if crop:
-                mid, up, down, xp, xm, yp, ym = (
-                    v[0:8, 0:256] for v in (mid, up, down, xp, xm, yp, ym)
-                )
-            total = 0.1 * mid + 0.12 * xp + 0.18 * xm + 0.17 * yp + 0.13 * ym
-            new.append(total + 0.14 * up + 0.16 * down)
-            east.append(xp - xm if field in (1, 4) else None)
-            north.append(yp - ym if field in (2, 4) else None)
-            depth.append(up - down if field in (3, 4) else None)
-        div = 0.1 * (east[1] + north[2] + depth[3])
-        new[0] = new[0] - div
-        new[1] = new[1] - 0.1 * east[4]
-        new[2] = new[2] - 0.1 * north[4]
-        new[3] = new[3] - 0.1 * depth[4]
-        new[4] = new[4] - (stiff[slot, 0:8, 0:256] if crop else stiff[slot]) * div
-        return new
+            side = jnp.where(first_lanes, turn(above, -base), turn(below, 124 - base))
+            base = 64 * (field % 2) + 4 * (slot ^ 8)
+            corner = jnp.where(
+                first_lanes[:8], turn(corner_above, -base), turn(corner_below, 124 - base)
+            )
+            to[0:8, 256:384] = side[:8]
+            to[8:16, 256:384] = jnp.where(beyond, corner, side[8:])
+
+    def terms(src, field, slot, crop):
+        mid = src[field, slot]
+        up, down = src[field, (slot + 1) & 15], src[field, (slot + 15) & 15]
+        xp, xm = pltpu.roll(mid, 15, 0), pltpu.roll(mid, 1, 0)
+        yp, ym = pltpu.roll(mid, 383, 1), pltpu.roll(mid, 1, 1)
+        if crop:
+            mid, up, down, xp, xm, yp, ym = (v[0:8, 0:256] for v in (mid, up, down, xp, xm, yp, ym))
+        total = 0.1 * mid + 0.12 * xp + 0.18 * xm + 0.17 * yp + 0.13 * ym
+        return total + 0.14 * up + 0.16 * down, xp - xm, yp - ym, up - down
+
+    def advance(src, slot, crop, store):
+        vx, east, _, _ = terms(src, 1, slot, crop)
+        vy, _, north, _ = terms(src, 2, slot, crop)
+        vz, _, _, depth = terms(src, 3, slot, crop)
+        div = 0.1 * (east + north + depth)
+        store(0, terms(src, 0, slot, crop)[0] - div)
+        pressure, east, north, depth = terms(src, 4, slot, crop)
+        store(1, vx - 0.1 * east)
+        store(2, vy - 0.1 * north)
+        store(3, vz - 0.1 * depth)
+        store(4, pressure - (stiff[slot, 0:8, 0:256] if crop else stiff[slot]) * div)
 
     for src, dst in ((a, b), (b, a), (a, None)):
 
         def body(slot, carry, src=src, dst=dst):
-            new = advance(src, slot, dst is None)
-            for field in range(5):
+            def store(field, new):
                 if dst is None:
                     rows = pl.ds(pl.multiple_of(slot * 8, 8), 8)
                     for h in range(2):
-                        last[field, h, rows, :] = new[field][:, 128 * h : 128 * h + 128]
+                        last[field, h, rows, :] = new[:, 128 * h : 128 * h + 128]
                 else:
-                    dst[field, slot] = new[field]
+                    dst[field, slot] = new
+
+            advance(src, slot, dst is None, store)
             return carry
 
         lax.fori_loop(0, 16, body, 0)
@@ -254,7 +281,7 @@
 
 
 def forward(
-    last, weight, bias, yf_far, zf_far, keep, send, out, sums, lifted, modes, yf, zf, sems
+    last, after, weight, bias, yf_far, zf_far, keep, send, out, sums, lifted, modes, yf, zf, sems
 ):
     copies = [
         pltpu.make_async_copy(yf_far.at[lax.axis_index("gy")], yf, sems.at[0]),
@@ -414,45 +441,66 @@
     swap = [(0, 1), (1, 0)]
     fp, sp = lax.ppermute(f, "ga", swap), lax.ppermute(s, "ga", swap)
     rows = pltpu.VMEM((6, 2, 128, 128), F32)
-    edges = ((6, 2, 24, 128), F32)
-    [own] = call(pack_own, [edges], [VMEM] * 2, [rows])(f, s)
-    [message] = call(
-        pack_other, [((6, 2, 48, 128), F32)], [VMEM] * 3, [pltpu.VMEM(*edges), rows]
-    )(fp, sp, own)
-    across = [(2 * i, 2 * ((i - 1) % 8) + 1) for i in range(8)]
-    across += [(2 * i + 1, 2 * ((i + 1) % 8)) for i in range(8)]
-    got = lax.ppermute(message, ("gx", "ga"), across)
+    edges, lanes = ((6, 2, 24, 128), F32), ((3, 16, 128), F32)
+    own, lows, highs = call(
+        pack_own,
+        [edges, lanes, lanes],
+        [HBM] * 2,
+        [
+            rows,
+            pltpu.VMEM((5, 128, 256), F32),
+            pltpu.VMEM((128, 256), F32),
+            pltpu.SemaphoreType.DMA((2,)),
+        ],
+    )(f, s)
+    corners = ((3, 8, 128), F32)
+    message, far, near, corner_far, corner_near = call(
+        pack_other,
+        [((6, 2, 48, 128), F32), lanes, lanes, corners, corners],
+        [VMEM] * 5,
+        [pltpu.VMEM(*edges), rows],
+    )(fp, sp, own, lows, highs)
+    meets = [(2 * i + a, 2 * ((i - 1 + 2 * a) % 8) + 1 - a) for i in range(8) for a in range(2)]
+    far_pairs = [(j, (j - 1 + 2 * (j % 2)) % 8) for j in range(8)]
+    near_pairs = [(j, j + 1 - 2 * (j % 2)) for j in range(8)]
+
+    def diagonal(pairs):
+        return [
+            (16 * (u // 2) + 2 * j + u % 2, 16 * (v // 2) + 2 * k + v % 2)
+            for u, v in meets
+            for j, k in pairs
+        ]
+
+    got = lax.ppermute(message, ("gx", "ga"), meets)
+    far = lax.ppermute(far, "gy", far_pairs)
+    got_far = lax.ppermute(corner_far, everyone, diagonal(far_pairs))
+    near = lax.ppermute(near, "gy", near_pairs)
+    got_near = lax.ppermute(corner_near, everyone, diagonal(near_pairs))
 
     [turned] = call(
         turn_weights,
         [((64, 32, 128), BF16)],
         [VMEM, anywhere],
         [pltpu.VMEM((64, 32, 128), F32)],
-        size=2 * 10**7,
-    )(spectral_weight.reshape(2048, 128), message)
+    )(spectral_weight.reshape(2048, 128), corner_near)
     weights = exchange(turned, ("gx", "gy"))
 
-    message = ((3, 16, 128), F32)
-    outer, far, near = call(
-        pack_y, [((6, 2, 128, 128), F32), message, message], [VMEM] * 5, flops=10**12
-    )(f, s, fp, sp, got)
-    far = lax.ppermute(far, "gy", [(j, (j - 1 + 2 * (j % 2)) % 8) for j in range(8)])
-    near = lax.ppermute(near, "gy", [(j, j + 1 - 2 * (j % 2)) for j in range(8)])
     [last] = call(
         stencil,
         [((5, 2, 128, 128), F32)],
-        [VMEM] * 7 + [anywhere],
+        [VMEM] * 9,
         [
             pltpu.VMEM((5, 16, 16, 384), F32),
             pltpu.VMEM((5, 16, 16, 384), F32),
             pltpu.VMEM((16, 16, 384), F32),
+            pltpu.VMEM((2, 128, 128), F32),
         ],
         flops=10**12,
-    )(f, s, fp, sp, outer, far, near, weights)
+    )(f, s, fp, sp, got, far, near, got_far, got_near)
     keep, send, modes = call(
         forward,
         [((160, 128), F32), ((160, 128), F32), ((64, 16, 128), F32)],
-        [VMEM, SMEM, SMEM, anywhere, anywhere],
+        [VMEM, anywhere, SMEM, SMEM, HBM, HBM],
         [
             pltpu.VMEM((320, 256), F32),
             pltpu.VMEM((4, 512, 128), BF16),
@@ -461,7 +509,7 @@
             pltpu.VMEM((256, 256), BF16),
             pltpu.SemaphoreType.DMA((2,)),
         ],
-    )(last, lift_weight, lift_bias, table["yf"], table["zf"])
+    )(last, weights, lift_weight, lift_bias, table["yf"], table["zf"])
     modes = exchange(modes.reshape(128, 8, 128), everyone)
     [direct] = call(
         pointwise,
@@ -478,7 +526,7 @@
     [out] = call(
         finish,
         [((8, 32, 8, 128), BF16)],
-        [VMEM, VMEM, anywhere, anywhere],
+        [VMEM, VMEM, HBM, HBM],
         [
             pltpu.VMEM((2048, 128), F32),
             pltpu.VMEM((2048, 128), F32),

time: 84.4 us -> 86.8 us (1.028)
  starting transfers between devices: 25.4 us -> 30.6 us
  waiting for transfers between devices: 16 us -> 12.4 us
    ppermute x3 -> x5, waiting for transfers between devices: 5.71 us -> 0.01 us  [the longest x1 0.01 us: shards(): got_far = lax.ppermute(corner_far, everyone, diagonal(far_pairs))]
    ppermute x3 -> x5, starting transfers between devices: 6.31 us -> 9.34 us  [the longest x1 5.92 us: shards(): far = lax.ppermute(far, 'gy', far_pairs)]
    all_to_all x2, starting transfers between devices: 16.3 us -> 18.7 us  [exchange(): return lax.all_to_all(value, axis, split_axis=0, concat_axis=0, tiled=True)]
    all_to_all x2, waiting for transfers between devices: 9.33 us -> 11.5 us  [exchange(): return lax.all_to_all(value, axis, split_axis=0, concat_axis=0, tiled=True)]
    pallas_call x5 -> x4, Pallas kernels: 10.3 us -> 11 us  [the longest x1 7.16 us: shards(): call(stencil, [((5, 2, 128, 128), F32)], [VMEM] * 9, [pltpu.VMEM((5, 16,...]
  transfers between devices with their start and end apart: 8 -> 10, of which waited for: 4 -> 3; matrix products, arithmetic and copies ran while one was open for 0% -> 0% of each run, Pallas kernels for 6% -> 15%
where the time goes in v8:
time: 86.8 us; the launch traced here: 86.4 us
  starting transfers between devices  30.6 us (35%)
  Pallas kernels  22.6 us (26%)
  blocking collectives  17.9 us (21%)
  waiting for transfers between devices  12.4 us (14%)
  local copies, waits for them, and re-layouts  2.71 us (3%)
    all_to_all x2, starting transfers between devices, exchange(): return lax.all_to_all(value, axis, split_axis=0, concat_axis=0, tiled=True)  18.7 us
    all_to_all x1, blocking collectives, exchange(): return lax.all_to_all(value, axis, split_axis=0, concat_axis=0, tiled=True)  17.9 us
    all_to_all x2, waiting for transfers between devices, exchange(): return lax.all_to_all(value, axis, split_axis=0, concat_axis=0, tiled=True)  11.5 us
    pallas_call x1, Pallas kernels, shards(): call(stencil, [((5, 2, 128, 128), F32)], [VMEM] * 9, [pltpu.VMEM((5, 16,...  7.16 us
    ppermute x1, starting transfers between devices, shards(): far = lax.ppermute(far, 'gy', far_pairs)  5.92 us
    pallas_call x1, Pallas kernels, shards(): call(forward, [((160, 128), F32), ((160, 128), F32), ((64, 16, 128), F32)...  4.28 us
    pallas_call x1, Pallas kernels, shards(): call(pointwise, [((8, 256, 128), F32)], [VMEM, VMEM, SMEM, SMEM, VMEM, VM...  3.18 us
    unnamed x30, local copies, waits for them, and re-layouts  2.71 us
  transfers between devices with their start and end apart: 10, of which 3 were waited for; matrix products, arithmetic and copies ran while one was open for 0% of the time, Pallas kernels for 15%

profile of v8, /device:TPU:1, one launch (start us, length us, event | category | flops | bytes accessed | tf_op | source)
XLA Modules:
  0.0 86.4 jit_solution(9256618788967650830)
XLA Ops:
  0.0 1.4 %collective-permute-start = (f32[5,128,256]{2,1,0:T(8,128)}, f32[5,128,256]{2,1,0:T(8,128)S(1)}, u32[]{:S(2)}, u32[]{:S(2)}) collective-permute-start(f32[5,128,256]{2,1,0:T(8,128)} %bitcast.12), channel_id=1, source_target_pairs={{0,1},{1,0},{2,3},{3,2},{4,5},{5,4},{6,7},{7,6},{8,9},{9,8},{10,11... | collective-permute-start | bytes 1966088 | tf_op jit(solution)/shard_map/ppermute | solution.py:442
  1.4 0.0 collective-permute-start.1
  1.4 1.1 %copy-done.1 = f32[5,8,16,256]{3,2,1,0:T(8,128)S(1)} copy-done((f32[5,8,16,256]{3,2,1,0:T(8,128)S(1)}, f32[5,8,16,256]{3,2,1,0:T(8,128)}, u32[]{:S(2)}) %copy-start.1) | copy-done | bytes 655384
  2.5 0.9 %copy-done.8 = f32[8,16,256]{2,1,0:T(8,128)S(1)} copy-done((f32[8,16,256]{2,1,0:T(8,128)S(1)}, f32[8,16,256]{2,1,0:T(8,128)}, u32[]{:S(2)}) %copy-start.8) | copy-done | bytes 131096
  3.4 0.8 shard_map.127
  4.2 0.0 collective-permute-done.1.sp
  4.2 0.0 collective-permute-done.fp
  4.2 0.4 shard_map.128
  4.6 1.8 %collective-permute-start.2 = (f32[6,2,48,128]{3,2,1,0:T(8,128)S(1)}, f32[6,2,48,128]{3,2,1,0:T(8,128)S(1)}, u32[]{:S(2)}, u32[]{:S(2)}) collective-permute-start(f32[6,2,48,128]{3,2,1,0:T(8,128)S(1)} %get-tuple-element.19), channel_id=1, source_target_pairs={{0,113},{1,16},{16,1},{17,32},{32,17},{33,48},{48,33},{49,64},{64,... | collective-permute-start | bytes 884744 | tf_op jit(solution)/shard_map/ppermute | solution.py:474
  6.4 5.9 %collective-permute-start.3 = (f32[3,16,128]{2,1,0:T(8,128)S(1)}, f32[3,16,128]{2,1,0:T(8,128)S(1)}, u32[]{:S(2)}, u32[]{:S(2)}) collective-permute-start(f32[3,16,128]{2,1,0:T(8,128)S(1)} %get-tuple-element.20), channel_id=1, source_target_pairs={{0,14},{2,4},{4,2},{6,8},{8,6},{10,12},{12,10},{14,0},{1,15},{3,5}... | collective-permute-start | bytes 73736 | tf_op jit(solution)/shard_map/ppermute | solution.py:475
  12.3 0.0 collective-permute-start.4
  12.3 0.0 collective-permute-start.5
  12.3 1.6 %collective-permute-start.6 = (f32[3,8,128]{2,1,0:T(8,128)S(1)}, f32[3,8,128]{2,1,0:T(8,128)S(1)}, u32[]{:S(2)}, u32[]{:S(2)}) collective-permute-start(f32[3,8,128]{2,1,0:T(8,128)S(1)} %get-tuple-element.23.after), channel_id=1, source_target_pairs={{0,115},{2,113},{4,119},{6,117},{8,123},{10,121},{12,127},{14,125}... | collective-permute-start | bytes 36872 | tf_op jit(solution)/shard_map/ppermute | solution.py:478
  14.0 0.0 copy-done
  14.0 1.6 %shard_map.130 = bf16[64,32,128]{2,1,0:T(8,128)(2,1)} custom-call(f32[2048,128]{1,0:T(8,128)S(1)} %bitcast.11, f32[3,8,128]{2,1,0:T(8,128)S(1)} %get-tuple-element.23.after), custom_call_target="tpu_custom_call" | custom-call | flops 10000000 | bytes 1048576 | tf_op jit(solution)/shard_map/pallas_call | solution.py:480
  15.6 10.8 %all-to-all-start = ((bf16[64,32,128]{2,1,0:T(8,128)(2,1)}), bf16[64,32,128]{2,1,0:T(8,128)(2,1)}, u32[]{:S(2)}, u32[]{:S(2)}) async-start(bf16[64,32,128]{2,1,0:T(8,128)(2,1)} %shard_map.130), calls=%async_computation | async-start | bytes 1048576 | tf_op jit(solution)/shard_map/all_to_all | solution.py:436
  26.4 0.0 collective-permute-done.5.corner_far
  26.4 0.0 collective-permute-done.6.corner_near
  26.4 0.0 collective-permute-done.3.far
  26.4 0.0 collective-permute-done.4.near
  26.4 0.0 collective-permute-done.2.got
  26.4 0.0 copy-done.2
  26.4 0.0 copy-done.9
  26.5 0.0 copy-start.4
  26.5 0.0 copy-start.10
  26.5 0.0 copy-start.11
  26.5 0.0 copy-start.13
  26.5 7.2 %shard_map.129.last = f32[5,2,128,128]{3,2,1,0:T(8,128)S(1)} custom-call(f32[5,128,256]{2,1,0:T(8,128)S(1)} %bitcast.14, f32[128,256]{1,0:T(8,128)S(1)} %bitcast.17, f32[5,128,256]{2,1,0:T(8,128)S(1)} %collective-permute-done.fp, f32[128,256]{1,0:T(8,128)S(1)} %collective-permute-done.1.sp, f32[6,2,48,128]{3,2,1,0:T(8,128)S(1)} %collective-permute-done.2.got, ...), custom_call_target="tpu_custom_call" | custom-call | flops 999999995904 | bytes 1048576 | tf_op jit(solution)/shard_map/pallas_call | solution.py:488
  33.7 3.5 %all-to-all-done.after.weights = bf16[64,32,128]{2,1,0:T(8,128)(2,1)} async-done(((bf16[64,32,128]{2,1,0:T(8,128)(2,1)}), bf16[64,32,128]{2,1,0:T(8,128)(2,1)}, u32[]{:S(2)}, u32[]{:S(2)}) %all-to-all-start) | async-done | bytes 524320 | tf_op jit(solution)/shard_map/all_to_all | solution.py:436
  37.2 0.0 copy-done.4
  37.2 0.0 copy-done.10
  37.2 0.0 copy-done.11
  37.2 0.0 copy-done.13
  37.2 4.3 %shard_map.131 = (f32[160,128]{1,0:T(8,128)S(1)}, f32[160,128]{1,0:T(8,128)S(1)}, f32[64,16,128]{2,1,0:T(8,128)}) custom-call(f32[5,2,128,128]{3,2,1,0:T(8,128)S(1)} %shard_map.129.last, bf16[64,32,128]{2,1,0:T(8,128)(2,1)} %all-to-all-done.after.weights, f32[5,32]{1,0:T(8,128)S(1)} %copy-done.11, f32[32]{0:T(128)S(1)} %copy-done.13, ...), custom_call_target="tpu_custom_call" | custom-call | flops 10000000 | bytes 1048576 | tf_op jit(solution)/shard_map/pallas_call | solution.py:500
  41.5 0.0 copy-start.12
  41.5 7.9 %all-to-all-start.1 = ((f32[128,8,128]{2,1,0:T(8,128)}), f32[128,8,128]{2,1,0:T(8,128)S(1)}, u32[]{:S(2)}, u32[]{:S(2)}) async-start(f32[128,8,128]{2,1,0:T(8,128)} %bitcast.3), calls=%async_computation.1 | async-start | bytes 1048576 | tf_op jit(solution)/shard_map/all_to_all | solution.py:436
  49.4 1.1 %collective-permute-start.7 = (f32[160,128]{1,0:T(8,128)S(1)}, f32[160,128]{1,0:T(8,128)S(1)}, u32[]{:S(2)}, u32[]{:S(2)}) collective-permute-start(f32[160,128]{1,0:T(8,128)S(1)} %get-tuple-element.26), channel_id=1, source_target_pairs={{0,1},{1,0},{2,3},{3,2},{4,5},{5,4},{6,7},{7,6},{8,9},{9,8},{10,11... | collective-permute-start | bytes 245768 | tf_op jit(solution)/shard_map/ppermute | solution.py:520
  50.6 0.9 %collective-permute-done.7.got = f32[160,128]{1,0:T(8,128)S(1)} collective-permute-done((f32[160,128]{1,0:T(8,128)S(1)}, f32[160,128]{1,0:T(8,128)S(1)}, u32[]{:S(2)}, u32[]{:S(2)}) %collective-permute-start.7) | collective-permute-done | bytes 81952 | tf_op jit(solution)/shard_map/ppermute | solution.py:520
  51.5 0.7 copy-done.14
  52.1 3.2 %shard_map.132.after.direct = f32[8,256,128]{2,1,0:T(8,128)S(1)} custom-call(f32[160,128]{1,0:T(8,128)S(1)} %get-tuple-element.25.keep, f32[160,128]{1,0:T(8,128)S(1)} %collective-permute-done.7.got, f32[5,32]{1,0:T(8,128)S(1)} %copy-done.11, f32[32]{0:T(128)S(1)} %copy-done.13, bf16[32,32]{1,0:T(8,128)(2,1)S(1)} %copy-done.12, f32[1,32]{1,0:T(1,128)S(1)} %bitcast.18), custom_call_target="tpu_custom_call" | custom-call | flops 300000000 | bytes 1048576 | tf_op jit(solution)/shard_map/pallas_call | solution.py:514
  55.3 7.9 %all-to-all-done.1 = f32[128,8,128]{2,1,0:T(8,128)S(1)} async-done(((f32[128,8,128]{2,1,0:T(8,128)}), f32[128,8,128]{2,1,0:T(8,128)S(1)}, u32[]{:S(2)}, u32[]{:S(2)}) %all-to-all-start.1) | async-done | bytes 524320 | tf_op jit(solution)/shard_map/all_to_all | solution.py:436
  63.3 0.0 copy-done.5
  63.3 2.5 %shard_map.133 = bf16[8,8,2,16,128]{4,3,2,1,0:T(8,128)(2,1)S(1)} custom-call(f32[8,8,16,128]{3,2,1,0:T(8,128)S(1)} %bitcast.8, bf16[64,32,128]{2,1,0:T(8,128)(2,1)} %all-to-all-done.after.weights, bf16[4,256,128]{2,1,0:T(8,128)(2,1)S(1)} %copy-done.5, bf16[2,128,256]{2,1,0:T(8,128)(2,1)S(1)} %copy-done.7, f32[8,256,128]{2,1,0:T(8,128)S(1)} %shard_map.132.after.direct), custom_call_target="tpu_custom_call" | custom-call | flops 10000000 | bytes 1048576 | tf_op jit(solution)/shard_map/pallas_call | solution.py:522
  65.8 0.0 copy-start.3
  65.8 0.0 copy-start.6
  65.9 17.9 %all_to_all.15 = bf16[128,16,128]{2,1,0:T(8,128)(2,1)S(1)} all-to-all(bf16[128,16,128]{2,1,0:T(8,128)(2,1)S(1)} %bitcast.9), channel_id=1, replica_groups=mesh['gx'=8,'gy'=8,'ga'=2] {'gx','gy','ga'}, dimensions={0} | all-to-all | bytes 1048576 | tf_op jit(solution)/shard_map/all_to_all | solution.py:436
  83.7 0.0 copy-done.6
  83.7 2.7 %shard_map.134 = bf16[8,32,8,128]{3,2,1,0:T(8,128)(2,1)} custom-call(bf16[2048,128]{1,0:T(8,128)(2,1)S(1)} %bitcast.10, f32[8,256,128]{2,1,0:T(8,128)S(1)} %shard_map.132.after.direct, bf16[8,128,256]{2,1,0:T(8,128)(2,1)S(1)} %copy-done.3, bf16[512,256]{1,0:T(8,128)(2,1)S(1)} %copy-done.6), custom_call_target="tpu_custom_call" | custom-call | flops 10000000 | bytes 1048576 | tf_op jit(solution)/shard_map/pallas_call | solution.py:526
  (11 shorter events, 0.0 us)
Async XLA Ops:
  0.0 14.0 %copy-start = (f32[4,4,32,4,128]{4,3,2,1,0:T(4,128)S(1)}, f32[4,4,32,4,128]{4,3,2,1,0:T(4,128)}, u32[]{:S(2)}) copy-start(f32[4,4,32,4,128]{4,3,2,1,0:T(4,128)} %param.18) | copy-start | bytes 3145732
  0.0 4.2 %collective-permute-start = (f32[5,128,256]{2,1,0:T(8,128)}, f32[5,128,256]{2,1,0:T(8,128)S(1)}, u32[]{:S(2)}, u32[]{:S(2)}) collective-permute-start(f32[5,128,256]{2,1,0:T(8,128)} %bitcast.12), channel_id=1, source_target_pairs={{0,1},{1,0},{2,3},{3,2},{4,5},{5,4},{6,7},{7,6},{8,9},{9,8},{10,11... | collective-permute-start | bytes 1966088 | tf_op jit(solution)/shard_map/ppermute | solution.py:442
  1.4 2.8 %collective-permute-start.1 = (f32[128,256]{1,0:T(8,128)}, f32[128,256]{1,0:T(8,128)S(1)}, u32[]{:S(2)}, u32[]{:S(2)}) collective-permute-start(f32[128,256]{1,0:T(8,128)} %bitcast.15), channel_id=1, source_target_pairs={{0,1},{1,0},{2,3},{3,2},{4,5},{5,4},{6,7},{7,6},{8,9},{9,8},{10,11... | collective-permute-start | bytes 393224 | tf_op jit(solution)/shard_map/ppermute | solution.py:442
  1.4 1.1 %copy-start.1 = (f32[5,8,16,256]{3,2,1,0:T(8,128)S(1)}, f32[5,8,16,256]{3,2,1,0:T(8,128)}, u32[]{:S(2)}) copy-start(f32[5,8,16,256]{3,2,1,0:T(8,128)} %param.13) | copy-start | bytes 1966084
  2.5 0.9 %copy-start.8 = (f32[8,16,256]{2,1,0:T(8,128)S(1)}, f32[8,16,256]{2,1,0:T(8,128)}, u32[]{:S(2)}) copy-start(f32[8,16,256]{2,1,0:T(8,128)} %param.14) | copy-start | bytes 393220
  4.6 21.8 %collective-permute-start.2 = (f32[6,2,48,128]{3,2,1,0:T(8,128)S(1)}, f32[6,2,48,128]{3,2,1,0:T(8,128)S(1)}, u32[]{:S(2)}, u32[]{:S(2)}) collective-permute-start(f32[6,2,48,128]{3,2,1,0:T(8,128)S(1)} %get-tuple-element.19), channel_id=1, source_target_pairs={{0,113},{1,16},{16,1},{17,32},{32,17},{33,48},{48,33},{49,64},{64,... | collective-permute-start | bytes 884744 | tf_op jit(solution)/shard_map/ppermute | solution.py:474
  6.4 20.0 %collective-permute-start.3 = (f32[3,16,128]{2,1,0:T(8,128)S(1)}, f32[3,16,128]{2,1,0:T(8,128)S(1)}, u32[]{:S(2)}, u32[]{:S(2)}) collective-permute-start(f32[3,16,128]{2,1,0:T(8,128)S(1)} %get-tuple-element.20), channel_id=1, source_target_pairs={{0,14},{2,4},{4,2},{6,8},{8,6},{10,12},{12,10},{14,0},{1,15},{3,5}... | collective-permute-start | bytes 73736 | tf_op jit(solution)/shard_map/ppermute | solution.py:475
  12.3 14.1 %collective-permute-start.4 = (f32[3,16,128]{2,1,0:T(8,128)S(1)}, f32[3,16,128]{2,1,0:T(8,128)S(1)}, u32[]{:S(2)}, u32[]{:S(2)}) collective-permute-start(f32[3,16,128]{2,1,0:T(8,128)S(1)} %get-tuple-element.21), channel_id=1, source_target_pairs={{0,2},{2,0},{4,6},{6,4},{8,10},{10,8},{12,14},{14,12},{1,3},{3,1},... | collective-permute-start | bytes 73736 | tf_op jit(solution)/shard_map/ppermute | solution.py:477
  12.3 14.1 %collective-permute-start.5 = (f32[3,8,128]{2,1,0:T(8,128)S(1)}, f32[3,8,128]{2,1,0:T(8,128)S(1)}, u32[]{:S(2)}, u32[]{:S(2)}) collective-permute-start(f32[3,8,128]{2,1,0:T(8,128)S(1)} %get-tuple-element.22), channel_id=1, source_target_pairs={{0,127},{2,117},{4,115},{6,121},{8,119},{10,125},{12,123},{14,113}... | collective-permute-start | bytes 36872 | tf_op jit(solution)/shard_map/ppermute | solution.py:476
  12.3 14.1 %collective-permute-start.6 = (f32[3,8,128]{2,1,0:T(8,128)S(1)}, f32[3,8,128]{2,1,0:T(8,128)S(1)}, u32[]{:S(2)}, u32[]{:S(2)}) collective-permute-start(f32[3,8,128]{2,1,0:T(8,128)S(1)} %get-tuple-element.23.after), channel_id=1, source_target_pairs={{0,115},{2,113},{4,119},{6,117},{8,123},{10,121},{12,127},{14,125}... | collective-permute-start | bytes 36872 | tf_op jit(solution)/shard_map/ppermute | solution.py:478
  15.6 10.9 %copy-start.2 = (f32[5,8,16,256]{3,2,1,0:T(8,128)S(1)}, f32[5,8,16,256]{3,2,1,0:T(8,128)}, u32[]{:S(2)}) copy-start(f32[5,8,16,256]{3,2,1,0:T(8,128)} %param.13) | copy-start | bytes 1966084
  15.6 10.9 %copy-start.9 = (f32[8,16,256]{2,1,0:T(8,128)S(1)}, f32[8,16,256]{2,1,0:T(8,128)}, u32[]{:S(2)}) copy-start(f32[8,16,256]{2,1,0:T(8,128)} %param.14) | copy-start | bytes 393220
  15.6 21.6 %all-to-all-start = ((bf16[64,32,128]{2,1,0:T(8,128)(2,1)}), bf16[64,32,128]{2,1,0:T(8,128)(2,1)}, u32[]{:S(2)}, u32[]{:S(2)}) async-start(bf16[64,32,128]{2,1,0:T(8,128)(2,1)} %shard_map.130), calls=%async_computation | async-start | bytes 1048576 | tf_op jit(solution)/shard_map/all_to_all | solution.py:436
  26.5 10.7 %copy-start.4 = (bf16[8,256,128]{2,1,0:T(8,128)(2,1)S(1)}, bf16[8,256,128]{2,1,0:T(8,128)(2,1)}, u32[]{:S(2)}) copy-start(bf16[8,256,128]{2,1,0:T(8,128)(2,1)} %constant.12.clone.yf_far) | copy-start | bytes 1572868
  26.5 10.7 %copy-start.10 = (bf16[256,256]{1,0:T(8,128)(2,1)S(1)}, bf16[256,256]{1,0:T(8,128)(2,1)}, u32[]{:S(2)}) copy-start(bf16[256,256]{1,0:T(8,128)(2,1)} %constant.14.clone.zf_far) | copy-start | bytes 393220
  26.5 10.7 %copy-start.11 = (f32[5,32]{1,0:T(8,128)S(1)}, f32[5,32]{1,0:T(8,128)}, u32[]{:S(2)}) copy-start(f32[5,32]{1,0:T(8,128)} %weight.3) | copy-start | bytes 1924
  26.5 10.7 %copy-start.13 = (f32[32]{0:T(128)S(1)}, f32[32]{0:T(128)}, u32[]{:S(2)}) copy-start(f32[32]{0:T(128)} %bias.3) | copy-start | bytes 388
  41.5 10.0 %copy-start.12 = (bf16[32,32]{1,0:T(8,128)(2,1)S(1)}, bf16[32,32]{1,0:T(8,128)(2,1)}, u32[]{:S(2)}) copy-start(bf16[32,32]{1,0:T(8,128)(2,1)} %mix.1) | copy-start | bytes 6148
  41.5 21.7 %all-to-all-start.1 = ((f32[128,8,128]{2,1,0:T(8,128)}), f32[128,8,128]{2,1,0:T(8,128)S(1)}, u32[]{:S(2)}, u32[]{:S(2)}) async-start(f32[128,8,128]{2,1,0:T(8,128)} %bitcast.3), calls=%async_computation.1 | async-start | bytes 1048576 | tf_op jit(solution)/shard_map/all_to_all | solution.py:436
  49.4 2.1 %collective-permute-start.7 = (f32[160,128]{1,0:T(8,128)S(1)}, f32[160,128]{1,0:T(8,128)S(1)}, u32[]{:S(2)}, u32[]{:S(2)}) collective-permute-start(f32[160,128]{1,0:T(8,128)S(1)} %get-tuple-element.26), channel_id=1, source_target_pairs={{0,1},{1,0},{2,3},{3,2},{4,5},{5,4},{6,7},{7,6},{8,9},{9,8},{10,11... | collective-permute-start | bytes 245768 | tf_op jit(solution)/shard_map/ppermute | solution.py:520
  51.5 0.7 copy-start.14
  52.1 11.1 %copy-start.5 = (bf16[4,256,128]{2,1,0:T(8,128)(2,1)S(1)}, bf16[4,256,128]{2,1,0:T(8,128)(2,1)}, u32[]{:S(2)}) copy-start(bf16[4,256,128]{2,1,0:T(8,128)(2,1)} %constant.16.clone.xf) | copy-start | bytes 786436
  52.1 11.1 %copy-start.7 = (bf16[2,128,256]{2,1,0:T(8,128)(2,1)S(1)}, bf16[2,128,256]{2,1,0:T(8,128)(2,1)}, u32[]{:S(2)}) copy-start(bf16[2,128,256]{2,1,0:T(8,128)(2,1)} %constant.17.clone.xi) | copy-start | bytes 393220
  65.8 17.9 %copy-start.3 = (bf16[8,128,256]{2,1,0:T(8,128)(2,1)S(1)}, bf16[8,128,256]{2,1,0:T(8,128)(2,1)}, u32[]{:S(2)}) copy-start(bf16[8,128,256]{2,1,0:T(8,128)(2,1)} %constant.13.clone.yi_far) | copy-start | bytes 1572868
  65.8 17.9 %copy-start.6 = (bf16[512,256]{1,0:T(8,128)(2,1)S(1)}, bf16[512,256]{1,0:T(8,128)(2,1)}, u32[]{:S(2)}) copy-start(bf16[512,256]{1,0:T(8,128)(2,1)} %constant.15.clone.zi_far) | copy-start | bytes 786436

commit v9 on v7

--- a/solution.py
+++ b/solution.py
@@ -64,12 +64,13 @@
             real, imag = sign * cr[:, :, :, a], sign * sr[:, :, :, a]
             xf[k, 0, :, k, :, :, a, :, 0], xf[k, 0, :, k, :, :, a, :, 1] = real, -imag
             xf[k, 1, :, k, :, :, a, :, 0], xf[k, 1, :, k, :, :, a, :, 1] = imag, real
-    out["xf"] = xf.reshape(4, 256, 128).astype(np.float32).astype(jnp.bfloat16)
+    xf = xf.reshape(4, 256, 128).transpose(1, 0, 2).reshape(256, 512)
+    out["xf"] = xf.astype(np.float32).astype(jnp.bfloat16)
     ic, is_ = (cx / 8.0).T.reshape(GX, 8, 1, 4), (sx / 8.0).T.reshape(GX, 8, 1, 4)
     xi = np.zeros((2, GX, 2, 8, 4, 4))
     xi[0, :, 0], xi[0, :, 1] = ic, -is_
     xi[1, :, 0], xi[1, :, 1] = is_, ic
-    out["xi"] = np.stack(split(xi.reshape(128, 256)))
+    out["xi"] = np.concatenate(split(xi.reshape(128, 256)))
     return out
 
 
@@ -131,7 +132,7 @@
     message[:, :, 24:48, :] = other[...]
 
 
-def pack_y(f, s, fp, sp, message, outer, far, near):
+def pack_y(f, s, fp, sp, message, after, far, near, outer):
     refs = (f, s, fp, sp)
     a = lax.axis_index("ga")
     row = lax.broadcasted_iota(jnp.int32, (8, 128), 0)
@@ -165,63 +166,74 @@
             near[field // 2] = jnp.where(even, highs, lows)
 
 
-def stencil(f, s, fp, sp, outer, far, near, after, last, a, b, stiff):
+def stencil(f, s, fp, sp, got, far, near, last, a, b, stiff, outer):
     refs = (f, s, fp, sp)
     core = lax.axis_index("ga")
     even = lax.axis_index("gy") % 2 == 0
     first_lanes = lax.broadcasted_iota(jnp.int32, (16, 128), 1) < 64
+    row = lax.broadcasted_iota(jnp.int32, (8, 128), 0)
+    beyond = jnp.where(core == 1, row, 7 - row) < 3
     for field in range(6):
+        for h in range(2):
+            for which in range(2):
+                for d in range(3):
+                    at = 24 * which + 8 * d
+                    value = got[field, h, at : at + 8, :]
+                    to = 64 * (1 - which)
+                    outer[h, pl.ds(to + d, 8, stride=8), :] = value
+                    outer[h, pl.ds(to + 7 - d, 8, stride=8), :] = value
+        one, two = near[field // 2], far[field // 2]
+        above, below = jnp.where(even, one, two), jnp.where(even, two, one)
         for slot in range(16):
             to = stiff.at[slot] if field == 5 else a.at[field, slot]
             to[0:8, 0:256] = rows_of(refs, field, slot, core)
+            block = rows_of(refs, field, slot, 1 - core)
             for h in range(2):
-                edge = outer[field, h, 8 * slot : 8 * slot + 8, :]
-                to[8:16, 128 * h : 128 * h + 128] = edge
+                lanes = slice(128 * h, 128 * h + 128)
+                edge = outer[h, 8 * slot : 8 * slot + 8, :]
+                to[8:16, lanes] = jnp.where(beyond, edge, block[:, lanes])
             base = 64 * (field % 2) + 4 * slot
-            one, two = near[field // 2], far[field // 2]
-            above, below = jnp.where(even, one, two), jnp.where(even, two, one)
-            above = pltpu.roll(above, 128 - base, 1) if base else above
-            below = pltpu.roll(below, 124 - base, 1) if base != 124 else below
-            to[:, 256:384] = jnp.where(first_lanes, above, below)
-
-    def advance(src, slot, crop):
-        new, east, north, depth = [], [], [], []
-        for field in range(5):
-            mid = src[field, slot]
-            up, down = src[field, (slot + 1) & 15], src[field, (slot + 15) & 15]
-            xp, xm = pltpu.roll(mid, 15, 0), pltpu.roll(mid, 1, 0)
-            yp, ym = pltpu.roll(mid, 383, 1), pltpu.roll(mid, 1, 1)
-            if crop:
-                mid, up, down, xp, xm, yp, ym = (
-                    v[0:8, 0:256] for v in (mid, up, down, xp, xm, yp, ym)
-                )
-            total = 0.1 * mid + 0.12 * xp + 0.18 * xm + 0.17 * yp + 0.13 * ym
-            new.append(total + 0.14 * up + 0.16 * down)
-            east.append(xp - xm if field in (1, 4) else None)
-            north.append(yp - ym if field in (2, 4) else None)
-            depth.append(up - down if field in (3, 4) else None)
-        div = 0.1 * (east[1] + north[2] + depth[3])
-        new[0] = new[0] - div
-        new[1] = new[1] - 0.1 * east[4]
-        new[2] = new[2] - 0.1 * north[4]
-        new[3] = new[3] - 0.1 * depth[4]
-        new[4] = new[4] - (stiff[slot, 0:8, 0:256] if crop else stiff[slot]) * div
-        return new
+            up = pltpu.roll(above, 128 - base, 1) if base else above
+            down = pltpu.roll(below, 124 - base, 1) if base != 124 else below
+            to[:, 256:384] = jnp.where(first_lanes, up, down)
+
+    def terms(src, field, slot, crop):
+        mid = src[field, slot]
+        up, down = src[field, (slot + 1) & 15], src[field, (slot + 15) & 15]
+        xp, xm = pltpu.roll(mid, 15, 0), pltpu.roll(mid, 1, 0)
+        yp, ym = pltpu.roll(mid, 383, 1), pltpu.roll(mid, 1, 1)
+        if crop:
+            mid, up, down, xp, xm, yp, ym = (v[0:8, 0:256] for v in (mid, up, down, xp, xm, yp, ym))
+        total = 0.1 * mid + 0.12 * xp + 0.18 * xm + 0.17 * yp + 0.13 * ym
+        return total + 0.14 * up + 0.16 * down, xp - xm, yp - ym, up - down
+
+    def advance(src, slot, crop, store):
+        vx, east, _, _ = terms(src, 1, slot, crop)
+        vy, _, north, _ = terms(src, 2, slot, crop)
+        vz, _, _, depth = terms(src, 3, slot, crop)
+        div = 0.1 * (east + north + depth)
+        store(0, terms(src, 0, slot, crop)[0] - div)
+        pressure, east, north, depth = terms(src, 4, slot, crop)
+        store(1, vx - 0.1 * east)
+        store(2, vy - 0.1 * north)
+        store(3, vz - 0.1 * depth)
+        store(4, pressure - (stiff[slot, 0:8, 0:256] if crop else stiff[slot]) * div)
 
     for src, dst in ((a, b), (b, a), (a, None)):
 
         def body(slot, carry, src=src, dst=dst):
-            new = advance(src, slot, dst is None)
-            for field in range(5):
+            def store(field, new):
                 if dst is None:
                     rows = pl.ds(pl.multiple_of(slot * 8, 8), 8)
                     for h in range(2):
-                        last[field, h, rows, :] = new[field][:, 128 * h : 128 * h + 128]
+                        last[field, h, rows, :] = new[:, 128 * h : 128 * h + 128]
                 else:
-                    dst[field, slot] = new[field]
+                    dst[field, slot] = new
+
+            advance(src, slot, dst is None, store)
             return carry
 
-        lax.fori_loop(0, 16, body, 0)
+        lax.fori_loop(0, 16, body, 0, unroll=True)
 
 
 def lift_rows(values, weight, bias):
@@ -254,7 +266,7 @@
 
 
 def forward(
-    last, weight, bias, yf_far, zf_far, keep, send, out, sums, lifted, modes, yf, zf, sems
+    last, after, weight, bias, yf_far, zf_far, keep, send, out, sums, lifted, modes, yf, zf, sems
 ):
     copies = [
         pltpu.make_async_copy(yf_far.at[lax.axis_index("gy")], yf, sems.at[0]),
@@ -306,34 +318,43 @@
                 moved = pltpu.roll(parts[group], (32 * (group - part)) % 128, 1)
                 total = jnp.where(lane == group, moved, total)
         for x in range(4):
-            out[:, 8 * (part // 2) + 2 * x + part % 2, :] = total[64 * x : 64 * x + 64]
+            rows = pl.ds(8 * (part // 2) + 2 * x + part % 2, 64, stride=16)
+            out[rows, :] = total[64 * x : 64 * x + 64]
 
 
 def mix_modes(got, weights, xf, xi, after, out):
     total = got[:, 0]
     for j in range(1, 8):
         total = total + got[:, j]
-    high, low = halves(total.reshape(128, 128))
-    row, lane = iotas((128, 128))
-    modes = jnp.zeros((256, 128), F32)
-    for k in range(4):
-        spread = (row // 8 % 4 == k) & (row // 32 * 8 + row % 8 == lane // 4)
-        spread = spread.astype(BF16)
-        modes = modes + dot(xf[k], dot(high, spread).astype(BF16))
-        modes = modes + dot(xf[k], dot(low, spread).astype(BF16))
+    both = jnp.concatenate(halves(total.reshape(128, 128)), axis=0)
+    row, lane = iotas((128, 512))
+    spread = (row // 8 % 4 == lane // 128) & (row // 32 * 8 + row % 8 == lane % 128 // 4)
+    wide = dot(both, spread.astype(BF16)).astype(BF16)
+    pieces = [
+        jnp.concatenate([wide[:128, 128 * k : 128 * k + 128], wide[128:, 128 * k : 128 * k + 128]], axis=1)
+        for k in range(4)
+    ]
+    modes = dot(xf[...], jnp.concatenate(pieces, axis=0))
+    modes = modes[:, :128] + modes[:, 128:]
     real, imag = modes[:128], modes[128:]
-    total = jnp.zeros((256, 128), F32)
+    highs, lows = [], []
     for i in range(8):
         wr = weights[8 * i : 8 * i + 8, 0:16, :].astype(F32).reshape(128, 128)
         wi = weights[8 * i : 8 * i + 8, 16:32, :].astype(F32).reshape(128, 128)
-        part = jnp.concatenate([wr * real - wi * imag, wr * imag + wi * real], axis=0)
-        p_high, p_low = halves(part)
-        gather = (lane // 64 * 16 + lane % 16 == 4 * i + row % 4).astype(BF16)
-        total = total + dot(p_high, gather) + dot(p_low, gather)
+        high, low = halves(
+            jnp.concatenate([wr * real - wi * imag, wr * imag + wi * real], axis=0)
+        )
+        highs.append(high)
+        lows.append(low)
+    row, lane = iotas((1024, 128))
+    gather = (lane // 64 * 16 + lane % 16 == 4 * (row // 128) + row % 4).astype(BF16)
+    parts = [jnp.concatenate(part, axis=1) for part in (highs, lows)]
+    total = dot(jnp.concatenate(parts, axis=0), gather)
+    total = total[:256] + total[256:]
     row, lane = iotas((256, 128))
     total = jnp.where((row // 4) % 4 == (lane // 16) % 4, total, 0.0)
-    t_high, t_low = halves(total)
-    back = dot(xi[0], t_high) + dot(xi[0], t_low) + dot(xi[1], t_high)
+    back = dot(xi[...], jnp.concatenate(halves(total), axis=1))
+    back = back[:128, :128] + back[:128, 128:] + back[128:, :128]
     real, imag = back[:64], back[64:]
     lane = lax.broadcasted_iota(jnp.int32, (64, 128), 1)
     parts = [
@@ -433,26 +454,27 @@
     weights = exchange(turned, ("gx", "gy"))
 
     message = ((3, 16, 128), F32)
-    outer, far, near = call(
-        pack_y, [((6, 2, 128, 128), F32), message, message], [VMEM] * 5, flops=10**12
-    )(f, s, fp, sp, got)
+    far, near = call(
+        pack_y, [message, message], [VMEM] * 5 + [anywhere], [pltpu.VMEM((6, 2, 128, 128), F32)]
+    )(f, s, fp, sp, got, turned)
     far = lax.ppermute(far, "gy", [(j, (j - 1 + 2 * (j % 2)) % 8) for j in range(8)])
     near = lax.ppermute(near, "gy", [(j, j + 1 - 2 * (j % 2)) for j in range(8)])
     [last] = call(
         stencil,
         [((5, 2, 128, 128), F32)],
-        [VMEM] * 7 + [anywhere],
+        [VMEM] * 7,
         [
             pltpu.VMEM((5, 16, 16, 384), F32),
             pltpu.VMEM((5, 16, 16, 384), F32),
             pltpu.VMEM((16, 16, 384), F32),
+            pltpu.VMEM((2, 128, 128), F32),
         ],
         flops=10**12,
-    )(f, s, fp, sp, outer, far, near, weights)
+    )(f, s, fp, sp, got, far, near)
     keep, send, modes = call(
         forward,
-        [((160, 128), F32), ((160, 128), F32), ((64, 16, 128), F32)],
-        [VMEM, SMEM, SMEM, anywhere, anywhere],
+        [((160, 128), F32), ((160, 128), F32), ((1024, 128), F32)],
+        [VMEM, anywhere, SMEM, SMEM, anywhere, anywhere],
         [
             pltpu.VMEM((320, 256), F32),
             pltpu.VMEM((4, 512, 128), BF16),
@@ -461,7 +483,7 @@
             pltpu.VMEM((256, 256), BF16),
             pltpu.SemaphoreType.DMA((2,)),
         ],
-    )(last, lift_weight, lift_bias, table["yf"], table["zf"])
+    )(last, weights, lift_weight, lift_bias, table["yf"], table["zf"])
     modes = exchange(modes.reshape(128, 8, 128), everyone)
     [direct] = call(
         pointwise,

time: 84.4 us -> 86.9 us (1.030)
  waiting for transfers between devices: 16 us -> 22.1 us
  Pallas kernels: 21.9 us -> 18.7 us
    all_to_all x2, waiting for transfers between devices: 9.33 us -> 15.7 us  [exchange(): return lax.all_to_all(value, axis, split_axis=0, concat_axis=0, tiled=True)]
    ppermute x1, waiting for transfers between devices: 5.7 us -> 0.01 us  [shards(): lax.ppermute(far, 'gy', [(j, (j - 1 + 2 * (j % 2)) % 8) for j in range(8)])]
    ppermute x1, waiting for transfers between devices: 0.01 us -> 5.44 us  [shards(): got = lax.ppermute(message, ('gx', 'ga'), across)]
    pallas_call x3, Pallas kernels: 11.7 us -> 8.64 us  [the longest x1 4.16 us: shards(): call(forward, [((160, 128), F32), ((160, 128), F32), ((1024, 128), F32)],...]
    all_to_all x2, starting transfers between devices: 16.3 us -> 13.6 us  [exchange(): return lax.all_to_all(value, axis, split_axis=0, concat_axis=0, tiled=True)]
    ppermute x1, starting transfers between devices: 4.63 us -> 6.47 us  [shards(): lax.ppermute(far, 'gy', [(j, (j - 1 + 2 * (j % 2)) % 8) for j in range(8)])]
  transfers between devices with their start and end apart: 8 -> 8, of which waited for: 4 -> 4; matrix products, arithmetic and copies ran while one was open for 0% -> 0% of each run, Pallas kernels for 6% -> 10%
where the time goes in v9:
time: 86.9 us; the launch traced here: 86.5 us
  starting transfers between devices  24.8 us (29%)
  waiting for transfers between devices  22.1 us (25%)
  Pallas kernels  18.7 us (22%)
  blocking collectives  17.9 us (21%)
  local copies, waits for them, and re-layouts  2.71 us (3%)
    all_to_all x1, blocking collectives, exchange(): return lax.all_to_all(value, axis, split_axis=0, concat_axis=0, tiled=True)  17.9 us
    all_to_all x2, waiting for transfers between devices, exchange(): return lax.all_to_all(value, axis, split_axis=0, concat_axis=0, tiled=True)  15.7 us
    all_to_all x2, starting transfers between devices, exchange(): return lax.all_to_all(value, axis, split_axis=0, concat_axis=0, tiled=True)  13.6 us
    ppermute x1, starting transfers between devices, shards(): lax.ppermute(far, 'gy', [(j, (j - 1 + 2 * (j % 2)) % 8) for j in range(8)])  6.47 us
    ppermute x1, waiting for transfers between devices, shards(): got = lax.ppermute(message, ('gx', 'ga'), across)  5.44 us
    pallas_call x1, Pallas kernels, shards(): call(forward, [((160, 128), F32), ((160, 128), F32), ((1024, 128), F32)],...  4.16 us
    pallas_call x1, Pallas kernels, shards(): call(stencil, [((5, 2, 128, 128), F32)], [VMEM] * 7, [pltpu.VMEM((5, 16,...  3.93 us
    pallas_call x1, Pallas kernels, shards(): call(pointwise, [((8, 256, 128), F32)], [VMEM, VMEM, SMEM, SMEM, VMEM, VM...  3.19 us
  transfers between devices with their start and end apart: 8, of which 4 were waited for; matrix products, arithmetic and copies ran while one was open for 0% of the time, Pallas kernels for 10%

profile of v9, /device:TPU:1, one launch (start us, length us, event | category | flops | bytes accessed | tf_op | source)
XLA Modules:
  0.0 86.5 jit_solution(3585058371811109659)
XLA Ops:
  0.0 1.4 %collective-permute-start = (f32[5,128,256]{2,1,0:T(8,128)}, f32[5,128,256]{2,1,0:T(8,128)S(1)}, u32[]{:S(2)}, u32[]{:S(2)}) collective-permute-start(f32[5,128,256]{2,1,0:T(8,128)} %bitcast.8), channel_id=1, source_target_pairs={{0,1},{1,0},{2,3},{3,2},{4,5},{5,4},{6,7},{7,6},{8,9},{9,8},{10,11... | collective-permute-start | bytes 1966088 | tf_op jit(solution)/shard_map/ppermute | solution.py:436
  1.4 0.0 collective-permute-start.1
  1.4 1.1 %copy-done = f32[5,8,16,256]{3,2,1,0:T(8,128)S(1)} copy-done((f32[5,8,16,256]{3,2,1,0:T(8,128)S(1)}, f32[5,8,16,256]{3,2,1,0:T(8,128)}, u32[]{:S(2)}) %copy-start) | copy-done | bytes 655384
  2.5 0.9 %copy-done.3 = f32[8,16,256]{2,1,0:T(8,128)S(1)} copy-done((f32[8,16,256]{2,1,0:T(8,128)S(1)}, f32[8,16,256]{2,1,0:T(8,128)}, u32[]{:S(2)}) %copy-start.3) | copy-done | bytes 131096
  3.4 0.1 shard_map.127.own
  3.6 0.0 collective-permute-done.1.sp
  3.6 0.0 collective-permute-done.fp
  3.6 0.1 shard_map.128.after
  3.7 1.8 %collective-permute-start.2 = (f32[6,2,48,128]{3,2,1,0:T(8,128)S(1)}, f32[6,2,48,128]{3,2,1,0:T(8,128)S(1)}, u32[]{:S(2)}, u32[]{:S(2)}) collective-permute-start(f32[6,2,48,128]{3,2,1,0:T(8,128)S(1)} %shard_map.128.after), channel_id=1, source_target_pairs={{0,113},{16,1},{32,17},{48,33},{64,49},{80,65},{96,81},{112,97},{1... | collective-permute-start | bytes 884744 | tf_op jit(solution)/shard_map/ppermute | solution.py:445
  5.5 0.0 copy-done.2
  5.5 1.6 %shard_map.129.after = bf16[64,32,128]{2,1,0:T(8,128)(2,1)} custom-call(f32[2048,128]{1,0:T(8,128)S(1)} %bitcast.15, f32[6,2,48,128]{3,2,1,0:T(8,128)S(1)} %shard_map.128.after), custom_call_target="tpu_custom_call" | custom-call | flops 10000000 | bytes 20000000 | tf_op jit(solution)/shard_map/pallas_call | solution.py:447
  7.1 5.4 %collective-permute-done.2.message.got = f32[6,2,48,128]{3,2,1,0:T(8,128)S(1)} collective-permute-done((f32[6,2,48,128]{3,2,1,0:T(8,128)S(1)}, f32[6,2,48,128]{3,2,1,0:T(8,128)S(1)}, u32[]{:S(2)}, u32[]{:S(2)}) %collective-permute-start.2) | collective-permute-done | bytes 294944 | tf_op jit(solution)/shard_map/ppermute | solution.py:445
  12.5 0.0 copy-done.1
  12.5 0.5 shard_map.130
  13.1 6.5 %collective-permute-start.3 = (f32[3,16,128]{2,1,0:T(8,128)S(1)}, f32[3,16,128]{2,1,0:T(8,128)S(1)}, u32[]{:S(2)}, u32[]{:S(2)}) collective-permute-start(f32[3,16,128]{2,1,0:T(8,128)S(1)} %get-tuple-element.10), channel_id=1, source_target_pairs={{0,14},{2,4},{4,2},{6,8},{8,6},{10,12},{12,10},{14,0},{1,15},{3,5}... | collective-permute-start | bytes 73736 | tf_op jit(solution)/shard_map/ppermute | solution.py:460
  19.6 0.0 collective-permute-start.4
  19.6 8.3 %all-to-all-start = ((bf16[64,32,128]{2,1,0:T(8,128)(2,1)}), bf16[64,32,128]{2,1,0:T(8,128)(2,1)}, u32[]{:S(2)}, u32[]{:S(2)}) async-start(bf16[64,32,128]{2,1,0:T(8,128)(2,1)} %shard_map.129.after), calls=%async_computation | async-start | bytes 1048576 | tf_op jit(solution)/shard_map/all_to_all | solution.py:430
  27.8 0.0 collective-permute-done.3.far
  27.8 0.0 collective-permute-done.4.near
  27.9 0.0 copy-done.4
  27.9 0.0 copy-start.6
  27.9 0.0 copy-start.10
  27.9 0.0 copy-start.11
  27.9 0.0 copy-start.13
  27.9 3.9 %shard_map.131.last = f32[5,2,128,128]{3,2,1,0:T(8,128)S(1)} custom-call(f32[5,128,256]{2,1,0:T(8,128)S(1)} %bitcast.11, f32[128,256]{1,0:T(8,128)S(1)} %bitcast.19, f32[5,128,256]{2,1,0:T(8,128)S(1)} %collective-permute-done.fp, f32[128,256]{1,0:T(8,128)S(1)} %collective-permute-done.1.sp, f32[6,2,48,128]{3,2,1,0:T(8,128)S(1)} %collective-permute-done.2.message.got, ...), custom_call_target="tpu_custom_call" | custom-call | flops 999999995904 | bytes 1048576 | tf_op jit(solution)/shard_map/pallas_call | solution.py:462
  31.9 7.9 %all-to-all-done.after.weights = bf16[64,32,128]{2,1,0:T(8,128)(2,1)} async-done(((bf16[64,32,128]{2,1,0:T(8,128)(2,1)}), bf16[64,32,128]{2,1,0:T(8,128)(2,1)}, u32[]{:S(2)}, u32[]{:S(2)}) %all-to-all-start) | async-done | bytes 524320 | tf_op jit(solution)/shard_map/all_to_all | solution.py:430
  39.8 0.0 copy-done.6
  39.8 0.0 copy-done.10
  39.8 0.0 copy-done.11
  39.8 0.0 copy-done.13
  39.8 4.2 %shard_map.132 = (f32[160,128]{1,0:T(8,128)S(1)}, f32[160,128]{1,0:T(8,128)S(1)}, f32[1024,128]{1,0:T(8,128)}) custom-call(f32[5,2,128,128]{3,2,1,0:T(8,128)S(1)} %shard_map.131.last, bf16[64,32,128]{2,1,0:T(8,128)(2,1)} %all-to-all-done.after.weights, f32[5,32]{1,0:T(8,128)S(1)} %copy-done.11, f32[32]{0:T(128)S(1)} %copy-done.13, ...), custom_call_target="tpu_custom_call" | custom-call | flops 10000000 | bytes 1048576 | tf_op jit(solution)/shard_map/pallas_call | solution.py:474
  44.0 0.0 copy-start.12
  44.0 5.4 %all-to-all-start.1 = ((f32[128,8,128]{2,1,0:T(8,128)}), f32[128,8,128]{2,1,0:T(8,128)S(1)}, u32[]{:S(2)}, u32[]{:S(2)}) async-start(f32[128,8,128]{2,1,0:T(8,128)} %bitcast.3), calls=%async_computation.1 | async-start | bytes 1048576 | tf_op jit(solution)/shard_map/all_to_all | solution.py:430
  49.4 1.5 %collective-permute-start.5 = (f32[160,128]{1,0:T(8,128)S(1)}, f32[160,128]{1,0:T(8,128)S(1)}, u32[]{:S(2)}, u32[]{:S(2)}) collective-permute-start(f32[160,128]{1,0:T(8,128)S(1)} %get-tuple-element.14), channel_id=1, source_target_pairs={{0,1},{1,0},{2,3},{3,2},{4,5},{5,4},{6,7},{7,6},{8,9},{9,8},{10,11... | collective-permute-start | bytes 245768 | tf_op jit(solution)/shard_map/ppermute | solution.py:494
  50.8 0.9 %collective-permute-done.5.got = f32[160,128]{1,0:T(8,128)S(1)} collective-permute-done((f32[160,128]{1,0:T(8,128)S(1)}, f32[160,128]{1,0:T(8,128)S(1)}, u32[]{:S(2)}, u32[]{:S(2)}) %collective-permute-start.5) | collective-permute-done | bytes 81952 | tf_op jit(solution)/shard_map/ppermute | solution.py:494
  51.8 0.0 copy-done.12
  51.8 0.7 copy-done.14
  52.4 3.2 %shard_map.133.after.direct = f32[8,256,128]{2,1,0:T(8,128)S(1)} custom-call(f32[160,128]{1,0:T(8,128)S(1)} %get-tuple-element.13.keep, f32[160,128]{1,0:T(8,128)S(1)} %collective-permute-done.5.got, f32[5,32]{1,0:T(8,128)S(1)} %copy-done.11, f32[32]{0:T(128)S(1)} %copy-done.13, bf16[32,32]{1,0:T(8,128)(2,1)S(1)} %copy-done.12, f32[1,32]{1,0:T(1,128)S(1)} %bitcast.20), custom_call_target="tpu_custom_call" | custom-call | flops 300000000 | bytes 1048576 | tf_op jit(solution)/shard_map/pallas_call | solution.py:488
  55.6 7.7 %all-to-all-done.1 = f32[128,8,128]{2,1,0:T(8,128)S(1)} async-done(((f32[128,8,128]{2,1,0:T(8,128)}), f32[128,8,128]{2,1,0:T(8,128)S(1)}, u32[]{:S(2)}, u32[]{:S(2)}) %all-to-all-start.1) | async-done | bytes 524320 | tf_op jit(solution)/shard_map/all_to_all | solution.py:430
  63.4 0.0 copy-done.7
  63.4 0.0 copy-done.9
  63.4 2.4 %shard_map.134 = bf16[8,8,2,16,128]{4,3,2,1,0:T(8,128)(2,1)S(1)} custom-call(f32[8,8,16,128]{3,2,1,0:T(8,128)S(1)} %bitcast.12, bf16[64,32,128]{2,1,0:T(8,128)(2,1)} %all-to-all-done.after.weights, bf16[256,512]{1,0:T(8,128)(2,1)S(1)} %copy-done.7, bf16[256,256]{1,0:T(8,128)(2,1)S(1)} %copy-done.9, f32[8,256,128]{2,1,0:T(8,128)S(1)} %shard_map.133.after.direct), custom_call_target="tpu_custom_call" | custom-call | flops 10000000 | bytes 1048576 | tf_op jit(solution)/shard_map/pallas_call | solution.py:496
  65.8 0.0 copy-start.5
  65.8 0.0 copy-start.8
  65.8 17.9 %all_to_all.15 = bf16[128,16,128]{2,1,0:T(8,128)(2,1)S(1)} all-to-all(bf16[128,16,128]{2,1,0:T(8,128)(2,1)S(1)} %bitcast.13), channel_id=1, replica_groups=mesh['gx'=8,'gy'=8,'ga'=2] {'gx','gy','ga'}, dimensions={0} | all-to-all | bytes 1048576 | tf_op jit(solution)/shard_map/all_to_all | solution.py:430
  83.7 0.0 copy-done.5
  83.7 0.0 copy-done.8
  83.7 2.7 %shard_map.135 = bf16[8,32,8,128]{3,2,1,0:T(8,128)(2,1)} custom-call(bf16[2048,128]{1,0:T(8,128)(2,1)S(1)} %bitcast.14, f32[8,256,128]{2,1,0:T(8,128)S(1)} %shard_map.133.after.direct, bf16[8,128,256]{2,1,0:T(8,128)(2,1)S(1)} %copy-done.5, bf16[512,256]{1,0:T(8,128)(2,1)S(1)} %copy-done.8), custom_call_target="tpu_custom_call" | custom-call | flops 10000000 | bytes 1048576 | tf_op jit(solution)/shard_map/pallas_call | solution.py:500
  (8 shorter events, 0.0 us)
Async XLA Ops:
  0.0 3.6 %collective-permute-start = (f32[5,128,256]{2,1,0:T(8,128)}, f32[5,128,256]{2,1,0:T(8,128)S(1)}, u32[]{:S(2)}, u32[]{:S(2)}) collective-permute-start(f32[5,128,256]{2,1,0:T(8,128)} %bitcast.8), channel_id=1, source_target_pairs={{0,1},{1,0},{2,3},{3,2},{4,5},{5,4},{6,7},{7,6},{8,9},{9,8},{10,11... | collective-permute-start | bytes 1966088 | tf_op jit(solution)/shard_map/ppermute | solution.py:436
  1.4 2.1 %collective-permute-start.1 = (f32[128,256]{1,0:T(8,128)}, f32[128,256]{1,0:T(8,128)S(1)}, u32[]{:S(2)}, u32[]{:S(2)}) collective-permute-start(f32[128,256]{1,0:T(8,128)} %bitcast.16), channel_id=1, source_target_pairs={{0,1},{1,0},{2,3},{3,2},{4,5},{5,4},{6,7},{7,6},{8,9},{9,8},{10,11... | collective-permute-start | bytes 393224 | tf_op jit(solution)/shard_map/ppermute | solution.py:436
  1.4 1.1 %copy-start = (f32[5,8,16,256]{3,2,1,0:T(8,128)S(1)}, f32[5,8,16,256]{3,2,1,0:T(8,128)}, u32[]{:S(2)}) copy-start(f32[5,8,16,256]{3,2,1,0:T(8,128)} %param.13) | copy-start | bytes 1966084
  2.5 0.9 %copy-start.3 = (f32[8,16,256]{2,1,0:T(8,128)S(1)}, f32[8,16,256]{2,1,0:T(8,128)}, u32[]{:S(2)}) copy-start(f32[8,16,256]{2,1,0:T(8,128)} %param.14) | copy-start | bytes 393220
  3.4 2.1 %copy-start.2 = (f32[4,4,32,4,128]{4,3,2,1,0:T(4,128)S(1)}, f32[4,4,32,4,128]{4,3,2,1,0:T(4,128)}, u32[]{:S(2)}) copy-start(f32[4,4,32,4,128]{4,3,2,1,0:T(4,128)} %param.18) | copy-start | bytes 3145732
  3.7 8.8 %collective-permute-start.2 = (f32[6,2,48,128]{3,2,1,0:T(8,128)S(1)}, f32[6,2,48,128]{3,2,1,0:T(8,128)S(1)}, u32[]{:S(2)}, u32[]{:S(2)}) collective-permute-start(f32[6,2,48,128]{3,2,1,0:T(8,128)S(1)} %shard_map.128.after), channel_id=1, source_target_pairs={{0,113},{16,1},{32,17},{48,33},{64,49},{80,65},{96,81},{112,97},{1... | collective-permute-start | bytes 884744 | tf_op jit(solution)/shard_map/ppermute | solution.py:445
  5.5 7.0 %copy-start.1 = (f32[5,8,16,256]{3,2,1,0:T(8,128)S(1)}, f32[5,8,16,256]{3,2,1,0:T(8,128)}, u32[]{:S(2)}) copy-start(f32[5,8,16,256]{3,2,1,0:T(8,128)} %param.13) | copy-start | bytes 1966084
  13.1 14.8 %collective-permute-start.3 = (f32[3,16,128]{2,1,0:T(8,128)S(1)}, f32[3,16,128]{2,1,0:T(8,128)S(1)}, u32[]{:S(2)}, u32[]{:S(2)}) collective-permute-start(f32[3,16,128]{2,1,0:T(8,128)S(1)} %get-tuple-element.10), channel_id=1, source_target_pairs={{0,14},{2,4},{4,2},{6,8},{8,6},{10,12},{12,10},{14,0},{1,15},{3,5}... | collective-permute-start | bytes 73736 | tf_op jit(solution)/shard_map/ppermute | solution.py:460
  19.6 8.3 %copy-start.4 = (f32[8,16,256]{2,1,0:T(8,128)S(1)}, f32[8,16,256]{2,1,0:T(8,128)}, u32[]{:S(2)}) copy-start(f32[8,16,256]{2,1,0:T(8,128)} %param.14) | copy-start | bytes 393220
  19.6 8.3 %collective-permute-start.4 = (f32[3,16,128]{2,1,0:T(8,128)S(1)}, f32[3,16,128]{2,1,0:T(8,128)S(1)}, u32[]{:S(2)}, u32[]{:S(2)}) collective-permute-start(f32[3,16,128]{2,1,0:T(8,128)S(1)} %get-tuple-element.11), channel_id=1, source_target_pairs={{0,2},{2,0},{4,6},{6,4},{8,10},{10,8},{12,14},{14,12},{1,3},{3,1},... | collective-permute-start | bytes 73736 | tf_op jit(solution)/shard_map/ppermute | solution.py:461
  19.6 20.2 %all-to-all-start = ((bf16[64,32,128]{2,1,0:T(8,128)(2,1)}), bf16[64,32,128]{2,1,0:T(8,128)(2,1)}, u32[]{:S(2)}, u32[]{:S(2)}) async-start(bf16[64,32,128]{2,1,0:T(8,128)(2,1)} %shard_map.129.after), calls=%async_computation | async-start | bytes 1048576 | tf_op jit(solution)/shard_map/all_to_all | solution.py:430
  27.9 11.9 %copy-start.6 = (bf16[8,256,128]{2,1,0:T(8,128)(2,1)S(1)}, bf16[8,256,128]{2,1,0:T(8,128)(2,1)}, u32[]{:S(2)}) copy-start(bf16[8,256,128]{2,1,0:T(8,128)(2,1)} %constant.12.clone.yf_far) | copy-start | bytes 1572868
  27.9 11.9 %copy-start.10 = (bf16[256,256]{1,0:T(8,128)(2,1)S(1)}, bf16[256,256]{1,0:T(8,128)(2,1)}, u32[]{:S(2)}) copy-start(bf16[256,256]{1,0:T(8,128)(2,1)} %constant.14.clone.zf_far) | copy-start | bytes 393220
  27.9 11.9 %copy-start.11 = (f32[5,32]{1,0:T(8,128)S(1)}, f32[5,32]{1,0:T(8,128)}, u32[]{:S(2)}) copy-start(f32[5,32]{1,0:T(8,128)} %weight.3) | copy-start | bytes 1924
  27.9 11.9 %copy-start.13 = (f32[32]{0:T(128)S(1)}, f32[32]{0:T(128)}, u32[]{:S(2)}) copy-start(f32[32]{0:T(128)} %bias.3) | copy-start | bytes 388
  44.0 7.8 %copy-start.12 = (bf16[32,32]{1,0:T(8,128)(2,1)S(1)}, bf16[32,32]{1,0:T(8,128)(2,1)}, u32[]{:S(2)}) copy-start(bf16[32,32]{1,0:T(8,128)(2,1)} %mix.1) | copy-start | bytes 6148
  44.0 19.4 %all-to-all-start.1 = ((f32[128,8,128]{2,1,0:T(8,128)}), f32[128,8,128]{2,1,0:T(8,128)S(1)}, u32[]{:S(2)}, u32[]{:S(2)}) async-start(f32[128,8,128]{2,1,0:T(8,128)} %bitcast.3), calls=%async_computation.1 | async-start | bytes 1048576 | tf_op jit(solution)/shard_map/all_to_all | solution.py:430
  49.4 2.4 %collective-permute-start.5 = (f32[160,128]{1,0:T(8,128)S(1)}, f32[160,128]{1,0:T(8,128)S(1)}, u32[]{:S(2)}, u32[]{:S(2)}) collective-permute-start(f32[160,128]{1,0:T(8,128)S(1)} %get-tuple-element.14), channel_id=1, source_target_pairs={{0,1},{1,0},{2,3},{3,2},{4,5},{5,4},{6,7},{7,6},{8,9},{9,8},{10,11... | collective-permute-start | bytes 245768 | tf_op jit(solution)/shard_map/ppermute | solution.py:494
  51.8 0.7 copy-start.14
  52.4 10.9 %copy-start.7 = (bf16[256,512]{1,0:T(8,128)(2,1)S(1)}, bf16[256,512]{1,0:T(8,128)(2,1)}, u32[]{:S(2)}) copy-start(bf16[256,512]{1,0:T(8,128)(2,1)} %constant.16.clone.xf) | copy-start | bytes 786436
  52.4 10.9 %copy-start.9 = (bf16[256,256]{1,0:T(8,128)(2,1)S(1)}, bf16[256,256]{1,0:T(8,128)(2,1)}, u32[]{:S(2)}) copy-start(bf16[256,256]{1,0:T(8,128)(2,1)} %constant.17.clone.xi) | copy-start | bytes 393220
  65.8 17.9 %copy-start.5 = (bf16[8,128,256]{2,1,0:T(8,128)(2,1)S(1)}, bf16[8,128,256]{2,1,0:T(8,128)(2,1)}, u32[]{:S(2)}) copy-start(bf16[8,128,256]{2,1,0:T(8,128)(2,1)} %constant.13.clone.yi_far) | copy-start | bytes 1572868
  65.8 17.9 %copy-start.8 = (bf16[512,256]{1,0:T(8,128)(2,1)S(1)}, bf16[512,256]{1,0:T(8,128)(2,1)}, u32[]{:S(2)}) copy-start(bf16[512,256]{1,0:T(8,128)(2,1)} %constant.15.clone.zi_far) | copy-start | bytes 786436

commit v10 on v9

--- a/solution.py
+++ b/solution.py
@@ -132,7 +132,7 @@
     message[:, :, 24:48, :] = other[...]
 
 
-def pack_y(f, s, fp, sp, message, after, far, near, outer):
+def pack_y(f, s, fp, sp, message, far, near, outer):
     refs = (f, s, fp, sp)
     a = lax.axis_index("ga")
     row = lax.broadcasted_iota(jnp.int32, (8, 128), 0)
@@ -455,8 +455,12 @@
 
     message = ((3, 16, 128), F32)
     far, near = call(
-        pack_y, [message, message], [VMEM] * 5 + [anywhere], [pltpu.VMEM((6, 2, 128, 128), F32)]
-    )(f, s, fp, sp, got, turned)
+        pack_y,
+        [message, message],
+        [VMEM] * 5,
+        [pltpu.VMEM((6, 2, 128, 128), F32)],
+        flops=10**12,
+    )(f, s, fp, sp, got)
     far = lax.ppermute(far, "gy", [(j, (j - 1 + 2 * (j % 2)) % 8) for j in range(8)])
     near = lax.ppermute(near, "gy", [(j, j + 1 - 2 * (j % 2)) for j in range(8)])
     [last] = call(
@@ -469,7 +473,6 @@
             pltpu.VMEM((16, 16, 384), F32),
             pltpu.VMEM((2, 128, 128), F32),
         ],
-        flops=10**12,
     )(f, s, fp, sp, got, far, near)
     keep, send, modes = call(
         forward,

time: 86.9 us -> 80.9 us (0.931)
  waiting for transfers between devices: 22.1 us -> 14.4 us
  starting transfers between devices: 24.8 us -> 26.4 us
    all_to_all x2, waiting for transfers between devices: 15.7 us -> 7.75 us  [exchange(): return lax.all_to_all(value, axis, split_axis=0, concat_axis=0, tiled=True)]
    ppermute x1, waiting for transfers between devices: 0.01 us -> 5.75 us  [shards(): lax.ppermute(far, 'gy', [(j, (j - 1 + 2 * (j % 2)) % 8) for j in range(8)])]
    ppermute x1, waiting for transfers between devices: 5.44 us -> 0.01 us  [shards(): got = lax.ppermute(message, ('gx', 'ga'), across)]
    all_to_all x2, starting transfers between devices: 13.6 us -> 17.1 us  [exchange(): return lax.all_to_all(value, axis, split_axis=0, concat_axis=0, tiled=True)]
    ppermute x1, starting transfers between devices: 6.47 us -> 4.63 us  [shards(): lax.ppermute(far, 'gy', [(j, (j - 1 + 2 * (j % 2)) % 8) for j in range(8)])]
  transfers between devices with their start and end apart: 8 -> 8, of which waited for: 4 -> 3; matrix products, arithmetic and copies ran while one was open for 0% -> 0% of each run, Pallas kernels for 10% -> 12%
where the time goes in v10:
time: 80.9 us; the launch traced here: 80.5 us
  starting transfers between devices  26.4 us (33%)
  Pallas kernels  18.7 us (23%)
  blocking collectives  17.9 us (22%)
  waiting for transfers between devices  14.4 us (18%)
  local copies, waits for them, and re-layouts  2.7 us (3%)
    all_to_all x1, blocking collectives, exchange(): return lax.all_to_all(value, axis, split_axis=0, concat_axis=0, tiled=True)  17.9 us
    all_to_all x2, starting transfers between devices, exchange(): return lax.all_to_all(value, axis, split_axis=0, concat_axis=0, tiled=True)  17.1 us
    all_to_all x2, waiting for transfers between devices, exchange(): return lax.all_to_all(value, axis, split_axis=0, concat_axis=0, tiled=True)  7.75 us
    ppermute x1, waiting for transfers between devices, shards(): lax.ppermute(far, 'gy', [(j, (j - 1 + 2 * (j % 2)) % 8) for j in range(8)])  5.75 us
    ppermute x1, starting transfers between devices, shards(): lax.ppermute(far, 'gy', [(j, (j - 1 + 2 * (j % 2)) % 8) for j in range(8)])  4.63 us
    pallas_call x1, Pallas kernels, shards(): call(forward, [((160, 128), F32), ((160, 128), F32), ((1024, 128), F32)],...  4.16 us
    pallas_call x1, Pallas kernels, shards(): call(stencil, [((5, 2, 128, 128), F32)], [VMEM] * 7, [pltpu.VMEM((5, 16,...  3.92 us
    pallas_call x1, Pallas kernels, shards(): call(pointwise, [((8, 256, 128), F32)], [VMEM, VMEM, SMEM, SMEM, VMEM, VM...  3.19 us
  transfers between devices with their start and end apart: 8, of which 3 were waited for; matrix products, arithmetic and copies ran while one was open for 0% of the time, Pallas kernels for 12%

profile of v10, /device:TPU:1, one launch (start us, length us, event | category | flops | bytes accessed | tf_op | source)
XLA Modules:
  0.0 80.5 jit_solution(10800967965155586209)
XLA Ops:
  0.0 1.4 %collective-permute-start = (f32[5,128,256]{2,1,0:T(8,128)}, f32[5,128,256]{2,1,0:T(8,128)S(1)}, u32[]{:S(2)}, u32[]{:S(2)}) collective-permute-start(f32[5,128,256]{2,1,0:T(8,128)} %bitcast.8), channel_id=1, source_target_pairs={{0,1},{1,0},{2,3},{3,2},{4,5},{5,4},{6,7},{7,6},{8,9},{9,8},{10,11... | collective-permute-start | bytes 1966088 | tf_op jit(solution)/shard_map/ppermute | solution.py:436
  1.4 0.0 collective-permute-start.1
  1.4 0.0 copy-start
  1.4 1.1 %copy-done = f32[5,8,16,256]{3,2,1,0:T(8,128)S(1)} copy-done((f32[5,8,16,256]{3,2,1,0:T(8,128)S(1)}, f32[5,8,16,256]{3,2,1,0:T(8,128)}, u32[]{:S(2)}) %copy-start) | copy-done | bytes 655384
  2.5 0.0 copy-start.3
  2.5 0.9 %copy-done.3 = f32[8,16,256]{2,1,0:T(8,128)S(1)} copy-done((f32[8,16,256]{2,1,0:T(8,128)S(1)}, f32[8,16,256]{2,1,0:T(8,128)}, u32[]{:S(2)}) %copy-start.3) | copy-done | bytes 131096
  3.4 0.0 copy-start.2
  3.4 0.1 shard_map.127.own
  3.6 0.0 collective-permute-done.1.sp
  3.6 0.0 collective-permute-done.fp
  3.6 0.1 shard_map.128.after
  3.7 1.8 %collective-permute-start.2 = (f32[6,2,48,128]{3,2,1,0:T(8,128)S(1)}, f32[6,2,48,128]{3,2,1,0:T(8,128)S(1)}, u32[]{:S(2)}, u32[]{:S(2)}) collective-permute-start(f32[6,2,48,128]{3,2,1,0:T(8,128)S(1)} %shard_map.128.after), channel_id=1, source_target_pairs={{0,113},{16,1},{32,17},{48,33},{64,49},{80,65},{96,81},{112,97},{1... | collective-permute-start | bytes 884744 | tf_op jit(solution)/shard_map/ppermute | solution.py:445
  5.5 0.0 copy-done.2
  5.5 1.6 %shard_map.131 = bf16[64,32,128]{2,1,0:T(8,128)(2,1)} custom-call(f32[2048,128]{1,0:T(8,128)S(1)} %bitcast.15, f32[6,2,48,128]{3,2,1,0:T(8,128)S(1)} %shard_map.128.after), custom_call_target="tpu_custom_call" | custom-call | flops 10000000 | bytes 20000000 | tf_op jit(solution)/shard_map/pallas_call | solution.py:447
  7.1 0.0 copy-start.1
  7.1 11.3 %all-to-all-start = ((bf16[64,32,128]{2,1,0:T(8,128)(2,1)}), bf16[64,32,128]{2,1,0:T(8,128)(2,1)}, u32[]{:S(2)}, u32[]{:S(2)}) async-start(bf16[64,32,128]{2,1,0:T(8,128)(2,1)} %shard_map.131), calls=%async_computation | async-start | bytes 1048576 | tf_op jit(solution)/shard_map/all_to_all | solution.py:430
  18.4 0.0 collective-permute-done.2.message.got
  18.4 0.0 copy-done.1
  18.4 0.0 copy-done.4
  18.4 0.5 shard_map.129
  19.0 4.6 %collective-permute-start.3 = (f32[3,16,128]{2,1,0:T(8,128)S(1)}, f32[3,16,128]{2,1,0:T(8,128)S(1)}, u32[]{:S(2)}, u32[]{:S(2)}) collective-permute-start(f32[3,16,128]{2,1,0:T(8,128)S(1)} %get-tuple-element.10), channel_id=1, source_target_pairs={{0,14},{2,4},{4,2},{6,8},{8,6},{10,12},{12,10},{14,0},{1,15},{3,5}... | collective-permute-start | bytes 73736 | tf_op jit(solution)/shard_map/ppermute | solution.py:464
  23.6 0.1 collective-permute-start.4
  23.7 5.8 %collective-permute-done.3.far = f32[3,16,128]{2,1,0:T(8,128)S(1)} collective-permute-done((f32[3,16,128]{2,1,0:T(8,128)S(1)}, f32[3,16,128]{2,1,0:T(8,128)S(1)}, u32[]{:S(2)}, u32[]{:S(2)}) %collective-permute-start.3) | collective-permute-done | bytes 24608 | tf_op jit(solution)/shard_map/ppermute | solution.py:464
  29.5 0.0 collective-permute-done.4.near
  29.5 3.9 %shard_map.130.last = f32[5,2,128,128]{3,2,1,0:T(8,128)S(1)} custom-call(f32[5,128,256]{2,1,0:T(8,128)S(1)} %bitcast.11, f32[128,256]{1,0:T(8,128)S(1)} %bitcast.19, f32[5,128,256]{2,1,0:T(8,128)S(1)} %collective-permute-done.fp, f32[128,256]{1,0:T(8,128)S(1)} %collective-permute-done.1.sp, f32[6,2,48,128]{3,2,1,0:T(8,128)S(1)} %collective-permute-done.2.message.got, ...), custom_call_target="tpu_custom_call" | custom-call | flops 10000000 | bytes 1048576 | tf_op jit(solution)/shard_map/pallas_call | solution.py:466
  33.4 0.0 all-to-all-done.after.weights
  33.4 0.0 copy-done.6
  33.4 0.0 copy-done.10
  33.4 0.0 copy-done.11
  33.5 0.0 copy-done.13
  33.5 4.2 %shard_map.132 = (f32[160,128]{1,0:T(8,128)S(1)}, f32[160,128]{1,0:T(8,128)S(1)}, f32[1024,128]{1,0:T(8,128)}) custom-call(f32[5,2,128,128]{3,2,1,0:T(8,128)S(1)} %shard_map.130.last, bf16[64,32,128]{2,1,0:T(8,128)(2,1)} %all-to-all-done.after.weights, f32[5,32]{1,0:T(8,128)S(1)} %copy-done.11, f32[32]{0:T(128)S(1)} %copy-done.13, ...), custom_call_target="tpu_custom_call" | custom-call | flops 10000000 | bytes 1048576 | tf_op jit(solution)/shard_map/pallas_call | solution.py:477
  37.6 0.0 copy-start.12
  37.7 5.8 %all-to-all-start.1 = ((f32[128,8,128]{2,1,0:T(8,128)}), f32[128,8,128]{2,1,0:T(8,128)S(1)}, u32[]{:S(2)}, u32[]{:S(2)}) async-start(f32[128,8,128]{2,1,0:T(8,128)} %bitcast.3), calls=%async_computation.1 | async-start | bytes 1048576 | tf_op jit(solution)/shard_map/all_to_all | solution.py:430
  43.5 1.3 %collective-permute-start.5 = (f32[160,128]{1,0:T(8,128)S(1)}, f32[160,128]{1,0:T(8,128)S(1)}, u32[]{:S(2)}, u32[]{:S(2)}) collective-permute-start(f32[160,128]{1,0:T(8,128)S(1)} %get-tuple-element.14), channel_id=1, source_target_pairs={{0,1},{1,0},{2,3},{3,2},{4,5},{5,4},{6,7},{7,6},{8,9},{9,8},{10,11... | collective-permute-start | bytes 245768 | tf_op jit(solution)/shard_map/ppermute | solution.py:497
  44.8 0.9 %collective-permute-done.5.got = f32[160,128]{1,0:T(8,128)S(1)} collective-permute-done((f32[160,128]{1,0:T(8,128)S(1)}, f32[160,128]{1,0:T(8,128)S(1)}, u32[]{:S(2)}, u32[]{:S(2)}) %collective-permute-start.5) | collective-permute-done | bytes 81952 | tf_op jit(solution)/shard_map/ppermute | solution.py:497
  45.7 0.0 copy-done.12
  45.7 0.7 copy-done.14
  46.4 3.2 %shard_map.133.after.direct = f32[8,256,128]{2,1,0:T(8,128)S(1)} custom-call(f32[160,128]{1,0:T(8,128)S(1)} %get-tuple-element.13.keep, f32[160,128]{1,0:T(8,128)S(1)} %collective-permute-done.5.got, f32[5,32]{1,0:T(8,128)S(1)} %copy-done.11, f32[32]{0:T(128)S(1)} %copy-done.13, bf16[32,32]{1,0:T(8,128)(2,1)S(1)} %copy-done.12, f32[1,32]{1,0:T(1,128)S(1)} %bitcast.20), custom_call_target="tpu_custom_call" | custom-call | flops 300000000 | bytes 1048576 | tf_op jit(solution)/shard_map/pallas_call | solution.py:491
  49.6 7.7 %all-to-all-done.1 = f32[128,8,128]{2,1,0:T(8,128)S(1)} async-done(((f32[128,8,128]{2,1,0:T(8,128)}), f32[128,8,128]{2,1,0:T(8,128)S(1)}, u32[]{:S(2)}, u32[]{:S(2)}) %all-to-all-start.1) | async-done | bytes 524320 | tf_op jit(solution)/shard_map/all_to_all | solution.py:430
  57.3 0.0 copy-done.7
  57.3 0.0 copy-done.9
  57.3 2.4 %shard_map.134 = bf16[8,8,2,16,128]{4,3,2,1,0:T(8,128)(2,1)S(1)} custom-call(f32[8,8,16,128]{3,2,1,0:T(8,128)S(1)} %bitcast.12, bf16[64,32,128]{2,1,0:T(8,128)(2,1)} %all-to-all-done.after.weights, bf16[256,512]{1,0:T(8,128)(2,1)S(1)} %copy-done.7, bf16[256,256]{1,0:T(8,128)(2,1)S(1)} %copy-done.9, f32[8,256,128]{2,1,0:T(8,128)S(1)} %shard_map.133.after.direct), custom_call_target="tpu_custom_call" | custom-call | flops 10000000 | bytes 1048576 | tf_op jit(solution)/shard_map/pallas_call | solution.py:499
  59.7 0.0 copy-start.5
  59.8 0.0 copy-start.8
  59.8 17.9 %all_to_all.15 = bf16[128,16,128]{2,1,0:T(8,128)(2,1)S(1)} all-to-all(bf16[128,16,128]{2,1,0:T(8,128)(2,1)S(1)} %bitcast.13), channel_id=1, replica_groups=mesh['gx'=8,'gy'=8,'ga'=2] {'gx','gy','ga'}, dimensions={0} | all-to-all | bytes 1048576 | tf_op jit(solution)/shard_map/all_to_all | solution.py:430
  77.6 0.0 copy-done.5
  77.6 0.0 copy-done.8
  77.6 2.7 %shard_map.135 = bf16[8,32,8,128]{3,2,1,0:T(8,128)(2,1)} custom-call(bf16[2048,128]{1,0:T(8,128)(2,1)S(1)} %bitcast.14, f32[8,256,128]{2,1,0:T(8,128)S(1)} %shard_map.133.after.direct, bf16[8,128,256]{2,1,0:T(8,128)(2,1)S(1)} %copy-done.5, bf16[512,256]{1,0:T(8,128)(2,1)S(1)} %copy-done.8), custom_call_target="tpu_custom_call" | custom-call | flops 10000000 | bytes 1048576 | tf_op jit(solution)/shard_map/pallas_call | solution.py:503
  (8 shorter events, 0.0 us)
Async XLA Ops:
  0.0 3.6 %collective-permute-start = (f32[5,128,256]{2,1,0:T(8,128)}, f32[5,128,256]{2,1,0:T(8,128)S(1)}, u32[]{:S(2)}, u32[]{:S(2)}) collective-permute-start(f32[5,128,256]{2,1,0:T(8,128)} %bitcast.8), channel_id=1, source_target_pairs={{0,1},{1,0},{2,3},{3,2},{4,5},{5,4},{6,7},{7,6},{8,9},{9,8},{10,11... | collective-permute-start | bytes 1966088 | tf_op jit(solution)/shard_map/ppermute | solution.py:436
  1.4 2.1 %collective-permute-start.1 = (f32[128,256]{1,0:T(8,128)}, f32[128,256]{1,0:T(8,128)S(1)}, u32[]{:S(2)}, u32[]{:S(2)}) collective-permute-start(f32[128,256]{1,0:T(8,128)} %bitcast.16), channel_id=1, source_target_pairs={{0,1},{1,0},{2,3},{3,2},{4,5},{5,4},{6,7},{7,6},{8,9},{9,8},{10,11... | collective-permute-start | bytes 393224 | tf_op jit(solution)/shard_map/ppermute | solution.py:436
  1.4 1.1 %copy-start = (f32[5,8,16,256]{3,2,1,0:T(8,128)S(1)}, f32[5,8,16,256]{3,2,1,0:T(8,128)}, u32[]{:S(2)}) copy-start(f32[5,8,16,256]{3,2,1,0:T(8,128)} %param.13) | copy-start | bytes 1966084
  2.5 0.9 %copy-start.3 = (f32[8,16,256]{2,1,0:T(8,128)S(1)}, f32[8,16,256]{2,1,0:T(8,128)}, u32[]{:S(2)}) copy-start(f32[8,16,256]{2,1,0:T(8,128)} %param.14) | copy-start | bytes 393220
  3.4 2.1 %copy-start.2 = (f32[4,4,32,4,128]{4,3,2,1,0:T(4,128)S(1)}, f32[4,4,32,4,128]{4,3,2,1,0:T(4,128)}, u32[]{:S(2)}) copy-start(f32[4,4,32,4,128]{4,3,2,1,0:T(4,128)} %param.18) | copy-start | bytes 3145732
  3.7 14.7 %collective-permute-start.2 = (f32[6,2,48,128]{3,2,1,0:T(8,128)S(1)}, f32[6,2,48,128]{3,2,1,0:T(8,128)S(1)}, u32[]{:S(2)}, u32[]{:S(2)}) collective-permute-start(f32[6,2,48,128]{3,2,1,0:T(8,128)S(1)} %shard_map.128.after), channel_id=1, source_target_pairs={{0,113},{16,1},{32,17},{48,33},{64,49},{80,65},{96,81},{112,97},{1... | collective-permute-start | bytes 884744 | tf_op jit(solution)/shard_map/ppermute | solution.py:445
  7.1 11.3 %copy-start.1 = (f32[5,8,16,256]{3,2,1,0:T(8,128)S(1)}, f32[5,8,16,256]{3,2,1,0:T(8,128)}, u32[]{:S(2)}) copy-start(f32[5,8,16,256]{3,2,1,0:T(8,128)} %param.13) | copy-start | bytes 1966084
  7.1 11.4 %copy-start.4 = (f32[8,16,256]{2,1,0:T(8,128)S(1)}, f32[8,16,256]{2,1,0:T(8,128)}, u32[]{:S(2)}) copy-start(f32[8,16,256]{2,1,0:T(8,128)} %param.14) | copy-start | bytes 393220
  7.1 26.3 %all-to-all-start = ((bf16[64,32,128]{2,1,0:T(8,128)(2,1)}), bf16[64,32,128]{2,1,0:T(8,128)(2,1)}, u32[]{:S(2)}, u32[]{:S(2)}) async-start(bf16[64,32,128]{2,1,0:T(8,128)(2,1)} %shard_map.131), calls=%async_computation | async-start | bytes 1048576 | tf_op jit(solution)/shard_map/all_to_all | solution.py:430
  19.0 10.5 %collective-permute-start.3 = (f32[3,16,128]{2,1,0:T(8,128)S(1)}, f32[3,16,128]{2,1,0:T(8,128)S(1)}, u32[]{:S(2)}, u32[]{:S(2)}) collective-permute-start(f32[3,16,128]{2,1,0:T(8,128)S(1)} %get-tuple-element.10), channel_id=1, source_target_pairs={{0,14},{2,4},{4,2},{6,8},{8,6},{10,12},{12,10},{14,0},{1,15},{3,5}... | collective-permute-start | bytes 73736 | tf_op jit(solution)/shard_map/ppermute | solution.py:464
  23.6 9.8 %copy-start.6 = (bf16[8,256,128]{2,1,0:T(8,128)(2,1)S(1)}, bf16[8,256,128]{2,1,0:T(8,128)(2,1)}, u32[]{:S(2)}) copy-start(bf16[8,256,128]{2,1,0:T(8,128)(2,1)} %constant.12.clone.yf_far) | copy-start | bytes 1572868
  23.6 9.8 %copy-start.10 = (bf16[256,256]{1,0:T(8,128)(2,1)S(1)}, bf16[256,256]{1,0:T(8,128)(2,1)}, u32[]{:S(2)}) copy-start(bf16[256,256]{1,0:T(8,128)(2,1)} %constant.14.clone.zf_far) | copy-start | bytes 393220
  23.6 9.8 %copy-start.11 = (f32[5,32]{1,0:T(8,128)S(1)}, f32[5,32]{1,0:T(8,128)}, u32[]{:S(2)}) copy-start(f32[5,32]{1,0:T(8,128)} %weight.3) | copy-start | bytes 1924
  23.6 9.8 %copy-start.13 = (f32[32]{0:T(128)S(1)}, f32[32]{0:T(128)}, u32[]{:S(2)}) copy-start(f32[32]{0:T(128)} %bias.3) | copy-start | bytes 388
  23.6 5.9 %collective-permute-start.4 = (f32[3,16,128]{2,1,0:T(8,128)S(1)}, f32[3,16,128]{2,1,0:T(8,128)S(1)}, u32[]{:S(2)}, u32[]{:S(2)}) collective-permute-start(f32[3,16,128]{2,1,0:T(8,128)S(1)} %get-tuple-element.11), channel_id=1, source_target_pairs={{0,2},{2,0},{4,6},{6,4},{8,10},{10,8},{12,14},{14,12},{1,3},{3,1},... | collective-permute-start | bytes 73736 | tf_op jit(solution)/shard_map/ppermute | solution.py:465
  37.6 8.1 %copy-start.12 = (bf16[32,32]{1,0:T(8,128)(2,1)S(1)}, bf16[32,32]{1,0:T(8,128)(2,1)}, u32[]{:S(2)}) copy-start(bf16[32,32]{1,0:T(8,128)(2,1)} %mix.1) | copy-start | bytes 6148
  37.7 19.7 %all-to-all-start.1 = ((f32[128,8,128]{2,1,0:T(8,128)}), f32[128,8,128]{2,1,0:T(8,128)S(1)}, u32[]{:S(2)}, u32[]{:S(2)}) async-start(f32[128,8,128]{2,1,0:T(8,128)} %bitcast.3), calls=%async_computation.1 | async-start | bytes 1048576 | tf_op jit(solution)/shard_map/all_to_all | solution.py:430
  43.5 2.3 %collective-permute-start.5 = (f32[160,128]{1,0:T(8,128)S(1)}, f32[160,128]{1,0:T(8,128)S(1)}, u32[]{:S(2)}, u32[]{:S(2)}) collective-permute-start(f32[160,128]{1,0:T(8,128)S(1)} %get-tuple-element.14), channel_id=1, source_target_pairs={{0,1},{1,0},{2,3},{3,2},{4,5},{5,4},{6,7},{7,6},{8,9},{9,8},{10,11... | collective-permute-start | bytes 245768 | tf_op jit(solution)/shard_map/ppermute | solution.py:497
  45.7 0.7 copy-start.14
  46.4 10.9 %copy-start.7 = (bf16[256,512]{1,0:T(8,128)(2,1)S(1)}, bf16[256,512]{1,0:T(8,128)(2,1)}, u32[]{:S(2)}) copy-start(bf16[256,512]{1,0:T(8,128)(2,1)} %constant.16.clone.xf) | copy-start | bytes 786436
  46.4 10.9 %copy-start.9 = (bf16[256,256]{1,0:T(8,128)(2,1)S(1)}, bf16[256,256]{1,0:T(8,128)(2,1)}, u32[]{:S(2)}) copy-start(bf16[256,256]{1,0:T(8,128)(2,1)} %constant.17.clone.xi) | copy-start | bytes 393220
  59.7 17.9 %copy-start.5 = (bf16[8,128,256]{2,1,0:T(8,128)(2,1)S(1)}, bf16[8,128,256]{2,1,0:T(8,128)(2,1)}, u32[]{:S(2)}) copy-start(bf16[8,128,256]{2,1,0:T(8,128)(2,1)} %constant.13.clone.yi_far) | copy-start | bytes 1572868
  59.8 17.9 %copy-start.8 = (bf16[512,256]{1,0:T(8,128)(2,1)S(1)}, bf16[512,256]{1,0:T(8,128)(2,1)}, u32[]{:S(2)}) copy-start(bf16[512,256]{1,0:T(8,128)(2,1)} %constant.15.clone.zi_far) | copy-start | bytes 786436

commit v11 on v10

--- a/solution.py
+++ b/solution.py
@@ -35,9 +35,8 @@
     ky = np.arange(MY) - MY // 2
     cy, sy = cos_sin(ky, np.arange(GY), GY)
     rows = np.concatenate([cy, -sy]) / math.sqrt(GY)
-    out["yf"] = np.concatenate(split(rows)).reshape(256, 8, 128).transpose(1, 0, 2)
-    high, low = (half.reshape(128, 8, 128).transpose(1, 0, 2) for half in split(rows))
-    out["yi"] = np.concatenate([high, low], axis=2)
+    out["yf"] = split(rows)[0].reshape(128, 8, 128).transpose(1, 0, 2)
+    out["yi"] = out["yf"]
     cf, sf = (
         np.einsum("kz,cd->czkd", w / math.sqrt(NZ), np.eye(8)).reshape(128, 2, 32)
         for w in cos_sin(np.arange(MZ), np.arange(NZ), NZ)
@@ -51,7 +50,7 @@
     )
     zi = np.zeros((2, 128, 2, 2, 64))
     zi[0, :, :, 0], zi[0, :, :, 1], zi[1, :, :, 0], zi[1, :, :, 1] = ci, -si, si, ci
-    out["zi"] = np.concatenate(split(zi.reshape(256, 256)))
+    out["zi"] = split(zi.reshape(256, 256))[0]
     kx = np.arange(MX) - MX // 2
     cx, sx = cos_sin(kx, np.arange(GX), GX)
     cr = (cx / 8.0).astype(np.float32).astype(jnp.bfloat16).astype(np.float64)
@@ -122,7 +121,7 @@
                 out[field, h, 8 * d : 8 * d + 8, :] = jnp.where(bottom, first, last)
 
 
-def pack_own(f, s, own, rows):
+def pack_own(f, s, after, own, rows):
     edge_rows(f, s, own, rows)
 
 
@@ -284,11 +283,10 @@
                     sums[at : at + 8, 128 * h : 128 * h + 128] = even + odd
     value = sums[...]
     high = value.astype(BF16)
-    rest = value - high.astype(F32)
-    mid, low = halves(rest)
+    low = (value - high.astype(F32)).astype(BF16)
     row, lane = iotas((256, 128))
     table = jnp.where(row // 2 == lane, 0.25, 0.0).astype(BF16)
-    mean = dot(high, table) + dot(mid, table) + dot(low, table)
+    mean = dot(high, table) + dot(low, table)
     keep[...] = mean[:160]
     send[...] = mean[160:]
     for x in range(4):
@@ -297,8 +295,7 @@
         lifted[x] = lift_rows(values, weight, bias)
     copies[0].wait()
     for x in range(4):
-        both = dot(yf[...], lifted[x], ((1,), (1,)))
-        modes[x] = both[:128] + both[128:]
+        modes[x] = dot(yf[...], lifted[x], ((1,), (1,)))
     copies[1].wait()
     parts = []
     for group in range(4):
@@ -322,7 +319,9 @@
             out[rows, :] = total[64 * x : 64 * x + 64]
 
 
-def mix_modes(got, weights, xf, xi, after, out):
+def mix_modes(got, weights_far, xf, xi, after, out, weights, sem):
+    copy = pltpu.make_async_copy(weights_far, weights, sem)
+    copy.start()
     total = got[:, 0]
     for j in range(1, 8):
         total = total + got[:, j]
@@ -338,6 +337,7 @@
     modes = modes[:, :128] + modes[:, 128:]
     real, imag = modes[:128], modes[128:]
     highs, lows = [], []
+    copy.wait()
     for i in range(8):
         wr = weights[8 * i : 8 * i + 8, 0:16, :].astype(F32).reshape(128, 128)
         wi = weights[8 * i : 8 * i + 8, 16:32, :].astype(F32).reshape(128, 128)
@@ -387,23 +387,19 @@
         for x in range(8):
             pair = [rows[pl.ds(16 * a + 8 * part + x, 64, stride=32), :] for a in range(2)]
             stack.append(jnp.concatenate(pair, axis=1).astype(BF16))
-        both = dot(zi[...], jnp.concatenate(stack, axis=0), ((1,), (1,)))
-        by_z.append(both[:256] + both[256:])
+        by_z.append(dot(zi[...], jnp.concatenate(stack, axis=0), ((1,), (1,))))
     blank = jnp.zeros((64, 128), BF16)
 
-    def twice(lanes):
-        real, imag = yi[0:64, lanes], yi[64:128, lanes]
-        pieces = [[real, blank], [blank, real], [imag, blank], [blank, imag]]
-        return jnp.concatenate([jnp.concatenate(row, axis=1) for row in pieces], axis=0)
-
-    t_high, t_low = twice(slice(0, 128)), twice(slice(128, 256))
+    real, imag = yi[0:64, :], yi[64:128, :]
+    pieces = [[real, blank], [blank, real], [imag, blank], [blank, imag]]
+    twice = jnp.concatenate([jnp.concatenate(row, axis=1) for row in pieces], axis=0)
     for pair in range(4):
         lanes = slice(128 * pair, 128 * pair + 128)
         value = jnp.concatenate(
             [jnp.concatenate([v[:128, lanes], v[128:, lanes]], axis=1) for v in by_z], axis=0
         )
         high, low = halves(value)
-        both = dot(high, t_high) + dot(low, t_high) + dot(high, t_low)
+        both = dot(high, twice) + dot(low, twice)
         for x in range(2):
             spectral[pl.ds(2 * pair + x, 256, stride=8), :] = both[:, 128 * x : 128 * x + 128]
     for part in range(2):
@@ -414,7 +410,7 @@
             out[z, 16 * part : 16 * part + 16] = total.reshape(16, 8, 128).astype(BF16)
 
 
-def turn_weights(weights, after, out, wide):
+def turn_weights(weights, out, wide):
     for chunk in range(16):
         turned = weights[128 * chunk : 128 * chunk + 128, :].T
         for ri in range(2):
@@ -436,7 +432,10 @@
     fp, sp = lax.ppermute(f, "ga", swap), lax.ppermute(s, "ga", swap)
     rows = pltpu.VMEM((6, 2, 128, 128), F32)
     edges = ((6, 2, 24, 128), F32)
-    [own] = call(pack_own, [edges], [VMEM] * 2, [rows])(f, s)
+    [turned] = call(
+        turn_weights, [((64, 32, 128), BF16)], [VMEM], [pltpu.VMEM((64, 32, 128), F32)]
+    )(spectral_weight.reshape(2048, 128))
+    [own] = call(pack_own, [edges], [VMEM] * 2 + [anywhere], [rows])(f, s, turned)
     [message] = call(
         pack_other, [((6, 2, 48, 128), F32)], [VMEM] * 3, [pltpu.VMEM(*edges), rows]
     )(fp, sp, own)
@@ -444,13 +443,6 @@
     across += [(2 * i + 1, 2 * ((i + 1) % 8)) for i in range(8)]
     got = lax.ppermute(message, ("gx", "ga"), across)
 
-    [turned] = call(
-        turn_weights,
-        [((64, 32, 128), BF16)],
-        [VMEM, anywhere],
-        [pltpu.VMEM((64, 32, 128), F32)],
-        size=2 * 10**7,
-    )(spectral_weight.reshape(2048, 128), message)
     weights = exchange(turned, ("gx", "gy"))
 
     message = ((3, 16, 128), F32)
@@ -482,7 +474,7 @@
             pltpu.VMEM((320, 256), F32),
             pltpu.VMEM((4, 512, 128), BF16),
             pltpu.VMEM((4, 128, 512), F32),
-            pltpu.VMEM((256, 128), BF16),
+            pltpu.VMEM((128, 128), BF16),
             pltpu.VMEM((256, 256), BF16),
             pltpu.SemaphoreType.DMA((2,)),
         ],
@@ -496,9 +488,12 @@
         flops=3 * 10**8,
     )(keep, lax.ppermute(send, "ga", swap), lift_weight, lift_bias, mix_weight, output_bias.reshape(1, C))
 
-    [mixed] = call(mix_modes, [((8, 8, 2, 16, 128), BF16)], [VMEM] * 4 + [anywhere])(
-        modes.reshape(8, 8, 16, 128), weights, table["xf"], table["xi"], direct
-    )
+    [mixed] = call(
+        mix_modes,
+        [((8, 8, 2, 16, 128), BF16)],
+        [VMEM, anywhere, VMEM, VMEM, anywhere],
+        [pltpu.VMEM((64, 32, 128), BF16), pltpu.SemaphoreType.DMA],
+    )(modes.reshape(8, 8, 16, 128), weights, table["xf"], table["xi"], direct)
     mixed = exchange(mixed.reshape(128, 16, 128), everyone)
     [out] = call(
         finish,
@@ -507,8 +502,8 @@
         [
             pltpu.VMEM((2048, 128), F32),
             pltpu.VMEM((2048, 128), F32),
-            pltpu.VMEM((128, 256), BF16),
-            pltpu.VMEM((512, 256), BF16),
+            pltpu.VMEM((128, 128), BF16),
+            pltpu.VMEM((256, 256), BF16),
             pltpu.SemaphoreType.DMA((2,)),
         ],
     )(mixed.reshape(2048, 128), direct, table["yi"], table["zi"])

time: 80.9 us -> 79 us (0.977)
  Pallas kernels: 18.7 us -> 17.8 us
    unnamed x30 -> x24, local copies, waits for them, and re-layouts: 2.7 us -> 1.92 us
where the time goes in v11:
time: 79 us; the launch traced here: 78.6 us
  starting transfers between devices  26.2 us (33%)
  blocking collectives  17.9 us (23%)
  Pallas kernels  17.8 us (23%)
  waiting for transfers between devices  14.5 us (18%)
  local copies, waits for them, and re-layouts  1.92 us (2%)
    all_to_all x1, blocking collectives, exchange(): return lax.all_to_all(value, axis, split_axis=0, concat_axis=0, tiled=True)  17.9 us
    all_to_all x2, starting transfers between devices, exchange(): return lax.all_to_all(value, axis, split_axis=0, concat_axis=0, tiled=True)  17 us
    all_to_all x2, waiting for transfers between devices, exchange(): return lax.all_to_all(value, axis, split_axis=0, concat_axis=0, tiled=True)  7.75 us
    ppermute x1, waiting for transfers between devices, shards(): lax.ppermute(far, 'gy', [(j, (j - 1 + 2 * (j % 2)) % 8) for j in range(8)])  5.79 us
    ppermute x1, starting transfers between devices, shards(): lax.ppermute(far, 'gy', [(j, (j - 1 + 2 * (j % 2)) % 8) for j in range(8)])  4.63 us
    pallas_call x1, Pallas kernels, shards(): call(stencil, [((5, 2, 128, 128), F32)], [VMEM] * 7, [pltpu.VMEM((5, 16,...  3.92 us
    pallas_call x1, Pallas kernels, shards(): call(forward, [((160, 128), F32), ((160, 128), F32), ((1024, 128), F32)],...  3.84 us
    pallas_call x1, Pallas kernels, shards(): call(pointwise, [((8, 256, 128), F32)], [VMEM, VMEM, SMEM, SMEM, VMEM, VM...  3.18 us
  transfers between devices with their start and end apart: 8, of which 3 were waited for; matrix products, arithmetic and copies ran while one was open for 0% of the time, Pallas kernels for 12%

profile of v11, /device:TPU:1, one launch (start us, length us, event | category | flops | bytes accessed | tf_op | source)
XLA Modules:
  0.0 78.6 jit_solution(13020046885114101148)
XLA Ops:
  0.0 1.4 %collective-permute-start = (f32[5,128,256]{2,1,0:T(8,128)}, f32[5,128,256]{2,1,0:T(8,128)S(1)}, u32[]{:S(2)}, u32[]{:S(2)}) collective-permute-start(f32[5,128,256]{2,1,0:T(8,128)} %bitcast.8), channel_id=1, source_target_pairs={{0,1},{1,0},{2,3},{3,2},{4,5},{5,4},{6,7},{7,6},{8,9},{9,8},{10,11... | collective-permute-start | bytes 1966088 | tf_op jit(solution)/shard_map/ppermute | solution.py:432
  1.4 0.0 collective-permute-start.1
  1.4 0.0 copy-start.1
  1.4 1.2 %copy-done.1 = f32[4,4,32,4,128]{4,3,2,1,0:T(4,128)S(1)} copy-done((f32[4,4,32,4,128]{4,3,2,1,0:T(4,128)S(1)}, f32[4,4,32,4,128]{4,3,2,1,0:T(4,128)}, u32[]{:S(2)}) %copy-start.1) | copy-done | bytes 1048600
  2.7 0.0 copy-start
  2.7 0.0 copy-start.3
  2.7 1.6 %shard_map.118.after = bf16[64,32,128]{2,1,0:T(8,128)(2,1)} custom-call(f32[2048,128]{1,0:T(8,128)S(1)} %bitcast.15), custom_call_target="tpu_custom_call" | custom-call | flops 10000000 | bytes 1048576 | tf_op jit(solution)/shard_map/pallas_call | solution.py:435
  4.2 0.0 copy-done
  4.2 0.0 copy-done.3
  4.2 0.1 shard_map.119.own
  4.4 0.0 collective-permute-done.1.sp
  4.4 0.0 collective-permute-done.fp
  4.4 0.1 shard_map.120
  4.6 1.8 %collective-permute-start.2 = (f32[6,2,48,128]{3,2,1,0:T(8,128)S(1)}, f32[6,2,48,128]{3,2,1,0:T(8,128)S(1)}, u32[]{:S(2)}, u32[]{:S(2)}) collective-permute-start(f32[6,2,48,128]{3,2,1,0:T(8,128)S(1)} %shard_map.120), channel_id=1, source_target_pairs={{0,113},{16,1},{32,17},{48,33},{64,49},{80,65},{96,81},{112,97},{1... | collective-permute-start | bytes 884744 | tf_op jit(solution)/shard_map/ppermute | solution.py:444
  6.3 11.2 %all-to-all-start = ((bf16[64,32,128]{2,1,0:T(8,128)(2,1)}), bf16[64,32,128]{2,1,0:T(8,128)(2,1)}, u32[]{:S(2)}, u32[]{:S(2)}) async-start(bf16[64,32,128]{2,1,0:T(8,128)(2,1)} %shard_map.118.after), calls=%async_computation | async-start | bytes 1048576 | tf_op jit(solution)/shard_map/all_to_all | solution.py:426
  17.5 0.0 collective-permute-done.2.message.got
  17.5 0.5 shard_map.121
  18.1 4.6 %collective-permute-start.3 = (f32[3,16,128]{2,1,0:T(8,128)S(1)}, f32[3,16,128]{2,1,0:T(8,128)S(1)}, u32[]{:S(2)}, u32[]{:S(2)}) collective-permute-start(f32[3,16,128]{2,1,0:T(8,128)S(1)} %get-tuple-element.10), channel_id=1, source_target_pairs={{0,14},{2,4},{4,2},{6,8},{8,6},{10,12},{12,10},{14,0},{1,15},{3,5}... | collective-permute-start | bytes 73736 | tf_op jit(solution)/shard_map/ppermute | solution.py:456
  22.7 0.0 copy-start.2
  22.7 0.0 copy-start.7
  22.7 0.0 copy-start.8
  22.7 0.0 copy-start.10
  22.7 0.1 collective-permute-start.4
  22.8 5.8 %collective-permute-done.3.far = f32[3,16,128]{2,1,0:T(8,128)S(1)} collective-permute-done((f32[3,16,128]{2,1,0:T(8,128)S(1)}, f32[3,16,128]{2,1,0:T(8,128)S(1)}, u32[]{:S(2)}, u32[]{:S(2)}) %collective-permute-start.3) | collective-permute-done | bytes 24608 | tf_op jit(solution)/shard_map/ppermute | solution.py:456
  28.6 0.0 collective-permute-done.4.near
  28.6 3.9 %shard_map.122.last = f32[5,2,128,128]{3,2,1,0:T(8,128)S(1)} custom-call(f32[5,128,256]{2,1,0:T(8,128)S(1)} %bitcast.11, f32[128,256]{1,0:T(8,128)S(1)} %bitcast.19, f32[5,128,256]{2,1,0:T(8,128)S(1)} %collective-permute-done.fp, f32[128,256]{1,0:T(8,128)S(1)} %collective-permute-done.1.sp, f32[6,2,48,128]{3,2,1,0:T(8,128)S(1)} %collective-permute-done.2.message.got, ...), custom_call_target="tpu_custom_call" | custom-call | flops 10000000 | bytes 1048576 | tf_op jit(solution)/shard_map/pallas_call | solution.py:458
  32.5 0.0 all-to-all-done.after.weights_far
  32.5 0.0 copy-done.2
  32.6 0.0 copy-done.7
  32.6 0.0 copy-done.8
  32.6 0.0 copy-done.10
  32.6 3.8 %shard_map.123 = (f32[160,128]{1,0:T(8,128)S(1)}, f32[160,128]{1,0:T(8,128)S(1)}, f32[1024,128]{1,0:T(8,128)}) custom-call(f32[5,2,128,128]{3,2,1,0:T(8,128)S(1)} %shard_map.122.last, bf16[64,32,128]{2,1,0:T(8,128)(2,1)} %all-to-all-done.after.weights_far, f32[5,32]{1,0:T(8,128)S(1)} %copy-done.8, f32[32]{0:T(128)S(1)} %copy-done.10, ...), custom_call_target="tpu_custom_call" | custom-call | flops 10000000 | bytes 1048576 | tf_op jit(solution)/shard_map/pallas_call | solution.py:469
  36.4 0.0 copy-start.9
  36.5 5.8 %all-to-all-start.1 = ((f32[128,8,128]{2,1,0:T(8,128)}), f32[128,8,128]{2,1,0:T(8,128)S(1)}, u32[]{:S(2)}, u32[]{:S(2)}) async-start(f32[128,8,128]{2,1,0:T(8,128)} %bitcast.3), calls=%async_computation.1 | async-start | bytes 1048576 | tf_op jit(solution)/shard_map/all_to_all | solution.py:426
  42.3 1.3 %collective-permute-start.5 = (f32[160,128]{1,0:T(8,128)S(1)}, f32[160,128]{1,0:T(8,128)S(1)}, u32[]{:S(2)}, u32[]{:S(2)}) collective-permute-start(f32[160,128]{1,0:T(8,128)S(1)} %get-tuple-element.14), channel_id=1, source_target_pairs={{0,1},{1,0},{2,3},{3,2},{4,5},{5,4},{6,7},{7,6},{8,9},{9,8},{10,11... | collective-permute-start | bytes 245768 | tf_op jit(solution)/shard_map/ppermute | solution.py:489
  43.6 0.9 %collective-permute-done.5.got = f32[160,128]{1,0:T(8,128)S(1)} collective-permute-done((f32[160,128]{1,0:T(8,128)S(1)}, f32[160,128]{1,0:T(8,128)S(1)}, u32[]{:S(2)}, u32[]{:S(2)}) %collective-permute-start.5) | collective-permute-done | bytes 81952 | tf_op jit(solution)/shard_map/ppermute | solution.py:489
  44.5 0.0 copy-start.11
  44.5 0.0 copy-done.9
  44.5 0.7 copy-done.11
  45.2 3.2 %shard_map.124.after.direct = f32[8,256,128]{2,1,0:T(8,128)S(1)} custom-call(f32[160,128]{1,0:T(8,128)S(1)} %get-tuple-element.13.keep, f32[160,128]{1,0:T(8,128)S(1)} %collective-permute-done.5.got, f32[5,32]{1,0:T(8,128)S(1)} %copy-done.8, f32[32]{0:T(128)S(1)} %copy-done.10, bf16[32,32]{1,0:T(8,128)(2,1)S(1)} %copy-done.9, f32[1,32]{1,0:T(1,128)S(1)} %bitcast.20), custom_call_target="tpu_custom_call" | custom-call | flops 300000000 | bytes 1048576 | tf_op jit(solution)/shard_map/pallas_call | solution.py:483
  48.4 7.8 %all-to-all-done.1 = f32[128,8,128]{2,1,0:T(8,128)S(1)} async-done(((f32[128,8,128]{2,1,0:T(8,128)}), f32[128,8,128]{2,1,0:T(8,128)S(1)}, u32[]{:S(2)}, u32[]{:S(2)}) %all-to-all-start.1) | async-done | bytes 524320 | tf_op jit(solution)/shard_map/all_to_all | solution.py:426
  56.1 0.0 copy-done.4
  56.1 0.0 copy-done.6
  56.1 1.9 %shard_map.125 = bf16[8,8,2,16,128]{4,3,2,1,0:T(8,128)(2,1)S(1)} custom-call(f32[8,8,16,128]{3,2,1,0:T(8,128)S(1)} %bitcast.13, bf16[64,32,128]{2,1,0:T(8,128)(2,1)} %all-to-all-done.after.weights_far, bf16[256,512]{1,0:T(8,128)(2,1)S(1)} %copy-done.4, bf16[256,256]{1,0:T(8,128)(2,1)S(1)} %copy-done.6, f32[8,256,128]{2,1,0:T(8,128)S(1)} %shard_map.124.after.direct), custom_call_target="tpu_custom_call" | custom-call | flops 10000000 | bytes 1048576 | tf_op jit(solution)/shard_map/pallas_call | solution.py:491
  58.0 0.0 copy-start.5
  58.1 17.9 %all_to_all.15 = bf16[128,16,128]{2,1,0:T(8,128)(2,1)S(1)} all-to-all(bf16[128,16,128]{2,1,0:T(8,128)(2,1)S(1)} %bitcast.14), channel_id=1, replica_groups=mesh['gx'=8,'gy'=8,'ga'=2] {'gx','gy','ga'}, dimensions={0} | all-to-all | bytes 1048576 | tf_op jit(solution)/shard_map/all_to_all | solution.py:426
  75.9 0.0 copy-done.5
  75.9 2.5 %shard_map.126 = bf16[8,32,8,128]{3,2,1,0:T(8,128)(2,1)} custom-call(bf16[2048,128]{1,0:T(8,128)(2,1)S(1)} %bitcast.12, f32[8,256,128]{2,1,0:T(8,128)S(1)} %shard_map.124.after.direct, bf16[8,128,128]{2,1,0:T(8,128)(2,1)S(1)} %copy-done.2, bf16[256,256]{1,0:T(8,128)(2,1)S(1)} %copy-done.5), custom_call_target="tpu_custom_call" | custom-call | flops 10000000 | bytes 1048576 | tf_op jit(solution)/shard_map/pallas_call | solution.py:498
  (2 shorter events, 0.0 us)
Async XLA Ops:
  0.0 4.4 %collective-permute-start = (f32[5,128,256]{2,1,0:T(8,128)}, f32[5,128,256]{2,1,0:T(8,128)S(1)}, u32[]{:S(2)}, u32[]{:S(2)}) collective-permute-start(f32[5,128,256]{2,1,0:T(8,128)} %bitcast.8), channel_id=1, source_target_pairs={{0,1},{1,0},{2,3},{3,2},{4,5},{5,4},{6,7},{7,6},{8,9},{9,8},{10,11... | collective-permute-start | bytes 1966088 | tf_op jit(solution)/shard_map/ppermute | solution.py:432
  1.4 3.0 %collective-permute-start.1 = (f32[128,256]{1,0:T(8,128)}, f32[128,256]{1,0:T(8,128)S(1)}, u32[]{:S(2)}, u32[]{:S(2)}) collective-permute-start(f32[128,256]{1,0:T(8,128)} %bitcast.16), channel_id=1, source_target_pairs={{0,1},{1,0},{2,3},{3,2},{4,5},{5,4},{6,7},{7,6},{8,9},{9,8},{10,11... | collective-permute-start | bytes 393224 | tf_op jit(solution)/shard_map/ppermute | solution.py:432
  1.4 1.2 %copy-start.1 = (f32[4,4,32,4,128]{4,3,2,1,0:T(4,128)S(1)}, f32[4,4,32,4,128]{4,3,2,1,0:T(4,128)}, u32[]{:S(2)}) copy-start(f32[4,4,32,4,128]{4,3,2,1,0:T(4,128)} %param.17) | copy-start | bytes 3145732
  2.7 1.6 %copy-start = (f32[5,8,16,256]{3,2,1,0:T(8,128)S(1)}, f32[5,8,16,256]{3,2,1,0:T(8,128)}, u32[]{:S(2)}) copy-start(f32[5,8,16,256]{3,2,1,0:T(8,128)} %param.12) | copy-start | bytes 1966084
  2.7 1.6 %copy-start.3 = (f32[8,16,256]{2,1,0:T(8,128)S(1)}, f32[8,16,256]{2,1,0:T(8,128)}, u32[]{:S(2)}) copy-start(f32[8,16,256]{2,1,0:T(8,128)} %param.13) | copy-start | bytes 393220
  4.6 13.0 %collective-permute-start.2 = (f32[6,2,48,128]{3,2,1,0:T(8,128)S(1)}, f32[6,2,48,128]{3,2,1,0:T(8,128)S(1)}, u32[]{:S(2)}, u32[]{:S(2)}) collective-permute-start(f32[6,2,48,128]{3,2,1,0:T(8,128)S(1)} %shard_map.120), channel_id=1, source_target_pairs={{0,113},{16,1},{32,17},{48,33},{64,49},{80,65},{96,81},{112,97},{1... | collective-permute-start | bytes 884744 | tf_op jit(solution)/shard_map/ppermute | solution.py:444
  6.3 26.2 %all-to-all-start = ((bf16[64,32,128]{2,1,0:T(8,128)(2,1)}), bf16[64,32,128]{2,1,0:T(8,128)(2,1)}, u32[]{:S(2)}, u32[]{:S(2)}) async-start(bf16[64,32,128]{2,1,0:T(8,128)(2,1)} %shard_map.118.after), calls=%async_computation | async-start | bytes 1048576 | tf_op jit(solution)/shard_map/all_to_all | solution.py:426
  18.1 10.5 %collective-permute-start.3 = (f32[3,16,128]{2,1,0:T(8,128)S(1)}, f32[3,16,128]{2,1,0:T(8,128)S(1)}, u32[]{:S(2)}, u32[]{:S(2)}) collective-permute-start(f32[3,16,128]{2,1,0:T(8,128)S(1)} %get-tuple-element.10), channel_id=1, source_target_pairs={{0,14},{2,4},{4,2},{6,8},{8,6},{10,12},{12,10},{14,0},{1,15},{3,5}... | collective-permute-start | bytes 73736 | tf_op jit(solution)/shard_map/ppermute | solution.py:456
  22.7 9.8 %copy-start.2 = (bf16[8,128,128]{2,1,0:T(8,128)(2,1)S(1)}, bf16[8,128,128]{2,1,0:T(8,128)(2,1)}, u32[]{:S(2)}) copy-start(bf16[8,128,128]{2,1,0:T(8,128)(2,1)} %constant.10.clone.yf_far.yi_far) | copy-start | bytes 786436
  22.7 9.8 %copy-start.7 = (bf16[256,256]{1,0:T(8,128)(2,1)S(1)}, bf16[256,256]{1,0:T(8,128)(2,1)}, u32[]{:S(2)}) copy-start(bf16[256,256]{1,0:T(8,128)(2,1)} %constant.11.clone.zf_far) | copy-start | bytes 393220
  22.7 9.9 %copy-start.8 = (f32[5,32]{1,0:T(8,128)S(1)}, f32[5,32]{1,0:T(8,128)}, u32[]{:S(2)}) copy-start(f32[5,32]{1,0:T(8,128)} %weight.3) | copy-start | bytes 1924
  22.7 9.9 %copy-start.10 = (f32[32]{0:T(128)S(1)}, f32[32]{0:T(128)}, u32[]{:S(2)}) copy-start(f32[32]{0:T(128)} %bias.3) | copy-start | bytes 388
  22.7 5.9 %collective-permute-start.4 = (f32[3,16,128]{2,1,0:T(8,128)S(1)}, f32[3,16,128]{2,1,0:T(8,128)S(1)}, u32[]{:S(2)}, u32[]{:S(2)}) collective-permute-start(f32[3,16,128]{2,1,0:T(8,128)S(1)} %get-tuple-element.11), channel_id=1, source_target_pairs={{0,2},{2,0},{4,6},{6,4},{8,10},{10,8},{12,14},{14,12},{1,3},{3,1},... | collective-permute-start | bytes 73736 | tf_op jit(solution)/shard_map/ppermute | solution.py:457
  36.4 8.1 %copy-start.9 = (bf16[32,32]{1,0:T(8,128)(2,1)S(1)}, bf16[32,32]{1,0:T(8,128)(2,1)}, u32[]{:S(2)}) copy-start(bf16[32,32]{1,0:T(8,128)(2,1)} %mix.1) | copy-start | bytes 6148
  36.5 19.7 %all-to-all-start.1 = ((f32[128,8,128]{2,1,0:T(8,128)}), f32[128,8,128]{2,1,0:T(8,128)S(1)}, u32[]{:S(2)}, u32[]{:S(2)}) async-start(f32[128,8,128]{2,1,0:T(8,128)} %bitcast.3), calls=%async_computation.1 | async-start | bytes 1048576 | tf_op jit(solution)/shard_map/all_to_all | solution.py:426
  42.3 2.3 %collective-permute-start.5 = (f32[160,128]{1,0:T(8,128)S(1)}, f32[160,128]{1,0:T(8,128)S(1)}, u32[]{:S(2)}, u32[]{:S(2)}) collective-permute-start(f32[160,128]{1,0:T(8,128)S(1)} %get-tuple-element.14), channel_id=1, source_target_pairs={{0,1},{1,0},{2,3},{3,2},{4,5},{5,4},{6,7},{7,6},{8,9},{9,8},{10,11... | collective-permute-start | bytes 245768 | tf_op jit(solution)/shard_map/ppermute | solution.py:489
  44.5 0.7 copy-start.11
  45.2 10.9 %copy-start.4 = (bf16[256,512]{1,0:T(8,128)(2,1)S(1)}, bf16[256,512]{1,0:T(8,128)(2,1)}, u32[]{:S(2)}) copy-start(bf16[256,512]{1,0:T(8,128)(2,1)} %constant.13.clone.xf) | copy-start | bytes 786436
  45.2 10.9 %copy-start.6 = (bf16[256,256]{1,0:T(8,128)(2,1)S(1)}, bf16[256,256]{1,0:T(8,128)(2,1)}, u32[]{:S(2)}) copy-start(bf16[256,256]{1,0:T(8,128)(2,1)} %constant.14.clone.xi) | copy-start | bytes 393220
  58.0 17.9 %copy-start.5 = (bf16[256,256]{1,0:T(8,128)(2,1)S(1)}, bf16[256,256]{1,0:T(8,128)(2,1)}, u32[]{:S(2)}) copy-start(bf16[256,256]{1,0:T(8,128)(2,1)} %constant.12.clone.zi_far) | copy-start | bytes 393220

commit v12 on v11

--- a/solution.py
+++ b/solution.py
@@ -90,12 +90,12 @@
     return 0.5 * v * (1.0 + jnp.tanh(ROOT * (v + 0.044715 * (v * v * v))))
 
 
-def call(kernel, outs, in_specs, scratch=(), mib=16, flops=10**7, size=2**20):
+def call(kernel, outs, in_specs, scratch=(), mib=16, flops=10**7, size=2**20, out_spec=VMEM):
     return pl.pallas_call(
         kernel,
         out_shape=[jax.ShapeDtypeStruct(s, d) for s, d in outs],
         in_specs=in_specs,
-        out_specs=[VMEM] * len(outs),
+        out_specs=[out_spec] * len(outs),
         scratch_shapes=list(scratch),
         compiler_params=pltpu.CompilerParams(vmem_limit_bytes=mib << 20),
         cost_estimate=pl.CostEstimate(flops=flops, bytes_accessed=size, transcendentals=0),
@@ -131,7 +131,7 @@
     message[:, :, 24:48, :] = other[...]
 
 
-def pack_y(f, s, fp, sp, message, far, near, outer):
+def pack_y(f, s, fp, sp, message, near, far, outer):
     refs = (f, s, fp, sp)
     a = lax.axis_index("ga")
     row = lax.broadcasted_iota(jnp.int32, (8, 128), 0)
@@ -165,7 +165,7 @@
             near[field // 2] = jnp.where(even, highs, lows)
 
 
-def stencil(f, s, fp, sp, got, far, near, last, a, b, stiff, outer):
+def stencil(f, s, fp, sp, got, near, far, last, a, b, stiff, outer):
     refs = (f, s, fp, sp)
     core = lax.axis_index("ga")
     even = lax.axis_index("gy") % 2 == 0
@@ -371,7 +371,7 @@
                 out[i, j, a] = tile
 
 
-def finish(got, direct, yi_far, zi_far, out, rows, spectral, yi, zi, sems):
+def finish(got, direct, yi_far, zi_far, out_far, rows, spectral, yi, zi, out, sems, out_sems):
     copies = [
         pltpu.make_async_copy(yi_far.at[lax.axis_index("gy")], yi, sems.at[0]),
         pltpu.make_async_copy(zi_far, zi, sems.at[1]),
@@ -379,8 +379,7 @@
     for copy in copies:
         copy.start()
     rows[...] = got[...].astype(F32)
-    for copy in copies:
-        copy.wait()
+    copies[1].wait()
     by_z = []
     for part in range(2):
         stack = []
@@ -390,6 +389,7 @@
         by_z.append(dot(zi[...], jnp.concatenate(stack, axis=0), ((1,), (1,))))
     blank = jnp.zeros((64, 128), BF16)
 
+    copies[0].wait()
     real, imag = yi[0:64, :], yi[64:128, :]
     pieces = [[real, blank], [blank, real], [imag, blank], [blank, imag]]
     twice = jnp.concatenate([jnp.concatenate(row, axis=1) for row in pieces], axis=0)
@@ -402,12 +402,17 @@
         both = dot(high, twice) + dot(low, twice)
         for x in range(2):
             spectral[pl.ds(2 * pair + x, 256, stride=8), :] = both[:, 128 * x : 128 * x + 128]
-    for part in range(2):
-        for z in range(ZL):
+    writes = []
+    for z in range(ZL):
+        for part in range(2):
             at = 128 * (8 * part + z)
             branch = spectral[at : at + 128, :].astype(BF16).astype(F32)
             total = gelu(direct[z, 128 * part : 128 * part + 128, :] + branch)
             out[z, 16 * part : 16 * part + 16] = total.reshape(16, 8, 128).astype(BF16)
+        writes.append(pltpu.make_async_copy(out.at[z], out_far.at[z], out_sems.at[z]))
+        writes[z].start()
+    for write in writes:
+        write.wait()
 
 
 def turn_weights(weights, out, wide):
@@ -446,15 +451,15 @@
     weights = exchange(turned, ("gx", "gy"))
 
     message = ((3, 16, 128), F32)
-    far, near = call(
+    near, far = call(
         pack_y,
         [message, message],
         [VMEM] * 5,
         [pltpu.VMEM((6, 2, 128, 128), F32)],
         flops=10**12,
     )(f, s, fp, sp, got)
+    near = lax.ppermute(near, "gy", [(j, j + 1 - 2 * (j % 2)) for j in range(8)])
     far = lax.ppermute(far, "gy", [(j, (j - 1 + 2 * (j % 2)) % 8) for j in range(8)])
-    near = lax.ppermute(near, "gy", [(j, j + 1 - 2 * (j % 2)) for j in range(8)])
     [last] = call(
         stencil,
         [((5, 2, 128, 128), F32)],
@@ -465,7 +470,7 @@
             pltpu.VMEM((16, 16, 384), F32),
             pltpu.VMEM((2, 128, 128), F32),
         ],
-    )(f, s, fp, sp, got, far, near)
+    )(f, s, fp, sp, got, near, far)
     keep, send, modes = call(
         forward,
         [((160, 128), F32), ((160, 128), F32), ((1024, 128), F32)],
@@ -504,8 +509,11 @@
             pltpu.VMEM((2048, 128), F32),
             pltpu.VMEM((128, 128), BF16),
             pltpu.VMEM((256, 256), BF16),
+            pltpu.VMEM((8, 32, 8, 128), BF16),
             pltpu.SemaphoreType.DMA((2,)),
+            pltpu.SemaphoreType.DMA((8,)),
         ],
+        out_spec=anywhere,
     )(mixed.reshape(2048, 128), direct, table["yi"], table["zi"])
     return out
 

time: 79 us -> 79.8 us (1.010)
  starting transfers between devices: 26.2 us -> 27.6 us
    ppermute x1, starting transfers between devices: 0.09 us -> 1.02 us  [shards(): lax.ppermute(near, 'gy', [(j, j + 1 - 2 * (j % 2)) for j in range(8)])]
where the time goes in v12:
time: 79.8 us; the launch traced here: 79.4 us
  starting transfers between devices  27.6 us (35%)
  blocking collectives  17.9 us (22%)
  Pallas kernels  17.8 us (22%)
  waiting for transfers between devices  13.9 us (17%)
  local copies, waits for them, and re-layouts  1.92 us (2%)
    all_to_all x1, blocking collectives, exchange(): return lax.all_to_all(value, axis, split_axis=0, concat_axis=0, tiled=True)  17.9 us
    all_to_all x2, starting transfers between devices, exchange(): return lax.all_to_all(value, axis, split_axis=0, concat_axis=0, tiled=True)  17.8 us
    all_to_all x2, waiting for transfers between devices, exchange(): return lax.all_to_all(value, axis, split_axis=0, concat_axis=0, tiled=True)  7.75 us
    ppermute x1, waiting for transfers between devices, shards(): lax.ppermute(far, 'gy', [(j, (j - 1 + 2 * (j % 2)) % 8) for j in range(8)])  5.23 us
    ppermute x1, starting transfers between devices, shards(): lax.ppermute(far, 'gy', [(j, (j - 1 + 2 * (j % 2)) % 8) for j in range(8)])  4.27 us
    pallas_call x1, Pallas kernels, shards(): call(stencil, [((5, 2, 128, 128), F32)], [VMEM] * 7, [pltpu.VMEM((5, 16,...  3.92 us
    pallas_call x1, Pallas kernels, shards(): call(forward, [((160, 128), F32), ((160, 128), F32), ((1024, 128), F32)],...  3.84 us
    pallas_call x1, Pallas kernels, shards(): call(pointwise, [((8, 256, 128), F32)], [VMEM, VMEM, SMEM, SMEM, VMEM, VM...  3.18 us
  transfers between devices with their start and end apart: 8, of which 3 were waited for; matrix products, arithmetic and copies ran while one was open for 0% of the time, Pallas kernels for 12%

profile of v12, /device:TPU:1, one launch (start us, length us, event | category | flops | bytes accessed | tf_op | source)
XLA Modules:
  0.0 79.4 jit_solution(1341389870048479984)
XLA Ops:
  0.0 1.4 %collective-permute-start = (f32[5,128,256]{2,1,0:T(8,128)}, f32[5,128,256]{2,1,0:T(8,128)S(1)}, u32[]{:S(2)}, u32[]{:S(2)}) collective-permute-start(f32[5,128,256]{2,1,0:T(8,128)} %bitcast.8), channel_id=1, source_target_pairs={{0,1},{1,0},{2,3},{3,2},{4,5},{5,4},{6,7},{7,6},{8,9},{9,8},{10,11... | collective-permute-start | bytes 1966088 | tf_op jit(solution)/shard_map/ppermute | solution.py:437
  1.4 0.0 collective-permute-start.1
  1.4 0.0 copy-start.1
  1.4 1.2 %copy-done.1 = f32[4,4,32,4,128]{4,3,2,1,0:T(4,128)S(1)} copy-done((f32[4,4,32,4,128]{4,3,2,1,0:T(4,128)S(1)}, f32[4,4,32,4,128]{4,3,2,1,0:T(4,128)}, u32[]{:S(2)}) %copy-start.1) | copy-done | bytes 1048600
  2.7 0.0 copy-start
  2.7 0.0 copy-start.3
  2.7 1.6 %shard_map.118.after = bf16[64,32,128]{2,1,0:T(8,128)(2,1)} custom-call(f32[2048,128]{1,0:T(8,128)S(1)} %bitcast.15), custom_call_target="tpu_custom_call" | custom-call | flops 10000000 | bytes 1048576 | tf_op jit(solution)/shard_map/pallas_call | solution.py:440
  4.2 0.0 copy-done
  4.2 0.0 copy-done.3
  4.2 0.1 shard_map.119.own
  4.4 0.0 collective-permute-done.1.sp
  4.4 0.0 collective-permute-done.fp
  4.4 0.1 shard_map.120
  4.6 1.8 %collective-permute-start.2 = (f32[6,2,48,128]{3,2,1,0:T(8,128)S(1)}, f32[6,2,48,128]{3,2,1,0:T(8,128)S(1)}, u32[]{:S(2)}, u32[]{:S(2)}) collective-permute-start(f32[6,2,48,128]{3,2,1,0:T(8,128)S(1)} %shard_map.120), channel_id=1, source_target_pairs={{0,113},{16,1},{32,17},{48,33},{64,49},{80,65},{96,81},{112,97},{1... | collective-permute-start | bytes 884744 | tf_op jit(solution)/shard_map/ppermute | solution.py:449
  6.3 11.2 %all-to-all-start = ((bf16[64,32,128]{2,1,0:T(8,128)(2,1)}), bf16[64,32,128]{2,1,0:T(8,128)(2,1)}, u32[]{:S(2)}, u32[]{:S(2)}) async-start(bf16[64,32,128]{2,1,0:T(8,128)(2,1)} %shard_map.118.after), calls=%async_computation | async-start | bytes 1048576 | tf_op jit(solution)/shard_map/all_to_all | solution.py:431
  17.5 0.0 collective-permute-done.2.message.got
  17.5 0.5 shard_map.121
  18.1 1.0 %collective-permute-start.3 = (f32[3,16,128]{2,1,0:T(8,128)S(1)}, f32[3,16,128]{2,1,0:T(8,128)S(1)}, u32[]{:S(2)}, u32[]{:S(2)}) collective-permute-start(f32[3,16,128]{2,1,0:T(8,128)S(1)} %get-tuple-element.10), channel_id=1, source_target_pairs={{0,2},{2,0},{4,6},{6,4},{8,10},{10,8},{12,14},{14,12},{1,3},{3,1},... | collective-permute-start | bytes 73736 | tf_op jit(solution)/shard_map/ppermute | solution.py:461
  19.1 0.0 copy-start.2
  19.1 0.0 copy-start.7
  19.1 0.0 copy-start.8
  19.1 0.0 copy-start.10
  19.1 4.3 %collective-permute-start.4 = (f32[3,16,128]{2,1,0:T(8,128)S(1)}, f32[3,16,128]{2,1,0:T(8,128)S(1)}, u32[]{:S(2)}, u32[]{:S(2)}) collective-permute-start(f32[3,16,128]{2,1,0:T(8,128)S(1)} %get-tuple-element.11), channel_id=1, source_target_pairs={{0,14},{2,4},{4,2},{6,8},{8,6},{10,12},{12,10},{14,0},{1,15},{3,5}... | collective-permute-start | bytes 73736 | tf_op jit(solution)/shard_map/ppermute | solution.py:462
  23.4 0.0 collective-permute-done.3.near
  23.4 5.2 %collective-permute-done.4.far = f32[3,16,128]{2,1,0:T(8,128)S(1)} collective-permute-done((f32[3,16,128]{2,1,0:T(8,128)S(1)}, f32[3,16,128]{2,1,0:T(8,128)S(1)}, u32[]{:S(2)}, u32[]{:S(2)}) %collective-permute-start.4) | collective-permute-done | bytes 24608 | tf_op jit(solution)/shard_map/ppermute | solution.py:462
  28.6 3.9 %shard_map.122.last = f32[5,2,128,128]{3,2,1,0:T(8,128)S(1)} custom-call(f32[5,128,256]{2,1,0:T(8,128)S(1)} %bitcast.11, f32[128,256]{1,0:T(8,128)S(1)} %bitcast.19, f32[5,128,256]{2,1,0:T(8,128)S(1)} %collective-permute-done.fp, f32[128,256]{1,0:T(8,128)S(1)} %collective-permute-done.1.sp, f32[6,2,48,128]{3,2,1,0:T(8,128)S(1)} %collective-permute-done.2.message.got, ...), custom_call_target="tpu_custom_call" | custom-call | flops 10000000 | bytes 1048576 | tf_op jit(solution)/shard_map/pallas_call | solution.py:463
  32.5 0.0 all-to-all-done.after.weights_far
  32.5 0.0 copy-done.2
  32.6 0.0 copy-done.7
  32.6 0.0 copy-done.8
  32.6 0.0 copy-done.10
  32.6 3.8 %shard_map.123 = (f32[160,128]{1,0:T(8,128)S(1)}, f32[160,128]{1,0:T(8,128)S(1)}, f32[1024,128]{1,0:T(8,128)}) custom-call(f32[5,2,128,128]{3,2,1,0:T(8,128)S(1)} %shard_map.122.last, bf16[64,32,128]{2,1,0:T(8,128)(2,1)} %all-to-all-done.after.weights_far, f32[5,32]{1,0:T(8,128)S(1)} %copy-done.8, f32[32]{0:T(128)S(1)} %copy-done.10, ...), custom_call_target="tpu_custom_call" | custom-call | flops 10000000 | bytes 1048576 | tf_op jit(solution)/shard_map/pallas_call | solution.py:474
  36.4 0.0 copy-start.9
  36.4 6.6 %all-to-all-start.1 = ((f32[128,8,128]{2,1,0:T(8,128)}), f32[128,8,128]{2,1,0:T(8,128)S(1)}, u32[]{:S(2)}, u32[]{:S(2)}) async-start(f32[128,8,128]{2,1,0:T(8,128)} %bitcast.3), calls=%async_computation.1 | async-start | bytes 1048576 | tf_op jit(solution)/shard_map/all_to_all | solution.py:431
  43.1 1.3 %collective-permute-start.5 = (f32[160,128]{1,0:T(8,128)S(1)}, f32[160,128]{1,0:T(8,128)S(1)}, u32[]{:S(2)}, u32[]{:S(2)}) collective-permute-start(f32[160,128]{1,0:T(8,128)S(1)} %get-tuple-element.14), channel_id=1, source_target_pairs={{0,1},{1,0},{2,3},{3,2},{4,5},{5,4},{6,7},{7,6},{8,9},{9,8},{10,11... | collective-permute-start | bytes 245768 | tf_op jit(solution)/shard_map/ppermute | solution.py:494
  44.4 0.9 %collective-permute-done.5.got = f32[160,128]{1,0:T(8,128)S(1)} collective-permute-done((f32[160,128]{1,0:T(8,128)S(1)}, f32[160,128]{1,0:T(8,128)S(1)}, u32[]{:S(2)}, u32[]{:S(2)}) %collective-permute-start.5) | collective-permute-done | bytes 81952 | tf_op jit(solution)/shard_map/ppermute | solution.py:494
  45.3 0.0 copy-start.11
  45.3 0.0 copy-done.9
  45.3 0.7 copy-done.11
  46.0 3.2 %shard_map.124.after.direct = f32[8,256,128]{2,1,0:T(8,128)S(1)} custom-call(f32[160,128]{1,0:T(8,128)S(1)} %get-tuple-element.13.keep, f32[160,128]{1,0:T(8,128)S(1)} %collective-permute-done.5.got, f32[5,32]{1,0:T(8,128)S(1)} %copy-done.8, f32[32]{0:T(128)S(1)} %copy-done.10, bf16[32,32]{1,0:T(8,128)(2,1)S(1)} %copy-done.9, f32[1,32]{1,0:T(1,128)S(1)} %bitcast.20), custom_call_target="tpu_custom_call" | custom-call | flops 300000000 | bytes 1048576 | tf_op jit(solution)/shard_map/pallas_call | solution.py:488
  49.2 7.7 %all-to-all-done.1 = f32[128,8,128]{2,1,0:T(8,128)S(1)} async-done(((f32[128,8,128]{2,1,0:T(8,128)}), f32[128,8,128]{2,1,0:T(8,128)S(1)}, u32[]{:S(2)}, u32[]{:S(2)}) %all-to-all-start.1) | async-done | bytes 524320 | tf_op jit(solution)/shard_map/all_to_all | solution.py:431
  56.9 0.0 copy-done.4
  56.9 0.0 copy-done.6
  56.9 1.9 %shard_map.125 = bf16[8,8,2,16,128]{4,3,2,1,0:T(8,128)(2,1)S(1)} custom-call(f32[8,8,16,128]{3,2,1,0:T(8,128)S(1)} %bitcast.13, bf16[64,32,128]{2,1,0:T(8,128)(2,1)} %all-to-all-done.after.weights_far, bf16[256,512]{1,0:T(8,128)(2,1)S(1)} %copy-done.4, bf16[256,256]{1,0:T(8,128)(2,1)S(1)} %copy-done.6, f32[8,256,128]{2,1,0:T(8,128)S(1)} %shard_map.124.after.direct), custom_call_target="tpu_custom_call" | custom-call | flops 10000000 | bytes 1048576 | tf_op jit(solution)/shard_map/pallas_call | solution.py:496
  58.8 0.0 copy-start.5
  58.8 17.9 %all_to_all.15 = bf16[128,16,128]{2,1,0:T(8,128)(2,1)S(1)} all-to-all(bf16[128,16,128]{2,1,0:T(8,128)(2,1)S(1)} %bitcast.14), channel_id=1, replica_groups=mesh['gx'=8,'gy'=8,'ga'=2] {'gx','gy','ga'}, dimensions={0} | all-to-all | bytes 1048576 | tf_op jit(solution)/shard_map/all_to_all | solution.py:431
  76.7 0.0 copy-done.5
  76.7 2.5 %shard_map.126 = bf16[8,32,8,128]{3,2,1,0:T(8,128)(2,1)} custom-call(bf16[2048,128]{1,0:T(8,128)(2,1)S(1)} %bitcast.12, f32[8,256,128]{2,1,0:T(8,128)S(1)} %shard_map.124.after.direct, bf16[8,128,128]{2,1,0:T(8,128)(2,1)S(1)} %copy-done.2, bf16[256,256]{1,0:T(8,128)(2,1)S(1)} %copy-done.5), custom_call_target="tpu_custom_call" | custom-call | flops 10000000 | bytes 1048576 | tf_op jit(solution)/shard_map/pallas_call | solution.py:503
  (2 shorter events, 0.0 us)
Async XLA Ops:
  0.0 4.4 %collective-permute-start = (f32[5,128,256]{2,1,0:T(8,128)}, f32[5,128,256]{2,1,0:T(8,128)S(1)}, u32[]{:S(2)}, u32[]{:S(2)}) collective-permute-start(f32[5,128,256]{2,1,0:T(8,128)} %bitcast.8), channel_id=1, source_target_pairs={{0,1},{1,0},{2,3},{3,2},{4,5},{5,4},{6,7},{7,6},{8,9},{9,8},{10,11... | collective-permute-start | bytes 1966088 | tf_op jit(solution)/shard_map/ppermute | solution.py:437
  1.4 3.0 %collective-permute-start.1 = (f32[128,256]{1,0:T(8,128)}, f32[128,256]{1,0:T(8,128)S(1)}, u32[]{:S(2)}, u32[]{:S(2)}) collective-permute-start(f32[128,256]{1,0:T(8,128)} %bitcast.16), channel_id=1, source_target_pairs={{0,1},{1,0},{2,3},{3,2},{4,5},{5,4},{6,7},{7,6},{8,9},{9,8},{10,11... | collective-permute-start | bytes 393224 | tf_op jit(solution)/shard_map/ppermute | solution.py:437
  1.4 1.2 %copy-start.1 = (f32[4,4,32,4,128]{4,3,2,1,0:T(4,128)S(1)}, f32[4,4,32,4,128]{4,3,2,1,0:T(4,128)}, u32[]{:S(2)}) copy-start(f32[4,4,32,4,128]{4,3,2,1,0:T(4,128)} %param.17) | copy-start | bytes 3145732
  2.7 1.6 %copy-start = (f32[5,8,16,256]{3,2,1,0:T(8,128)S(1)}, f32[5,8,16,256]{3,2,1,0:T(8,128)}, u32[]{:S(2)}) copy-start(f32[5,8,16,256]{3,2,1,0:T(8,128)} %param.12) | copy-start | bytes 1966084
  2.7 1.6 %copy-start.3 = (f32[8,16,256]{2,1,0:T(8,128)S(1)}, f32[8,16,256]{2,1,0:T(8,128)}, u32[]{:S(2)}) copy-start(f32[8,16,256]{2,1,0:T(8,128)} %param.13) | copy-start | bytes 393220
  4.6 13.0 %collective-permute-start.2 = (f32[6,2,48,128]{3,2,1,0:T(8,128)S(1)}, f32[6,2,48,128]{3,2,1,0:T(8,128)S(1)}, u32[]{:S(2)}, u32[]{:S(2)}) collective-permute-start(f32[6,2,48,128]{3,2,1,0:T(8,128)S(1)} %shard_map.120), channel_id=1, source_target_pairs={{0,113},{16,1},{32,17},{48,33},{64,49},{80,65},{96,81},{112,97},{1... | collective-permute-start | bytes 884744 | tf_op jit(solution)/shard_map/ppermute | solution.py:449
  6.3 26.2 %all-to-all-start = ((bf16[64,32,128]{2,1,0:T(8,128)(2,1)}), bf16[64,32,128]{2,1,0:T(8,128)(2,1)}, u32[]{:S(2)}, u32[]{:S(2)}) async-start(bf16[64,32,128]{2,1,0:T(8,128)(2,1)} %shard_map.118.after), calls=%async_computation | async-start | bytes 1048576 | tf_op jit(solution)/shard_map/all_to_all | solution.py:431
  18.1 5.3 %collective-permute-start.3 = (f32[3,16,128]{2,1,0:T(8,128)S(1)}, f32[3,16,128]{2,1,0:T(8,128)S(1)}, u32[]{:S(2)}, u32[]{:S(2)}) collective-permute-start(f32[3,16,128]{2,1,0:T(8,128)S(1)} %get-tuple-element.10), channel_id=1, source_target_pairs={{0,2},{2,0},{4,6},{6,4},{8,10},{10,8},{12,14},{14,12},{1,3},{3,1},... | collective-permute-start | bytes 73736 | tf_op jit(solution)/shard_map/ppermute | solution.py:461
  19.1 13.4 %copy-start.2 = (bf16[8,128,128]{2,1,0:T(8,128)(2,1)S(1)}, bf16[8,128,128]{2,1,0:T(8,128)(2,1)}, u32[]{:S(2)}) copy-start(bf16[8,128,128]{2,1,0:T(8,128)(2,1)} %constant.10.clone.yf_far.yi_far) | copy-start | bytes 786436
  19.1 13.5 %copy-start.7 = (bf16[256,256]{1,0:T(8,128)(2,1)S(1)}, bf16[256,256]{1,0:T(8,128)(2,1)}, u32[]{:S(2)}) copy-start(bf16[256,256]{1,0:T(8,128)(2,1)} %constant.11.clone.zf_far) | copy-start | bytes 393220
  19.1 13.5 %copy-start.8 = (f32[5,32]{1,0:T(8,128)S(1)}, f32[5,32]{1,0:T(8,128)}, u32[]{:S(2)}) copy-start(f32[5,32]{1,0:T(8,128)} %weight.3) | copy-start | bytes 1924
  19.1 13.5 %copy-start.10 = (f32[32]{0:T(128)S(1)}, f32[32]{0:T(128)}, u32[]{:S(2)}) copy-start(f32[32]{0:T(128)} %bias.3) | copy-start | bytes 388
  19.1 9.5 %collective-permute-start.4 = (f32[3,16,128]{2,1,0:T(8,128)S(1)}, f32[3,16,128]{2,1,0:T(8,128)S(1)}, u32[]{:S(2)}, u32[]{:S(2)}) collective-permute-start(f32[3,16,128]{2,1,0:T(8,128)S(1)} %get-tuple-element.11), channel_id=1, source_target_pairs={{0,14},{2,4},{4,2},{6,8},{8,6},{10,12},{12,10},{14,0},{1,15},{3,5}... | collective-permute-start | bytes 73736 | tf_op jit(solution)/shard_map/ppermute | solution.py:462
  36.4 8.9 %copy-start.9 = (bf16[32,32]{1,0:T(8,128)(2,1)S(1)}, bf16[32,32]{1,0:T(8,128)(2,1)}, u32[]{:S(2)}) copy-start(bf16[32,32]{1,0:T(8,128)(2,1)} %mix.1) | copy-start | bytes 6148
  36.4 20.5 %all-to-all-start.1 = ((f32[128,8,128]{2,1,0:T(8,128)}), f32[128,8,128]{2,1,0:T(8,128)S(1)}, u32[]{:S(2)}, u32[]{:S(2)}) async-start(f32[128,8,128]{2,1,0:T(8,128)} %bitcast.3), calls=%async_computation.1 | async-start | bytes 1048576 | tf_op jit(solution)/shard_map/all_to_all | solution.py:431
  43.1 2.3 %collective-permute-start.5 = (f32[160,128]{1,0:T(8,128)S(1)}, f32[160,128]{1,0:T(8,128)S(1)}, u32[]{:S(2)}, u32[]{:S(2)}) collective-permute-start(f32[160,128]{1,0:T(8,128)S(1)} %get-tuple-element.14), channel_id=1, source_target_pairs={{0,1},{1,0},{2,3},{3,2},{4,5},{5,4},{6,7},{7,6},{8,9},{9,8},{10,11... | collective-permute-start | bytes 245768 | tf_op jit(solution)/shard_map/ppermute | solution.py:494
  45.3 0.7 copy-start.11
  46.0 10.9 %copy-start.4 = (bf16[256,512]{1,0:T(8,128)(2,1)S(1)}, bf16[256,512]{1,0:T(8,128)(2,1)}, u32[]{:S(2)}) copy-start(bf16[256,512]{1,0:T(8,128)(2,1)} %constant.13.clone.xf) | copy-start | bytes 786436
  46.0 10.9 %copy-start.6 = (bf16[256,256]{1,0:T(8,128)(2,1)S(1)}, bf16[256,256]{1,0:T(8,128)(2,1)}, u32[]{:S(2)}) copy-start(bf16[256,256]{1,0:T(8,128)(2,1)} %constant.14.clone.xi) | copy-start | bytes 393220
  58.8 17.9 %copy-start.5 = (bf16[256,256]{1,0:T(8,128)(2,1)S(1)}, bf16[256,256]{1,0:T(8,128)(2,1)}, u32[]{:S(2)}) copy-start(bf16[256,256]{1,0:T(8,128)(2,1)} %constant.12.clone.zi_far) | copy-start | bytes 393220

commit v13 on v11

--- a/solution.py
+++ b/solution.py
@@ -304,9 +304,8 @@
             jnp.concatenate([modes[x, 0:64, lanes], modes[x, 64:128, lanes]], axis=1)
             for x in range(4)
         ]
-        m_high, m_low = halves(jnp.concatenate(stack, axis=0))
-        both = dot(m_high, zf[...])
-        parts.append(both[:, :128] + both[:, 128:] + dot(m_low, zf[:, :128]))
+        both = dot(jnp.concatenate(stack, axis=0).astype(BF16), zf[...])
+        parts.append(both[:, :128] + both[:, 128:])
     lane = lax.broadcasted_iota(jnp.int32, (256, 128), 1) // 32
     for part in range(4):
         total = parts[part]
@@ -336,21 +335,16 @@
     modes = dot(xf[...], jnp.concatenate(pieces, axis=0))
     modes = modes[:, :128] + modes[:, 128:]
     real, imag = modes[:128], modes[128:]
-    highs, lows = [], []
     copy.wait()
+    products = []
     for i in range(8):
         wr = weights[8 * i : 8 * i + 8, 0:16, :].astype(F32).reshape(128, 128)
         wi = weights[8 * i : 8 * i + 8, 16:32, :].astype(F32).reshape(128, 128)
-        high, low = halves(
-            jnp.concatenate([wr * real - wi * imag, wr * imag + wi * real], axis=0)
-        )
-        highs.append(high)
-        lows.append(low)
+        product = jnp.concatenate([wr * real - wi * imag, wr * imag + wi * real], axis=0)
+        products.append(product.astype(BF16))
     row, lane = iotas((1024, 128))
     gather = (lane // 64 * 16 + lane % 16 == 4 * (row // 128) + row % 4).astype(BF16)
-    parts = [jnp.concatenate(part, axis=1) for part in (highs, lows)]
-    total = dot(jnp.concatenate(parts, axis=0), gather)
-    total = total[:256] + total[256:]
+    total = dot(jnp.concatenate(products, axis=1), gather)
     row, lane = iotas((256, 128))
     total = jnp.where((row // 4) % 4 == (lane // 16) % 4, total, 0.0)
     back = dot(xi[...], jnp.concatenate(halves(total), axis=1))
@@ -379,8 +373,7 @@
     for copy in copies:
         copy.start()
     rows[...] = got[...].astype(F32)
-    for copy in copies:
-        copy.wait()
+    copies[1].wait()
     by_z = []
     for part in range(2):
         stack = []
@@ -390,6 +383,7 @@
         by_z.append(dot(zi[...], jnp.concatenate(stack, axis=0), ((1,), (1,))))
     blank = jnp.zeros((64, 128), BF16)
 
+    copies[0].wait()
     real, imag = yi[0:64, :], yi[64:128, :]
     pieces = [[real, blank], [blank, real], [imag, blank], [blank, imag]]
     twice = jnp.concatenate([jnp.concatenate(row, axis=1) for row in pieces], axis=0)
@@ -398,8 +392,7 @@
         value = jnp.concatenate(
             [jnp.concatenate([v[:128, lanes], v[128:, lanes]], axis=1) for v in by_z], axis=0
         )
-        high, low = halves(value)
-        both = dot(high, twice) + dot(low, twice)
+        both = dot(value.astype(BF16), twice)
         for x in range(2):
             spectral[pl.ds(2 * pair + x, 256, stride=8), :] = both[:, 128 * x : 128 * x + 128]
     for part in range(2):

time: 79 us -> 78.8 us (level)
  no operation moved by 1% of the time
where the time goes in v13:
time: 78.8 us; the launch traced here: 78.4 us
  starting transfers between devices  26.2 us (33%)
  blocking collectives  17.9 us (23%)
  Pallas kernels  17.6 us (22%)
  waiting for transfers between devices  14.5 us (18%)
  local copies, waits for them, and re-layouts  1.92 us (2%)
    all_to_all x1, blocking collectives, exchange(): return lax.all_to_all(value, axis, split_axis=0, concat_axis=0, tiled=True)  17.9 us
    all_to_all x2, starting transfers between devices, exchange(): return lax.all_to_all(value, axis, split_axis=0, concat_axis=0, tiled=True)  17 us
    all_to_all x2, waiting for transfers between devices, exchange(): return lax.all_to_all(value, axis, split_axis=0, concat_axis=0, tiled=True)  7.75 us
    ppermute x1, waiting for transfers between devices, shards(): lax.ppermute(far, 'gy', [(j, (j - 1 + 2 * (j % 2)) % 8) for j in range(8)])  5.79 us
    ppermute x1, starting transfers between devices, shards(): lax.ppermute(far, 'gy', [(j, (j - 1 + 2 * (j % 2)) % 8) for j in range(8)])  4.63 us
    pallas_call x1, Pallas kernels, shards(): call(stencil, [((5, 2, 128, 128), F32)], [VMEM] * 7, [pltpu.VMEM((5, 16,...  3.92 us
    pallas_call x1, Pallas kernels, shards(): call(forward, [((160, 128), F32), ((160, 128), F32), ((1024, 128), F32)],...  3.85 us
    pallas_call x1, Pallas kernels, shards(): call(pointwise, [((8, 256, 128), F32)], [VMEM, VMEM, SMEM, SMEM, VMEM, VM...  3.19 us
  transfers between devices with their start and end apart: 8, of which 3 were waited for; matrix products, arithmetic and copies ran while one was open for 0% of the time, Pallas kernels for 12%

profile of v13, /device:TPU:1, one launch (start us, length us, event | category | flops | bytes accessed | tf_op | source)
XLA Modules:
  0.0 78.4 jit_solution(7959822011981942430)
XLA Ops:
  0.0 1.4 %collective-permute-start = (f32[5,128,256]{2,1,0:T(8,128)}, f32[5,128,256]{2,1,0:T(8,128)S(1)}, u32[]{:S(2)}, u32[]{:S(2)}) collective-permute-start(f32[5,128,256]{2,1,0:T(8,128)} %bitcast.8), channel_id=1, source_target_pairs={{0,1},{1,0},{2,3},{3,2},{4,5},{5,4},{6,7},{7,6},{8,9},{9,8},{10,11... | collective-permute-start | bytes 1966088 | tf_op jit(solution)/shard_map/ppermute | solution.py:425
  1.4 0.0 collective-permute-start.1
  1.4 0.0 copy-start.1
  1.4 1.2 %copy-done.1 = f32[4,4,32,4,128]{4,3,2,1,0:T(4,128)S(1)} copy-done((f32[4,4,32,4,128]{4,3,2,1,0:T(4,128)S(1)}, f32[4,4,32,4,128]{4,3,2,1,0:T(4,128)}, u32[]{:S(2)}) %copy-start.1) | copy-done | bytes 1048600
  2.7 0.0 copy-start
  2.7 0.0 copy-start.3
  2.7 1.6 %shard_map.118.after = bf16[64,32,128]{2,1,0:T(8,128)(2,1)} custom-call(f32[2048,128]{1,0:T(8,128)S(1)} %bitcast.15), custom_call_target="tpu_custom_call" | custom-call | flops 10000000 | bytes 1048576 | tf_op jit(solution)/shard_map/pallas_call | solution.py:428
  4.2 0.0 copy-done
  4.2 0.0 copy-done.3
  4.2 0.1 shard_map.119.own
  4.4 0.0 collective-permute-done.1.sp
  4.4 0.0 collective-permute-done.fp
  4.4 0.1 shard_map.120
  4.6 1.8 %collective-permute-start.2 = (f32[6,2,48,128]{3,2,1,0:T(8,128)S(1)}, f32[6,2,48,128]{3,2,1,0:T(8,128)S(1)}, u32[]{:S(2)}, u32[]{:S(2)}) collective-permute-start(f32[6,2,48,128]{3,2,1,0:T(8,128)S(1)} %shard_map.120), channel_id=1, source_target_pairs={{0,113},{16,1},{32,17},{48,33},{64,49},{80,65},{96,81},{112,97},{1... | collective-permute-start | bytes 884744 | tf_op jit(solution)/shard_map/ppermute | solution.py:437
  6.3 11.2 %all-to-all-start = ((bf16[64,32,128]{2,1,0:T(8,128)(2,1)}), bf16[64,32,128]{2,1,0:T(8,128)(2,1)}, u32[]{:S(2)}, u32[]{:S(2)}) async-start(bf16[64,32,128]{2,1,0:T(8,128)(2,1)} %shard_map.118.after), calls=%async_computation | async-start | bytes 1048576 | tf_op jit(solution)/shard_map/all_to_all | solution.py:419
  17.5 0.0 collective-permute-done.2.message.got
  17.5 0.5 shard_map.121
  18.1 4.6 %collective-permute-start.3 = (f32[3,16,128]{2,1,0:T(8,128)S(1)}, f32[3,16,128]{2,1,0:T(8,128)S(1)}, u32[]{:S(2)}, u32[]{:S(2)}) collective-permute-start(f32[3,16,128]{2,1,0:T(8,128)S(1)} %get-tuple-element.10), channel_id=1, source_target_pairs={{0,14},{2,4},{4,2},{6,8},{8,6},{10,12},{12,10},{14,0},{1,15},{3,5}... | collective-permute-start | bytes 73736 | tf_op jit(solution)/shard_map/ppermute | solution.py:449
  22.7 0.0 copy-start.2
  22.7 0.0 copy-start.7
  22.7 0.0 copy-start.8
  22.7 0.0 copy-start.10
  22.7 0.1 collective-permute-start.4
  22.8 5.8 %collective-permute-done.3.far = f32[3,16,128]{2,1,0:T(8,128)S(1)} collective-permute-done((f32[3,16,128]{2,1,0:T(8,128)S(1)}, f32[3,16,128]{2,1,0:T(8,128)S(1)}, u32[]{:S(2)}, u32[]{:S(2)}) %collective-permute-start.3) | collective-permute-done | bytes 24608 | tf_op jit(solution)/shard_map/ppermute | solution.py:449
  28.6 0.0 collective-permute-done.4.near
  28.6 3.9 %shard_map.122.last = f32[5,2,128,128]{3,2,1,0:T(8,128)S(1)} custom-call(f32[5,128,256]{2,1,0:T(8,128)S(1)} %bitcast.11, f32[128,256]{1,0:T(8,128)S(1)} %bitcast.19, f32[5,128,256]{2,1,0:T(8,128)S(1)} %collective-permute-done.fp, f32[128,256]{1,0:T(8,128)S(1)} %collective-permute-done.1.sp, f32[6,2,48,128]{3,2,1,0:T(8,128)S(1)} %collective-permute-done.2.message.got, ...), custom_call_target="tpu_custom_call" | custom-call | flops 10000000 | bytes 1048576 | tf_op jit(solution)/shard_map/pallas_call | solution.py:451
  32.5 0.0 all-to-all-done.after.weights_far
  32.5 0.0 copy-done.2
  32.6 0.0 copy-done.7
  32.6 0.0 copy-done.8
  32.6 0.0 copy-done.10
  32.6 3.8 %shard_map.123 = (f32[160,128]{1,0:T(8,128)S(1)}, f32[160,128]{1,0:T(8,128)S(1)}, f32[1024,128]{1,0:T(8,128)}) custom-call(f32[5,2,128,128]{3,2,1,0:T(8,128)S(1)} %shard_map.122.last, bf16[64,32,128]{2,1,0:T(8,128)(2,1)} %all-to-all-done.after.weights_far, f32[5,32]{1,0:T(8,128)S(1)} %copy-done.8, f32[32]{0:T(128)S(1)} %copy-done.10, ...), custom_call_target="tpu_custom_call" | custom-call | flops 10000000 | bytes 1048576 | tf_op jit(solution)/shard_map/pallas_call | solution.py:462
  36.4 0.0 copy-start.9
  36.5 5.8 %all-to-all-start.1 = ((f32[128,8,128]{2,1,0:T(8,128)}), f32[128,8,128]{2,1,0:T(8,128)S(1)}, u32[]{:S(2)}, u32[]{:S(2)}) async-start(f32[128,8,128]{2,1,0:T(8,128)} %bitcast.3), calls=%async_computation.1 | async-start | bytes 1048576 | tf_op jit(solution)/shard_map/all_to_all | solution.py:419
  42.3 1.3 %collective-permute-start.5 = (f32[160,128]{1,0:T(8,128)S(1)}, f32[160,128]{1,0:T(8,128)S(1)}, u32[]{:S(2)}, u32[]{:S(2)}) collective-permute-start(f32[160,128]{1,0:T(8,128)S(1)} %get-tuple-element.14), channel_id=1, source_target_pairs={{0,1},{1,0},{2,3},{3,2},{4,5},{5,4},{6,7},{7,6},{8,9},{9,8},{10,11... | collective-permute-start | bytes 245768 | tf_op jit(solution)/shard_map/ppermute | solution.py:482
  43.6 0.9 %collective-permute-done.5.got = f32[160,128]{1,0:T(8,128)S(1)} collective-permute-done((f32[160,128]{1,0:T(8,128)S(1)}, f32[160,128]{1,0:T(8,128)S(1)}, u32[]{:S(2)}, u32[]{:S(2)}) %collective-permute-start.5) | collective-permute-done | bytes 81952 | tf_op jit(solution)/shard_map/ppermute | solution.py:482
  44.5 0.0 copy-start.11
  44.5 0.0 copy-done.9
  44.5 0.7 copy-done.11
  45.2 3.2 %shard_map.124.after.direct = f32[8,256,128]{2,1,0:T(8,128)S(1)} custom-call(f32[160,128]{1,0:T(8,128)S(1)} %get-tuple-element.13.keep, f32[160,128]{1,0:T(8,128)S(1)} %collective-permute-done.5.got, f32[5,32]{1,0:T(8,128)S(1)} %copy-done.8, f32[32]{0:T(128)S(1)} %copy-done.10, bf16[32,32]{1,0:T(8,128)(2,1)S(1)} %copy-done.9, f32[1,32]{1,0:T(1,128)S(1)} %bitcast.20), custom_call_target="tpu_custom_call" | custom-call | flops 300000000 | bytes 1048576 | tf_op jit(solution)/shard_map/pallas_call | solution.py:476
  48.4 7.7 %all-to-all-done.1 = f32[128,8,128]{2,1,0:T(8,128)S(1)} async-done(((f32[128,8,128]{2,1,0:T(8,128)}), f32[128,8,128]{2,1,0:T(8,128)S(1)}, u32[]{:S(2)}, u32[]{:S(2)}) %all-to-all-start.1) | async-done | bytes 524320 | tf_op jit(solution)/shard_map/all_to_all | solution.py:419
  56.1 0.0 copy-done.4
  56.1 0.0 copy-done.6
  56.1 1.7 %shard_map.125 = bf16[8,8,2,16,128]{4,3,2,1,0:T(8,128)(2,1)S(1)} custom-call(f32[8,8,16,128]{3,2,1,0:T(8,128)S(1)} %bitcast.13, bf16[64,32,128]{2,1,0:T(8,128)(2,1)} %all-to-all-done.after.weights_far, bf16[256,512]{1,0:T(8,128)(2,1)S(1)} %copy-done.4, bf16[256,256]{1,0:T(8,128)(2,1)S(1)} %copy-done.6, f32[8,256,128]{2,1,0:T(8,128)S(1)} %shard_map.124.after.direct), custom_call_target="tpu_custom_call" | custom-call | flops 10000000 | bytes 1048576 | tf_op jit(solution)/shard_map/pallas_call | solution.py:484
  57.9 0.0 copy-start.5
  57.9 17.9 %all_to_all.15 = bf16[128,16,128]{2,1,0:T(8,128)(2,1)S(1)} all-to-all(bf16[128,16,128]{2,1,0:T(8,128)(2,1)S(1)} %bitcast.14), channel_id=1, replica_groups=mesh['gx'=8,'gy'=8,'ga'=2] {'gx','gy','ga'}, dimensions={0} | all-to-all | bytes 1048576 | tf_op jit(solution)/shard_map/all_to_all | solution.py:419
  75.8 0.0 copy-done.5
  75.8 2.5 %shard_map.126 = bf16[8,32,8,128]{3,2,1,0:T(8,128)(2,1)} custom-call(bf16[2048,128]{1,0:T(8,128)(2,1)S(1)} %bitcast.12, f32[8,256,128]{2,1,0:T(8,128)S(1)} %shard_map.124.after.direct, bf16[8,128,128]{2,1,0:T(8,128)(2,1)S(1)} %copy-done.2, bf16[256,256]{1,0:T(8,128)(2,1)S(1)} %copy-done.5), custom_call_target="tpu_custom_call" | custom-call | flops 10000000 | bytes 1048576 | tf_op jit(solution)/shard_map/pallas_call | solution.py:491
  (2 shorter events, 0.0 us)
Async XLA Ops:
  0.0 4.4 %collective-permute-start = (f32[5,128,256]{2,1,0:T(8,128)}, f32[5,128,256]{2,1,0:T(8,128)S(1)}, u32[]{:S(2)}, u32[]{:S(2)}) collective-permute-start(f32[5,128,256]{2,1,0:T(8,128)} %bitcast.8), channel_id=1, source_target_pairs={{0,1},{1,0},{2,3},{3,2},{4,5},{5,4},{6,7},{7,6},{8,9},{9,8},{10,11... | collective-permute-start | bytes 1966088 | tf_op jit(solution)/shard_map/ppermute | solution.py:425
  1.4 3.0 %collective-permute-start.1 = (f32[128,256]{1,0:T(8,128)}, f32[128,256]{1,0:T(8,128)S(1)}, u32[]{:S(2)}, u32[]{:S(2)}) collective-permute-start(f32[128,256]{1,0:T(8,128)} %bitcast.16), channel_id=1, source_target_pairs={{0,1},{1,0},{2,3},{3,2},{4,5},{5,4},{6,7},{7,6},{8,9},{9,8},{10,11... | collective-permute-start | bytes 393224 | tf_op jit(solution)/shard_map/ppermute | solution.py:425
  1.4 1.2 %copy-start.1 = (f32[4,4,32,4,128]{4,3,2,1,0:T(4,128)S(1)}, f32[4,4,32,4,128]{4,3,2,1,0:T(4,128)}, u32[]{:S(2)}) copy-start(f32[4,4,32,4,128]{4,3,2,1,0:T(4,128)} %param.17) | copy-start | bytes 3145732
  2.7 1.6 %copy-start = (f32[5,8,16,256]{3,2,1,0:T(8,128)S(1)}, f32[5,8,16,256]{3,2,1,0:T(8,128)}, u32[]{:S(2)}) copy-start(f32[5,8,16,256]{3,2,1,0:T(8,128)} %param.12) | copy-start | bytes 1966084
  2.7 1.6 %copy-start.3 = (f32[8,16,256]{2,1,0:T(8,128)S(1)}, f32[8,16,256]{2,1,0:T(8,128)}, u32[]{:S(2)}) copy-start(f32[8,16,256]{2,1,0:T(8,128)} %param.13) | copy-start | bytes 393220
  4.6 13.0 %collective-permute-start.2 = (f32[6,2,48,128]{3,2,1,0:T(8,128)S(1)}, f32[6,2,48,128]{3,2,1,0:T(8,128)S(1)}, u32[]{:S(2)}, u32[]{:S(2)}) collective-permute-start(f32[6,2,48,128]{3,2,1,0:T(8,128)S(1)} %shard_map.120), channel_id=1, source_target_pairs={{0,113},{16,1},{32,17},{48,33},{64,49},{80,65},{96,81},{112,97},{1... | collective-permute-start | bytes 884744 | tf_op jit(solution)/shard_map/ppermute | solution.py:437
  6.3 26.2 %all-to-all-start = ((bf16[64,32,128]{2,1,0:T(8,128)(2,1)}), bf16[64,32,128]{2,1,0:T(8,128)(2,1)}, u32[]{:S(2)}, u32[]{:S(2)}) async-start(bf16[64,32,128]{2,1,0:T(8,128)(2,1)} %shard_map.118.after), calls=%async_computation | async-start | bytes 1048576 | tf_op jit(solution)/shard_map/all_to_all | solution.py:419
  18.1 10.5 %collective-permute-start.3 = (f32[3,16,128]{2,1,0:T(8,128)S(1)}, f32[3,16,128]{2,1,0:T(8,128)S(1)}, u32[]{:S(2)}, u32[]{:S(2)}) collective-permute-start(f32[3,16,128]{2,1,0:T(8,128)S(1)} %get-tuple-element.10), channel_id=1, source_target_pairs={{0,14},{2,4},{4,2},{6,8},{8,6},{10,12},{12,10},{14,0},{1,15},{3,5}... | collective-permute-start | bytes 73736 | tf_op jit(solution)/shard_map/ppermute | solution.py:449
  22.7 9.8 %copy-start.2 = (bf16[8,128,128]{2,1,0:T(8,128)(2,1)S(1)}, bf16[8,128,128]{2,1,0:T(8,128)(2,1)}, u32[]{:S(2)}) copy-start(bf16[8,128,128]{2,1,0:T(8,128)(2,1)} %constant.10.clone.yf_far.yi_far) | copy-start | bytes 786436
  22.7 9.8 %copy-start.7 = (bf16[256,256]{1,0:T(8,128)(2,1)S(1)}, bf16[256,256]{1,0:T(8,128)(2,1)}, u32[]{:S(2)}) copy-start(bf16[256,256]{1,0:T(8,128)(2,1)} %constant.11.clone.zf_far) | copy-start | bytes 393220
  22.7 9.9 %copy-start.8 = (f32[5,32]{1,0:T(8,128)S(1)}, f32[5,32]{1,0:T(8,128)}, u32[]{:S(2)}) copy-start(f32[5,32]{1,0:T(8,128)} %weight.3) | copy-start | bytes 1924
  22.7 9.9 %copy-start.10 = (f32[32]{0:T(128)S(1)}, f32[32]{0:T(128)}, u32[]{:S(2)}) copy-start(f32[32]{0:T(128)} %bias.3) | copy-start | bytes 388
  22.7 5.9 %collective-permute-start.4 = (f32[3,16,128]{2,1,0:T(8,128)S(1)}, f32[3,16,128]{2,1,0:T(8,128)S(1)}, u32[]{:S(2)}, u32[]{:S(2)}) collective-permute-start(f32[3,16,128]{2,1,0:T(8,128)S(1)} %get-tuple-element.11), channel_id=1, source_target_pairs={{0,2},{2,0},{4,6},{6,4},{8,10},{10,8},{12,14},{14,12},{1,3},{3,1},... | collective-permute-start | bytes 73736 | tf_op jit(solution)/shard_map/ppermute | solution.py:450
  36.4 8.1 %copy-start.9 = (bf16[32,32]{1,0:T(8,128)(2,1)S(1)}, bf16[32,32]{1,0:T(8,128)(2,1)}, u32[]{:S(2)}) copy-start(bf16[32,32]{1,0:T(8,128)(2,1)} %mix.1) | copy-start | bytes 6148
  36.5 19.7 %all-to-all-start.1 = ((f32[128,8,128]{2,1,0:T(8,128)}), f32[128,8,128]{2,1,0:T(8,128)S(1)}, u32[]{:S(2)}, u32[]{:S(2)}) async-start(f32[128,8,128]{2,1,0:T(8,128)} %bitcast.3), calls=%async_computation.1 | async-start | bytes 1048576 | tf_op jit(solution)/shard_map/all_to_all | solution.py:419
  42.3 2.3 %collective-permute-start.5 = (f32[160,128]{1,0:T(8,128)S(1)}, f32[160,128]{1,0:T(8,128)S(1)}, u32[]{:S(2)}, u32[]{:S(2)}) collective-permute-start(f32[160,128]{1,0:T(8,128)S(1)} %get-tuple-element.14), channel_id=1, source_target_pairs={{0,1},{1,0},{2,3},{3,2},{4,5},{5,4},{6,7},{7,6},{8,9},{9,8},{10,11... | collective-permute-start | bytes 245768 | tf_op jit(solution)/shard_map/ppermute | solution.py:482
  44.5 0.7 copy-start.11
  45.2 10.9 %copy-start.4 = (bf16[256,512]{1,0:T(8,128)(2,1)S(1)}, bf16[256,512]{1,0:T(8,128)(2,1)}, u32[]{:S(2)}) copy-start(bf16[256,512]{1,0:T(8,128)(2,1)} %constant.13.clone.xf) | copy-start | bytes 786436
  45.2 10.9 %copy-start.6 = (bf16[256,256]{1,0:T(8,128)(2,1)S(1)}, bf16[256,256]{1,0:T(8,128)(2,1)}, u32[]{:S(2)}) copy-start(bf16[256,256]{1,0:T(8,128)(2,1)} %constant.14.clone.xi) | copy-start | bytes 393220
  57.9 17.9 %copy-start.5 = (bf16[256,256]{1,0:T(8,128)(2,1)S(1)}, bf16[256,256]{1,0:T(8,128)(2,1)}, u32[]{:S(2)}) copy-start(bf16[256,256]{1,0:T(8,128)(2,1)} %constant.12.clone.zi_far) | copy-start | bytes 393220

commit v14 on v13

--- a/solution.py
+++ b/solution.py
@@ -372,13 +372,14 @@
     ]
     for copy in copies:
         copy.start()
-    rows[...] = got[...].astype(F32)
+    for ky in range(64):
+        rows[33 * ky : 33 * ky + 32, :] = got[32 * ky : 32 * ky + 32, :].astype(F32)
     copies[1].wait()
     by_z = []
     for part in range(2):
         stack = []
         for x in range(8):
-            pair = [rows[pl.ds(16 * a + 8 * part + x, 64, stride=32), :] for a in range(2)]
+            pair = [rows[pl.ds(16 * a + 8 * part + x, 64, stride=33), :] for a in range(2)]
             stack.append(jnp.concatenate(pair, axis=1).astype(BF16))
         by_z.append(dot(zi[...], jnp.concatenate(stack, axis=0), ((1,), (1,))))
     blank = jnp.zeros((64, 128), BF16)
@@ -394,11 +395,12 @@
         )
         both = dot(value.astype(BF16), twice)
         for x in range(2):
-            spectral[pl.ds(2 * pair + x, 256, stride=8), :] = both[:, 128 * x : 128 * x + 128]
+            spectral[pl.ds(2 * pair + x, 256, stride=9), :] = both[:, 128 * x : 128 * x + 128]
     for part in range(2):
         for z in range(ZL):
-            at = 128 * (8 * part + z)
-            branch = spectral[at : at + 128, :].astype(BF16).astype(F32)
+            first = 16 * (8 * part + z)
+            branch = [spectral[9 * n : 9 * n + 8, :] for n in range(first, first + 16)]
+            branch = jnp.concatenate(branch, axis=0).astype(BF16).astype(F32)
             total = gelu(direct[z, 128 * part : 128 * part + 128, :] + branch)
             out[z, 16 * part : 16 * part + 16] = total.reshape(16, 8, 128).astype(BF16)
 
@@ -493,8 +495,8 @@
         [((8, 32, 8, 128), BF16)],
         [VMEM, VMEM, anywhere, anywhere],
         [
-            pltpu.VMEM((2048, 128), F32),
-            pltpu.VMEM((2048, 128), F32),
+            pltpu.VMEM((64 * 33, 128), F32),
+            pltpu.VMEM((256 * 9, 128), F32),
             pltpu.VMEM((128, 128), BF16),
             pltpu.VMEM((256, 256), BF16),
             pltpu.SemaphoreType.DMA((2,)),

time: 78.8 us -> 78.4 us (level)
  no operation moved by 1% of the time
where the time goes in v14:
time: 78.4 us; the launch traced here: 78 us
  starting transfers between devices  26.2 us (33%)
  blocking collectives  17.9 us (23%)
  Pallas kernels  17.2 us (22%)
  waiting for transfers between devices  14.5 us (18%)
  local copies, waits for them, and re-layouts  1.92 us (2%)
    all_to_all x1, blocking collectives, exchange(): return lax.all_to_all(value, axis, split_axis=0, concat_axis=0, tiled=True)  17.9 us
    all_to_all x2, starting transfers between devices, exchange(): return lax.all_to_all(value, axis, split_axis=0, concat_axis=0, tiled=True)  17 us
    all_to_all x2, waiting for transfers between devices, exchange(): return lax.all_to_all(value, axis, split_axis=0, concat_axis=0, tiled=True)  7.75 us
    ppermute x1, waiting for transfers between devices, shards(): lax.ppermute(far, 'gy', [(j, (j - 1 + 2 * (j % 2)) % 8) for j in range(8)])  5.79 us
    ppermute x1, starting transfers between devices, shards(): lax.ppermute(far, 'gy', [(j, (j - 1 + 2 * (j % 2)) % 8) for j in range(8)])  4.63 us
    pallas_call x1, Pallas kernels, shards(): call(stencil, [((5, 2, 128, 128), F32)], [VMEM] * 7, [pltpu.VMEM((5, 16,...  3.92 us
    pallas_call x1, Pallas kernels, shards(): call(forward, [((160, 128), F32), ((160, 128), F32), ((1024, 128), F32)],...  3.85 us
    pallas_call x1, Pallas kernels, shards(): call(pointwise, [((8, 256, 128), F32)], [VMEM, VMEM, SMEM, SMEM, VMEM, VM...  3.19 us
  transfers between devices with their start and end apart: 8, of which 3 were waited for; matrix products, arithmetic and copies ran while one was open for 0% of the time, Pallas kernels for 12%

profile of v14, /device:TPU:1, one launch (start us, length us, event | category | flops | bytes accessed | tf_op | source)
XLA Modules:
  0.0 78.0 jit_solution(13877038996348282211)
XLA Ops:
  0.0 1.4 %collective-permute-start = (f32[5,128,256]{2,1,0:T(8,128)}, f32[5,128,256]{2,1,0:T(8,128)S(1)}, u32[]{:S(2)}, u32[]{:S(2)}) collective-permute-start(f32[5,128,256]{2,1,0:T(8,128)} %bitcast.8), channel_id=1, source_target_pairs={{0,1},{1,0},{2,3},{3,2},{4,5},{5,4},{6,7},{7,6},{8,9},{9,8},{10,11... | collective-permute-start | bytes 1966088 | tf_op jit(solution)/shard_map/ppermute | solution.py:427
  1.4 0.0 collective-permute-start.1
  1.4 0.0 copy-start.1
  1.4 1.2 %copy-done.1 = f32[4,4,32,4,128]{4,3,2,1,0:T(4,128)S(1)} copy-done((f32[4,4,32,4,128]{4,3,2,1,0:T(4,128)S(1)}, f32[4,4,32,4,128]{4,3,2,1,0:T(4,128)}, u32[]{:S(2)}) %copy-start.1) | copy-done | bytes 1048600
  2.7 0.0 copy-start
  2.7 0.0 copy-start.3
  2.7 1.6 %shard_map.118.after = bf16[64,32,128]{2,1,0:T(8,128)(2,1)} custom-call(f32[2048,128]{1,0:T(8,128)S(1)} %bitcast.15), custom_call_target="tpu_custom_call" | custom-call | flops 10000000 | bytes 1048576 | tf_op jit(solution)/shard_map/pallas_call | solution.py:430
  4.2 0.0 copy-done
  4.2 0.0 copy-done.3
  4.2 0.1 shard_map.119.own
  4.4 0.0 collective-permute-done.1.sp
  4.4 0.0 collective-permute-done.fp
  4.4 0.1 shard_map.120
  4.6 1.8 %collective-permute-start.2 = (f32[6,2,48,128]{3,2,1,0:T(8,128)S(1)}, f32[6,2,48,128]{3,2,1,0:T(8,128)S(1)}, u32[]{:S(2)}, u32[]{:S(2)}) collective-permute-start(f32[6,2,48,128]{3,2,1,0:T(8,128)S(1)} %shard_map.120), channel_id=1, source_target_pairs={{0,113},{16,1},{32,17},{48,33},{64,49},{80,65},{96,81},{112,97},{1... | collective-permute-start | bytes 884744 | tf_op jit(solution)/shard_map/ppermute | solution.py:439
  6.3 11.2 %all-to-all-start = ((bf16[64,32,128]{2,1,0:T(8,128)(2,1)}), bf16[64,32,128]{2,1,0:T(8,128)(2,1)}, u32[]{:S(2)}, u32[]{:S(2)}) async-start(bf16[64,32,128]{2,1,0:T(8,128)(2,1)} %shard_map.118.after), calls=%async_computation | async-start | bytes 1048576 | tf_op jit(solution)/shard_map/all_to_all | solution.py:421
  17.5 0.0 collective-permute-done.2.message.got
  17.5 0.5 shard_map.121
  18.1 4.6 %collective-permute-start.3 = (f32[3,16,128]{2,1,0:T(8,128)S(1)}, f32[3,16,128]{2,1,0:T(8,128)S(1)}, u32[]{:S(2)}, u32[]{:S(2)}) collective-permute-start(f32[3,16,128]{2,1,0:T(8,128)S(1)} %get-tuple-element.10), channel_id=1, source_target_pairs={{0,14},{2,4},{4,2},{6,8},{8,6},{10,12},{12,10},{14,0},{1,15},{3,5}... | collective-permute-start | bytes 73736 | tf_op jit(solution)/shard_map/ppermute | solution.py:451
  22.7 0.0 copy-start.2
  22.7 0.0 copy-start.7
  22.7 0.0 copy-start.8
  22.7 0.0 copy-start.10
  22.7 0.1 collective-permute-start.4
  22.8 5.8 %collective-permute-done.3.far = f32[3,16,128]{2,1,0:T(8,128)S(1)} collective-permute-done((f32[3,16,128]{2,1,0:T(8,128)S(1)}, f32[3,16,128]{2,1,0:T(8,128)S(1)}, u32[]{:S(2)}, u32[]{:S(2)}) %collective-permute-start.3) | collective-permute-done | bytes 24608 | tf_op jit(solution)/shard_map/ppermute | solution.py:451
  28.6 0.0 collective-permute-done.4.near
  28.6 3.9 %shard_map.122.last = f32[5,2,128,128]{3,2,1,0:T(8,128)S(1)} custom-call(f32[5,128,256]{2,1,0:T(8,128)S(1)} %bitcast.11, f32[128,256]{1,0:T(8,128)S(1)} %bitcast.19, f32[5,128,256]{2,1,0:T(8,128)S(1)} %collective-permute-done.fp, f32[128,256]{1,0:T(8,128)S(1)} %collective-permute-done.1.sp, f32[6,2,48,128]{3,2,1,0:T(8,128)S(1)} %collective-permute-done.2.message.got, ...), custom_call_target="tpu_custom_call" | custom-call | flops 10000000 | bytes 1048576 | tf_op jit(solution)/shard_map/pallas_call | solution.py:453
  32.5 0.0 all-to-all-done.after.weights_far
  32.5 0.0 copy-done.2
  32.6 0.0 copy-done.7
  32.6 0.0 copy-done.8
  32.6 0.0 copy-done.10
  32.6 3.8 %shard_map.123 = (f32[160,128]{1,0:T(8,128)S(1)}, f32[160,128]{1,0:T(8,128)S(1)}, f32[1024,128]{1,0:T(8,128)}) custom-call(f32[5,2,128,128]{3,2,1,0:T(8,128)S(1)} %shard_map.122.last, bf16[64,32,128]{2,1,0:T(8,128)(2,1)} %all-to-all-done.after.weights_far, f32[5,32]{1,0:T(8,128)S(1)} %copy-done.8, f32[32]{0:T(128)S(1)} %copy-done.10, ...), custom_call_target="tpu_custom_call" | custom-call | flops 10000000 | bytes 1048576 | tf_op jit(solution)/shard_map/pallas_call | solution.py:464
  36.4 0.0 copy-start.9
  36.5 5.8 %all-to-all-start.1 = ((f32[128,8,128]{2,1,0:T(8,128)}), f32[128,8,128]{2,1,0:T(8,128)S(1)}, u32[]{:S(2)}, u32[]{:S(2)}) async-start(f32[128,8,128]{2,1,0:T(8,128)} %bitcast.3), calls=%async_computation.1 | async-start | bytes 1048576 | tf_op jit(solution)/shard_map/all_to_all | solution.py:421
  42.3 1.3 %collective-permute-start.5 = (f32[160,128]{1,0:T(8,128)S(1)}, f32[160,128]{1,0:T(8,128)S(1)}, u32[]{:S(2)}, u32[]{:S(2)}) collective-permute-start(f32[160,128]{1,0:T(8,128)S(1)} %get-tuple-element.14), channel_id=1, source_target_pairs={{0,1},{1,0},{2,3},{3,2},{4,5},{5,4},{6,7},{7,6},{8,9},{9,8},{10,11... | collective-permute-start | bytes 245768 | tf_op jit(solution)/shard_map/ppermute | solution.py:484
  43.6 0.9 %collective-permute-done.5.got = f32[160,128]{1,0:T(8,128)S(1)} collective-permute-done((f32[160,128]{1,0:T(8,128)S(1)}, f32[160,128]{1,0:T(8,128)S(1)}, u32[]{:S(2)}, u32[]{:S(2)}) %collective-permute-start.5) | collective-permute-done | bytes 81952 | tf_op jit(solution)/shard_map/ppermute | solution.py:484
  44.5 0.0 copy-start.11
  44.5 0.0 copy-done.9
  44.5 0.7 copy-done.11
  45.2 3.2 %shard_map.124.after.direct = f32[8,256,128]{2,1,0:T(8,128)S(1)} custom-call(f32[160,128]{1,0:T(8,128)S(1)} %get-tuple-element.13.keep, f32[160,128]{1,0:T(8,128)S(1)} %collective-permute-done.5.got, f32[5,32]{1,0:T(8,128)S(1)} %copy-done.8, f32[32]{0:T(128)S(1)} %copy-done.10, bf16[32,32]{1,0:T(8,128)(2,1)S(1)} %copy-done.9, f32[1,32]{1,0:T(1,128)S(1)} %bitcast.20), custom_call_target="tpu_custom_call" | custom-call | flops 300000000 | bytes 1048576 | tf_op jit(solution)/shard_map/pallas_call | solution.py:478
  48.4 7.7 %all-to-all-done.1 = f32[128,8,128]{2,1,0:T(8,128)S(1)} async-done(((f32[128,8,128]{2,1,0:T(8,128)}), f32[128,8,128]{2,1,0:T(8,128)S(1)}, u32[]{:S(2)}, u32[]{:S(2)}) %all-to-all-start.1) | async-done | bytes 524320 | tf_op jit(solution)/shard_map/all_to_all | solution.py:421
  56.1 0.0 copy-done.4
  56.1 0.0 copy-done.6
  56.1 1.7 %shard_map.125 = bf16[8,8,2,16,128]{4,3,2,1,0:T(8,128)(2,1)S(1)} custom-call(f32[8,8,16,128]{3,2,1,0:T(8,128)S(1)} %bitcast.13, bf16[64,32,128]{2,1,0:T(8,128)(2,1)} %all-to-all-done.after.weights_far, bf16[256,512]{1,0:T(8,128)(2,1)S(1)} %copy-done.4, bf16[256,256]{1,0:T(8,128)(2,1)S(1)} %copy-done.6, f32[8,256,128]{2,1,0:T(8,128)S(1)} %shard_map.124.after.direct), custom_call_target="tpu_custom_call" | custom-call | flops 10000000 | bytes 1048576 | tf_op jit(solution)/shard_map/pallas_call | solution.py:486
  57.9 0.0 copy-start.5
  57.9 17.9 %all_to_all.15 = bf16[128,16,128]{2,1,0:T(8,128)(2,1)S(1)} all-to-all(bf16[128,16,128]{2,1,0:T(8,128)(2,1)S(1)} %bitcast.14), channel_id=1, replica_groups=mesh['gx'=8,'gy'=8,'ga'=2] {'gx','gy','ga'}, dimensions={0} | all-to-all | bytes 1048576 | tf_op jit(solution)/shard_map/all_to_all | solution.py:421
  75.8 0.0 copy-done.5
  75.8 2.1 %shard_map.126 = bf16[8,32,8,128]{3,2,1,0:T(8,128)(2,1)} custom-call(bf16[2048,128]{1,0:T(8,128)(2,1)S(1)} %bitcast.12, f32[8,256,128]{2,1,0:T(8,128)S(1)} %shard_map.124.after.direct, bf16[8,128,128]{2,1,0:T(8,128)(2,1)S(1)} %copy-done.2, bf16[256,256]{1,0:T(8,128)(2,1)S(1)} %copy-done.5), custom_call_target="tpu_custom_call" | custom-call | flops 10000000 | bytes 1048576 | tf_op jit(solution)/shard_map/pallas_call | solution.py:493
  (2 shorter events, 0.0 us)
Async XLA Ops:
  0.0 4.4 %collective-permute-start = (f32[5,128,256]{2,1,0:T(8,128)}, f32[5,128,256]{2,1,0:T(8,128)S(1)}, u32[]{:S(2)}, u32[]{:S(2)}) collective-permute-start(f32[5,128,256]{2,1,0:T(8,128)} %bitcast.8), channel_id=1, source_target_pairs={{0,1},{1,0},{2,3},{3,2},{4,5},{5,4},{6,7},{7,6},{8,9},{9,8},{10,11... | collective-permute-start | bytes 1966088 | tf_op jit(solution)/shard_map/ppermute | solution.py:427
  1.4 3.0 %collective-permute-start.1 = (f32[128,256]{1,0:T(8,128)}, f32[128,256]{1,0:T(8,128)S(1)}, u32[]{:S(2)}, u32[]{:S(2)}) collective-permute-start(f32[128,256]{1,0:T(8,128)} %bitcast.16), channel_id=1, source_target_pairs={{0,1},{1,0},{2,3},{3,2},{4,5},{5,4},{6,7},{7,6},{8,9},{9,8},{10,11... | collective-permute-start | bytes 393224 | tf_op jit(solution)/shard_map/ppermute | solution.py:427
  1.4 1.2 %copy-start.1 = (f32[4,4,32,4,128]{4,3,2,1,0:T(4,128)S(1)}, f32[4,4,32,4,128]{4,3,2,1,0:T(4,128)}, u32[]{:S(2)}) copy-start(f32[4,4,32,4,128]{4,3,2,1,0:T(4,128)} %param.17) | copy-start | bytes 3145732
  2.7 1.6 %copy-start = (f32[5,8,16,256]{3,2,1,0:T(8,128)S(1)}, f32[5,8,16,256]{3,2,1,0:T(8,128)}, u32[]{:S(2)}) copy-start(f32[5,8,16,256]{3,2,1,0:T(8,128)} %param.12) | copy-start | bytes 1966084
  2.7 1.6 %copy-start.3 = (f32[8,16,256]{2,1,0:T(8,128)S(1)}, f32[8,16,256]{2,1,0:T(8,128)}, u32[]{:S(2)}) copy-start(f32[8,16,256]{2,1,0:T(8,128)} %param.13) | copy-start | bytes 393220
  4.6 13.0 %collective-permute-start.2 = (f32[6,2,48,128]{3,2,1,0:T(8,128)S(1)}, f32[6,2,48,128]{3,2,1,0:T(8,128)S(1)}, u32[]{:S(2)}, u32[]{:S(2)}) collective-permute-start(f32[6,2,48,128]{3,2,1,0:T(8,128)S(1)} %shard_map.120), channel_id=1, source_target_pairs={{0,113},{16,1},{32,17},{48,33},{64,49},{80,65},{96,81},{112,97},{1... | collective-permute-start | bytes 884744 | tf_op jit(solution)/shard_map/ppermute | solution.py:439
  6.3 26.2 %all-to-all-start = ((bf16[64,32,128]{2,1,0:T(8,128)(2,1)}), bf16[64,32,128]{2,1,0:T(8,128)(2,1)}, u32[]{:S(2)}, u32[]{:S(2)}) async-start(bf16[64,32,128]{2,1,0:T(8,128)(2,1)} %shard_map.118.after), calls=%async_computation | async-start | bytes 1048576 | tf_op jit(solution)/shard_map/all_to_all | solution.py:421
  18.1 10.5 %collective-permute-start.3 = (f32[3,16,128]{2,1,0:T(8,128)S(1)}, f32[3,16,128]{2,1,0:T(8,128)S(1)}, u32[]{:S(2)}, u32[]{:S(2)}) collective-permute-start(f32[3,16,128]{2,1,0:T(8,128)S(1)} %get-tuple-element.10), channel_id=1, source_target_pairs={{0,14},{2,4},{4,2},{6,8},{8,6},{10,12},{12,10},{14,0},{1,15},{3,5}... | collective-permute-start | bytes 73736 | tf_op jit(solution)/shard_map/ppermute | solution.py:451
  22.7 9.8 %copy-start.2 = (bf16[8,128,128]{2,1,0:T(8,128)(2,1)S(1)}, bf16[8,128,128]{2,1,0:T(8,128)(2,1)}, u32[]{:S(2)}) copy-start(bf16[8,128,128]{2,1,0:T(8,128)(2,1)} %constant.10.clone.yf_far.yi_far) | copy-start | bytes 786436
  22.7 9.8 %copy-start.7 = (bf16[256,256]{1,0:T(8,128)(2,1)S(1)}, bf16[256,256]{1,0:T(8,128)(2,1)}, u32[]{:S(2)}) copy-start(bf16[256,256]{1,0:T(8,128)(2,1)} %constant.11.clone.zf_far) | copy-start | bytes 393220
  22.7 9.9 %copy-start.8 = (f32[5,32]{1,0:T(8,128)S(1)}, f32[5,32]{1,0:T(8,128)}, u32[]{:S(2)}) copy-start(f32[5,32]{1,0:T(8,128)} %weight.3) | copy-start | bytes 1924
  22.7 9.9 %copy-start.10 = (f32[32]{0:T(128)S(1)}, f32[32]{0:T(128)}, u32[]{:S(2)}) copy-start(f32[32]{0:T(128)} %bias.3) | copy-start | bytes 388
  22.7 5.9 %collective-permute-start.4 = (f32[3,16,128]{2,1,0:T(8,128)S(1)}, f32[3,16,128]{2,1,0:T(8,128)S(1)}, u32[]{:S(2)}, u32[]{:S(2)}) collective-permute-start(f32[3,16,128]{2,1,0:T(8,128)S(1)} %get-tuple-element.11), channel_id=1, source_target_pairs={{0,2},{2,0},{4,6},{6,4},{8,10},{10,8},{12,14},{14,12},{1,3},{3,1},... | collective-permute-start | bytes 73736 | tf_op jit(solution)/shard_map/ppermute | solution.py:452
  36.4 8.1 %copy-start.9 = (bf16[32,32]{1,0:T(8,128)(2,1)S(1)}, bf16[32,32]{1,0:T(8,128)(2,1)}, u32[]{:S(2)}) copy-start(bf16[32,32]{1,0:T(8,128)(2,1)} %mix.1) | copy-start | bytes 6148
  36.5 19.7 %all-to-all-start.1 = ((f32[128,8,128]{2,1,0:T(8,128)}), f32[128,8,128]{2,1,0:T(8,128)S(1)}, u32[]{:S(2)}, u32[]{:S(2)}) async-start(f32[128,8,128]{2,1,0:T(8,128)} %bitcast.3), calls=%async_computation.1 | async-start | bytes 1048576 | tf_op jit(solution)/shard_map/all_to_all | solution.py:421
  42.3 2.3 %collective-permute-start.5 = (f32[160,128]{1,0:T(8,128)S(1)}, f32[160,128]{1,0:T(8,128)S(1)}, u32[]{:S(2)}, u32[]{:S(2)}) collective-permute-start(f32[160,128]{1,0:T(8,128)S(1)} %get-tuple-element.14), channel_id=1, source_target_pairs={{0,1},{1,0},{2,3},{3,2},{4,5},{5,4},{6,7},{7,6},{8,9},{9,8},{10,11... | collective-permute-start | bytes 245768 | tf_op jit(solution)/shard_map/ppermute | solution.py:484
  44.5 0.7 copy-start.11
  45.2 10.9 %copy-start.4 = (bf16[256,512]{1,0:T(8,128)(2,1)S(1)}, bf16[256,512]{1,0:T(8,128)(2,1)}, u32[]{:S(2)}) copy-start(bf16[256,512]{1,0:T(8,128)(2,1)} %constant.13.clone.xf) | copy-start | bytes 786436
  45.2 10.9 %copy-start.6 = (bf16[256,256]{1,0:T(8,128)(2,1)S(1)}, bf16[256,256]{1,0:T(8,128)(2,1)}, u32[]{:S(2)}) copy-start(bf16[256,256]{1,0:T(8,128)(2,1)} %constant.14.clone.xi) | copy-start | bytes 393220
  57.9 17.9 %copy-start.5 = (bf16[256,256]{1,0:T(8,128)(2,1)S(1)}, bf16[256,256]{1,0:T(8,128)(2,1)}, u32[]{:S(2)}) copy-start(bf16[256,256]{1,0:T(8,128)(2,1)} %constant.12.clone.zi_far) | copy-start | bytes 393220

commit v15 on v14

--- a/solution.py
+++ b/solution.py
@@ -223,7 +223,7 @@
         def body(slot, carry, src=src, dst=dst):
             def store(field, new):
                 if dst is None:
-                    rows = pl.ds(pl.multiple_of(slot * 8, 8), 8)
+                    rows = pl.ds(slot * 9, 8)
                     for h in range(2):
                         last[field, h, rows, :] = new[:, 128 * h : 128 * h + 128]
                 else:
@@ -278,8 +278,8 @@
             for field in range(5):
                 at = 160 * half + 40 * x + 8 * field
                 for h in range(2):
-                    even = last[field, h, pl.ds(64 * half + 2 * x, 8, stride=8), :]
-                    odd = last[field, h, pl.ds(64 * half + 2 * x + 1, 8, stride=8), :]
+                    even = last[field, h, pl.ds(72 * half + 2 * x, 8, stride=9), :]
+                    odd = last[field, h, pl.ds(72 * half + 2 * x + 1, 8, stride=9), :]
                     sums[at : at + 8, 128 * h : 128 * h + 128] = even + odd
     value = sums[...]
     high = value.astype(BF16)
@@ -452,7 +452,7 @@
     near = lax.ppermute(near, "gy", [(j, j + 1 - 2 * (j % 2)) for j in range(8)])
     [last] = call(
         stencil,
-        [((5, 2, 128, 128), F32)],
+        [((5, 2, 144, 128), F32)],
         [VMEM] * 7,
         [
             pltpu.VMEM((5, 16, 16, 384), F32),

time: 78.4 us -> 78.4 us (level)
  no operation moved by 1% of the time
where the time goes in v15:
time: 78.4 us; the launch traced here: 78 us
  starting transfers between devices  26.2 us (33%)
  blocking collectives  17.9 us (23%)
  Pallas kernels  17.2 us (22%)
  waiting for transfers between devices  14.5 us (18%)
  local copies, waits for them, and re-layouts  1.92 us (2%)
    all_to_all x1, blocking collectives, exchange(): return lax.all_to_all(value, axis, split_axis=0, concat_axis=0, tiled=True)  17.9 us
    all_to_all x2, starting transfers between devices, exchange(): return lax.all_to_all(value, axis, split_axis=0, concat_axis=0, tiled=True)  17 us
    all_to_all x2, waiting for transfers between devices, exchange(): return lax.all_to_all(value, axis, split_axis=0, concat_axis=0, tiled=True)  7.75 us
    ppermute x1, waiting for transfers between devices, shards(): lax.ppermute(far, 'gy', [(j, (j - 1 + 2 * (j % 2)) % 8) for j in range(8)])  5.79 us
    ppermute x1, starting transfers between devices, shards(): lax.ppermute(far, 'gy', [(j, (j - 1 + 2 * (j % 2)) % 8) for j in range(8)])  4.63 us
    pallas_call x1, Pallas kernels, shards(): call(stencil, [((5, 2, 144, 128), F32)], [VMEM] * 7, [pltpu.VMEM((5, 16,...  3.92 us
    pallas_call x1, Pallas kernels, shards(): call(forward, [((160, 128), F32), ((160, 128), F32), ((1024, 128), F32)],...  3.84 us
    pallas_call x1, Pallas kernels, shards(): call(pointwise, [((8, 256, 128), F32)], [VMEM, VMEM, SMEM, SMEM, VMEM, VM...  3.18 us
  transfers between devices with their start and end apart: 8, of which 3 were waited for; matrix products, arithmetic and copies ran while one was open for 0% of the time, Pallas kernels for 12%

profile of v15, /device:TPU:1, one launch (start us, length us, event | category | flops | bytes accessed | tf_op | source)
XLA Modules:
  0.0 78.0 jit_solution(6157725931680851899)
XLA Ops:
  0.0 1.4 %collective-permute-start = (f32[5,128,256]{2,1,0:T(8,128)}, f32[5,128,256]{2,1,0:T(8,128)S(1)}, u32[]{:S(2)}, u32[]{:S(2)}) collective-permute-start(f32[5,128,256]{2,1,0:T(8,128)} %bitcast.8), channel_id=1, source_target_pairs={{0,1},{1,0},{2,3},{3,2},{4,5},{5,4},{6,7},{7,6},{8,9},{9,8},{10,11... | collective-permute-start | bytes 1966088 | tf_op jit(solution)/shard_map/ppermute | solution.py:427
  1.4 0.0 collective-permute-start.1
  1.4 0.0 copy-start.1
  1.4 1.2 %copy-done.1 = f32[4,4,32,4,128]{4,3,2,1,0:T(4,128)S(1)} copy-done((f32[4,4,32,4,128]{4,3,2,1,0:T(4,128)S(1)}, f32[4,4,32,4,128]{4,3,2,1,0:T(4,128)}, u32[]{:S(2)}) %copy-start.1) | copy-done | bytes 1048600
  2.7 0.0 copy-start
  2.7 0.0 copy-start.3
  2.7 1.6 %shard_map.118.after = bf16[64,32,128]{2,1,0:T(8,128)(2,1)} custom-call(f32[2048,128]{1,0:T(8,128)S(1)} %bitcast.15), custom_call_target="tpu_custom_call" | custom-call | flops 10000000 | bytes 1048576 | tf_op jit(solution)/shard_map/pallas_call | solution.py:430
  4.2 0.0 copy-done
  4.2 0.0 copy-done.3
  4.2 0.1 shard_map.119.own
  4.4 0.0 collective-permute-done.1.sp
  4.4 0.0 collective-permute-done.fp
  4.4 0.1 shard_map.120
  4.6 1.8 %collective-permute-start.2 = (f32[6,2,48,128]{3,2,1,0:T(8,128)S(1)}, f32[6,2,48,128]{3,2,1,0:T(8,128)S(1)}, u32[]{:S(2)}, u32[]{:S(2)}) collective-permute-start(f32[6,2,48,128]{3,2,1,0:T(8,128)S(1)} %shard_map.120), channel_id=1, source_target_pairs={{0,113},{16,1},{32,17},{48,33},{64,49},{80,65},{96,81},{112,97},{1... | collective-permute-start | bytes 884744 | tf_op jit(solution)/shard_map/ppermute | solution.py:439
  6.3 11.2 %all-to-all-start = ((bf16[64,32,128]{2,1,0:T(8,128)(2,1)}), bf16[64,32,128]{2,1,0:T(8,128)(2,1)}, u32[]{:S(2)}, u32[]{:S(2)}) async-start(bf16[64,32,128]{2,1,0:T(8,128)(2,1)} %shard_map.118.after), calls=%async_computation | async-start | bytes 1048576 | tf_op jit(solution)/shard_map/all_to_all | solution.py:421
  17.5 0.0 collective-permute-done.2.message.got
  17.5 0.5 shard_map.121
  18.1 4.6 %collective-permute-start.3 = (f32[3,16,128]{2,1,0:T(8,128)S(1)}, f32[3,16,128]{2,1,0:T(8,128)S(1)}, u32[]{:S(2)}, u32[]{:S(2)}) collective-permute-start(f32[3,16,128]{2,1,0:T(8,128)S(1)} %get-tuple-element.10), channel_id=1, source_target_pairs={{0,14},{2,4},{4,2},{6,8},{8,6},{10,12},{12,10},{14,0},{1,15},{3,5}... | collective-permute-start | bytes 73736 | tf_op jit(solution)/shard_map/ppermute | solution.py:451
  22.7 0.0 copy-start.7
  22.7 0.0 copy-start.8
  22.7 0.0 copy-start.10
  22.7 0.1 collective-permute-start.4
  22.8 5.8 %collective-permute-done.3.far = f32[3,16,128]{2,1,0:T(8,128)S(1)} collective-permute-done((f32[3,16,128]{2,1,0:T(8,128)S(1)}, f32[3,16,128]{2,1,0:T(8,128)S(1)}, u32[]{:S(2)}, u32[]{:S(2)}) %collective-permute-start.3) | collective-permute-done | bytes 24608 | tf_op jit(solution)/shard_map/ppermute | solution.py:451
  28.6 0.0 collective-permute-done.4.near
  28.6 3.9 %shard_map.122.last = f32[5,2,144,128]{3,2,1,0:T(8,128)S(1)} custom-call(f32[5,128,256]{2,1,0:T(8,128)S(1)} %bitcast.11, f32[128,256]{1,0:T(8,128)S(1)} %bitcast.19, f32[5,128,256]{2,1,0:T(8,128)S(1)} %collective-permute-done.fp, f32[128,256]{1,0:T(8,128)S(1)} %collective-permute-done.1.sp, f32[6,2,48,128]{3,2,1,0:T(8,128)S(1)} %collective-permute-done.2.message.got, ...), custom_call_target="tpu_custom_call" | custom-call | flops 10000000 | bytes 1048576 | tf_op jit(solution)/shard_map/pallas_call | solution.py:453
  32.5 0.0 all-to-all-done.after.weights_far
  32.5 0.0 copy-done.2
  32.6 0.0 copy-done.7
  32.6 0.0 copy-done.8
  32.6 0.0 copy-done.10
  32.6 3.8 %shard_map.123 = (f32[160,128]{1,0:T(8,128)S(1)}, f32[160,128]{1,0:T(8,128)S(1)}, f32[1024,128]{1,0:T(8,128)}) custom-call(f32[5,2,144,128]{3,2,1,0:T(8,128)S(1)} %shard_map.122.last, bf16[64,32,128]{2,1,0:T(8,128)(2,1)} %all-to-all-done.after.weights_far, f32[5,32]{1,0:T(8,128)S(1)} %copy-done.8, f32[32]{0:T(128)S(1)} %copy-done.10, ...), custom_call_target="tpu_custom_call" | custom-call | flops 10000000 | bytes 1048576 | tf_op jit(solution)/shard_map/pallas_call | solution.py:464
  36.4 0.0 copy-start.9
  36.5 5.8 %all-to-all-start.1 = ((f32[128,8,128]{2,1,0:T(8,128)}), f32[128,8,128]{2,1,0:T(8,128)S(1)}, u32[]{:S(2)}, u32[]{:S(2)}) async-start(f32[128,8,128]{2,1,0:T(8,128)} %bitcast.3), calls=%async_computation.1 | async-start | bytes 1048576 | tf_op jit(solution)/shard_map/all_to_all | solution.py:421
  42.3 1.3 %collective-permute-start.5 = (f32[160,128]{1,0:T(8,128)S(1)}, f32[160,128]{1,0:T(8,128)S(1)}, u32[]{:S(2)}, u32[]{:S(2)}) collective-permute-start(f32[160,128]{1,0:T(8,128)S(1)} %get-tuple-element.14), channel_id=1, source_target_pairs={{0,1},{1,0},{2,3},{3,2},{4,5},{5,4},{6,7},{7,6},{8,9},{9,8},{10,11... | collective-permute-start | bytes 245768 | tf_op jit(solution)/shard_map/ppermute | solution.py:484
  43.6 0.9 %collective-permute-done.5.got = f32[160,128]{1,0:T(8,128)S(1)} collective-permute-done((f32[160,128]{1,0:T(8,128)S(1)}, f32[160,128]{1,0:T(8,128)S(1)}, u32[]{:S(2)}, u32[]{:S(2)}) %collective-permute-start.5) | collective-permute-done | bytes 81952 | tf_op jit(solution)/shard_map/ppermute | solution.py:484
  44.5 0.0 copy-start.11
  44.5 0.0 copy-done.9
  44.5 0.7 copy-done.11
  45.2 0.0 copy-start.6
  45.2 3.2 %shard_map.124.after.direct = f32[8,256,128]{2,1,0:T(8,128)S(1)} custom-call(f32[160,128]{1,0:T(8,128)S(1)} %get-tuple-element.13.keep, f32[160,128]{1,0:T(8,128)S(1)} %collective-permute-done.5.got, f32[5,32]{1,0:T(8,128)S(1)} %copy-done.8, f32[32]{0:T(128)S(1)} %copy-done.10, bf16[32,32]{1,0:T(8,128)(2,1)S(1)} %copy-done.9, f32[1,32]{1,0:T(1,128)S(1)} %bitcast.20), custom_call_target="tpu_custom_call" | custom-call | flops 300000000 | bytes 1048576 | tf_op jit(solution)/shard_map/pallas_call | solution.py:478
  48.4 7.7 %all-to-all-done.1 = f32[128,8,128]{2,1,0:T(8,128)S(1)} async-done(((f32[128,8,128]{2,1,0:T(8,128)}), f32[128,8,128]{2,1,0:T(8,128)S(1)}, u32[]{:S(2)}, u32[]{:S(2)}) %all-to-all-start.1) | async-done | bytes 524320 | tf_op jit(solution)/shard_map/all_to_all | solution.py:421
  56.1 0.0 copy-done.4
  56.1 0.0 copy-done.6
  56.1 1.7 %shard_map.125 = bf16[8,8,2,16,128]{4,3,2,1,0:T(8,128)(2,1)S(1)} custom-call(f32[8,8,16,128]{3,2,1,0:T(8,128)S(1)} %bitcast.13, bf16[64,32,128]{2,1,0:T(8,128)(2,1)} %all-to-all-done.after.weights_far, bf16[256,512]{1,0:T(8,128)(2,1)S(1)} %copy-done.4, bf16[256,256]{1,0:T(8,128)(2,1)S(1)} %copy-done.6, f32[8,256,128]{2,1,0:T(8,128)S(1)} %shard_map.124.after.direct), custom_call_target="tpu_custom_call" | custom-call | flops 10000000 | bytes 1048576 | tf_op jit(solution)/shard_map/pallas_call | solution.py:486
  57.9 0.0 copy-start.5
  57.9 17.9 %all_to_all.15 = bf16[128,16,128]{2,1,0:T(8,128)(2,1)S(1)} all-to-all(bf16[128,16,128]{2,1,0:T(8,128)(2,1)S(1)} %bitcast.14), channel_id=1, replica_groups=mesh['gx'=8,'gy'=8,'ga'=2] {'gx','gy','ga'}, dimensions={0} | all-to-all | bytes 1048576 | tf_op jit(solution)/shard_map/all_to_all | solution.py:421
  75.8 0.0 copy-done.5
  75.8 2.1 %shard_map.126 = bf16[8,32,8,128]{3,2,1,0:T(8,128)(2,1)} custom-call(bf16[2048,128]{1,0:T(8,128)(2,1)S(1)} %bitcast.12, f32[8,256,128]{2,1,0:T(8,128)S(1)} %shard_map.124.after.direct, bf16[8,128,128]{2,1,0:T(8,128)(2,1)S(1)} %copy-done.2, bf16[256,256]{1,0:T(8,128)(2,1)S(1)} %copy-done.5), custom_call_target="tpu_custom_call" | custom-call | flops 10000000 | bytes 1048576 | tf_op jit(solution)/shard_map/pallas_call | solution.py:493
  (2 shorter events, 0.0 us)
Async XLA Ops:
  0.0 4.4 %collective-permute-start = (f32[5,128,256]{2,1,0:T(8,128)}, f32[5,128,256]{2,1,0:T(8,128)S(1)}, u32[]{:S(2)}, u32[]{:S(2)}) collective-permute-start(f32[5,128,256]{2,1,0:T(8,128)} %bitcast.8), channel_id=1, source_target_pairs={{0,1},{1,0},{2,3},{3,2},{4,5},{5,4},{6,7},{7,6},{8,9},{9,8},{10,11... | collective-permute-start | bytes 1966088 | tf_op jit(solution)/shard_map/ppermute | solution.py:427
  1.4 3.0 %collective-permute-start.1 = (f32[128,256]{1,0:T(8,128)}, f32[128,256]{1,0:T(8,128)S(1)}, u32[]{:S(2)}, u32[]{:S(2)}) collective-permute-start(f32[128,256]{1,0:T(8,128)} %bitcast.16), channel_id=1, source_target_pairs={{0,1},{1,0},{2,3},{3,2},{4,5},{5,4},{6,7},{7,6},{8,9},{9,8},{10,11... | collective-permute-start | bytes 393224 | tf_op jit(solution)/shard_map/ppermute | solution.py:427
  1.4 1.2 %copy-start.1 = (f32[4,4,32,4,128]{4,3,2,1,0:T(4,128)S(1)}, f32[4,4,32,4,128]{4,3,2,1,0:T(4,128)}, u32[]{:S(2)}) copy-start(f32[4,4,32,4,128]{4,3,2,1,0:T(4,128)} %param.17) | copy-start | bytes 3145732
  2.7 1.6 %copy-start = (f32[5,8,16,256]{3,2,1,0:T(8,128)S(1)}, f32[5,8,16,256]{3,2,1,0:T(8,128)}, u32[]{:S(2)}) copy-start(f32[5,8,16,256]{3,2,1,0:T(8,128)} %param.12) | copy-start | bytes 1966084
  2.7 1.6 %copy-start.3 = (f32[8,16,256]{2,1,0:T(8,128)S(1)}, f32[8,16,256]{2,1,0:T(8,128)}, u32[]{:S(2)}) copy-start(f32[8,16,256]{2,1,0:T(8,128)} %param.13) | copy-start | bytes 393220
  4.6 13.0 %collective-permute-start.2 = (f32[6,2,48,128]{3,2,1,0:T(8,128)S(1)}, f32[6,2,48,128]{3,2,1,0:T(8,128)S(1)}, u32[]{:S(2)}, u32[]{:S(2)}) collective-permute-start(f32[6,2,48,128]{3,2,1,0:T(8,128)S(1)} %shard_map.120), channel_id=1, source_target_pairs={{0,113},{16,1},{32,17},{48,33},{64,49},{80,65},{96,81},{112,97},{1... | collective-permute-start | bytes 884744 | tf_op jit(solution)/shard_map/ppermute | solution.py:439
  6.3 26.2 %all-to-all-start = ((bf16[64,32,128]{2,1,0:T(8,128)(2,1)}), bf16[64,32,128]{2,1,0:T(8,128)(2,1)}, u32[]{:S(2)}, u32[]{:S(2)}) async-start(bf16[64,32,128]{2,1,0:T(8,128)(2,1)} %shard_map.118.after), calls=%async_computation | async-start | bytes 1048576 | tf_op jit(solution)/shard_map/all_to_all | solution.py:421
  18.1 10.5 %collective-permute-start.3 = (f32[3,16,128]{2,1,0:T(8,128)S(1)}, f32[3,16,128]{2,1,0:T(8,128)S(1)}, u32[]{:S(2)}, u32[]{:S(2)}) collective-permute-start(f32[3,16,128]{2,1,0:T(8,128)S(1)} %get-tuple-element.10), channel_id=1, source_target_pairs={{0,14},{2,4},{4,2},{6,8},{8,6},{10,12},{12,10},{14,0},{1,15},{3,5}... | collective-permute-start | bytes 73736 | tf_op jit(solution)/shard_map/ppermute | solution.py:451
  22.7 9.8 %copy-start.2 = (bf16[8,128,128]{2,1,0:T(8,128)(2,1)S(1)}, bf16[8,128,128]{2,1,0:T(8,128)(2,1)}, u32[]{:S(2)}) copy-start(bf16[8,128,128]{2,1,0:T(8,128)(2,1)} %constant.10.clone.yf_far.yi_far) | copy-start | bytes 786436
  22.7 9.8 %copy-start.7 = (bf16[256,256]{1,0:T(8,128)(2,1)S(1)}, bf16[256,256]{1,0:T(8,128)(2,1)}, u32[]{:S(2)}) copy-start(bf16[256,256]{1,0:T(8,128)(2,1)} %constant.11.clone.zf_far) | copy-start | bytes 393220
  22.7 9.9 %copy-start.8 = (f32[5,32]{1,0:T(8,128)S(1)}, f32[5,32]{1,0:T(8,128)}, u32[]{:S(2)}) copy-start(f32[5,32]{1,0:T(8,128)} %weight.3) | copy-start | bytes 1924
  22.7 9.9 %copy-start.10 = (f32[32]{0:T(128)S(1)}, f32[32]{0:T(128)}, u32[]{:S(2)}) copy-start(f32[32]{0:T(128)} %bias.3) | copy-start | bytes 388
  22.7 5.9 %collective-permute-start.4 = (f32[3,16,128]{2,1,0:T(8,128)S(1)}, f32[3,16,128]{2,1,0:T(8,128)S(1)}, u32[]{:S(2)}, u32[]{:S(2)}) collective-permute-start(f32[3,16,128]{2,1,0:T(8,128)S(1)} %get-tuple-element.11), channel_id=1, source_target_pairs={{0,2},{2,0},{4,6},{6,4},{8,10},{10,8},{12,14},{14,12},{1,3},{3,1},... | collective-permute-start | bytes 73736 | tf_op jit(solution)/shard_map/ppermute | solution.py:452
  36.4 8.1 %copy-start.9 = (bf16[32,32]{1,0:T(8,128)(2,1)S(1)}, bf16[32,32]{1,0:T(8,128)(2,1)}, u32[]{:S(2)}) copy-start(bf16[32,32]{1,0:T(8,128)(2,1)} %mix.1) | copy-start | bytes 6148
  36.5 19.7 %all-to-all-start.1 = ((f32[128,8,128]{2,1,0:T(8,128)}), f32[128,8,128]{2,1,0:T(8,128)S(1)}, u32[]{:S(2)}, u32[]{:S(2)}) async-start(f32[128,8,128]{2,1,0:T(8,128)} %bitcast.3), calls=%async_computation.1 | async-start | bytes 1048576 | tf_op jit(solution)/shard_map/all_to_all | solution.py:421
  42.3 2.3 %collective-permute-start.5 = (f32[160,128]{1,0:T(8,128)S(1)}, f32[160,128]{1,0:T(8,128)S(1)}, u32[]{:S(2)}, u32[]{:S(2)}) collective-permute-start(f32[160,128]{1,0:T(8,128)S(1)} %get-tuple-element.14), channel_id=1, source_target_pairs={{0,1},{1,0},{2,3},{3,2},{4,5},{5,4},{6,7},{7,6},{8,9},{9,8},{10,11... | collective-permute-start | bytes 245768 | tf_op jit(solution)/shard_map/ppermute | solution.py:484
  44.5 0.7 copy-start.11
  45.2 10.9 %copy-start.4 = (bf16[256,512]{1,0:T(8,128)(2,1)S(1)}, bf16[256,512]{1,0:T(8,128)(2,1)}, u32[]{:S(2)}) copy-start(bf16[256,512]{1,0:T(8,128)(2,1)} %constant.13.clone.xf) | copy-start | bytes 786436
  45.2 10.9 %copy-start.6 = (bf16[256,256]{1,0:T(8,128)(2,1)S(1)}, bf16[256,256]{1,0:T(8,128)(2,1)}, u32[]{:S(2)}) copy-start(bf16[256,256]{1,0:T(8,128)(2,1)} %constant.14.clone.xi) | copy-start | bytes 393220
  57.9 17.9 %copy-start.5 = (bf16[256,256]{1,0:T(8,128)(2,1)S(1)}, bf16[256,256]{1,0:T(8,128)(2,1)}, u32[]{:S(2)}) copy-start(bf16[256,256]{1,0:T(8,128)(2,1)} %constant.12.clone.zi_far) | copy-start | bytes 393220
